TPU v7x, 32 devices: a whole 2x2x4 slice. The times are simulated.
32 devices in a mesh: dp: 4 (over y, x), seq: 4 (over z), head: 2 (over core).
Axes of the slice: x: 2, y: 2, z: 4, core: 2. Of those that a mesh axis runs over, the one named last changes fastest.
Arguments:
- tokens_in: bfloat16 [4, 1024, 2048], P('dp', 'seq', 'head'), may hold values from -6 to 6
- lengths: int32 [4], P('dp'), may hold values from 256 to 1024, as said below
- first_gain: bfloat16 [2048], P('head'), may hold values from 0.25 to 1.75
- query_weight: bfloat16 [2048, 2048], P(None, 'head'), may hold values from -0.125 to 0.125
- key_weight: bfloat16 [2048, 2048], P(None, 'head'), may hold values from -0.125 to 0.125
- value_weight: bfloat16 [2048, 2048], P(None, 'head'), may hold values from -0.125 to 0.125
- beta_weight: bfloat16 [2048, 16], P(None, 'head'), may hold values from -0.125 to 0.125
- query_conv: bfloat16 [4, 2048], P(None, 'head'), may hold values from -3 to 3
- key_conv: bfloat16 [4, 2048], P(None, 'head'), may hold values from -3 to 3
- value_conv: bfloat16 [4, 2048], P(None, 'head'), may hold values from -3 to 3
- mixer_gain: bfloat16 [128], replicated, may hold values from 0.25 to 1.75
- output_weight: bfloat16 [2048, 2048], P('head'), may hold values from -0.125 to 0.125
- second_gain: bfloat16 [2048], P('head'), may hold values from 0.25 to 1.75
- gate_weight: bfloat16 [2048, 5632], P(None, 'head'), may hold values from -0.125 to 0.125
- up_weight: bfloat16 [2048, 5632], P(None, 'head'), may hold values from -0.125 to 0.125
- down_weight: bfloat16 [5632, 2048], P('head'), may hold values from -0.078125 to 0.078125
- upstream: bfloat16 [4, 1024, 2048], P('dp', 'seq', 'head'), may hold values from -6 to 6
Outputs:
- layer_out: bfloat16 [4, 1024, 2048], P('dp', 'seq', 'head')
- grad_tokens: float32 [4, 1024, 2048], P('dp', 'seq', 'head')
- grad_first_gain: float32 [2048], P('head')
- grad_query_weight: float32 [2048, 2048], P(('dp', 'seq'), 'head')
- grad_key_weight: float32 [2048, 2048], P(('dp', 'seq'), 'head')
- grad_value_weight: float32 [2048, 2048], P(('dp', 'seq'), 'head')
- grad_beta_weight: float32 [2048, 16], P(('dp', 'seq'), 'head')
- grad_query_conv: float32 [4, 2048], P(None, 'head')
- grad_key_conv: float32 [4, 2048], P(None, 'head')
- grad_value_conv: float32 [4, 2048], P(None, 'head')
- grad_mixer_gain: float32 [128], replicated
- grad_output_weight: float32 [2048, 2048], P('head', ('dp', 'seq'))
- grad_second_gain: float32 [2048], P('head')
- grad_gate_weight: float32 [2048, 5632], P(('dp', 'seq'), 'head')
- grad_up_weight: float32 [2048, 5632], P(('dp', 'seq'), 'head')
- grad_down_weight: float32 [5632, 2048], P('head', ('dp', 'seq'))
Inputs may be any that keep to these rules, and one draw needn't show every extreme that they name: `lengths`: among the 1 row of each index of dp, one holds a sequence of 1024 tokens; every row's positions from its length on are padding.
All inputs are finite; a program needn't handle non-finite values.
Results may differ from a plain program's by a relative error of at most 0.025.
Values may be sent and summed in bfloat16 or wider, within the bound.
A program may use at most 256 MiB of HBM per device.

v0:
```python
import jax
import jax.numpy as jnp
from jax import lax
from jax.sharding import PartitionSpec as P

HEAD_DIM = 128
STRETCH = 64


HIGH = lax.Precision.HIGHEST
EPSILON = 1e-05
UNIT_EPSILON = 1e-06


def passed_along(value, axis, by):
    peers = lax.axis_size(axis)
    pairs = [(i, i + by) for i in range(peers) if 0 <= i + by < peers]
    return lax.ppermute(value, axis, pairs)


def prefix_2(value, axis, combine, identity, reverse):
    peers, position = (lax.axis_size(axis), lax.axis_index(axis))
    everything = jax.tree.map(
        lambda part, kind: lax.all_gather(part.astype(kind), axis),
        value,
        jax.tree.map(lambda a: jnp.bfloat16 if a.dtype == jnp.float32 else a.dtype, value),
    )
    start = jax.tree.map(
        lambda part, zero: jnp.broadcast_to(jnp.asarray(zero, part.dtype), part.shape),
        value,
        identity,
    )

    def turn(k, before):
        at = peers - 1 - k if reverse else k
        reached = at > position if reverse else at < position
        new = combine(
            before, jax.tree.map(lambda part, own: part[at].astype(own.dtype), everything, value)
        )
        return jax.tree.map(lambda a, b: jnp.where(reached, a, b), new, before)

    return lax.fori_loop(0, peers, turn, start)


def inverse_rms(values):
    return lax.rsqrt(jnp.mean(values * values, axis=-1, keepdims=True) + EPSILON)


def unit_rows(values):
    return values * lax.rsqrt(jnp.sum(values * values, axis=-1, keepdims=True) + UNIT_EPSILON)


def round_trip(values):
    return lax.optimization_barrier(values.astype(jnp.bfloat16)).astype(jnp.float32)


def mixer_inputs(padded, beta_logit, kernels, live_mask, head_size):
    local_len = live_mask.shape[-1]
    tap_count = kernels.shape[0]
    seq_axis = padded.ndim - 2
    summed = kernels[0] * lax.slice_in_dim(padded, 0, local_len, axis=seq_axis)
    for tap_index in range(1, tap_count):
        summed = summed + kernels[tap_index] * lax.slice_in_dim(
            padded, tap_index, tap_index + local_len, axis=seq_axis
        )
    active = jax.nn.silu(summed)
    channels = active.shape[-1] // 3
    head_shape = active.shape[:-1] + (channels // head_size, head_size)
    query = unit_rows(active[..., :channels].reshape(head_shape))
    key_rows = (
        unit_rows(active[..., channels : 2 * channels].reshape(head_shape))
        * live_mask[..., None, None]
    )
    value_rows = active[..., 2 * channels :].reshape(head_shape)
    beta = jax.nn.sigmoid(beta_logit) * live_mask[..., None]
    return (query, key_rows, value_rows, beta)


def prepare(key_rows, value_rows, beta):
    block_size = key_rows.shape[-2]
    head_size = key_rows.shape[-1]
    gram = jnp.einsum("...cd,...ed->...ce", key_rows, key_rows, precision=HIGH)
    strict = jnp.tril(jnp.ones((block_size, block_size), jnp.float32), -1)
    system = jnp.eye(block_size, dtype=jnp.float32) + beta[..., :, None] * gram * strict
    weighted = beta[..., :, None] * jnp.concatenate([key_rows, value_rows], -1)
    solved = lax.linalg.triangular_solve(
        system, weighted, left_side=True, lower=True, unit_diagonal=True
    )
    return (solved[..., :head_size], solved[..., head_size:])


def block_step(state, block):
    query, key_rows, wy_keys, wy_values = block
    block_size = query.shape[-2]
    causal = jnp.tril(jnp.ones((block_size, block_size), jnp.float32))
    fresh = wy_values - jnp.einsum("...cd,...de->...ce", wy_keys, state, precision=HIGH)
    scores = jnp.einsum("...cd,...ed->...ce", query, key_rows, precision=HIGH) * causal
    mixed = jnp.einsum("...cd,...de->...ce", query, state, precision=HIGH) + jnp.einsum(
        "...ce,...ed->...cd", scores, fresh, precision=HIGH
    )
    state = state + jnp.einsum("...cd,...ce->...de", key_rows, fresh, precision=HIGH)
    return (state, mixed)


def run_blocks(query, key_rows, wy_keys, wy_values, state):
    moved = tuple((jnp.moveaxis(item, -3, 0) for item in (query, key_rows, wy_keys, wy_values)))
    state, mixed = lax.scan(block_step, state, moved)
    return (jnp.moveaxis(mixed, 0, -3), state)


def compose(earlier, later):
    first_map, first_shift = earlier
    next_map, next_shift = later
    joined_map = jnp.einsum("...ij,...jk->...ik", next_map, first_map, precision=HIGH)
    joined_shift = (
        jnp.einsum("...ij,...jk->...ik", next_map, first_shift, precision=HIGH) + next_shift
    )
    return (joined_map, joined_shift)


def device_map(key_rows, wy_keys, wy_values):
    head_size = key_rows.shape[-1]
    unit = jnp.eye(head_size, dtype=jnp.float32)
    block_maps = unit - jnp.einsum("...cd,...ce->...de", key_rows, wy_keys, precision=HIGH)
    block_shifts = jnp.einsum("...cd,...ce->...de", key_rows, wy_values, precision=HIGH)
    lead_shape = block_maps.shape[:-3] + (head_size, head_size)
    start = (jnp.broadcast_to(unit, lead_shape), jnp.zeros(lead_shape, jnp.float32))

    def fold_block(carry, block):
        return (compose(carry, block), None)

    total, unused = lax.scan(
        fold_block, start, (jnp.moveaxis(block_maps, -3, 0), jnp.moveaxis(block_shifts, -3, 0))
    )
    return total


def head_blocks(values):
    num_rows, local_len, local_heads, head_size = values.shape
    shaped = values.reshape(num_rows, local_len // STRETCH, STRETCH, local_heads, head_size)
    return shaped.transpose(0, 3, 1, 2, 4)


def seq_layout(values):
    num_rows, local_heads, blocks, block_size, head_size = values.shape
    return values.transpose(0, 2, 3, 1, 4).reshape(
        num_rows, blocks * block_size, local_heads, head_size
    )


def beta_blocks(values):
    num_rows, local_len, local_heads = values.shape
    return values.reshape(num_rows, local_len // STRETCH, STRETCH, local_heads).transpose(
        0, 3, 1, 2
    )


def beta_layout(values):
    num_rows, local_heads, blocks, block_size = values.shape
    return values.transpose(0, 2, 3, 1).reshape(num_rows, blocks * block_size, local_heads)


def mixer_norm(mixed_seq, gain):
    return mixed_seq * inverse_rms(mixed_seq) * gain


def shards(
    tokens_in,
    lengths,
    first_gain,
    query_weight,
    key_weight,
    value_weight,
    beta_weight,
    query_conv,
    key_conv,
    value_conv,
    mixer_gain,
    output_weight,
    second_gain,
    gate_weight,
    up_weight,
    down_weight,
    upstream,
):
    num_rows, local_len, local_width = tokens_in.shape
    full_width = query_weight.shape[0]
    channels = query_weight.shape[1]
    local_heads = beta_weight.shape[1]
    groups = lax.axis_size("head")
    shares = lax.axis_size("dp") * lax.axis_size("seq")
    rim_len = query_conv.shape[0] - 1
    positions = lax.axis_index("seq") * local_len + jnp.arange(local_len, dtype=jnp.int32)
    live_mask = (positions[None, :] < lengths[:, None]).astype(jnp.float32)
    gathered, gain_one, gain_two = (
        lax.all_gather(tokens_in, "head", axis=2, tiled=True),
        lax.all_gather(first_gain, "head", axis=0, tiled=True),
        lax.all_gather(second_gain, "head", axis=0, tiled=True),
    )
    stream_full = gathered.astype(jnp.float32)
    gain_one = gain_one.astype(jnp.float32)
    gain_two = gain_two.astype(jnp.float32)
    scale_one = inverse_rms(stream_full)
    normed_one = (stream_full * scale_one * gain_one).astype(jnp.bfloat16)
    pre_act = jnp.concatenate(
        [
            jnp.dot(normed_one, query_weight, preferred_element_type=jnp.float32),
            jnp.dot(normed_one, key_weight, preferred_element_type=jnp.float32),
            jnp.dot(normed_one, value_weight, preferred_element_type=jnp.float32),
        ],
        2,
    ).astype(jnp.bfloat16)
    beta_logit = jnp.dot(normed_one, beta_weight, preferred_element_type=jnp.float32)
    carried_rim = passed_along(pre_act[:, local_len - rim_len :, :], "seq", 1)
    pre_ext = jnp.concatenate([carried_rim, pre_act], 1).astype(jnp.float32)
    kernels = jnp.concatenate([query_conv, key_conv, value_conv], 1).astype(jnp.float32)

    def inputs_fn(padded, logits, weights):
        return mixer_inputs(padded, logits, weights, live_mask, HEAD_DIM)

    mixer_in, pull_inputs = jax.vjp(inputs_fn, pre_ext, beta_logit, kernels)
    query_blk = head_blocks(round_trip(mixer_in[0]))
    key_blk = head_blocks(round_trip(mixer_in[1]))
    value_blk = head_blocks(round_trip(mixer_in[2]))
    beta_blk = beta_blocks(mixer_in[3])
    wy_pair, pull_prep = jax.vjp(prepare, key_blk, value_blk, beta_blk)
    device_maps = device_map(key_blk, wy_pair[0], wy_pair[1])
    identity = (
        jnp.broadcast_to(jnp.eye(HEAD_DIM, dtype=jnp.float32), device_maps[0].shape),
        jnp.zeros_like(device_maps[1]),
    )
    prefix = prefix_2(device_maps, "seq", compose, identity, False)
    mixed_pair, pull_blocks = jax.vjp(
        run_blocks, query_blk, key_blk, wy_pair[0], wy_pair[1], prefix[1]
    )
    mixed_seq = seq_layout(mixed_pair[0])
    normed_mix, pull_norm = jax.vjp(mixer_norm, mixed_seq, mixer_gain.astype(jnp.float32))
    head_out = normed_mix.reshape(num_rows, local_len, channels).astype(jnp.bfloat16)
    mixer_part = jnp.dot(head_out, output_weight, preferred_element_type=jnp.float32)
    stream_local = tokens_in.astype(jnp.float32) + lax.psum_scatter(
        mixer_part.astype(jnp.bfloat16), "head", scatter_dimension=2, tiled=True
    ).astype(jnp.float32)
    stream_mid = lax.all_gather(
        stream_local.astype(jnp.bfloat16), "head", axis=2, tiled=True
    ).astype(stream_local.dtype)
    scale_two = inverse_rms(stream_mid)
    normed_two = (stream_mid * scale_two * gain_two).astype(jnp.bfloat16)
    gate_pre = jnp.dot(normed_two, gate_weight, preferred_element_type=jnp.float32)
    up_pre = jnp.dot(normed_two, up_weight, preferred_element_type=jnp.float32)
    hidden = (jax.nn.silu(gate_pre) * up_pre).astype(jnp.bfloat16)
    feed_part = jnp.dot(hidden, down_weight, preferred_element_type=jnp.float32)
    feed_local = lax.psum_scatter(
        feed_part.astype(jnp.bfloat16), "head", scatter_dimension=2, tiled=True
    ).astype(jnp.float32)
    layer_out = (stream_local + feed_local).astype(jnp.bfloat16)
    masked_up = upstream * live_mask[..., None].astype(jnp.bfloat16)
    upstream_full = lax.all_gather(masked_up, "head", axis=2, tiled=True)
    d_hidden = jnp.einsum(
        "rsd,fd->rsf", upstream_full, down_weight, preferred_element_type=jnp.float32
    )
    grad_down_part = jnp.einsum(
        "rsd,rsf->df", upstream_full, hidden, preferred_element_type=jnp.float32
    )
    gate_sig = jax.nn.sigmoid(gate_pre)
    d_gate = (d_hidden * up_pre * gate_sig * (1.0 + gate_pre * (1.0 - gate_sig))).astype(
        jnp.bfloat16
    )
    d_up = (d_hidden * gate_pre * gate_sig).astype(jnp.bfloat16)
    d_normed_two = jnp.einsum(
        "rsf,df->rsd", d_gate, gate_weight, preferred_element_type=jnp.float32
    ) + jnp.einsum("rsf,df->rsd", d_up, up_weight, preferred_element_type=jnp.float32)
    grad_gate_part = jnp.einsum(
        "rsd,rsf->df", normed_two, d_gate, preferred_element_type=jnp.float32
    )
    grad_up_part = jnp.einsum("rsd,rsf->df", normed_two, d_up, preferred_element_type=jnp.float32)
    stat_two = jnp.sum(d_normed_two * stream_mid * gain_two, axis=-1, keepdims=True)
    d_two_local, stat_two_sum = (
        lax.psum_scatter(
            d_normed_two.astype(jnp.bfloat16), "head", scatter_dimension=2, tiled=True
        ).astype(jnp.float32),
        lax.psum_scatter(
            jnp.broadcast_to(stat_two, (num_rows, local_len, groups)).astype(jnp.bfloat16),
            "head",
            scatter_dimension=2,
            tiled=True,
        ).astype(jnp.float32),
    )
    second_local = second_gain.astype(jnp.float32)
    d_stream = (
        masked_up.astype(jnp.float32)
        + scale_two * second_local * d_two_local
        - stream_local * scale_two * scale_two * scale_two * stat_two_sum / full_width
    )
    grad_second = jnp.sum(d_two_local * stream_local * scale_two, axis=(0, 1))
    d_stream_low = d_stream.astype(jnp.bfloat16)
    residual_full = lax.all_gather(d_stream_low, "head", axis=2, tiled=True)
    d_head_out = jnp.einsum(
        "rsd,cd->rsc", residual_full, output_weight, preferred_element_type=jnp.float32
    )
    grad_out_part = jnp.einsum(
        "rsd,rsc->dc", residual_full, head_out, preferred_element_type=jnp.float32
    )
    d_mixed_seq, grad_gain_part = pull_norm(
        d_head_out.reshape(num_rows, local_len, local_heads, HEAD_DIM)
    )
    d_mixed_blk = head_blocks(d_mixed_seq)
    first_pass = pull_blocks((d_mixed_blk, jnp.zeros_like(prefix[1])))
    reverse_maps = (jnp.swapaxes(device_maps[0], -1, -2), first_pass[4])
    suffix = prefix_2(reverse_maps, "seq", compose, identity, True)
    second_pass = pull_blocks((jnp.zeros_like(d_mixed_blk), suffix[1]))
    d_query_blk = first_pass[0] + second_pass[0]
    d_key_blk = first_pass[1] + second_pass[1]
    d_wy_keys = first_pass[2] + second_pass[2]
    d_wy_values = first_pass[3] + second_pass[3]
    d_key_prep, d_value_blk, d_beta_blk = pull_prep((d_wy_keys, d_wy_values))
    d_mixer_in = (
        seq_layout(d_query_blk),
        seq_layout(d_key_blk + d_key_prep),
        seq_layout(d_value_blk),
        beta_layout(d_beta_blk),
    )
    d_pre_ext, d_beta_logit, grad_kernels = pull_inputs(d_mixer_in)
    rim_grad = passed_along(d_pre_ext[:, :rim_len, :], "seq", -1)
    d_pre_own = d_pre_ext[:, rim_len:, :]
    d_pre = jnp.concatenate(
        [d_pre_own[:, : local_len - rim_len, :], d_pre_own[:, local_len - rim_len :, :] + rim_grad],
        1,
    ).astype(jnp.bfloat16)
    d_logit_low = d_beta_logit.astype(jnp.bfloat16)
    d_pre_query = d_pre[..., :channels]
    d_pre_key = d_pre[..., channels : 2 * channels]
    d_pre_value = d_pre[..., 2 * channels :]
    d_normed_one = (
        jnp.einsum("rsc,dc->rsd", d_pre_query, query_weight, preferred_element_type=jnp.float32)
        + jnp.einsum("rsc,dc->rsd", d_pre_key, key_weight, preferred_element_type=jnp.float32)
        + jnp.einsum("rsc,dc->rsd", d_pre_value, value_weight, preferred_element_type=jnp.float32)
        + jnp.einsum("rsh,dh->rsd", d_logit_low, beta_weight, preferred_element_type=jnp.float32)
    )
    grad_query_part = jnp.einsum(
        "rsd,rsc->dc", normed_one, d_pre_query, preferred_element_type=jnp.float32
    )
    grad_key_part = jnp.einsum(
        "rsd,rsc->dc", normed_one, d_pre_key, preferred_element_type=jnp.float32
    )
    grad_value_part = jnp.einsum(
        "rsd,rsc->dc", normed_one, d_pre_value, preferred_element_type=jnp.float32
    )
    grad_beta_part = jnp.einsum(
        "rsd,rsh->dh", normed_one, d_logit_low, preferred_element_type=jnp.float32
    )
    stat_one = jnp.sum(d_normed_one * stream_full * gain_one, axis=-1, keepdims=True)
    gain_spread = jnp.broadcast_to(grad_gain_part[None, :, None], (1, HEAD_DIM, groups))
    d_one_local, stat_one_sum, gain_total = (
        lax.psum_scatter(
            d_normed_one.astype(jnp.bfloat16), "head", scatter_dimension=2, tiled=True
        ).astype(jnp.float32),
        lax.psum_scatter(
            jnp.broadcast_to(stat_one, (num_rows, local_len, groups)).astype(jnp.bfloat16),
            "head",
            scatter_dimension=2,
            tiled=True,
        ).astype(jnp.float32),
        lax.psum_scatter(
            gain_spread.astype(jnp.bfloat16), "head", scatter_dimension=2, tiled=True
        ).astype(jnp.float32),
    )
    tokens_local = tokens_in.astype(jnp.float32)
    first_local = first_gain.astype(jnp.float32)
    grad_tokens = (
        d_stream
        + scale_one * first_local * d_one_local
        - tokens_local * scale_one * scale_one * scale_one * stat_one_sum / full_width
    )
    grad_first = jnp.sum(d_one_local * tokens_local * scale_one, axis=(0, 1))

    def spread_rows(values):
        return jnp.broadcast_to(values[None], (shares,) + values.shape)

    reduced = (
        lax.psum_scatter(
            grad_query_part.astype(jnp.bfloat16), ("dp", "seq"), scatter_dimension=0, tiled=True
        ).astype(jnp.float32),
        lax.psum_scatter(
            grad_key_part.astype(jnp.bfloat16), ("dp", "seq"), scatter_dimension=0, tiled=True
        ).astype(jnp.float32),
        lax.psum_scatter(
            grad_value_part.astype(jnp.bfloat16), ("dp", "seq"), scatter_dimension=0, tiled=True
        ).astype(jnp.float32),
        lax.psum_scatter(
            grad_beta_part.astype(jnp.bfloat16), ("dp", "seq"), scatter_dimension=0, tiled=True
        ).astype(jnp.float32),
        lax.psum_scatter(
            grad_gate_part.astype(jnp.bfloat16), ("dp", "seq"), scatter_dimension=0, tiled=True
        ).astype(jnp.float32),
        lax.psum_scatter(
            grad_up_part.astype(jnp.bfloat16), ("dp", "seq"), scatter_dimension=0, tiled=True
        ).astype(jnp.float32),
        lax.psum_scatter(
            grad_out_part.astype(jnp.bfloat16), ("dp", "seq"), scatter_dimension=0, tiled=True
        ).astype(jnp.float32),
        lax.psum_scatter(
            grad_down_part.astype(jnp.bfloat16), ("dp", "seq"), scatter_dimension=0, tiled=True
        ).astype(jnp.float32),
        lax.psum_scatter(
            spread_rows(grad_first).astype(jnp.bfloat16),
            ("dp", "seq"),
            scatter_dimension=0,
            tiled=True,
        ).astype(jnp.float32),
        lax.psum_scatter(
            spread_rows(grad_kernels).astype(jnp.bfloat16),
            ("dp", "seq"),
            scatter_dimension=0,
            tiled=True,
        ).astype(jnp.float32),
        lax.psum_scatter(
            spread_rows(gain_total.reshape(HEAD_DIM)).astype(jnp.bfloat16),
            ("dp", "seq"),
            scatter_dimension=0,
            tiled=True,
        ).astype(jnp.float32),
        lax.psum_scatter(
            spread_rows(grad_second).astype(jnp.bfloat16),
            ("dp", "seq"),
            scatter_dimension=0,
            tiled=True,
        ).astype(jnp.float32),
    )
    kernel_sum = reduced[9][0]
    return (
        layer_out,
        grad_tokens,
        reduced[8][0],
        reduced[0],
        reduced[1],
        reduced[2],
        reduced[3],
        kernel_sum[:, :channels],
        kernel_sum[:, channels : 2 * channels],
        kernel_sum[:, 2 * channels :],
        reduced[10][0],
        reduced[6].T,
        reduced[11][0],
        reduced[4],
        reduced[5],
        reduced[7].T,
    )


def solution(mesh):
    placed = (
        P("dp", "seq", "head"),
        P("dp"),
        P("head"),
        P(None, "head"),
        P(None, "head"),
        P(None, "head"),
        P(None, "head"),
        P(None, "head"),
        P(None, "head"),
        P(None, "head"),
        P(),
        P("head", None),
        P("head"),
        P(None, "head"),
        P(None, "head"),
        P("head", None),
        P("dp", "seq", "head"),
    )
    return jax.shard_map(
        shards,
        mesh=mesh,
        in_specs=placed,
        out_specs=(
            P("dp", "seq", "head"),
            P("dp", "seq", "head"),
            P("head"),
            P(("dp", "seq"), "head"),
            P(("dp", "seq"), "head"),
            P(("dp", "seq"), "head"),
            P(("dp", "seq"), "head"),
            P(None, "head"),
            P(None, "head"),
            P(None, "head"),
            P(),
            P("head", ("dp", "seq")),
            P("head"),
            P(("dp", "seq"), "head"),
            P(("dp", "seq"), "head"),
            P("head", ("dp", "seq")),
        ),
        check_vma=False,
    )
```

profile of v0, /device:TPU:0, one launch (start us, length us, event | category | flops | bytes accessed | tf_op | source)
XLA Modules:
  0.0 2100.4 jit_solution(18041772197201414401)
XLA Ops:
  11.8 9.6 all-gather.13.cloned.1.call-done
  47.1 158.7 %custom-call.7 = f32[1,8,4,1,64,64]{4,5,3,2,1,0:T(8,128)} custom-call(f32[1,8,4,1,64,64]{5,4,3,2,1,0:T(8,128)} %add_bitcast_fusion.3), custom_call_target="InvertDiagBlocksLowerTriangular" | custom-call | tf_op jit(solution)/shard_map/jvp()/triangular_solve | solution.py:86
  212.9 9.9 while.107
  230.6 22.8 %all-gather.21.cloned.1.call-done = bf16[4,8,128,128]{3,2,1,0:T(8,128)(2,1)} async-done(((bf16[1,8,128,128]{3,2,1,0:T(8,128)(2,1)}), bf16[4,8,128,128]{3,2,1,0:T(8,128)(2,1)}) %all-gather.21.cloned.1.call-update) | async-done | bytes 1048592 | tf_op jit(solution)/shard_map/all_gather | solution.py:24
  253.4 29.6 %all-gather.23.cloned.1.call-done = bf16[4,8,128,128]{3,2,1,0:T(8,128)(2,1)} async-done(((bf16[1,8,128,128]{3,2,1,0:T(8,128)(2,1)}), bf16[4,8,128,128]{3,2,1,0:T(8,128)(2,1)}) %all-gather.23.cloned.1.call-update) | async-done | bytes 1048592 | tf_op jit(solution)/shard_map/all_gather | solution.py:24
  283.0 6.3 while.110
  291.5 29.3 %while.108 = (s32[]{:T(128)}, f32[1,8,128,128]{3,2,1,0:T(8,128)S(1)}, f32[4,1,8,64,128]{4,3,2,1,0:T(8,128)}, f32[4,1,8,128,128]{4,3,2,1,0:T(8,128)}, f32[4,1,8,6...) while((s32[]{:T(128)}, ...), condition=%wide.region_8.9_spmd.clone, body=%wide.region_7.8_spmd.clone.sunk | while | flops 402956288 | bytes 7522441 | solution.py:107
  330.4 8.1 reduce-scatter.18.cloned.1.call-done
  343.8 7.1 all-gather.15.cloned.1.call-done
  352.4 9.5 fusion.269
  362.0 9.0 fusion.267
  371.0 11.5 multiply_convert_fusion
  382.5 7.1 fusion.287
  389.6 9.1 fusion.179
  414.2 7.6 all-gather.19.cloned.1.call-done
  434.1 60.4 %while.111 = (s32[]{:T(128)}, f32[1,8,128,128]{2,3,1,0:T(8,128)S(1)}, f32[4,1,8,64,128]{4,2,3,0,1:T(8,128)}, f32[4,1,8,64,128]{4,3,0,2,1:T(8,128)}, f32[4,1,8,64...) while((s32[]{:T(128)}, ...), condition=%wide.region_18.19_spmd.clone, body=%wide.region_17.18_spmd.clone.sunk | while | flops 806330368 | bytes 24551168 | solution.py:107
  503.9 8.9 fusion.169
  512.9 11.7 all-gather.27.cloned.1.call-done
  524.6 6.3 while.112
  535.5 58.2 %while.109 = (s32[]{:T(128)}, f32[1,8,128,128]{2,3,1,0:T(8,128)S(1)}, f32[4,1,8,64,128]{4,2,3,0,1:T(8,128)}, f32[4,1,8,64,128]{4,3,0,2,1:T(8,128)}, f32[4,1,8,64...) while((s32[]{:T(128)}, ...), condition=%wide.region_22.23_spmd.clone, body=%wide.region_21.22_spmd.clone.sunk | while | flops 805937152 | bytes 19303636 | solution.py:107
  693.5 6.2 convolution_convert_fusion.2
  701.0 6.1 convolution_convert_fusion.1
  708.3 35.1 %reduce-scatter.40.cloned.1.call-done = bf16[128,8]{1,0:T(8,128)(2,1)} async-done(((bf16[2048,8]{1,0:T(8,128)(2,1)}), bf16[128,8]{1,0:T(8,128)(2,1)}) %reduce-scatter.40.cloned.1.call-update) | async-done | bytes 2064
  744.8 109.2 %all-reduce.25.cloned.1.call-done = bf16[16,4,3072]{2,1,0:T(4,128)(2,1)} async-done(((bf16[16,4,3072]{2,1,0:T(4,128)(2,1)}), bf16[16,4,3072]{2,1,0:T(4,128)(2,1)}) %all-reduce.25.cloned.1.call-update) | async-done | bytes 393232
  856.0 108.3 %all-reduce.27.cloned.1.call-done = (bf16[16,1024]{1,0:T(8,128)(2,1)}, bf16[16,128]{1,0:T(8,128)(2,1)}, bf16[16,1024]{1,0:T(8,128)(2,1)}) async-done(((bf16[16,1024]{1,0:T(8,128)(2,1)}, bf16[16,128]{1,0:T(8,128)(2,1)}, bf16[16,1024]{1,0:T(8,128)(2,1)}), (bf16[16,1024]{1,0:T(8,128)(2,1)}, bf16[16,128]{1,0:T(8,128)(2,1)}, bf16[16,1024]{1,0:T(8,128)(2,1)})) %all-reduce.27.cloned.1.call-update) | async-done | bytes 69648
  970.1 92.8 %reduce-scatter.32.cloned.1.call-done = bf16[128,1024]{1,0:T(8,128)(2,1)} async-done(((bf16[2048,1024]{1,0:T(8,128)(2,1)}), bf16[128,1024]{1,0:T(8,128)(2,1)}) %reduce-scatter.32.cloned.1.call-update) | async-done | bytes 262160 | tf_op jit(solution)/shard_map/reduce_scatter | solution.py:398
  1064.8 94.8 %reduce-scatter.26.cloned.1.call-done = bf16[128,1024]{1,0:T(8,128)(2,1)} async-done(((bf16[2048,1024]{1,0:T(8,128)(2,1)}), bf16[128,1024]{1,0:T(8,128)(2,1)}) %reduce-scatter.26.cloned.1.call-update) | async-done | bytes 262160 | tf_op jit(solution)/shard_map/reduce_scatter | solution.py:380
  1161.4 95.0 %reduce-scatter.28.cloned.1.call-done = bf16[128,1024]{1,0:T(8,128)(2,1)} async-done(((bf16[2048,1024]{1,0:T(8,128)(2,1)}), bf16[128,1024]{1,0:T(8,128)(2,1)}) %reduce-scatter.28.cloned.1.call-update) | async-done | bytes 262160 | tf_op jit(solution)/shard_map/reduce_scatter | solution.py:383
  1258.3 95.2 %reduce-scatter.30.cloned.1.call-done = bf16[128,1024]{1,0:T(8,128)(2,1)} async-done(((bf16[2048,1024]{1,0:T(8,128)(2,1)}), bf16[128,1024]{1,0:T(8,128)(2,1)}) %reduce-scatter.30.cloned.1.call-update) | async-done | bytes 262160 | tf_op jit(solution)/shard_map/reduce_scatter | solution.py:386
  1355.2 244.1 %reduce-scatter.38.cloned.1.call-done = bf16[128,2816]{1,0:T(8,128)(2,1)} async-done(((bf16[2048,2816]{1,0:T(8,128)(2,1)}), bf16[128,2816]{1,0:T(8,128)(2,1)}) %reduce-scatter.38.cloned.1.call-update) | async-done | bytes 720912 | tf_op jit(solution)/shard_map/reduce_scatter | solution.py:401
  1602.1 243.1 %reduce-scatter.34.cloned.1.call-done = bf16[128,2816]{1,0:T(8,128)(2,1)} async-done(((bf16[2048,2816]{1,0:T(8,128)(2,1)}), bf16[128,2816]{1,0:T(8,128)(2,1)}) %reduce-scatter.34.cloned.1.call-update) | async-done | bytes 720912 | tf_op jit(solution)/shard_map/reduce_scatter | solution.py:392
  1847.5 243.5 %reduce-scatter.36.cloned.1.call-done = bf16[128,2816]{1,0:T(8,128)(2,1)} async-done(((bf16[2048,2816]{1,0:T(8,128)(2,1)}), bf16[128,2816]{1,0:T(8,128)(2,1)}) %reduce-scatter.36.cloned.1.call-update) | async-done | bytes 720912 | tf_op jit(solution)/shard_map/reduce_scatter | solution.py:395
  (588 shorter events, 398.6 us)
Async XLA Ops:
  7.2 27.3 %copy-start = (bf16[2048,8]{0,1:T(8,128)(2,1)S(1)}, bf16[2048,8]{0,1:T(8,128)(2,1)}, u32[]{:S(2)}) copy-start(bf16[2048,8]{0,1:T(8,128)(2,1)} %param.35) | copy-start | bytes 98308
  7.2 14.1 all-gather.13.cloned.1.call-start
  7.9 245.5 %all-gather.21.cloned.1.call-start = ((), (), s32[]{:S(2)}) async-start(), calls=%async_computation.27 | async-start | bytes 1310720 | tf_op jit(solution)/shard_map/all_gather | solution.py:24
  11.7 24.5 %copy-start.69 = (f32[1,3072]{1,0:T(1,128)}, f32[1,3072]{1,0:T(1,128)S(1)}, u32[]{:S(2)}) copy-start(f32[1,3072]{1,0:T(1,128)S(1)} %get-tuple-element.1409) | copy-start | bytes 36868
  11.7 24.5 %copy-start.71 = (f32[1,3072]{1,0:T(1,128)}, f32[1,3072]{1,0:T(1,128)S(1)}, u32[]{:S(2)}) copy-start(f32[1,3072]{1,0:T(1,128)S(1)} %get-tuple-element.1410) | copy-start | bytes 36868
  11.7 24.5 %copy-start.73 = (f32[1,3072]{1,0:T(1,128)}, f32[1,3072]{1,0:T(1,128)S(1)}, u32[]{:S(2)}) copy-start(f32[1,3072]{1,0:T(1,128)S(1)} %get-tuple-element.1411) | copy-start | bytes 36868
  11.7 24.5 %copy-start.75 = (f32[1,3072]{1,0:T(1,128)}, f32[1,3072]{1,0:T(1,128)S(1)}, u32[]{:S(2)}) copy-start(f32[1,3072]{1,0:T(1,128)S(1)} %get-tuple-element.1412) | copy-start | bytes 36868
  30.6 5.2 collective-permute-start
  42.8 168.9 %copy-start.17 = (bf16[1,256,8,128]{3,1,2,0:T(8,128)(2,1)}, bf16[1,256,8,128]{3,1,2,0:T(8,128)(2,1)S(1)}, u32[]{:S(2)}) copy-start(bf16[1,256,8,128]{3,1,2,0:T(8,128)(2,1)S(1)} %copy.179) | copy-start | bytes 1572868
  43.0 162.7 %copy-start.29 = (f32[1,256,8,128]{3,1,2,0:T(8,128)}, f32[1,256,8,128]{3,1,2,0:T(8,128)S(1)}, u32[]{:S(2)}) copy-start(f32[1,256,8,128]{3,1,2,0:T(8,128)S(1)} %copy.181) | copy-start | bytes 3145732
  44.3 161.4 %copy-start.31 = (f32[8,4,64,128]{3,2,1,0:T(8,128)}, f32[8,4,64,128]{3,2,1,0:T(8,128)S(1)}, u32[]{:S(2)}) copy-start(f32[8,4,64,128]{3,2,1,0:T(8,128)S(1)} %get-tuple-element.1405) | copy-start | bytes 3145732
  223.6 59.4 %all-gather.23.cloned.1.call-start = ((), (), s32[]{:S(2)}) async-start(), calls=%async_computation.28 | async-start | bytes 1310720 | tf_op jit(solution)/shard_map/all_gather | solution.py:24
  224.4 114.1 %reduce-scatter.18.cloned.1.call-start = ((), (), s32[]{:S(2)}) async-start(), calls=%async_computation.13 | async-start | bytes 1572864 | tf_op jit(solution)/shard_map/reduce_scatter | solution.py:240
  330.3 20.6 all-gather.15.cloned.1.call-start
  340.5 30.4 %all-gather.17.cloned.1.call-start = ((), (), s32[]{:S(2)}) async-start(), calls=%async_computation.16 | async-start | bytes 1572864 | tf_op jit(solution)/shard_map/all_gather | solution.py:257
  341.6 67.0 %reduce-scatter.22.cloned.1.call-start = ((), (), s32[]{:S(2)}) async-start(), calls=%async_computation.17 | async-start | bytes 1572864 | tf_op jit(solution)/shard_map/reduce_scatter | solution.py:278
  398.7 23.1 %all-gather.19.cloned.1.call-start = ((), (), s32[]{:S(2)}) async-start(), calls=%async_computation.18 | async-start | bytes 1572864 | tf_op jit(solution)/shard_map/all_gather | solution.py:296
  411.5 101.4 %all-gather.25.cloned.1.call-start = ((), (), s32[]{:S(2)}) async-start(), calls=%async_computation.29 | async-start | bytes 1310720 | tf_op jit(solution)/shard_map/all_gather | solution.py:24
  414.1 110.4 %all-gather.27.cloned.1.call-start = ((), (), s32[]{:S(2)}) async-start(), calls=%async_computation.30 | async-start | bytes 1310720 | tf_op jit(solution)/shard_map/all_gather | solution.py:24
  495.3 166.5 %reduce-scatter.20.cloned.1.call-start = ((), (), s32[]{:S(2)}) async-start(), calls=%async_computation.15 | async-start | bytes 1572864 | tf_op jit(solution)/shard_map/reduce_scatter | solution.py:252
  512.8 149.5 %reduce-scatter.24.cloned.1.call-start = ((), (), s32[]{:S(2)}) async-start(), calls=%async_computation.19 | async-start | bytes 1572864 | tf_op jit(solution)/shard_map/reduce_scatter | solution.py:354
  638.4 6.0 collective-permute-start.1
  654.1 89.3 %reduce-scatter.40.cloned.1.call-start = ((), (), s32[]{:S(2)}) async-start(), calls=%async_computation.31 | async-start | bytes 557056
  656.8 197.2 %all-reduce.25.cloned.1.call-start = ((), (), s32[]{:S(2)}) async-start(), calls=%async_computation.32 | async-start | bytes 786432
  657.8 306.5 %all-reduce.27.cloned.1.call-start = ((), (), s32[]{:S(2)}) async-start(), calls=%async_computation.33 | async-start | bytes 139264
  668.1 394.8 %reduce-scatter.32.cloned.1.call-start = ((), (), s32[]{:S(2)}) async-start(), calls=%async_computation.23 | async-start | bytes 4456448 | tf_op jit(solution)/shard_map/reduce_scatter | solution.py:398
  672.8 486.9 %reduce-scatter.26.cloned.1.call-start = ((), (), s32[]{:S(2)}) async-start(), calls=%async_computation.20 | async-start | bytes 4456448 | tf_op jit(solution)/shard_map/reduce_scatter | solution.py:380
  676.2 580.2 %reduce-scatter.28.cloned.1.call-start = ((), (), s32[]{:S(2)}) async-start(), calls=%async_computation.21 | async-start | bytes 4456448 | tf_op jit(solution)/shard_map/reduce_scatter | solution.py:383
  679.8 673.6 %reduce-scatter.30.cloned.1.call-start = ((), (), s32[]{:S(2)}) async-start(), calls=%async_computation.22 | async-start | bytes 4456448 | tf_op jit(solution)/shard_map/reduce_scatter | solution.py:386
  684.2 915.2 %reduce-scatter.38.cloned.1.call-start = ((), (), s32[]{:S(2)}) async-start(), calls=%async_computation.26 | async-start | bytes 12255232 | tf_op jit(solution)/shard_map/reduce_scatter | solution.py:401
  691.8 1153.3 %reduce-scatter.34.cloned.1.call-start = ((), (), s32[]{:S(2)}) async-start(), calls=%async_computation.24 | async-start | bytes 12255232 | tf_op jit(solution)/shard_map/reduce_scatter | solution.py:392
  699.7 1391.3 %reduce-scatter.36.cloned.1.call-start = ((), (), s32[]{:S(2)}) async-start(), calls=%async_computation.25 | async-start | bytes 12255232 | tf_op jit(solution)/shard_map/reduce_scatter | solution.py:395
  (91 other events, 343.3 us)
Sparse Core Ops, SparseCore 0:
  9.6 11.7 all-gather.12
  223.7 29.6 all-gather.20
  255.6 27.4 all-gather.22
  330.4 8.0 reduce-scatter.17
  340.7 10.1 all-gather.14
  352.9 10.1 all-gather.16
  398.8 9.7 reduce-scatter.21
  411.6 10.1 all-gather.18
  424.0 29.1 all-gather.24
  495.5 29.0 all-gather.26
  526.8 8.0 reduce-scatter.19
  654.2 8.0 reduce-scatter.23
  665.1 78.2 reduce-scatter.39
  749.8 104.1 all-reduce.24
  860.4 103.9 all-reduce.26
  966.5 96.3 reduce-scatter.31
  1065.0 94.6 reduce-scatter.25
  1161.8 94.6 reduce-scatter.27
  1258.8 94.6 reduce-scatter.29
  1355.6 243.7 reduce-scatter.37
  1601.6 243.4 reduce-scatter.33
  1847.5 243.4 reduce-scatter.35
where the time goes:
time: 2110 us; the launch traced here: 2100 us
  waiting for transfers between devices  1470 us (70%)
  matrix products  282 us (13%)
  other arithmetic  224 us (11%)
  local copies, waits for them, and re-layouts  93.8 us (4%)
    unnamed x25, waiting for transfers between devices  254 us
    reduce_scatter x1, waiting for transfers between devices, shards(): lax.psum_scatter(grad_down_part.astype(jnp.bfloat16), ('dp', 'seq'), scat...  244 us
    reduce_scatter x1, waiting for transfers between devices, shards(): lax.psum_scatter(grad_up_part.astype(jnp.bfloat16), ('dp', 'seq'), scatte...  244 us
    reduce_scatter x1, waiting for transfers between devices, shards(): lax.psum_scatter(grad_gate_part.astype(jnp.bfloat16), ('dp', 'seq'), scat...  243 us
    another operation x5, other arithmetic, prepare(): lax.linalg.triangular_solve(system, weighted, left_side=True, lower=True,...  160 us
    reduce_scatter x1, waiting for transfers between devices, shards(): lax.psum_scatter(grad_value_part.astype(jnp.bfloat16), ('dp', 'seq'), sca...  95.2 us
    reduce_scatter x1, waiting for transfers between devices, shards(): lax.psum_scatter(grad_key_part.astype(jnp.bfloat16), ('dp', 'seq'), scatt...  95 us
    reduce_scatter x1, waiting for transfers between devices, shards(): lax.psum_scatter(grad_query_part.astype(jnp.bfloat16), ('dp', 'seq'), sca...  94.8 us
  transfers between devices with their start and end apart: 24, of which 21 were waited for; matrix products, arithmetic and copies ran while one was open for 15% of the time, Pallas kernels for 0%

commit v1 on v0

--- a/solution.py
+++ b/solution.py
@@ -18,28 +18,77 @@
     return lax.ppermute(value, axis, pairs)
 
 
-def prefix_2(value, axis, combine, identity, reverse):
-    peers, position = (lax.axis_size(axis), lax.axis_index(axis))
-    everything = jax.tree.map(
-        lambda part, kind: lax.all_gather(part.astype(kind), axis),
-        value,
-        jax.tree.map(lambda a: jnp.bfloat16 if a.dtype == jnp.float32 else a.dtype, value),
-    )
-    start = jax.tree.map(
-        lambda part, zero: jnp.broadcast_to(jnp.asarray(zero, part.dtype), part.shape),
-        value,
-        identity,
-    )
-
-    def turn(k, before):
-        at = peers - 1 - k if reverse else k
-        reached = at > position if reverse else at < position
-        new = combine(
-            before, jax.tree.map(lambda part, own: part[at].astype(own.dtype), everything, value)
+def swap_pairs(axis, by):
+    peers = lax.axis_size(axis)
+    return [(i, i ^ by) for i in range(peers)]
+
+
+def exchanged(values, axis):
+    peers = lax.axis_size(axis)
+    own = lax.axis_index(axis)
+    parts = [lax.dynamic_index_in_dim(values, own, 0, keepdims=False)]
+    for by in range(1, peers):
+        out = lax.dynamic_index_in_dim(values, own ^ by, 0, keepdims=False)
+        parts.append(lax.ppermute(out, axis, swap_pairs(axis, by)))
+    return parts
+
+
+def spread(value, axis):
+    peers = lax.axis_size(axis)
+    return [value] + [
+        lax.ppermute(value, axis, swap_pairs(axis, by)) for by in range(1, peers)
+    ]
+
+
+def in_order(parts, axis):
+    stacked = jnp.stack(parts, 0)
+    own = lax.axis_index(axis)
+    return [
+        lax.dynamic_index_in_dim(stacked, own ^ k, 0, keepdims=False) for k in range(len(parts))
+    ]
+
+
+def gather_head(value, axis):
+    if lax.axis_size("head") == 2:
+        other = lax.ppermute(value, "head", [(0, 1), (1, 0)])
+        first = lax.axis_index("head") == 0
+        return jnp.concatenate(
+            [jnp.where(first, value, other), jnp.where(first, other, value)], axis
         )
-        return jax.tree.map(lambda a, b: jnp.where(reached, a, b), new, before)
-
-    return lax.fori_loop(0, peers, turn, start)
+    return lax.all_gather(value, "head", axis=axis, tiled=True)
+
+
+def sum_head(value):
+    low = value.astype(jnp.bfloat16)
+    if lax.axis_size("head") == 2:
+        other = lax.ppermute(low, "head", [(0, 1), (1, 0)])
+        return low.astype(jnp.float32) + other.astype(jnp.float32)
+    return lax.psum(low, "head").astype(jnp.float32)
+
+
+def sum_doubling(value, axes):
+    for axis in axes:
+        by = 1
+        while by < lax.axis_size(axis):
+            value = value + lax.ppermute(value, axis, swap_pairs(axis, by))
+            by *= 2
+    return value
+
+
+def own_half(value, width):
+    return lax.dynamic_slice_in_dim(value, lax.axis_index("head") * width, width, value.ndim - 1)
+
+
+def chain_state(maps, shifts, reverse):
+    peers, position = lax.axis_size("seq"), lax.axis_index("seq")
+    by = -1 if reverse else 1
+    state = jnp.zeros_like(shifts)
+    for step in range(peers - 1):
+        out = (
+            jnp.einsum("...ij,...jk->...ik", maps, state, precision=HIGH) + shifts
+        ).astype(jnp.bfloat16)
+        state = passed_along(out, "seq", by).astype(jnp.float32)
+    return state
 
 
 def inverse_rms(values):
@@ -188,20 +237,45 @@
     channels = query_weight.shape[1]
     local_heads = beta_weight.shape[1]
     groups = lax.axis_size("head")
-    shares = lax.axis_size("dp") * lax.axis_size("seq")
+    ways = lax.axis_size("dp")
+    spans = lax.axis_size("seq")
     rim_len = query_conv.shape[0] - 1
     positions = lax.axis_index("seq") * local_len + jnp.arange(local_len, dtype=jnp.int32)
     live_mask = (positions[None, :] < lengths[:, None]).astype(jnp.float32)
-    gathered, gain_one, gain_two = (
-        lax.all_gather(tokens_in, "head", axis=2, tiled=True),
-        lax.all_gather(first_gain, "head", axis=0, tiled=True),
-        lax.all_gather(second_gain, "head", axis=0, tiled=True),
-    )
+    masked_up = upstream * live_mask[..., None].astype(jnp.bfloat16)
+    gathered = gather_head(tokens_in, 2)
+    upstream_full = gather_head(masked_up, 2)
+    gains = gather_head(jnp.stack([first_gain, second_gain]), 1).astype(jnp.float32)
+    gain_one, gain_two = gains[0], gains[1]
     stream_full = gathered.astype(jnp.float32)
-    gain_one = gain_one.astype(jnp.float32)
-    gain_two = gain_two.astype(jnp.float32)
     scale_one = inverse_rms(stream_full)
     normed_one = (stream_full * scale_one * gain_one).astype(jnp.bfloat16)
+
+    def tokens_of_plane(value):
+        parts = spread(own_half(value, local_width)[0], "dp")
+        part = gather_head(jnp.concatenate(parts, 0), 1)
+        return part.reshape(part.shape[0], ways, spans, -1).transpose(2, 0, 1, 3).reshape(
+            spans, part.shape[0], -1
+        )
+
+    def columns_of_plane(values):
+        turned = values.T
+        turned = turned.reshape(ways, turned.shape[0] // ways, turned.shape[1])
+        return turned
+
+    def reduced_piece(left, right):
+        part = jnp.einsum("ct,stk->sck", left, right, preferred_element_type=jnp.float32)
+        return lax.psum_scatter(
+            part.astype(jnp.bfloat16), "seq", scatter_dimension=0, tiled=False
+        )
+
+    def to_owner(piece):
+        c = piece.shape[0]
+        blocks = piece.reshape(c, ways, -1).transpose(1, 0, 2)
+        return jnp.stack(in_order(exchanged(blocks, "dp"), "dp"), 0)
+
+    tokens_one = tokens_of_plane(normed_one)
+    tokens_up = tokens_of_plane(upstream_full)
     pre_act = jnp.concatenate(
         [
             jnp.dot(normed_one, query_weight, preferred_element_type=jnp.float32),
@@ -225,41 +299,25 @@
     beta_blk = beta_blocks(mixer_in[3])
     wy_pair, pull_prep = jax.vjp(prepare, key_blk, value_blk, beta_blk)
     device_maps = device_map(key_blk, wy_pair[0], wy_pair[1])
-    identity = (
-        jnp.broadcast_to(jnp.eye(HEAD_DIM, dtype=jnp.float32), device_maps[0].shape),
-        jnp.zeros_like(device_maps[1]),
-    )
-    prefix = prefix_2(device_maps, "seq", compose, identity, False)
+    entering = chain_state(device_maps[0], device_maps[1], False)
     mixed_pair, pull_blocks = jax.vjp(
-        run_blocks, query_blk, key_blk, wy_pair[0], wy_pair[1], prefix[1]
+        run_blocks, query_blk, key_blk, wy_pair[0], wy_pair[1], entering
     )
     mixed_seq = seq_layout(mixed_pair[0])
     normed_mix, pull_norm = jax.vjp(mixer_norm, mixed_seq, mixer_gain.astype(jnp.float32))
     head_out = normed_mix.reshape(num_rows, local_len, channels).astype(jnp.bfloat16)
     mixer_part = jnp.dot(head_out, output_weight, preferred_element_type=jnp.float32)
-    stream_local = tokens_in.astype(jnp.float32) + lax.psum_scatter(
-        mixer_part.astype(jnp.bfloat16), "head", scatter_dimension=2, tiled=True
-    ).astype(jnp.float32)
-    stream_mid = lax.all_gather(
-        stream_local.astype(jnp.bfloat16), "head", axis=2, tiled=True
-    ).astype(stream_local.dtype)
+    stream_mid = stream_full + sum_head(mixer_part)
     scale_two = inverse_rms(stream_mid)
     normed_two = (stream_mid * scale_two * gain_two).astype(jnp.bfloat16)
     gate_pre = jnp.dot(normed_two, gate_weight, preferred_element_type=jnp.float32)
     up_pre = jnp.dot(normed_two, up_weight, preferred_element_type=jnp.float32)
     hidden = (jax.nn.silu(gate_pre) * up_pre).astype(jnp.bfloat16)
     feed_part = jnp.dot(hidden, down_weight, preferred_element_type=jnp.float32)
-    feed_local = lax.psum_scatter(
-        feed_part.astype(jnp.bfloat16), "head", scatter_dimension=2, tiled=True
-    ).astype(jnp.float32)
-    layer_out = (stream_local + feed_local).astype(jnp.bfloat16)
-    masked_up = upstream * live_mask[..., None].astype(jnp.bfloat16)
-    upstream_full = lax.all_gather(masked_up, "head", axis=2, tiled=True)
+    layer_out = own_half(stream_mid + sum_head(feed_part), local_width).astype(jnp.bfloat16)
+    tokens_two = tokens_of_plane(normed_two)
     d_hidden = jnp.einsum(
         "rsd,fd->rsf", upstream_full, down_weight, preferred_element_type=jnp.float32
-    )
-    grad_down_part = jnp.einsum(
-        "rsd,rsf->df", upstream_full, hidden, preferred_element_type=jnp.float32
     )
     gate_sig = jax.nn.sigmoid(gate_pre)
     d_gate = (d_hidden * up_pre * gate_sig * (1.0 + gate_pre * (1.0 - gate_sig))).astype(
@@ -269,45 +327,42 @@
     d_normed_two = jnp.einsum(
         "rsf,df->rsd", d_gate, gate_weight, preferred_element_type=jnp.float32
     ) + jnp.einsum("rsf,df->rsd", d_up, up_weight, preferred_element_type=jnp.float32)
-    grad_gate_part = jnp.einsum(
-        "rsd,rsf->df", normed_two, d_gate, preferred_element_type=jnp.float32
-    )
-    grad_up_part = jnp.einsum("rsd,rsf->df", normed_two, d_up, preferred_element_type=jnp.float32)
-    stat_two = jnp.sum(d_normed_two * stream_mid * gain_two, axis=-1, keepdims=True)
-    d_two_local, stat_two_sum = (
-        lax.psum_scatter(
-            d_normed_two.astype(jnp.bfloat16), "head", scatter_dimension=2, tiled=True
-        ).astype(jnp.float32),
-        lax.psum_scatter(
-            jnp.broadcast_to(stat_two, (num_rows, local_len, groups)).astype(jnp.bfloat16),
-            "head",
-            scatter_dimension=2,
-            tiled=True,
-        ).astype(jnp.float32),
-    )
-    second_local = second_gain.astype(jnp.float32)
+    feed_cols = exchanged(
+        jnp.concatenate(
+            [columns_of_plane(hidden[0]), columns_of_plane(d_gate[0]), columns_of_plane(d_up[0])], 1
+        ),
+        "dp",
+    )
+    feed_cols = jnp.concatenate(feed_cols, 1)
+    units = feed_cols.shape[0] // 3
+    down_piece = reduced_piece(feed_cols[:units], tokens_up)
+    gate_piece = reduced_piece(feed_cols[units : 2 * units], tokens_two)
+    up_piece = reduced_piece(feed_cols[2 * units :], tokens_two)
+    d_two = sum_head(d_normed_two)
     d_stream = (
-        masked_up.astype(jnp.float32)
-        + scale_two * second_local * d_two_local
-        - stream_local * scale_two * scale_two * scale_two * stat_two_sum / full_width
-    )
-    grad_second = jnp.sum(d_two_local * stream_local * scale_two, axis=(0, 1))
-    d_stream_low = d_stream.astype(jnp.bfloat16)
-    residual_full = lax.all_gather(d_stream_low, "head", axis=2, tiled=True)
+        upstream_full.astype(jnp.float32)
+        + scale_two * gain_two * d_two
+        - stream_mid
+        * scale_two
+        * scale_two
+        * scale_two
+        * (jnp.sum(d_two * gain_two * stream_mid, axis=-1, keepdims=True) / full_width)
+    )
+    grad_second = own_half(jnp.sum(d_two * stream_mid * scale_two, axis=(0, 1)), local_width)
+    residual_full = d_stream.astype(jnp.bfloat16)
+    tokens_res = tokens_of_plane(residual_full)
     d_head_out = jnp.einsum(
         "rsd,cd->rsc", residual_full, output_weight, preferred_element_type=jnp.float32
     )
-    grad_out_part = jnp.einsum(
-        "rsd,rsc->dc", residual_full, head_out, preferred_element_type=jnp.float32
-    )
+    out_cols = jnp.concatenate(exchanged(columns_of_plane(head_out[0]), "dp"), 1)
+    out_piece = reduced_piece(out_cols, tokens_res)
     d_mixed_seq, grad_gain_part = pull_norm(
         d_head_out.reshape(num_rows, local_len, local_heads, HEAD_DIM)
     )
     d_mixed_blk = head_blocks(d_mixed_seq)
-    first_pass = pull_blocks((d_mixed_blk, jnp.zeros_like(prefix[1])))
-    reverse_maps = (jnp.swapaxes(device_maps[0], -1, -2), first_pass[4])
-    suffix = prefix_2(reverse_maps, "seq", compose, identity, True)
-    second_pass = pull_blocks((jnp.zeros_like(d_mixed_blk), suffix[1]))
+    first_pass = pull_blocks((d_mixed_blk, jnp.zeros_like(entering)))
+    leaving = chain_state(jnp.swapaxes(device_maps[0], -1, -2), first_pass[4], True)
+    second_pass = pull_blocks((jnp.zeros_like(d_mixed_blk), leaving))
     d_query_blk = first_pass[0] + second_pass[0]
     d_key_blk = first_pass[1] + second_pass[1]
     d_wy_keys = first_pass[2] + second_pass[2]
@@ -336,114 +391,69 @@
         + jnp.einsum("rsc,dc->rsd", d_pre_value, value_weight, preferred_element_type=jnp.float32)
         + jnp.einsum("rsh,dh->rsd", d_logit_low, beta_weight, preferred_element_type=jnp.float32)
     )
-    grad_query_part = jnp.einsum(
-        "rsd,rsc->dc", normed_one, d_pre_query, preferred_element_type=jnp.float32
-    )
-    grad_key_part = jnp.einsum(
-        "rsd,rsc->dc", normed_one, d_pre_key, preferred_element_type=jnp.float32
-    )
-    grad_value_part = jnp.einsum(
-        "rsd,rsc->dc", normed_one, d_pre_value, preferred_element_type=jnp.float32
-    )
+    mix_cols = exchanged(
+        jnp.concatenate(
+            [
+                columns_of_plane(d_pre_query[0]),
+                columns_of_plane(d_pre_key[0]),
+                columns_of_plane(d_pre_value[0]),
+            ],
+            1,
+        ),
+        "dp",
+    )
+    mix_piece = reduced_piece(jnp.concatenate(mix_cols, 1), tokens_one)
     grad_beta_part = jnp.einsum(
         "rsd,rsh->dh", normed_one, d_logit_low, preferred_element_type=jnp.float32
     )
-    stat_one = jnp.sum(d_normed_one * stream_full * gain_one, axis=-1, keepdims=True)
-    gain_spread = jnp.broadcast_to(grad_gain_part[None, :, None], (1, HEAD_DIM, groups))
-    d_one_local, stat_one_sum, gain_total = (
-        lax.psum_scatter(
-            d_normed_one.astype(jnp.bfloat16), "head", scatter_dimension=2, tiled=True
-        ).astype(jnp.float32),
-        lax.psum_scatter(
-            jnp.broadcast_to(stat_one, (num_rows, local_len, groups)).astype(jnp.bfloat16),
-            "head",
-            scatter_dimension=2,
-            tiled=True,
-        ).astype(jnp.float32),
-        lax.psum_scatter(
-            gain_spread.astype(jnp.bfloat16), "head", scatter_dimension=2, tiled=True
-        ).astype(jnp.float32),
-    )
-    tokens_local = tokens_in.astype(jnp.float32)
-    first_local = first_gain.astype(jnp.float32)
-    grad_tokens = (
+    d_one = sum_head(d_normed_one)
+    grad_tokens = own_half(
         d_stream
-        + scale_one * first_local * d_one_local
-        - tokens_local * scale_one * scale_one * scale_one * stat_one_sum / full_width
-    )
-    grad_first = jnp.sum(d_one_local * tokens_local * scale_one, axis=(0, 1))
-
-    def spread_rows(values):
-        return jnp.broadcast_to(values[None], (shares,) + values.shape)
-
-    reduced = (
-        lax.psum_scatter(
-            grad_query_part.astype(jnp.bfloat16), ("dp", "seq"), scatter_dimension=0, tiled=True
-        ).astype(jnp.float32),
-        lax.psum_scatter(
-            grad_key_part.astype(jnp.bfloat16), ("dp", "seq"), scatter_dimension=0, tiled=True
-        ).astype(jnp.float32),
-        lax.psum_scatter(
-            grad_value_part.astype(jnp.bfloat16), ("dp", "seq"), scatter_dimension=0, tiled=True
-        ).astype(jnp.float32),
-        lax.psum_scatter(
-            grad_beta_part.astype(jnp.bfloat16), ("dp", "seq"), scatter_dimension=0, tiled=True
-        ).astype(jnp.float32),
-        lax.psum_scatter(
-            grad_gate_part.astype(jnp.bfloat16), ("dp", "seq"), scatter_dimension=0, tiled=True
-        ).astype(jnp.float32),
-        lax.psum_scatter(
-            grad_up_part.astype(jnp.bfloat16), ("dp", "seq"), scatter_dimension=0, tiled=True
-        ).astype(jnp.float32),
-        lax.psum_scatter(
-            grad_out_part.astype(jnp.bfloat16), ("dp", "seq"), scatter_dimension=0, tiled=True
-        ).astype(jnp.float32),
-        lax.psum_scatter(
-            grad_down_part.astype(jnp.bfloat16), ("dp", "seq"), scatter_dimension=0, tiled=True
-        ).astype(jnp.float32),
-        lax.psum_scatter(
-            spread_rows(grad_first).astype(jnp.bfloat16),
-            ("dp", "seq"),
-            scatter_dimension=0,
-            tiled=True,
-        ).astype(jnp.float32),
-        lax.psum_scatter(
-            spread_rows(grad_kernels).astype(jnp.bfloat16),
-            ("dp", "seq"),
-            scatter_dimension=0,
-            tiled=True,
-        ).astype(jnp.float32),
-        lax.psum_scatter(
-            spread_rows(gain_total.reshape(HEAD_DIM)).astype(jnp.bfloat16),
-            ("dp", "seq"),
-            scatter_dimension=0,
-            tiled=True,
-        ).astype(jnp.float32),
-        lax.psum_scatter(
-            spread_rows(grad_second).astype(jnp.bfloat16),
-            ("dp", "seq"),
-            scatter_dimension=0,
-            tiled=True,
-        ).astype(jnp.float32),
-    )
-    kernel_sum = reduced[9][0]
+        + scale_one * gain_one * d_one
+        - stream_full
+        * scale_one
+        * scale_one
+        * scale_one
+        * (jnp.sum(d_one * gain_one * stream_full, axis=-1, keepdims=True) / full_width),
+        local_width,
+    )
+    grad_first = own_half(jnp.sum(d_one * stream_full * scale_one, axis=(0, 1)), local_width)
+    small = [grad_first, grad_second, grad_kernels.reshape(-1), grad_beta_part.reshape(-1)]
+    total = sum_doubling(jnp.concatenate(small), ("dp", "seq"))
+    gain_total = sum_doubling(grad_gain_part, ("dp", "seq"))
+    gain_total = sum_doubling(gain_total, ("head",))
+    grad_first = total[:local_width]
+    grad_second = total[local_width : 2 * local_width]
+    kernel_end = 2 * local_width + grad_kernels.size
+    kernel_sum = total[2 * local_width : kernel_end].reshape(grad_kernels.shape)
+    share = lax.axis_index("dp") * spans + lax.axis_index("seq")
+    rows = full_width // (ways * spans)
+    grad_beta = lax.dynamic_slice_in_dim(
+        total[kernel_end:].reshape(full_width, local_heads), share * rows, rows, 0
+    )
+    down = to_owner(down_piece).reshape(-1, rows).astype(jnp.float32)
+    gate = to_owner(gate_piece).reshape(-1, rows).astype(jnp.float32)
+    up = to_owner(up_piece).reshape(-1, rows).astype(jnp.float32)
+    out = to_owner(out_piece).reshape(-1, rows).astype(jnp.float32)
+    mix = to_owner(mix_piece).astype(jnp.float32)
+    third = mix.shape[1] // 3
     return (
         layer_out,
         grad_tokens,
-        reduced[8][0],
-        reduced[0],
-        reduced[1],
-        reduced[2],
-        reduced[3],
+        grad_first,
+        mix[:, :third].reshape(-1, rows).T,
+        mix[:, third : 2 * third].reshape(-1, rows).T,
+        mix[:, 2 * third :].reshape(-1, rows).T,
+        grad_beta,
         kernel_sum[:, :channels],
         kernel_sum[:, channels : 2 * channels],
         kernel_sum[:, 2 * channels :],
-        reduced[10][0],
-        reduced[6].T,
-        reduced[11][0],
-        reduced[4],
-        reduced[5],
-        reduced[7].T,
+        gain_total,
+        out,
+        grad_second,
+        gate.T,
+        up.T,
+        down,
     )
 
 

time: 2110 us -> 960 us (0.45)
  waiting for transfers between devices: 1470 us -> 106 us
  local copies, waits for them, and re-layouts: 93.8 us -> 208 us
  starting transfers between devices: 6.87 us -> 80.7 us
  other arithmetic: 224 us -> 262 us
    reduce_scatter x11 -> x5, waiting for transfers between devices: 1120 us -> 0.09 us  [reduced_piece(): lax.psum_scatter(part.astype(jnp.bfloat16), 'seq', scatter_dimension=0, t...]
    unnamed x25 -> x5, waiting for transfers between devices: 254 us -> 0.08 us
    all_gather x8 -> x0, waiting for transfers between devices: 88.4 us -> none  [the longest x4 64.1 us: prefix_2(): lax.all_gather(part.astype(kind), axis)]
    ppermute x0 -> x56, waiting for transfers between devices: none -> 85.3 us  [the longest x12 42.5 us: spread(): lax.ppermute(value, axis, swap_pairs(axis, by))]
    reshape x0 -> x17, local copies, waits for them, and re-layouts: none -> 65 us  [the longest x8 57 us: tokens_of_plane(): part.reshape(part.shape[0], ways, spans, -1).transpose(2, 0, 1, 3)]
    ppermute x0 -> x56, starting transfers between devices: none -> 57.5 us  [the longest x24 28.8 us: exchanged(): parts.append(lax.ppermute(out, axis, swap_pairs(axis, by)))]
    concatenate x0 -> x11, other arithmetic: none -> 27.7 us  [the longest x4 12.2 us: gather_head(): jnp.concatenate([jnp.where(first, value, other), jnp.where(first, other,...]
    dynamic_slice x0 -> x19, local copies, waits for them, and re-layouts: none -> 22.7 us  [the longest x6 11.6 us: exchanged(): out = lax.dynamic_index_in_dim(values, own ^ by, 0, keepdims=False)]
  transfers between devices with their start and end apart: 24 -> 69, of which waited for: 21 -> 27; matrix products, arithmetic and copies ran while one was open for 15% -> 76% of each run, Pallas kernels for 0% -> 0%
where the time goes in v1:
time: 960 us; the launch traced here: 947 us
  matrix products  272 us (28%)
  other arithmetic  262 us (27%)
  local copies, waits for them, and re-layouts  208 us (22%)
  waiting for transfers between devices  106 us (11%)
  starting transfers between devices  80.7 us (8%)
  between operations  17.2 us (2%)
    another operation x5, other arithmetic, prepare(): lax.linalg.triangular_solve(system, weighted, left_side=True, lower=True,...  160 us
    reshape x8, local copies, waits for them, and re-layouts, tokens_of_plane(): part.reshape(part.shape[0], ways, spans, -1).transpose(2, 0, 1, 3)  57 us
    ppermute x12, waiting for transfers between devices, spread(): lax.ppermute(value, axis, swap_pairs(axis, by))  42.5 us
    dot_general x20, matrix products, block_step(): jnp.einsum('...cd,...de->...ce', wy_keys, state, precision=HIGH)  39.6 us
    dot_general x20, matrix products, block_step(): jnp.einsum('...ce,...ed->...cd', scores, fresh, precision=HIGH)  33.2 us
    dot_general x20, matrix products, block_step(): jnp.einsum('...cd,...ce->...de', key_rows, fresh, precision=HIGH)  32.3 us
    ppermute x24, starting transfers between devices, exchanged(): parts.append(lax.ppermute(out, axis, swap_pairs(axis, by)))  28.8 us
    dot_general x5, matrix products, reduced_piece(): jnp.einsum('ct,stk->sck', left, right, preferred_element_type=jnp.float32)  28.3 us
  transfers between devices with their start and end apart: 69, of which 27 were waited for; matrix products, arithmetic and copies ran while one was open for 76% of the time, Pallas kernels for 0%

profile of v1, /device:TPU:0, one launch (start us, length us, event | category | flops | bytes accessed | tf_op | source)
XLA Modules:
  0.0 947.0 jit_solution(3448257638014150140)
XLA Ops:
  43.4 158.7 %custom-call.7 = f32[1,8,4,1,64,64]{4,5,3,2,1,0:T(8,128)} custom-call(f32[1,8,4,1,64,64]{5,4,3,2,1,0:T(8,128)} %add_bitcast_fusion.3), custom_call_target="InvertDiagBlocksLowerTriangular" | custom-call | tf_op jit(solution)/shard_map/jvp()/triangular_solve | solution.py:135
  212.1 14.7 %while.77 = (s32[]{:T(128)}, f32[1,8,128,128]{3,2,1,0:T(8,128)S(1)}, f32[1,8,128,128]{3,2,1,0:T(8,128)S(1)}, f32[4,1,8,128,128]{4,3,0,2,1:T(8,128)}, f32[4,1,8,128,128]{4,3,0,2,1:T(8,128)}, /*index=5*/s32[]{:T(128)}) while((s32[]{:T(128)}, f32[1,8,128,128]{3,2,1,0:T(8,128)S(1)}, f32[1,8,128,128]{3,2,1,0:T(8,128)S(1)}, ...), condition=%wide.region_3.4_spmd, body=%wide.region_2.3_spmd.sunk | while | flops 402784256 | bytes 5768273 | solution.py:181
  256.0 36.0 %while.78 = (s32[]{:T(128)}, f32[1,8,128,128]{3,2,1,0:T(8,128)S(1)}, f32[4,1,8,64,128]{4,3,2,1,0:T(8,128)}, f32[4,1,8,128,128]{4,3,2,1,0:T(8,128)}, f32[4,1,8,64...) while((s32[]{:T(128)}, ...), condition=%wide.region_6.7_spmd.clone, body=%wide.region_5.6_spmd.clone.sunk | while | flops 402956288 | bytes 7653513 | solution.py:156
  299.7 9.2 fusion.217
  339.2 6.9 fusion.221
  346.2 6.5 fusion.153
  352.7 10.1 %fusion.180 = f32[256,2048]{1,0:T(8,128)} fusion(bf16[2048,2816]{1,0:T(8,128)(2,1)} %param.38, f32[256,2816]{1,0:T(8,128)S(1)} %fusion.221, f32[256,2816]{1,0:T(8,128)S(1)} %copy-done.120, f32[256,2816]{1,0:T(8,128)} %get-tuple-element.1222), kind=kOutput, calls=%fused_computation.293 | convolution fusion | flops 2959998976 | bytes 22282240 | tf_op jit(solution)/shard_map/rsf,df->rsd/dot_general | solution.py:327
  362.8 13.1 %fusion.163 = bf16[1,256,2048]{2,1,0:T(8,128)(2,1)} fusion(f32[256,2048]{1,0:T(8,128)} %fusion.180, bf16[2048,2816]{1,0:T(8,128)(2,1)} %param.39, f32[256,2816]{1,0:T(8,128)S(1)} %copy-done.120, f32[256,2816]{1,0:T(8,128)S(1)} %fusion.221), kind=kOutput, calls=%fused_computation.237 | convolution fusion | flops 2958163968 | bytes 20447232 | tf_op jit(solution)/shard_map/rsf,df->rsd/dot_general | solution.py:329
  413.3 10.1 %collective-permute-done.36 = bf16[256,1024]{1,0:T(8,128)(2,1)S(1)} collective-permute-done((bf16[256,1024]{1,0:T(8,128)(2,1)S(1)}, bf16[256,1024]{1,0:T(8,128)(2,1)S(1)}, u32[]{:S(2)}, u32[]{:S(2)}) %collective-permute-start.36) | collective-permute-done | bytes 524320 | tf_op jit(solution)/shard_map/ppermute | solution.py:39
  423.9 9.6 %collective-permute-done.35 = bf16[256,1024]{1,0:T(8,128)(2,1)S(1)} collective-permute-done((bf16[256,1024]{1,0:T(8,128)(2,1)S(1)}, bf16[256,1024]{1,0:T(8,128)(2,1)S(1)}, u32[]{:S(2)}, u32[]{:S(2)}) %collective-permute-start.35) | collective-permute-done | bytes 524320 | tf_op jit(solution)/shard_map/ppermute | solution.py:39
  440.9 63.3 %while.80 = (s32[]{:T(128)}, f32[1,8,128,128]{2,3,1,0:T(8,128)S(1)}, f32[4,1,8,64,128]{4,2,3,0,1:T(8,128)}, f32[4,1,8,64,128]{4,3,0,2,1:T(8,128)}, f32[4,1,8,64,...) while((s32[]{:T(128)}, ...), condition=%wide.region_12.13_spmd.clone, body=%wide.region_11.12_spmd.clone.sunk | while | flops 806330368 | bytes 24551168 | solution.py:156
  514.6 7.7 reshape.1954
  522.3 7.6 copy.427
  535.8 4.8 pad_maximum_fusion.5
  540.6 7.8 reshape.1962
  548.3 5.8 copy.584
  554.2 7.3 reshape.1963
  567.1 7.9 collective-permute-done.11
  590.1 58.2 %while.79 = (s32[]{:T(128)}, f32[1,8,128,128]{2,3,1,0:T(8,128)S(1)}, f32[4,1,8,64,128]{4,2,3,0,1:T(8,128)}, f32[4,1,8,64,128]{4,3,0,2,1:T(8,128)}, f32[4,1,8,64,...) while((s32[]{:T(128)}, ...), condition=%wide.region_14.15_spmd.clone, body=%wide.region_13.14_spmd.clone.sunk | while | flops 805937152 | bytes 19303636 | solution.py:156
  674.8 5.1 add_add_fusion.1
  684.9 7.7 reshape.1957
  692.6 5.8 copy.585
  698.5 7.2 reshape.1958
  705.7 7.5 convert_bitcast_fusion.3
  724.4 5.5 pad_add_fusion
  740.9 5.9 convert_bitcast_fusion.2
  755.7 12.2 %collective-permute-done.21 = bf16[256,1024]{1,0:T(8,128)(2,1)S(1)} collective-permute-done((bf16[256,1024]{1,0:T(8,128)(2,1)S(1)}, bf16[256,1024]{1,0:T(8,128)(2,1)S(1)}, u32[]{:S(2)}, u32[]{:S(2)}) %collective-permute-start.21) | collective-permute-done | bytes 524320 | tf_op jit(solution)/shard_map/ppermute | solution.py:39
  767.9 10.5 %collective-permute-done.20 = bf16[256,1024]{1,0:T(8,128)(2,1)S(1)} collective-permute-done((bf16[256,1024]{1,0:T(8,128)(2,1)S(1)}, bf16[256,1024]{1,0:T(8,128)(2,1)S(1)}, u32[]{:S(2)}, u32[]{:S(2)}) %collective-permute-start.20) | collective-permute-done | bytes 524320 | tf_op jit(solution)/shard_map/ppermute | solution.py:39
  808.9 6.4 copy.414
  818.0 6.0 convert_bitcast_fusion
  824.1 9.4 fusion.162
  863.3 11.6 %collective-permute-done.18 = f32[30720]{0:T(1024)S(1)} collective-permute-done((f32[30720]{0:T(1024)S(1)}, f32[30720]{0:T(1024)S(1)}, u32[]{:S(2)}, u32[]{:S(2)}) %collective-permute-start.18) | collective-permute-done | bytes 122912 | tf_op jit(solution)/shard_map/ppermute | solution.py:73
  (813 shorter events, 554.4 us)
Async XLA Ops:
  7.2 869.6 %reduce-scatter.8.cloned.1.call-start = ((), (), s32[]{:S(2)}) async-start(), calls=%async_computation.6 | async-start | bytes 1310720 | tf_op jit(solution)/shard_map/reduce_scatter | solution.py:268
  15.8 300.5 %collective-permute-start.59 = (bf16[256,1024]{1,0:T(8,128)(2,1)}, bf16[256,1024]{1,0:T(8,128)(2,1)}, u32[]{:S(2)}, u32[]{:S(2)}) collective-permute-start(bf16[256,1024]{1,0:T(8,128)(2,1)} %fusion.236), channel_id=1, source_target_pairs={{0,24},{8,16},{16,8},{24,0},{1,25},{9,17},{17,9},{25,1},{2,26},{10... | collective-permute-start | bytes 1572872 | tf_op jit(solution)/shard_map/ppermute | solution.py:39
  19.3 297.1 %collective-permute-start.58 = (bf16[256,1024]{1,0:T(8,128)(2,1)}, bf16[256,1024]{1,0:T(8,128)(2,1)}, u32[]{:S(2)}, u32[]{:S(2)}) collective-permute-start(bf16[256,1024]{1,0:T(8,128)(2,1)} %fusion.236), channel_id=1, source_target_pairs={{0,16},{8,24},{16,0},{24,8},{1,17},{9,25},{17,1},{25,9},{2,18},{10... | collective-permute-start | bytes 1572872 | tf_op jit(solution)/shard_map/ppermute | solution.py:39
  19.8 296.5 %collective-permute-start.57 = (bf16[256,1024]{1,0:T(8,128)(2,1)}, bf16[256,1024]{1,0:T(8,128)(2,1)}, u32[]{:S(2)}, u32[]{:S(2)}) collective-permute-start(bf16[256,1024]{1,0:T(8,128)(2,1)} %fusion.236), channel_id=1, source_target_pairs={{0,8},{8,0},{16,24},{24,16},{1,9},{9,1},{17,25},{25,17},{2,10},{10... | collective-permute-start | bytes 1572872 | tf_op jit(solution)/shard_map/ppermute | solution.py:39
  299.7 32.0 %collective-permute-start.6 = (bf16[1,256,2048]{2,1,0:T(8,128)(2,1)}, bf16[1,256,2048]{2,1,0:T(8,128)(2,1)}, u32[]{:S(2)}, u32[]{:S(2)}) collective-permute-start(bf16[1,256,2048]{2,1,0:T(8,128)(2,1)} %fusion.161), channel_id=1, source_target_pairs={{0,1},{1,0},{2,3},{3,2},{4,5},{5,4},{6,7},{7,6},{8,9},{9,8},{10,11... | collective-permute-start | bytes 3145736 | tf_op jit(solution)/shard_map/ppermute | solution.py:64
  319.4 74.4 %collective-permute-start.60 = (bf16[1024,1024]{1,0:T(8,128)(2,1)}, bf16[1024,1024]{1,0:T(8,128)(2,1)}, u32[]{:S(2)}, u32[]{:S(2)}) collective-permute-start(bf16[1024,1024]{1,0:T(8,128)(2,1)} %pad_maximum_fusion.10), channel_id=1, source_target_pairs={{0,1},{1,0},{2,3},{3,2},{4,5},{5,4},{6,7},{7,6},{8,9},{9,8},{10,11... | collective-permute-start | bytes 6291464 | tf_op jit(solution)/shard_map/ppermute | solution.py:53
  335.6 52.4 %collective-permute-start.46 = (bf16[256,1024]{1,0:T(8,128)(2,1)S(1)}, bf16[256,1024]{1,0:T(8,128)(2,1)}, u32[]{:S(2)}, u32[]{:S(2)}) collective-permute-start(bf16[256,1024]{1,0:T(8,128)(2,1)S(1)} %dynamic-slice_bitcast_fusion.4), channel_id=1, source_target_pairs={{0,24},{8,16},{16,8},{24,0},{1,25},{9,17},{17,9},{25,1},{2,26},{10... | collective-permute-start | bytes 1572872 | tf_op jit(solution)/shard_map/ppermute | solution.py:39
  338.1 52.4 %collective-permute-start.45 = (bf16[256,1024]{1,0:T(8,128)(2,1)S(1)}, bf16[256,1024]{1,0:T(8,128)(2,1)}, u32[]{:S(2)}, u32[]{:S(2)}) collective-permute-start(bf16[256,1024]{1,0:T(8,128)(2,1)S(1)} %dynamic-slice_bitcast_fusion.4), channel_id=1, source_target_pairs={{0,16},{8,24},{16,0},{24,8},{1,17},{9,25},{17,1},{25,9},{2,18},{10... | collective-permute-start | bytes 1572872 | tf_op jit(solution)/shard_map/ppermute | solution.py:39
  338.6 52.4 %collective-permute-start.44 = (bf16[256,1024]{1,0:T(8,128)(2,1)S(1)}, bf16[256,1024]{1,0:T(8,128)(2,1)}, u32[]{:S(2)}, u32[]{:S(2)}) collective-permute-start(bf16[256,1024]{1,0:T(8,128)(2,1)S(1)} %dynamic-slice_bitcast_fusion.4), channel_id=1, source_target_pairs={{0,8},{8,0},{16,24},{24,16},{1,9},{9,1},{17,25},{25,17},{2,10},{10... | collective-permute-start | bytes 1572872 | tf_op jit(solution)/shard_map/ppermute | solution.py:39
  375.9 22.5 %collective-permute-start.9 = (bf16[1,256,2048]{2,1,0:T(8,128)(2,1)}, bf16[1,256,2048]{2,1,0:T(8,128)(2,1)}, u32[]{:S(2)}, u32[]{:S(2)}) collective-permute-start(bf16[1,256,2048]{2,1,0:T(8,128)(2,1)} %fusion.163), channel_id=1, source_target_pairs={{0,1},{1,0},{2,3},{3,2},{4,5},{5,4},{6,7},{7,6},{8,9},{9,8},{10,11... | collective-permute-start | bytes 3145736 | tf_op jit(solution)/shard_map/ppermute | solution.py:64
  388.1 122.5 %collective-permute-start.40 = (bf16[256,256]{1,0:T(8,128)(2,1)}, bf16[256,256]{1,0:T(8,128)(2,1)}, u32[]{:S(2)}, u32[]{:S(2)}) collective-permute-start(bf16[256,256]{1,0:T(8,128)(2,1)} %bitcast.125), channel_id=1, source_target_pairs={{0,24},{8,16},{16,8},{24,0},{1,25},{9,17},{17,9},{25,1},{2,26},{10... | collective-permute-start | bytes 393224 | tf_op jit(solution)/shard_map/ppermute | solution.py:32
  390.5 139.4 %collective-permute-start.39 = (bf16[256,256]{1,0:T(8,128)(2,1)}, bf16[256,256]{1,0:T(8,128)(2,1)}, u32[]{:S(2)}, u32[]{:S(2)}) collective-permute-start(bf16[256,256]{1,0:T(8,128)(2,1)} %bitcast.124), channel_id=1, source_target_pairs={{0,16},{8,24},{16,0},{24,8},{1,17},{9,25},{17,1},{25,9},{2,18},{10... | collective-permute-start | bytes 393224 | tf_op jit(solution)/shard_map/ppermute | solution.py:32
  409.1 24.4 %collective-permute-start.35 = (bf16[256,1024]{1,0:T(8,128)(2,1)S(1)}, bf16[256,1024]{1,0:T(8,128)(2,1)S(1)}, u32[]{:S(2)}, u32[]{:S(2)}) collective-permute-start(bf16[256,1024]{1,0:T(8,128)(2,1)S(1)} %dynamic-slice_bitcast_fusion.5), channel_id=1, source_target_pairs={{0,16},{8,24},{16,0},{24,8},{1,17},{9,25},{17,1},{25,9},{2,18},{10... | collective-permute-start | bytes 1572872 | tf_op jit(solution)/shard_map/ppermute | solution.py:39
  409.6 25.4 %collective-permute-start.34 = (bf16[256,1024]{1,0:T(8,128)(2,1)S(1)}, bf16[256,1024]{1,0:T(8,128)(2,1)S(1)}, u32[]{:S(2)}, u32[]{:S(2)}) collective-permute-start(bf16[256,1024]{1,0:T(8,128)(2,1)S(1)} %dynamic-slice_bitcast_fusion.5), channel_id=1, source_target_pairs={{0,8},{8,0},{16,24},{24,16},{1,9},{9,1},{17,25},{25,17},{2,10},{10... | collective-permute-start | bytes 1572872 | tf_op jit(solution)/shard_map/ppermute | solution.py:39
  423.4 106.5 %collective-permute-start.38 = (bf16[256,256]{1,0:T(8,128)(2,1)}, bf16[256,256]{1,0:T(8,128)(2,1)}, u32[]{:S(2)}, u32[]{:S(2)}) collective-permute-start(bf16[256,256]{1,0:T(8,128)(2,1)} %bitcast.123), channel_id=1, source_target_pairs={{0,8},{8,0},{16,24},{24,16},{1,9},{9,1},{17,25},{25,17},{2,10},{10... | collective-permute-start | bytes 393224 | tf_op jit(solution)/shard_map/ppermute | solution.py:32
  433.6 130.8 %collective-permute-start.50 = (bf16[2112,256]{1,0:T(8,128)(2,1)}, bf16[2112,256]{1,0:T(8,128)(2,1)}, u32[]{:S(2)}, u32[]{:S(2)}) collective-permute-start(bf16[2112,256]{1,0:T(8,128)(2,1)} %get-tuple-element.1116), channel_id=1, source_target_pairs={{0,24},{8,16},{16,8},{24,0},{1,25},{9,17},{17,9},{25,1},{2,26},{10... | collective-permute-start | bytes 3244040 | tf_op jit(solution)/shard_map/ppermute | solution.py:32
  436.6 70.7 %collective-permute-start.37 = (bf16[1024,1024]{1,0:T(8,128)(2,1)}, bf16[1024,1024]{1,0:T(8,128)(2,1)}, u32[]{:S(2)}, u32[]{:S(2)}) collective-permute-start(bf16[1024,1024]{1,0:T(8,128)(2,1)} %pad_maximum_fusion.8), channel_id=1, source_target_pairs={{0,1},{1,0},{2,3},{3,2},{4,5},{5,4},{6,7},{7,6},{8,9},{9,8},{10,11... | collective-permute-start | bytes 6291464 | tf_op jit(solution)/shard_map/ppermute | solution.py:53
  507.3 57.1 %collective-permute-start.49 = (bf16[2112,256]{1,0:T(8,128)(2,1)}, bf16[2112,256]{1,0:T(8,128)(2,1)}, u32[]{:S(2)}, u32[]{:S(2)}) collective-permute-start(bf16[2112,256]{1,0:T(8,128)(2,1)} %get-tuple-element.1117), channel_id=1, source_target_pairs={{0,16},{8,24},{16,0},{24,8},{1,17},{9,25},{17,1},{25,9},{2,18},{10... | collective-permute-start | bytes 3244040 | tf_op jit(solution)/shard_map/ppermute | solution.py:32
  510.6 53.9 %collective-permute-start.48 = (bf16[2112,256]{1,0:T(8,128)(2,1)}, bf16[2112,256]{1,0:T(8,128)(2,1)}, u32[]{:S(2)}, u32[]{:S(2)}) collective-permute-start(bf16[2112,256]{1,0:T(8,128)(2,1)} %get-tuple-element.1118), channel_id=1, source_target_pairs={{0,8},{8,0},{16,24},{24,16},{1,9},{9,1},{17,25},{25,17},{2,10},{10... | collective-permute-start | bytes 3244040 | tf_op jit(solution)/shard_map/ppermute | solution.py:32
  529.9 150.0 %collective-permute-start.47 = (bf16[1024,1024]{1,0:T(8,128)(2,1)}, bf16[1024,1024]{1,0:T(8,128)(2,1)}, u32[]{:S(2)}, u32[]{:S(2)}) collective-permute-start(bf16[1024,1024]{1,0:T(8,128)(2,1)} %pad_maximum_fusion.9), channel_id=1, source_target_pairs={{0,1},{1,0},{2,3},{3,2},{4,5},{5,4},{6,7},{7,6},{8,9},{9,8},{10,11... | collective-permute-start | bytes 6291464 | tf_op jit(solution)/shard_map/ppermute | solution.py:53
  529.9 31.6 %collective-permute-start.10 = (bf16[1,8,128,128]{3,2,1,0:T(8,128)(2,1)S(1)}, bf16[1,8,128,128]{3,2,1,0:T(8,128)(2,1)}, u32[]{:S(2)}, u32[]{:S(2)}) collective-permute-start(bf16[1,8,128,128]{3,2,1,0:T(8,128)(2,1)S(1)} %fusion.200), channel_id=1, source_target_pairs={{2,0},{4,2},{6,4},{3,1},{5,3},{7,5},{10,8},{12,10},{14,12},{11,9},... | collective-permute-start | bytes 786440 | tf_op jit(solution)/shard_map/ppermute | solution.py:18
  535.7 349.6 %reduce-scatter.14.cloned.1.call-start = ((), (), s32[]{:S(2)}) async-start(), calls=%async_computation.9 | async-start | bytes 3604480 | tf_op jit(solution)/shard_map/reduce_scatter | solution.py:268
  581.5 317.5 %reduce-scatter.10.cloned.1.call-start = ((), (), s32[]{:S(2)}) async-start(), calls=%async_computation.7 | async-start | bytes 3604480 | tf_op jit(solution)/shard_map/reduce_scatter | solution.py:268
  713.2 194.2 %reduce-scatter.12.cloned.1.call-start = ((), (), s32[]{:S(2)}) async-start(), calls=%async_computation.8 | async-start | bytes 3604480 | tf_op jit(solution)/shard_map/reduce_scatter | solution.py:268
  746.8 175.3 %reduce-scatter.6.cloned.1.call-start = ((), (), s32[]{:S(2)}) async-start(), calls=%async_computation.5 | async-start | bytes 3932160 | tf_op jit(solution)/shard_map/reduce_scatter | solution.py:268
  754.2 24.2 %collective-permute-start.20 = (bf16[256,1024]{1,0:T(8,128)(2,1)S(1)}, bf16[256,1024]{1,0:T(8,128)(2,1)S(1)}, u32[]{:S(2)}, u32[]{:S(2)}) collective-permute-start(bf16[256,1024]{1,0:T(8,128)(2,1)S(1)} %get-tuple-element.1135), channel_id=1, source_target_pairs={{0,16},{8,24},{16,0},{24,8},{1,17},{9,25},{17,1},{25,9},{2,18},{10... | collective-permute-start | bytes 1572872 | tf_op jit(solution)/shard_map/ppermute | solution.py:39
  754.7 23.7 %collective-permute-start.19 = (bf16[256,1024]{1,0:T(8,128)(2,1)S(1)}, bf16[256,1024]{1,0:T(8,128)(2,1)S(1)}, u32[]{:S(2)}, u32[]{:S(2)}) collective-permute-start(bf16[256,1024]{1,0:T(8,128)(2,1)S(1)} %get-tuple-element.1135), channel_id=1, source_target_pairs={{0,8},{8,0},{16,24},{24,16},{1,9},{9,1},{17,25},{25,17},{2,10},{10... | collective-permute-start | bytes 1572872 | tf_op jit(solution)/shard_map/ppermute | solution.py:39
  780.1 23.9 %collective-permute-start.22 = (bf16[1024,1024]{1,0:T(8,128)(2,1)}, bf16[1024,1024]{1,0:T(8,128)(2,1)}, u32[]{:S(2)}, u32[]{:S(2)}) collective-permute-start(bf16[1024,1024]{1,0:T(8,128)(2,1)} %pad_maximum_fusion.7), channel_id=1, source_target_pairs={{0,1},{1,0},{2,3},{3,2},{4,5},{5,4},{6,7},{7,6},{8,9},{9,8},{10,11... | collective-permute-start | bytes 6291464 | tf_op jit(solution)/shard_map/ppermute | solution.py:53
  793.3 24.7 %collective-permute-start.25 = (bf16[768,256]{1,0:T(8,128)(2,1)}, bf16[768,256]{1,0:T(8,128)(2,1)}, u32[]{:S(2)}, u32[]{:S(2)}) collective-permute-start(bf16[768,256]{1,0:T(8,128)(2,1)} %bitcast.1025), channel_id=1, source_target_pairs={{0,24},{8,16},{16,8},{24,0},{1,25},{9,17},{17,9},{25,1},{2,26},{10... | collective-permute-start | bytes 1179656 | tf_op jit(solution)/shard_map/ppermute | solution.py:32
  796.8 21.3 %collective-permute-start.24 = (bf16[768,256]{1,0:T(8,128)(2,1)}, bf16[768,256]{1,0:T(8,128)(2,1)}, u32[]{:S(2)}, u32[]{:S(2)}) collective-permute-start(bf16[768,256]{1,0:T(8,128)(2,1)} %bitcast.1026), channel_id=1, source_target_pairs={{0,16},{8,24},{16,0},{24,8},{1,17},{9,25},{17,1},{25,9},{2,18},{10... | collective-permute-start | bytes 1179656 | tf_op jit(solution)/shard_map/ppermute | solution.py:32
  803.0 30.6 %collective-permute-start.15 = (f32[30720]{0:T(1024)}, f32[30720]{0:T(1024)}, u32[]{:S(2)}, u32[]{:S(2)}) collective-permute-start(f32[30720]{0:T(1024)} %pad_maximum_fusion.25), channel_id=1, source_target_pairs={{0,8},{8,0},{16,24},{24,16},{1,9},{9,1},{17,25},{25,17},{2,10},{10... | collective-permute-start | bytes 368648 | tf_op jit(solution)/shard_map/ppermute | solution.py:73
  833.5 27.1 %collective-permute-start.7 = (bf16[1,256,2048]{2,1,0:T(8,128)(2,1)S(1)}, bf16[1,256,2048]{2,1,0:T(8,128)(2,1)}, u32[]{:S(2)}, u32[]{:S(2)}) collective-permute-start(bf16[1,256,2048]{2,1,0:T(8,128)(2,1)S(1)} %fusion.162), channel_id=1, source_target_pairs={{0,1},{1,0},{2,3},{3,2},{4,5},{5,4},{6,7},{7,6},{8,9},{9,8},{10,11... | collective-permute-start | bytes 3145736 | tf_op jit(solution)/shard_map/ppermute | solution.py:64
  (171 other events, 2019.3 us)
Sparse Core Ops, SparseCore 0:
  535.9 30.1 reduce-scatter.7
  581.6 57.9 reduce-scatter.13
  713.3 56.5 reduce-scatter.9
  772.1 56.0 reduce-scatter.11
  830.4 65.3 reduce-scatter.5

commit v2 on v1

v2 whole, which is shorter than its diff:
```python
import functools

import jax
import jax.numpy as jnp
from jax import lax
from jax.experimental import pallas as pl
from jax.experimental.pallas import tpu as pltpu
from jax.sharding import PartitionSpec as P

HEAD_DIM = 128


HIGH = lax.Precision.HIGHEST
EPSILON = 1e-05
UNIT_EPSILON = 1e-06


def passed_along(value, axis, by):
    peers = lax.axis_size(axis)
    pairs = [(i, i + by) for i in range(peers) if 0 <= i + by < peers]
    return lax.ppermute(value, axis, pairs)


def swap_pairs(axis, by):
    peers = lax.axis_size(axis)
    return [(i, i ^ by) for i in range(peers)]


def exchanged(values, axis):
    peers = lax.axis_size(axis)
    own = lax.axis_index(axis)
    parts = [lax.dynamic_index_in_dim(values, own, 0, keepdims=False)]
    for by in range(1, peers):
        out = lax.dynamic_index_in_dim(values, own ^ by, 0, keepdims=False)
        parts.append(lax.ppermute(out, axis, swap_pairs(axis, by)))
    return parts


def spread(value, axis):
    peers = lax.axis_size(axis)
    return [value] + [
        lax.ppermute(value, axis, swap_pairs(axis, by)) for by in range(1, peers)
    ]


def in_order(parts, axis):
    stacked = jnp.stack(parts, 0)
    own = lax.axis_index(axis)
    return [
        lax.dynamic_index_in_dim(stacked, own ^ k, 0, keepdims=False) for k in range(len(parts))
    ]


def gather_head(value, axis):
    if lax.axis_size("head") == 2:
        other = lax.ppermute(value, "head", [(0, 1), (1, 0)])
        first = lax.axis_index("head") == 0
        return jnp.concatenate(
            [jnp.where(first, value, other), jnp.where(first, other, value)], axis
        )
    return lax.all_gather(value, "head", axis=axis, tiled=True)


def sum_head(value):
    low = value.astype(jnp.bfloat16)
    if lax.axis_size("head") == 2:
        other = lax.ppermute(low, "head", [(0, 1), (1, 0)])
        return low.astype(jnp.float32) + other.astype(jnp.float32)
    return lax.psum(low, "head").astype(jnp.float32)


def sum_doubling(value, axes):
    for axis in axes:
        by = 1
        while by < lax.axis_size(axis):
            value = value + lax.ppermute(value, axis, swap_pairs(axis, by))
            by *= 2
    return value


def own_half(value, width):
    return lax.dynamic_slice_in_dim(value, lax.axis_index("head") * width, width, value.ndim - 1)


def chain_state(maps, shifts, reverse):
    peers = lax.axis_size("seq")
    by = -1 if reverse else 1
    states = [passed_along(shifts.astype(jnp.bfloat16), "seq", by)]
    for step in range(peers - 2):
        out = (
            jnp.einsum("hij,hjk->hik", maps, states[-1].astype(jnp.float32), precision=HIGH)
            + shifts
        )
        states.append(passed_along(out.astype(jnp.bfloat16), "seq", by))
    return states[-1]


def inverse_rms(values):
    return lax.rsqrt(jnp.mean(values * values, axis=-1, keepdims=True) + EPSILON)


def halves(a):
    top = a.astype(jnp.bfloat16)
    return top, (a - top.astype(jnp.float32)).astype(jnp.bfloat16)


def dot_low(a, b, dims=(1, 0)):
    return lax.dot_general(
        a, b, (((dims[0],), (dims[1],)), ((), ())), preferred_element_type=jnp.float32
    )


def dot_left(a, b, dims=(1, 0)):
    top, rest = halves(a)
    return dot_low(top, b, dims) + dot_low(rest, b, dims)


def dot_right(a, b, dims=(1, 0)):
    top, rest = halves(b)
    return dot_low(a, top, dims) + dot_low(a, rest, dims)


def dot_both(a, b, dims=(1, 0)):
    a_top, a_rest = halves(a)
    b_top, b_rest = halves(b)
    return dot_low(a_top, b_top, dims) + (
        dot_low(a_top, b_rest, dims) + dot_low(a_rest, b_top, dims)
    )


def grid_marks(size):
    row = lax.broadcasted_iota(jnp.int32, (size, size), 0)
    col = lax.broadcasted_iota(jnp.int32, (size, size), 1)
    return row, col


def unit_lower_inverses(tiles):
    size = tiles[0].shape[0]
    row, col = grid_marks(size)
    unit = (row == col).astype(jnp.float32)
    base = 8
    near = (row // base == col // base) & (row > col)
    cores = [jnp.where(near, tile, 0.0) for tile in tiles]
    squares = [dot_both(core, core) for core in cores]
    fourths = [dot_both(square, square) for square in squares]
    found = [dot_both(unit - core, unit + square) for core, square in zip(cores, squares)]
    found = [dot_both(part, unit + fourth) for part, fourth in zip(found, fourths)]
    while base < size:
        wide = 2 * base
        near = (row // wide == col // wide) & (row // base > col // base)
        links = [jnp.where(near, tile, 0.0) for tile in tiles]
        steps = [dot_both(part, link) for part, link in zip(found, links)]
        found = [part - dot_both(step, part) for part, step in zip(found, steps)]
        base = wide
    return found


def lower_inverses(systems, tile):
    size = systems[0].shape[0]
    if size <= tile:
        return unit_lower_inverses(systems)
    half = size // 2
    diagonals = [s[:half, :half] for s in systems] + [s[half:, half:] for s in systems]
    found = lower_inverses(diagonals, tile)
    firsts, seconds = found[: len(systems)], found[len(systems) :]
    steps = [dot_both(second, s[half:, :half]) for second, s in zip(seconds, systems)]
    corners = [-dot_both(step, first) for step, first in zip(steps, firsts)]
    empty = jnp.zeros((half, half), jnp.float32)
    return [
        jnp.concatenate(
            [jnp.concatenate([first, empty], 1), jnp.concatenate([corner, second], 1)], 0
        )
        for first, corner, second in zip(firsts, corners, seconds)
    ]


RIM = 16


def conv_sum(ext, pre, rim, weights, taps, length):
    ext[:RIM, :] = rim.astype(jnp.float32)
    ext[RIM : RIM + length, :] = pre.astype(jnp.float32)
    first = RIM - taps + 1
    summed = weights[0:1, :] * ext[first : first + length, :]
    for tap in range(1, taps):
        summed = summed + weights[tap : tap + 1, :] * ext[first + tap : first + tap + length, :]
    return summed


def head_columns(refs, index):
    span = slice(index * HEAD_DIM, (index + 1) * HEAD_DIM)
    return [ref[:, span] for ref in refs]


def unit_scale(rows):
    return lax.rsqrt(jnp.sum(rows * rows, axis=-1, keepdims=True) + UNIT_EPSILON)


def column_of(values, index):
    lane = lax.broadcasted_iota(jnp.int32, values.shape, 1)
    return jnp.sum(jnp.where(lane == index, values, 0.0), axis=-1, keepdims=True)


def row_of(values, index):
    place = lax.broadcasted_iota(jnp.int32, values.shape, 0)
    return jnp.sum(jnp.where(place == index, values, 0.0), axis=0, keepdims=True)


def mixer_local_kernel(
    per_step, taps, *refs
):
    (q_pre, k_pre, v_pre, q_rim, k_rim, v_rim, q_w, k_w, v_w, logit, logit_t, live, live_t) = refs[:13]
    q_out, k_out, v_out, wy_out, inv_out, mix_out, end_out, ext = refs[13:]
    length = q_pre.shape[0]
    step = pl.program_id(0)
    row, col = grid_marks(length)
    live_col = live[...]
    queries, keys, values, systems, beta_rows = [], [], [], [], []
    for i in range(per_step):
        pres = head_columns((q_pre, k_pre, v_pre), i)
        rims = head_columns((q_rim, k_rim, v_rim), i)
        weights = head_columns((q_w, k_w, v_w), i)
        active = []
        for pre, rim, weight in zip(pres, rims, weights):
            summed = conv_sum(ext, pre, rim, weight.astype(jnp.float32), taps, length)
            active.append(summed * jax.nn.sigmoid(summed))
        q, k, v = active
        q = (q * unit_scale(q)).astype(jnp.bfloat16)
        k = (k * unit_scale(k) * live_col).astype(jnp.bfloat16)
        v = v.astype(jnp.bfloat16)
        beta = jax.nn.sigmoid(column_of(logit[...], step * per_step + i)) * live_col
        beta_rows.append(jax.nn.sigmoid(row_of(logit_t[...], step * per_step + i)) * live_t[...])
        gram = dot_low(k, k, (1, 1))
        systems.append(jnp.where(row > col, beta * gram, 0.0))
        span = slice(i * HEAD_DIM, (i + 1) * HEAD_DIM)
        q_out[:, span] = q
        k_out[:, span] = k
        v_out[:, span] = v
        queries.append(q)
        keys.append(k)
        values.append(v)
    inverses = lower_inverses(systems, 128)
    wys = [
        dot_left(inverse * beta_row, jnp.concatenate([k, v], 1))
        for inverse, beta_row, k, v in zip(inverses, beta_rows, keys, values)
    ]
    unit = (lax.broadcasted_iota(jnp.int32, (HEAD_DIM, 2 * HEAD_DIM), 0)
            == lax.broadcasted_iota(jnp.int32, (HEAD_DIM, 2 * HEAD_DIM), 1)).astype(jnp.float32)
    left = (lax.broadcasted_iota(jnp.int32, (HEAD_DIM, 2 * HEAD_DIM), 1) < HEAD_DIM)
    for i in range(per_step):
        wy_out[i] = wys[i]
        inv_out[i] = inverses[i]
        ends = dot_right(keys[i], wys[i], (0, 0))
        end_out[i] = unit + jnp.where(left, -ends, ends)
        scores = jnp.where(row >= col, dot_low(queries[i], keys[i], (1, 1)), 0.0)
        seen = dot_both(scores, wys[i])
        mix_out[i, :, :HEAD_DIM] = queries[i].astype(jnp.float32) - seen[:, :HEAD_DIM]
        mix_out[i, :, HEAD_DIM:] = seen[:, HEAD_DIM:]


def mixer_finish_kernel(per_step, mix, state, gain, token, mixed_out, head_out):
    for i in range(per_step):
        span = slice(i * HEAD_DIM, (i + 1) * HEAD_DIM)
        mixed = mix[i, :, HEAD_DIM:] + dot_left(mix[i, :, :HEAD_DIM], state[i])
        scale = lax.rsqrt(jnp.mean(mixed * mixed, axis=-1, keepdims=True) + EPSILON)
        mixed_out[:, span] = mixed
        head_out[:, span] = (mixed * scale * gain[...]).astype(jnp.bfloat16)


def mixer_back_local_kernel(
    per_step, d_head, mixed_ref, gain_ref, q_ref, k_ref, wy, token,
    d_mixed_out, d_fresh_out, end_out, gain_out,
):
    length = q_ref.shape[0]
    row, col = grid_marks(length)
    gain = gain_ref[...]
    gain_total = jnp.zeros((1, HEAD_DIM), jnp.float32)
    for i in range(per_step):
        d_out, mixed, q, k = head_columns((d_head, mixed_ref, q_ref, k_ref), i)
        scale = lax.rsqrt(jnp.mean(mixed * mixed, axis=-1, keepdims=True) + EPSILON)
        weighted = gain * d_out
        inner = jnp.sum(weighted * mixed, axis=-1, keepdims=True)
        d_mixed = scale * weighted - mixed * (scale * scale * scale * inner / HEAD_DIM)
        gain_total += jnp.sum(d_out * mixed * scale, axis=0, keepdims=True)
        scores_t = jnp.where(col >= row, dot_low(k, q, (1, 1)), 0.0)
        d_fresh = dot_both(scores_t, d_mixed)
        d_mixed_out[i] = d_mixed
        d_fresh_out[i] = d_fresh
        end_out[i] = dot_right(q, d_mixed, (0, 0)) - dot_both(wy[i, :, :HEAD_DIM], d_fresh, (0, 0))

    @pl.when(pl.program_id(0) == 0)
    def _():
        gain_out[...] = jnp.zeros_like(gain_out)

    gain_out[...] += jnp.broadcast_to(gain_total, gain_out.shape)


def mixer_back_kernel(per_step, taps, *refs):
    (q_pre, k_pre, v_pre, q_rim, k_rim, v_rim, q_w, k_w, v_w, logit, live) = refs[:11]
    (q_ref, k_ref, v_ref, wy, inv, state, d_mixed_ref, d_fresh_ref, d_state) = refs[11:20]
    d_q_out, d_k_out, d_v_out, tail_out, rim_out, conv_out, d_logit_out, ext, ext_back = refs[20:]
    length = q_pre.shape[0]
    step = pl.program_id(0)
    row, col = grid_marks(length)
    live_col = live[...]

    @pl.when(step == 0)
    def _():
        d_logit_out[...] = jnp.zeros_like(d_logit_out)

    for i in range(per_step):
        q, k, v = head_columns((q_ref, k_ref, v_ref), i)
        entering, leaving = state[i], d_state[i]
        wy_both = wy[i]
        d_mixed = d_mixed_ref[i]
        d_fresh = d_fresh_ref[i] + dot_low(k, leaving)
        fresh = wy_both[:, HEAD_DIM:] - dot_left(wy_both[:, :HEAD_DIM], entering)
        d_scores = jnp.where(row >= col, dot_both(d_mixed, fresh, (1, 1)), 0.0)
        d_q = dot_left(d_mixed, entering, (1, 1)) + dot_left(d_scores, k)
        d_k = dot_left(d_scores, q, (0, 0)) + dot_left(fresh, leaving, (1, 1))
        d_wy = jnp.concatenate([-dot_left(d_fresh, entering, (1, 1)), d_fresh], 1)
        d_rhs = dot_both(inv[i], d_wy, (0, 0))
        edges = jnp.where(row > col, -dot_both(d_rhs, wy_both, (1, 1)), 0.0)
        logits = column_of(logit[...], step * per_step + i)
        sig = jax.nn.sigmoid(logits)
        beta = sig * live_col
        both = jnp.concatenate([k, v], 1).astype(jnp.float32)
        gram = dot_low(k, k, (1, 1))
        d_beta = jnp.sum(d_rhs * both, axis=-1, keepdims=True) + jnp.sum(
            edges * gram, axis=-1, keepdims=True
        )
        scaled = beta * edges
        d_k = d_k + beta * d_rhs[:, :HEAD_DIM] + dot_left(scaled, k) + dot_left(scaled, k, (0, 0))
        d_v = beta * d_rhs[:, HEAD_DIM:]
        d_k = d_k * live_col
        d_logit = d_beta * live_col * sig * (1.0 - sig)
        lane = lax.broadcasted_iota(jnp.int32, d_logit_out.shape, 1)
        d_logit_out[...] += jnp.where(lane == step * per_step + i, d_logit, 0.0)
        span = slice(i * HEAD_DIM, (i + 1) * HEAD_DIM)
        pres = head_columns((q_pre, k_pre, v_pre), i)
        rims = head_columns((q_rim, k_rim, v_rim), i)
        weights = head_columns((q_w, k_w, v_w), i)
        outs = (d_q_out, d_k_out, d_v_out)
        for part, (pre, rim, weight, grad) in enumerate(zip(pres, rims, weights, (d_q, d_k, d_v))):
            weight = weight.astype(jnp.float32)
            summed = conv_sum(ext, pre, rim, weight, taps, length)
            gate = jax.nn.sigmoid(summed)
            if part < 2:
                active = summed * gate
                scale = unit_scale(active)
                inner = jnp.sum(active * grad, axis=-1, keepdims=True)
                grad = scale * grad - active * (scale * scale * scale * inner)
            d_conv = grad * gate * (1.0 + summed * (1.0 - gate))
            first = RIM - taps + 1
            rows = [
                jnp.sum(d_conv * ext[first + tap : first + tap + length, :], axis=0, keepdims=True)
                for tap in range(taps)
            ]
            conv_out[part, :, span] = jnp.concatenate(rows, 0)
            ext_back[:8, :] = jnp.zeros((8, HEAD_DIM), jnp.float32)
            ext_back[8 : 8 + length, :] = d_conv
            ext_back[8 + length :, :] = jnp.zeros((8, HEAD_DIM), jnp.float32)
            own = jnp.zeros((length, HEAD_DIM), jnp.float32)
            before = jnp.zeros((8, HEAD_DIM), jnp.float32)
            for tap in range(taps):
                shift = taps - 1 - tap
                own = own + weight[tap : tap + 1, :] * ext_back[8 + shift : 8 + shift + length, :]
                before = before + weight[tap : tap + 1, :] * ext_back[shift : shift + 8, :]
            outs[part][:, span] = own.astype(jnp.bfloat16)
            tail_out[part, :, span] = own[length - 8 :, :]
            rim_out[part, :, span] = before


def mixer_specs(length, heads, per_step):
    width = per_step * HEAD_DIM

    def flat(rows):
        return pl.BlockSpec((rows, width), lambda h: (0, h))

    def whole(*shape):
        return pl.BlockSpec(shape, lambda h: (0,) * len(shape))

    def by_head(*shape):
        return pl.BlockSpec((per_step,) + shape, lambda h: (h,) + (0,) * len(shape))

    return flat, whole, by_head


def mixer_call(kernel, heads, per_step, ins, outs, scratch, flops, args):
    moved = sum(a.size * a.dtype.itemsize for a in args)
    return pl.pallas_call(
        kernel,
        grid=(heads // per_step,),
        in_specs=ins,
        out_specs=[spec for spec, _ in outs],
        out_shape=[shape for _, shape in outs],
        scratch_shapes=scratch,
        compiler_params=pltpu.CompilerParams(vmem_limit_bytes=40 * 1024 * 1024),
        cost_estimate=pl.CostEstimate(flops=flops, bytes_accessed=moved, transcendentals=0),
    )(*args)


def f32(*shape):
    return jax.ShapeDtypeStruct(shape, jnp.float32)


def b16(*shape):
    return jax.ShapeDtypeStruct(shape, jnp.bfloat16)


def mixer_local(pres, rims, convs, logit, live, per_step):
    length, channels = pres[0].shape
    heads = channels // HEAD_DIM
    taps = convs[0].shape[0]
    flat, whole, by_head = mixer_specs(length, heads, per_step)
    args = (*pres, *rims, *convs, logit, logit.T, live, live.T)
    return mixer_call(
        functools.partial(mixer_local_kernel, per_step, taps),
        heads,
        per_step,
        [flat(length)] * 3
        + [flat(RIM)] * 3
        + [flat(taps)] * 3
        + [whole(length, heads), whole(heads, length), whole(length, 1), whole(1, length)],
        [(flat(length), b16(length, channels))] * 3
        + [
            (by_head(length, 2 * HEAD_DIM), f32(heads, length, 2 * HEAD_DIM)),
            (by_head(length, length), f32(heads, length, length)),
            (by_head(length, 2 * HEAD_DIM), f32(heads, length, 2 * HEAD_DIM)),
            (by_head(HEAD_DIM, 2 * HEAD_DIM), f32(heads, HEAD_DIM, 2 * HEAD_DIM)),
        ],
        [pltpu.VMEM((RIM + length, HEAD_DIM), jnp.float32)],
        heads * 2 * length**3 * 30,
        args,
    )


def mixer_finish(mix, state, gain, token, per_step):
    heads, length, _ = mix.shape
    flat, whole, by_head = mixer_specs(length, heads, per_step)
    return mixer_call(
        functools.partial(mixer_finish_kernel, per_step),
        heads,
        per_step,
        [
            by_head(length, 2 * HEAD_DIM),
            by_head(HEAD_DIM, HEAD_DIM),
            whole(1, HEAD_DIM),
            pl.BlockSpec(memory_space=pl.ANY),
        ],
        [
            (flat(length), f32(length, heads * HEAD_DIM)),
            (flat(length), b16(length, heads * HEAD_DIM)),
        ],
        [],
        heads * 2 * length**3,
        (mix, state, gain, token),
    )


def mixer_back_local(d_head, mixed, gain, q, k, wy, token, per_step):
    heads, length, _ = wy.shape
    flat, whole, by_head = mixer_specs(length, heads, per_step)
    return mixer_call(
        functools.partial(mixer_back_local_kernel, per_step),
        heads,
        per_step,
        [flat(length)] * 2
        + [whole(1, HEAD_DIM)]
        + [flat(length)] * 2
        + [by_head(length, 2 * HEAD_DIM), pl.BlockSpec(memory_space=pl.ANY)],
        [
            (by_head(length, HEAD_DIM), f32(heads, length, HEAD_DIM)),
            (by_head(length, HEAD_DIM), f32(heads, length, HEAD_DIM)),
            (by_head(HEAD_DIM, HEAD_DIM), f32(heads, HEAD_DIM, HEAD_DIM)),
            (whole(8, HEAD_DIM), f32(8, HEAD_DIM)),
        ],
        [],
        heads * 2 * length**3 * 5,
        (d_head, mixed, gain, q, k, wy, token),
    )


def mixer_back(pres, rims, convs, logit, live, q, k, v, wy, inv, state, d_mixed, d_fresh, d_state, per_step):
    length, channels = pres[0].shape
    heads = channels // HEAD_DIM
    taps = convs[0].shape[0]
    flat, whole, by_head = mixer_specs(length, heads, per_step)
    three = pl.BlockSpec((3, 8, per_step * HEAD_DIM), lambda h: (0, 0, h))
    return mixer_call(
        functools.partial(mixer_back_kernel, per_step, taps),
        heads,
        per_step,
        [flat(length)] * 3
        + [flat(RIM)] * 3
        + [flat(taps)] * 3
        + [whole(length, heads), whole(length, 1)]
        + [flat(length)] * 3
        + [
            by_head(length, 2 * HEAD_DIM),
            by_head(length, length),
            by_head(HEAD_DIM, HEAD_DIM),
            by_head(length, HEAD_DIM),
            by_head(length, HEAD_DIM),
            by_head(HEAD_DIM, HEAD_DIM),
        ],
        [(flat(length), b16(length, channels))] * 3
        + [
            (three, f32(3, 8, channels)),
            (three, f32(3, 8, channels)),
            (
                pl.BlockSpec((3, taps, per_step * HEAD_DIM), lambda h: (0, 0, h)),
                f32(3, taps, channels),
            ),
            (whole(length, heads), f32(length, heads)),
        ],
        [
            pltpu.VMEM((RIM + length, HEAD_DIM), jnp.float32),
            pltpu.VMEM((16 + length, HEAD_DIM), jnp.float32),
        ],
        heads * 2 * length**3 * 20,
        (*pres, *rims, *convs, logit, live, q, k, v, wy, inv, state, d_mixed, d_fresh, d_state),
    )


def feed_kernel(x_ref, d_ref, gate_w, up_w, down_w, feed_out, d_x_out, turned_out, feed_sum, d_x_sum):
    step = pl.program_id(0)
    x = x_ref[...]
    d_out = d_ref[...]
    gate = dot_low(x, gate_w[...])
    up = dot_low(x, up_w[...])
    d_hidden = dot_low(d_out, down_w[...], (1, 1))
    sig = jax.nn.sigmoid(gate)
    hidden = (gate * sig * up).astype(jnp.bfloat16)
    d_gate = (d_hidden * up * sig * (1.0 + gate * (1.0 - sig))).astype(jnp.bfloat16)
    d_up = (d_hidden * gate * sig).astype(jnp.bfloat16)
    for place, part in enumerate((hidden, d_gate, d_up)):
        turned_out[place] = part.T
    feed = dot_low(hidden, down_w[...])
    d_x = dot_low(d_gate, gate_w[...], (1, 1)) + dot_low(d_up, up_w[...], (1, 1))

    @pl.when(step == 0)
    def _():
        feed_sum[...] = feed
        d_x_sum[...] = d_x

    @pl.when(step > 0)
    def _():
        feed_sum[...] += feed
        d_x_sum[...] += d_x

    @pl.when(step == pl.num_programs(0) - 1)
    def _():
        feed_out[...] = feed_sum[...].astype(jnp.bfloat16)
        d_x_out[...] = d_x_sum[...].astype(jnp.bfloat16)


def feed_forward(x, d_out, gate_weight, up_weight, down_weight):
    length, width = x.shape
    units = gate_weight.shape[1]
    tile = 256 if units % 256 == 0 else units
    whole = pl.BlockSpec((length, width), lambda f: (0, 0))
    column = pl.BlockSpec((width, tile), lambda f: (0, f))
    return pl.pallas_call(
        feed_kernel,
        grid=(units // tile,),
        in_specs=[whole, whole, column, column, pl.BlockSpec((tile, width), lambda f: (f, 0))],
        out_specs=[whole, whole, pl.BlockSpec((3, tile, length), lambda f: (0, f, 0))],
        out_shape=[b16(length, width), b16(length, width), b16(3, units, length)],
        scratch_shapes=[pltpu.VMEM((length, width), jnp.float32)] * 2,
        compiler_params=pltpu.CompilerParams(vmem_limit_bytes=40 * 1024 * 1024),
        cost_estimate=pl.CostEstimate(
            flops=12 * length * width * units,
            bytes_accessed=6 * width * units,
            transcendentals=length * units,
        ),
    )(x, d_out, gate_weight, up_weight, down_weight)


MESH = pl.DeviceIdType.MESH


def partner(own, by):
    other = own
    bit = 1
    while bit <= by:
        if by & bit:
            other = other + bit - 2 * bit * ((own // bit) % 2)
        bit *= 2
    return other


def place(name, index):
    return {name: index}


def meet(devices):
    barrier = pltpu.get_barrier_semaphore()
    for device in devices:
        pl.semaphore_signal(barrier, inc=1, device_id=device, device_id_type=MESH)
    pl.semaphore_wait(barrier, len(devices))


def exchange_kernel(ways, kinds, *refs):
    count = len(kinds)
    sources, outs = refs[:count], refs[-4 - count : -4]
    sends, receives, hand_sends, hand_receives = refs[-4:]
    own = lax.axis_index("dp")
    core = lax.axis_index("head")
    peers = [partner(own, by) for by in range(1, ways)]
    other_core = place("head", 1 - core)
    shared = any(kind[0] == "halves" for kind in kinds)
    meet([place("dp", peer) for peer in peers] + ([other_core] if shared else []))
    copies, halves = [], []
    for index, (kind, source, out) in enumerate(zip(kinds, sources, outs)):
        for by in range(1, ways):
            peer = peers[by - 1]
            if kind[0] == "rows":
                src = source.at[kind[1] : kind[2], peer]
                dst = out.at[by - 1]
            elif kind[0] == "columns":
                width = source.shape[1] // ways
                src = source.at[:, pl.ds(pl.multiple_of(peer * width, width), width)]
                dst = out.at[by - 1]
            else:
                width = source.shape[1] // 2
                mine = pl.ds(pl.multiple_of(core * width, width), width)
                src = source.at[:, mine]
                dst = out.at[by - 1, :, mine]
            copy = pltpu.make_async_remote_copy(
                src_ref=src,
                dst_ref=dst,
                send_sem=sends.at[index * (ways - 1) + by - 1],
                recv_sem=receives.at[index * (ways - 1) + by - 1],
                device_id=place("dp", peer),
                device_id_type=MESH,
            )
            copy.start()
            copies.append(copy)
            if kind[0] == "halves":
                halves.append((index, by, copy, dst))
    handed = []
    for index, by, copy, dst in halves:
        copy.wait_recv()
        hand = pltpu.make_async_remote_copy(
            src_ref=dst,
            dst_ref=dst,
            send_sem=hand_sends.at[index * (ways - 1) + by - 1],
            recv_sem=hand_receives.at[index * (ways - 1) + by - 1],
            device_id=other_core,
            device_id_type=MESH,
        )
        hand.start()
        handed.append(hand)
    first_hops = [copy for _, _, copy, _ in halves]
    for copy in copies:
        copy.wait_send()
        if not any(copy is first for first in first_hops):
            copy.wait_recv()
    for hand in handed:
        hand.wait()


def plane_exchange(sources, kinds, tokens, number):
    ways = lax.axis_size("dp")
    shapes = []
    for source, kind in zip(sources, kinds):
        if kind[0] == "rows":
            shape = (ways - 1, kind[2] - kind[1]) + source.shape[2:]
        elif kind[0] == "columns":
            shape = (ways - 1, source.shape[0], source.shape[1] // ways)
        else:
            shape = (ways - 1,) + source.shape
        shapes.append(b16(*shape))
    anywhere = pl.BlockSpec(memory_space=pl.ANY)
    sems = pltpu.SemaphoreType.DMA((len(sources) * (ways - 1),))
    return pl.pallas_call(
        functools.partial(exchange_kernel, ways, kinds),
        out_shape=shapes,
        in_specs=[anywhere] * (len(sources) + len(tokens)),
        out_specs=[anywhere] * len(sources),
        scratch_shapes=[sems] * 4,
        compiler_params=pltpu.CompilerParams(collective_id=number, has_side_effects=True),
        cost_estimate=pl.CostEstimate(
            flops=0, bytes_accessed=40 * sum(s.size for s in shapes), transcendentals=0
        ),
    )(*sources, *tokens)


def chain_kernel(spans, reverse, ends, shifts, out, arriving, leaving, sends, receives):
    position = lax.axis_index("seq")
    heads = out.shape[0]
    step = -1 if reverse else 1
    first, last = (spans - 1, 0) if reverse else (0, spans - 1)
    meet([place("seq", (position + spans - 1) % spans), place("seq", (position + 1) % spans)])

    def copy_of(head):
        return pltpu.make_async_remote_copy(
            src_ref=leaving.at[head],
            dst_ref=arriving.at[head],
            send_sem=sends.at[head],
            recv_sem=receives.at[head],
            device_id=place("seq", position + step),
            device_id_type=MESH,
        )

    for head in range(heads):

        @pl.when(position == first)
        def _():
            out[head] = jnp.zeros_like(out[head])
            leaving[head] = shifts[head].astype(jnp.bfloat16)

        @pl.when(position != first)
        def _():
            copy_of(head).wait_recv()
            out[head] = arriving[head]

            @pl.when(position != last)
            def _():
                dims = (0, 0) if reverse else (1, 0)
                moved = dot_left(ends[head, :, :HEAD_DIM], arriving[head], dims)
                leaving[head] = (moved + shifts[head]).astype(jnp.bfloat16)

        @pl.when(position != last)
        def _():
            copy_of(head).start()

    @pl.when(position != last)
    def _():
        for head in range(heads):
            copy_of(head).wait_send()


def chained_states(ends, shifts, reverse, number):
    heads = ends.shape[0]
    state = (heads, HEAD_DIM, HEAD_DIM)
    inside = pl.BlockSpec(memory_space=pltpu.VMEM)
    return pl.pallas_call(
        functools.partial(chain_kernel, lax.axis_size("seq"), reverse),
        out_shape=b16(*state),
        in_specs=[inside] * 2,
        out_specs=inside,
        scratch_shapes=[
            pltpu.VMEM(state, jnp.bfloat16),
            pltpu.VMEM(state, jnp.bfloat16),
            pltpu.SemaphoreType.DMA((heads,)),
            pltpu.SemaphoreType.DMA((heads,)),
        ],
        compiler_params=pltpu.CompilerParams(collective_id=number, has_side_effects=True),
        cost_estimate=pl.CostEstimate(
            flops=0, bytes_accessed=40 * heads * HEAD_DIM * HEAD_DIM * 16, transcendentals=0
        ),
    )(ends, shifts)


def pieces_kernel(slots, ways, turned, at, *refs):
    lefts = refs[:slots]
    rights = refs[slots : slots + slots * ways]
    out, left_all, right_all = refs[slots + slots * ways + 1 :]
    length = rights[0].shape[0]
    rows = rights[0].shape[1]

    @pl.when(pl.program_id(0) == 0)
    def _():
        for slot in range(slots):
            span = slice(slot * length, (slot + 1) * length)
            block = lefts[slot][...]
            block = block.reshape((-1,) + block.shape[-2:])
            count = left_all.shape[0] // block.shape[0]
            for part in range(block.shape[0]):
                left_all[part * count : (part + 1) * count, span] = (
                    block[part] if turned else block[part].T
                )

    for slot in range(slots):
        for way in range(ways):
            right = rights[slot * ways + way][...]
            right_all[
                slot * length : (slot + 1) * length, way * rows : (way + 1) * rows
            ] = right.reshape(right.shape[-2:])
    out[0] = dot_low(left_all[...], right_all[...]).astype(jnp.bfloat16)


def span_pieces(lefts, count, rights, length, width, spans, turned, token):
    slots = len(lefts)
    ways = lax.axis_size("dp")
    rows = width // (ways * spans)

    def left_block(block, at_place):
        return pl.BlockSpec(block, lambda s, at: at_place(at[0]))

    def right_block(block, at_place, way):
        return pl.BlockSpec(
            block + (rows,), lambda s, at: tuple(at_place(at[0])) + (way * spans + s,)
        )

    return pl.pallas_call(
        functools.partial(pieces_kernel, slots, ways, turned),
        grid_spec=pltpu.PrefetchScalarGridSpec(
            num_scalar_prefetch=1,
            grid=(spans,),
            in_specs=[left_block(block, where) for _, block, where in lefts]
            + [right_block(block, where, way) for _, block, where in rights for way in range(ways)]
            + [pl.BlockSpec(memory_space=pl.ANY)],
            out_specs=pl.BlockSpec((1, count, ways * rows), lambda s, at: (s, 0, 0)),
            scratch_shapes=[
                pltpu.VMEM((count, slots * length), jnp.bfloat16),
                pltpu.VMEM((slots * length, ways * rows), jnp.bfloat16),
            ],
        ),
        out_shape=b16(spans, count, ways * rows),
        compiler_params=pltpu.CompilerParams(vmem_limit_bytes=32 * 1024 * 1024),
        cost_estimate=pl.CostEstimate(
            flops=2 * count * width * slots * length,
            bytes_accessed=4 * slots * length * width,
            transcendentals=0,
        ),
    )(
        lax.axis_index("dp")[None],
        *[array for array, _, _ in lefts],
        *[array for array, _, _ in rights for _ in range(ways)],
        token,
    )


def shards(
    tokens_in,
    lengths,
    first_gain,
    query_weight,
    key_weight,
    value_weight,
    beta_weight,
    query_conv,
    key_conv,
    value_conv,
    mixer_gain,
    output_weight,
    second_gain,
    gate_weight,
    up_weight,
    down_weight,
    upstream,
):
    num_rows, local_len, local_width = tokens_in.shape
    full_width = query_weight.shape[0]
    channels = query_weight.shape[1]
    local_heads = beta_weight.shape[1]
    groups = lax.axis_size("head")
    ways = lax.axis_size("dp")
    spans = lax.axis_size("seq")
    positions = lax.axis_index("seq") * local_len + jnp.arange(local_len, dtype=jnp.int32)
    live_mask = (positions[None, :] < lengths[:, None]).astype(jnp.float32)
    masked_up = upstream * live_mask[..., None].astype(jnp.bfloat16)
    gains = jnp.stack([first_gain, second_gain] + [first_gain] * 14)
    everything = gather_head(jnp.concatenate([tokens_in[0], masked_up[0], gains], 0), 1)
    gathered = everything[None, :local_len]
    upstream_full = everything[None, local_len : 2 * local_len]
    gain_one = everything[2 * local_len].astype(jnp.float32)
    gain_two = everything[2 * local_len + 1].astype(jnp.float32)
    stream_full = gathered.astype(jnp.float32)
    scale_one = inverse_rms(stream_full)
    normed_one = (stream_full * scale_one * gain_one).astype(jnp.bfloat16)

    def scattered(pieces):
        return lax.psum_scatter(pieces, "seq", scatter_dimension=0, tiled=False)

    def to_owner(piece):
        c = piece.shape[0]
        blocks = piece.reshape(c, ways, -1).transpose(1, 0, 2)
        return jnp.stack(in_order(exchanged(blocks, "dp"), "dp"), 0)

    if groups == 2:
        half_up = lax.all_gather(masked_up[0], "dp", axis=0, tiled=True)
        half_one = lax.all_gather(own_half(normed_one[0], local_width), "dp", axis=0, tiled=True)
        tokens_up = gather_head(half_up, 1)
        tokens_one = gather_head(half_one, 1)
    else:
        tokens_up = jnp.stack(spread(upstream_full[0], "dp")[1:])
        tokens_one = jnp.stack(spread(normed_one[0], "dp")[1:])
    per_step = 2 if local_heads % 2 == 0 else 1
    pres = [
        jnp.dot(normed_one[0], weight, preferred_element_type=jnp.float32).astype(jnp.bfloat16)
        for weight in (query_weight, key_weight, value_weight)
    ]
    beta_logit = jnp.dot(normed_one[0], beta_weight, preferred_element_type=jnp.float32)
    rims = passed_along(jnp.stack([pre[local_len - RIM :, :] for pre in pres]), "seq", 1)
    rims = [rims[0], rims[1], rims[2]]
    convs = [query_conv, key_conv, value_conv]
    live_col = live_mask[0][:, None]
    query, key, value, wy, inverse, mix, ends = mixer_local(
        pres, rims, convs, beta_logit, live_col, per_step
    )
    fused = groups == 2
    if fused:
        entering = chained_states(ends, ends[:, :, HEAD_DIM:], False, 1)
    else:
        entering = chain_state(ends[:, :, :HEAD_DIM], ends[:, :, HEAD_DIM:], False)
    head_gain = mixer_gain.astype(jnp.float32)[None, :]
    mixed, head_out = mixer_finish(
        mix, entering, head_gain, half_up if fused else entering, per_step
    )
    head_out = head_out[None]
    mixer_part = jnp.dot(head_out, output_weight, preferred_element_type=jnp.float32)
    stream_mid = stream_full + sum_head(mixer_part)
    scale_two = inverse_rms(stream_mid)
    normed_two = (stream_mid * scale_two * gain_two).astype(jnp.bfloat16)
    feed_part, d_two_part, turned = feed_forward(
        normed_two[0], upstream_full[0], gate_weight, up_weight, down_weight
    )
    layer_out = own_half(stream_mid + sum_head(feed_part[None]), local_width).astype(jnp.bfloat16)
    units = turned.shape[1] // ways
    turned = turned.reshape(3, ways, units, local_len)

    def piece(lefts, count, rights, is_turned, token):
        return scattered(
            span_pieces(
                lefts, count, rights, local_len, full_width, spans, is_turned, token
            )
        )

    def slots_of(own, others):
        return [(own, (local_len,), lambda at: (0,))] + [
            (others, (1, local_len), lambda at, by=by: (by, 0)) for by in range(ways - 1)
        ]

    def by_position(array):
        return [(array, (local_len,), lambda at, by=by: (at ^ by,)) for by in range(ways)]

    def feed_slots(which, others, index):
        own = [(turned, (1, 1, units, local_len), lambda at: (which, at, 0, 0))]
        return own + [
            (others, (1, 1, units, local_len), lambda at, by=by: (by, index, 0, 0))
            for by in range(ways - 1)
        ]

    normed_full = normed_two[0]
    if fused:
        (hidden_others,) = plane_exchange([turned], [("rows", 0, 1)], [half_one], 2)
        down_raw = span_pieces(
            feed_slots(0, hidden_others, 0), units, by_position(tokens_up),
            local_len, full_width, spans, True, feed_part,
        )
        d_others, two_others = plane_exchange(
            [turned, normed_full], [("rows", 1, 3), ("halves",)], [down_raw], 3
        )
    else:
        hidden_others = jnp.stack(exchanged(turned[:1].transpose(1, 0, 2, 3), "dp")[1:])
        down_raw = span_pieces(
            feed_slots(0, hidden_others, 0), units, slots_of(upstream_full[0], tokens_up),
            local_len, full_width, spans, True, feed_part,
        )
        d_others = jnp.stack(exchanged(turned[1:].transpose(1, 0, 2, 3), "dp")[1:])
        two_others = jnp.stack(spread(normed_full, "dp")[1:])
    down_piece = scattered(down_raw)
    two_slots = slots_of(normed_full, two_others)
    gate_piece = piece(feed_slots(1, d_others, 0), units, two_slots, True, down_piece)
    up_raw = span_pieces(
        feed_slots(2, d_others, 1), units, two_slots,
        local_len, full_width, spans, True, feed_part,
    )
    up_piece = scattered(up_raw)
    d_two = sum_head(d_two_part[None])
    d_stream = (
        upstream_full.astype(jnp.float32)
        + scale_two * gain_two * d_two
        - stream_mid
        * scale_two
        * scale_two
        * scale_two
        * (jnp.sum(d_two * gain_two * stream_mid, axis=-1, keepdims=True) / full_width)
    )
    grad_second = own_half(jnp.sum(d_two * stream_mid * scale_two, axis=(0, 1)), local_width)
    residual_full = d_stream.astype(jnp.bfloat16)
    d_head_out = jnp.einsum(
        "rsd,cd->rsc", residual_full, output_weight, preferred_element_type=jnp.float32
    )
    d_mixed, d_fresh, d_ends, grad_gain_part = mixer_back_local(
        d_head_out[0], mixed, head_gain, query, key, wy, up_raw, per_step
    )
    grad_gain_part = grad_gain_part[0]
    if fused:
        leaving = chained_states(ends, d_ends, True, 4)
    else:
        leaving = chain_state(jnp.swapaxes(ends[:, :, :HEAD_DIM], 1, 2), d_ends, True)
    *d_pres, tails, d_rims, grad_kernels, d_beta_logit = mixer_back(
        pres, rims, convs, beta_logit, live_col, query, key, value, wy, inverse,
        entering, d_mixed, d_fresh, leaving, per_step,
    )
    share_width = channels // ways
    residual = residual_full[0]
    if fused:
        out_others, res_others = plane_exchange(
            [head_out[0], residual], [("columns",), ("halves",)], [gate_piece], 5
        )
    else:
        out_others = jnp.stack(
            exchanged(head_out[0].reshape(local_len, ways, -1).transpose(1, 0, 2), "dp")[1:]
        )
        res_others = jnp.stack(spread(residual, "dp")[1:])

    def column_slots(own, others):
        if fused:
            first = [(own, (local_len, share_width), lambda at: (0, at))]
        else:
            mine = lax.dynamic_slice_in_dim(
                own, lax.axis_index("dp") * share_width, share_width, 1
            )
            first = [(mine, (local_len, share_width), lambda at: (0, 0))]
        return first + [
            (others, (1, local_len, share_width), lambda at, by=by: (by, 0, 0))
            for by in range(ways - 1)
        ]

    out_raw = span_pieces(
        column_slots(head_out[0], out_others), share_width, slots_of(residual, res_others),
        local_len, full_width, spans, False, d_rims,
    )
    out_piece = scattered(out_raw)
    tails = (tails + passed_along(d_rims, "seq", -1)).astype(jnp.bfloat16)
    d_pre_query, d_pre_key, d_pre_value = [
        jnp.concatenate([part[: local_len - 8], tail], 0)[None] for part, tail in zip(d_pres, tails)
    ]
    d_logit_low = d_beta_logit.astype(jnp.bfloat16)[None]
    d_normed_one = (
        jnp.einsum("rsc,dc->rsd", d_pre_query, query_weight, preferred_element_type=jnp.float32)
        + jnp.einsum("rsc,dc->rsd", d_pre_key, key_weight, preferred_element_type=jnp.float32)
        + jnp.einsum("rsc,dc->rsd", d_pre_value, value_weight, preferred_element_type=jnp.float32)
        + jnp.einsum("rsh,dh->rsd", d_logit_low, beta_weight, preferred_element_type=jnp.float32)
    )
    mix_sources = [d_pre_query[0], d_pre_key[0], d_pre_value[0]]
    if fused:
        mix_others = plane_exchange(mix_sources, [("columns",)] * 3, [up_piece, out_raw], 6)
        one_slots = by_position(tokens_one)
    else:
        mix_others = [
            jnp.stack(exchanged(part.reshape(local_len, ways, -1).transpose(1, 0, 2), "dp")[1:])
            for part in mix_sources
        ]
        one_slots = slots_of(normed_one[0], tokens_one)
    mix_raw = jnp.concatenate(
        [
            span_pieces(
                column_slots(own, others), share_width, one_slots,
                local_len, full_width, spans, False, d_rims,
            )
            for own, others in zip(mix_sources, mix_others)
        ],
        1,
    )
    mix_piece = scattered(mix_raw)
    grad_beta_part = jnp.einsum(
        "rsd,rsh->dh", normed_one, d_logit_low, preferred_element_type=jnp.float32
    )
    d_one = sum_head(d_normed_one)
    grad_tokens = own_half(
        d_stream
        + scale_one * gain_one * d_one
        - stream_full
        * scale_one
        * scale_one
        * scale_one
        * (jnp.sum(d_one * gain_one * stream_full, axis=-1, keepdims=True) / full_width),
        local_width,
    )
    grad_first = own_half(jnp.sum(d_one * stream_full * scale_one, axis=(0, 1)), local_width)
    small = [grad_first, grad_second, grad_kernels.reshape(-1), grad_beta_part.reshape(-1)]
    total = sum_doubling(jnp.concatenate(small + [grad_gain_part]), ("dp", "seq"))
    gain_total = sum_doubling(total[-HEAD_DIM:], ("head",))
    grad_first = total[:local_width]
    grad_second = total[local_width : 2 * local_width]
    kernel_end = 2 * local_width + grad_kernels.size
    kernel_sum = total[2 * local_width : kernel_end].reshape(grad_kernels.shape)
    share = lax.axis_index("dp") * spans + lax.axis_index("seq")
    rows = full_width // (ways * spans)
    grad_beta = lax.dynamic_slice_in_dim(
        total[kernel_end:-HEAD_DIM].reshape(full_width, local_heads), share * rows, rows, 0
    )
    feed = to_owner(jnp.concatenate([down_piece, gate_piece, up_piece], 0)).astype(jnp.float32)
    down, gate, up = [
        feed[:, place * units : (place + 1) * units].reshape(-1, rows) for place in range(3)
    ]
    out = to_owner(out_piece).reshape(-1, rows).astype(jnp.float32)
    mix = to_owner(mix_piece).astype(jnp.float32)
    third = mix.shape[1] // 3
    return (
        layer_out,
        grad_tokens,
        grad_first,
        mix[:, :third].reshape(-1, rows).T,
        mix[:, third : 2 * third].reshape(-1, rows).T,
        mix[:, 2 * third :].reshape(-1, rows).T,
        grad_beta,
        kernel_sum[0],
        kernel_sum[1],
        kernel_sum[2],
        gain_total,
        out,
        grad_second,
        gate.T,
        up.T,
        down,
    )


def solution(mesh):
    placed = (
        P("dp", "seq", "head"),
        P("dp"),
        P("head"),
        P(None, "head"),
        P(None, "head"),
        P(None, "head"),
        P(None, "head"),
        P(None, "head"),
        P(None, "head"),
        P(None, "head"),
        P(),
        P("head", None),
        P("head"),
        P(None, "head"),
        P(None, "head"),
        P("head", None),
        P("dp", "seq", "head"),
    )
    return jax.shard_map(
        shards,
        mesh=mesh,
        in_specs=placed,
        out_specs=(
            P("dp", "seq", "head"),
            P("dp", "seq", "head"),
            P("head"),
            P(("dp", "seq"), "head"),
            P(("dp", "seq"), "head"),
            P(("dp", "seq"), "head"),
            P(("dp", "seq"), "head"),
            P(None, "head"),
            P(None, "head"),
            P(None, "head"),
            P(),
            P("head", ("dp", "seq")),
            P("head"),
            P(("dp", "seq"), "head"),
            P(("dp", "seq"), "head"),
            P("head", ("dp", "seq")),
        ),
        check_vma=False,
    )
```

time: 960 us -> 565 us (0.59)
  Pallas kernels: 0 us -> 283 us
  matrix products: 272 us -> 19.4 us
  other arithmetic: 262 us -> 34.2 us
  local copies, waits for them, and re-layouts: 208 us -> 105 us
  starting transfers between devices: 80.7 us -> 21.7 us
  waiting for transfers between devices: 106 us -> 75.5 us
    pallas_call x0 -> x18, Pallas kernels: none -> 283 us  [the longest x4 134 us: plane_exchange(): pl.pallas_call(functools.partial(exchange_kernel, ways, kinds), out_shape...]
    dot_general x135 -> x4, matrix products: 254 us -> 4.17 us  [the longest x3 3.8 us: shards(): jnp.dot(normed_one[0], weight, preferred_element_type=jnp.float32)]
    another operation x10 -> x2, other arithmetic: 163 us -> 2.38 us  [the longest x5 160 us: prepare(): lax.linalg.triangular_solve(system, weighted, left_side=True, lower=True,...]
    reshape x17 -> x0, local copies, waits for them, and re-layouts: 63 us -> none  [the longest x8 57 us: tokens_of_plane(): part.reshape(part.shape[0], ways, spans, -1).transpose(2, 0, 1, 3)]
    unnamed x277 -> x244, local copies, waits for them, and re-layouts: 26.9 us -> 75.2 us
    ppermute x12 -> x0, waiting for transfers between devices: 42.5 us -> none  [spread(): lax.ppermute(value, axis, swap_pairs(axis, by))]
    dynamic_update_slice x20 -> x0, local copies, waits for them, and re-layouts: 20.3 us -> none  [run_blocks(): state, mixed = lax.scan(block_step, state, moved)]
    another operation x22 -> x7, local copies, waits for them, and re-layouts: 23.8 us -> 3.57 us
  transfers between devices with their start and end apart: 69 -> 30, of which waited for: 27 -> 14; matrix products, arithmetic and copies ran while one was open for 76% -> 13% of each run, Pallas kernels for 0% -> 48%
where the time goes in v2:
time: 565 us; the launch traced here: 555 us
  Pallas kernels  283 us (50%)
  local copies, waits for them, and re-layouts  105 us (19%)
  waiting for transfers between devices  75.5 us (13%)
  other arithmetic  34.2 us (6%)
  starting transfers between devices  21.7 us (4%)
  matrix products  19.4 us (3%)
  between operations  16.4 us (3%)
    pallas_call x4, Pallas kernels, plane_exchange(): pl.pallas_call(functools.partial(exchange_kernel, ways, kinds), out_shape...  134 us
    unnamed x244, local copies, waits for them, and re-layouts  75.2 us
    pallas_call x2, Pallas kernels, chained_states(): pl.pallas_call(functools.partial(chain_kernel, lax.axis_size('seq'), reve...  45 us
    pallas_call x4, Pallas kernels, mixer_call(): pl.pallas_call(kernel, grid=(heads // per_step,), in_specs=ins, out_specs...  39.4 us
    pallas_call x7, Pallas kernels, span_pieces(): pl.pallas_call(functools.partial(pieces_kernel, slots, ways, turned), gri...  36.5 us
    ppermute x5, waiting for transfers between devices, sum_doubling(): value = value + lax.ppermute(value, axis, swap_pairs(axis, by))  31.7 us
    pallas_call x1, Pallas kernels, feed_forward(): pl.pallas_call(feed_kernel, grid=(units // tile,), in_specs=[whole, whole...  28.3 us
    ppermute x9, waiting for transfers between devices, exchanged(): parts.append(lax.ppermute(out, axis, swap_pairs(axis, by)))  25.3 us
  transfers between devices with their start and end apart: 30, of which 14 were waited for; matrix products, arithmetic and copies ran while one was open for 13% of the time, Pallas kernels for 48%

profile of v2, /device:TPU:0, one launch (start us, length us, event | category | flops | bytes accessed | tf_op | source)
XLA Modules:
  0.0 555.5 jit_solution(9184432441001775299)
XLA Ops:
  26.3 4.9 collective-permute-start.1
  38.8 15.2 %shard_map.288 = (bf16[256,1024]{1,0:T(8,128)(2,1)S(1)}, bf16[256,1024]{1,0:T(8,128)(2,1)S(1)}, bf16[256,1024]{1,0:T(8,128)(2,1)S(1)}, f32[8,256,256]{2,1,0:T(8,...) custom-call(bf16[256,1024]{1,0:T(8,128)(2,1)S(1)} %copy-done.55, ...), custom_call_target="tpu_custom_call" | custom-call | flops 8053063680 | bytes 1714176 | tf_op jit(solution)/shard_map/pallas_call | solution.py:391
  60.3 11.7 %shard_map.289.state.refs_16_ = bf16[8,128,128]{2,1,0:T(8,128)(2,1)} custom-call(f32[8,128,256]{2,1,0:T(8,128)} %copy-done.25, f32[8,128,128]{2,1,0:T(8,128)} %slice.121.shifts), custom_call_target="tpu_custom_call" | custom-call | bytes 83886080 | tf_op jit(solution)/shard_map/pallas_call | solution.py:739
  86.0 28.3 %shard_map.291 = (bf16[256,2048]{1,0:T(8,128)(2,1)S(1)}, bf16[256,2048]{1,0:T(8,128)(2,1)S(1)}, bf16[3,2816,256]{2,1,0:T(8,128)(2,1)S(1)}) custom-call(bf16[256,2048]{1,0:T(8,128)(2,1)S(1)} %fusion.17.x_ref.refs_1_.refs_4_.refs_5_.refs_6_.refs_7_, bf16[256,2048]{1,0:T(8,128)(2,1)S(1)} %pad_maximum_fusion.4.d_ref, bf16[2048,2816]{1,0:T(8,128)(2,1)} %gate_w.1, ...), custom_call_target="tpu_custom_call" | custom-call | flops 17716740096 | bytes 34603008 | tf_op jit(solution)/shard_map/pallas_call | solution.py:564
  118.3 4.4 all-gather.4.cloned.1.call-done.refs_1_
  122.7 19.2 %shard_map.292.refs_1_.refs_2_.refs_3_ = bf16[3,1,704,256]{3,2,1,0:T(8,128)(2,1)} custom-call(bf16[3,4,704,256]{3,2,1,0:T(8,128)(2,1)} %bitcast.152, bf16[1024,1024]{1,0:T(8,128)(2,1)} %all-gather.4.cloned.1.call-done.refs_1_), custom_call_target="tpu_custom_call" | custom-call | bytes 21626880 | tf_op jit(solution)/shard_map/pallas_call | solution.py:677
  146.6 7.1 %shard_map.293.refs_2_ = bf16[4,704,512]{2,1,0:T(8,128)(2,1)} custom-call(s32[1]{0:T(128)} %bitcast.22.at, bf16[3,4,704,256]{3,2,1,0:T(8,128)(2,1)S(1)} %bitcast.156, bf16[3,1,704,256]{3,2,1,0:T(8,128)(2,1)S(1)} %copy-done.17, bf16[3,1,704,256]{3,2,1,0:T(8,128)(2,1)S(1)} %copy-done.17, bf16[3,1,704,256]{3,2,1,0:T(8,128)(2,1)S(1)} %copy-done.17, ...), custom_call_target="tpu_custom_call" | custom-call | flops 2952790016 | bytes 8388608 | tf_op jit(solution)/shard_map/pallas_call | solution.py:798
  153.7 58.7 %shard_map.294 = (bf16[3,2,704,256]{3,2,1,0:T(8,128)(2,1)}, bf16[3,256,2048]{2,1,0:T(8,128)(2,1)}) custom-call(bf16[3,4,704,256]{3,2,1,0:T(8,128)(2,1)} %bitcast.153, bf16[256,2048]{1,0:T(8,128)(2,1)} %copy-done.8, bf16[4,704,512]{2,1,0:T(8,128)(2,1)} %shard_map.293.refs_2_), custom_call_target="tpu_custom_call" | custom-call | bytes 106168320 | tf_op jit(solution)/shard_map/pallas_call | solution.py:677
  221.6 5.8 %shard_map.299 = bf16[4,704,512]{2,1,0:T(8,128)(2,1)S(1)} custom-call(s32[1]{0:T(128)} %bitcast.22.at, bf16[3,4,704,256]{3,2,1,0:T(8,128)(2,1)S(1)} %bitcast.157, bf16[3,2,704,256]{3,2,1,0:T(8,128)(2,1)S(1)} %copy-done.11, bf16[3,2,704,256]{3,2,1,0:T(8,128)(2,1)S(1)} %copy-done.11, bf16[3,2,704,256]{3,2,1,0:T(8,128)(2,1)S(1)} %copy-done.11, ...), custom_call_target="tpu_custom_call" | custom-call | flops 2952790016 | bytes 8388608 | tf_op jit(solution)/shard_map/pallas_call | solution.py:798
  235.3 5.8 %shard_map.295.token = bf16[4,704,512]{2,1,0:T(8,128)(2,1)S(1)} custom-call(s32[1]{0:T(128)} %bitcast.22.at, bf16[3,4,704,256]{3,2,1,0:T(8,128)(2,1)S(1)} %bitcast.158, bf16[3,2,704,256]{3,2,1,0:T(8,128)(2,1)S(1)} %copy-done.12, bf16[3,2,704,256]{3,2,1,0:T(8,128)(2,1)S(1)} %copy-done.12, bf16[3,2,704,256]{3,2,1,0:T(8,128)(2,1)S(1)} %copy-done.12, ...), custom_call_target="tpu_custom_call" | custom-call | flops 2952790016 | bytes 8388608 | tf_op jit(solution)/shard_map/pallas_call | solution.py:798
  246.6 3.0 multiply_reduce_fusion
  255.4 4.7 shard_map.296
  262.9 33.3 %shard_map.297.refs_19_ = bf16[8,128,128]{2,1,0:T(8,128)(2,1)} custom-call(f32[8,128,256]{2,1,0:T(8,128)} %copy-done.25, f32[8,128,128]{2,1,0:T(8,128)} %copy-done.52), custom_call_target="tpu_custom_call" | custom-call | bytes 83886080 | tf_op jit(solution)/shard_map/pallas_call | solution.py:739
  307.2 18.0 %shard_map.298 = (bf16[256,1024]{1,0:T(8,128)(2,1)S(1)}, bf16[256,1024]{1,0:T(8,128)(2,1)S(1)}, bf16[256,1024]{1,0:T(8,128)(2,1)S(1)}, f32[3,8,1024]{2,1,0:T(8,1...) custom-call(bf16[256,1024]{1,0:T(8,128)(2,1)S(1)} %copy-done.56, ...), custom_call_target="tpu_custom_call" | custom-call | flops 5368709120 | bytes 10093568 | tf_op jit(solution)/shard_map/pallas_call | solution.py:391
  329.7 8.6 %collective-permute-done.6 = f32[3,8,1024]{2,1,0:T(8,128)S(1)} collective-permute-done((f32[3,8,1024]{2,1,0:T(8,128)S(1)}, f32[3,8,1024]{2,1,0:T(8,128)S(1)}, u32[]{:S(2)}, u32[]{:S(2)}) %collective-permute-start.6) | collective-permute-done | bytes 98336 | tf_op jit(solution)/shard_map/ppermute | solution.py:21
  338.4 3.8 fusion.29
  342.2 2.6 convolution_add_fusion.2
  344.8 34.2 %shard_map.300 = (bf16[3,256,256]{2,1,0:T(8,128)(2,1)}, bf16[3,256,2048]{2,1,0:T(8,128)(2,1)}) custom-call(bf16[256,1024]{1,0:T(8,128)(2,1)} %copy-done.39, bf16[256,2048]{1,0:T(8,128)(2,1)} %copy-done.13, bf16[704,512]{1,0:T(8,128)(2,1)} %bitcast.169), custom_call_target="tpu_custom_call" | custom-call | bytes 70778880 | tf_op jit(solution)/shard_map/pallas_call | solution.py:677
  381.9 4.6 shard_map.301.refs_4_
  386.5 4.5 convolution_add_fusion.1
  399.1 21.4 %shard_map.302 = (bf16[3,256,256]{2,1,0:T(8,128)(2,1)}, bf16[3,256,256]{2,1,0:T(8,128)(2,1)}, bf16[3,256,256]{2,1,0:T(8,128)(2,1)}) custom-call(bf16[256,1024]{1,0:T(8,128)(2,1)} %pad_maximum_fusion.6.refs_0_, bf16[256,1024]{1,0:T(8,128)(2,1)} %pad_maximum_fusion.7.refs_1_.refs_0_, bf16[256,1024]{1,0:T(8,128)(2,1)} %pad_maximum_fusion.8.refs_2_.refs_0_, ...), custom_call_target="tpu_custom_call" | custom-call | bytes 23592960 | tf_op jit(solution)/shard_map/pallas_call | solution.py:677
  423.8 4.5 shard_map.303
  428.4 4.4 shard_map.304
  432.8 4.4 shard_map.305
  448.1 4.4 collective-permute-done.9
  453.0 11.8 %collective-permute-done.10 = f32[30848]{0:T(1024)S(1)} collective-permute-done((f32[30848]{0:T(1024)S(1)}, f32[30848]{0:T(1024)S(1)}, u32[]{:S(2)}, u32[]{:S(2)}) %collective-permute-start.10) | collective-permute-done | bytes 123424 | tf_op jit(solution)/shard_map/ppermute | solution.py:76
  466.2 13.2 %collective-permute-done.11 = f32[30848]{0:T(1024)S(1)} collective-permute-done((f32[30848]{0:T(1024)S(1)}, f32[30848]{0:T(1024)S(1)}, u32[]{:S(2)}, u32[]{:S(2)}) %collective-permute-start.11) | collective-permute-done | bytes 123424 | tf_op jit(solution)/shard_map/ppermute | solution.py:76
  496.4 7.3 %collective-permute-done.20 = bf16[2112,128]{1,0:T(8,128)(2,1)S(1)} collective-permute-done((bf16[2112,128]{1,0:T(8,128)(2,1)}, bf16[2112,128]{1,0:T(8,128)(2,1)S(1)}, u32[]{:S(2)}, u32[]{:S(2)}) %collective-permute-start.20) | collective-permute-done | bytes 540704 | tf_op jit(solution)/shard_map/ppermute | solution.py:35
  503.7 12.0 %collective-permute-done.21 = bf16[2112,128]{1,0:T(8,128)(2,1)S(1)} collective-permute-done((bf16[2112,128]{1,0:T(8,128)(2,1)}, bf16[2112,128]{1,0:T(8,128)(2,1)S(1)}, u32[]{:S(2)}, u32[]{:S(2)}) %collective-permute-start.21) | collective-permute-done | bytes 540704 | tf_op jit(solution)/shard_map/ppermute | solution.py:35
  523.9 3.6 fusion.33
  539.0 3.0 collective-permute-done.13
  542.0 3.0 collective-permute-done.14
  (396 shorter events, 167.8 us)
Async XLA Ops:
  7.2 64.8 %all-gather.6.cloned.1.call-start = ((), (), s32[]{:S(2)}) async-start(), calls=%async_computation.11 | async-start | bytes 2621440 | tf_op jit(solution)/shard_map/all_gather | solution.py:875
  12.7 2.9 collective-permute-start
  14.2 108.5 %all-gather.4.cloned.1.call-start = ((), (), s32[]{:S(2)}) async-start(), calls=%async_computation.5 | async-start | bytes 2621440 | tf_op jit(solution)/shard_map/all_gather | solution.py:876
  26.3 7.2 %collective-permute-start.1 = (bf16[3,16,1024]{2,1,0:T(8,128)(2,1)S(1)}, bf16[3,16,1024]{2,1,0:T(8,128)(2,1)S(1)}, u32[]{:S(2)}, u32[]{:S(2)}) collective-permute-start(bf16[3,16,1024]{2,1,0:T(8,128)(2,1)S(1)} %pad_maximum_fusion.11), channel_id=1, source_target_pairs={{0,2},{2,4},{4,6},{1,3},{3,5},{5,7},{8,10},{10,12},{12,14},{9,11},... | collective-permute-start | bytes 294920 | tf_op jit(solution)/shard_map/ppermute | solution.py:21
  79.0 3.3 collective-permute-start.2
  79.9 133.6 %reduce-scatter.8.cloned.1.call-start = ((), (), s32[]{:S(2)}) async-start(), calls=%async_computation.7 | async-start | bytes 3604480 | tf_op jit(solution)/shard_map/reduce_scatter | solution.py:867
  81.8 60.1 %collective-permute-start.5 = (bf16[1024,1024]{1,0:T(8,128)(2,1)S(1)}, bf16[1024,1024]{1,0:T(8,128)(2,1)}, u32[]{:S(2)}, u32[]{:S(2)}) collective-permute-start(bf16[1024,1024]{1,0:T(8,128)(2,1)S(1)} %bitcast.160), channel_id=1, source_target_pairs={{0,1},{1,0},{2,3},{3,2},{4,5},{5,4},{6,7},{7,6},{8,9},{9,8},{10,11... | collective-permute-start | bytes 6291464 | tf_op jit(solution)/shard_map/ppermute | solution.py:56
  153.7 191.1 %reduce-scatter.10.cloned.1.call-start = ((), (), s32[]{:S(2)}) async-start(), calls=%async_computation.8 | async-start | bytes 3604480 | tf_op jit(solution)/shard_map/reduce_scatter | solution.py:867
  229.0 170.2 %reduce-scatter.6.cloned.1.call-start = ((), (), s32[]{:S(2)}) async-start(), calls=%async_computation.6 | async-start | bytes 3604480 | tf_op jit(solution)/shard_map/reduce_scatter | solution.py:867
  242.7 275.8 %reduce-scatter.14.cloned.1.call-start = ((), (), s32[]{:S(2)}) async-start(), calls=%async_computation.10 | async-start | bytes 1310720 | tf_op jit(solution)/shard_map/reduce_scatter | solution.py:867
  243.9 2.7 collective-permute-start.4
  244.6 198.5 %collective-permute-start.3 = (bf16[1,256,2048]{2,1,0:T(8,128)(2,1)S(1)}, bf16[1,256,2048]{2,1,0:T(8,128)(2,1)}, u32[]{:S(2)}, u32[]{:S(2)}) collective-permute-start(bf16[1,256,2048]{2,1,0:T(8,128)(2,1)S(1)} %bitcast.161), channel_id=1, source_target_pairs={{0,1},{1,0},{2,3},{3,2},{4,5},{5,4},{6,7},{7,6},{8,9},{9,8},{10,11... | collective-permute-start | bytes 3145736 | tf_op jit(solution)/shard_map/ppermute | solution.py:67
  245.2 149.3 %collective-permute-start.12 = (bf16[1024,1024]{1,0:T(8,128)(2,1)}, bf16[1024,1024]{1,0:T(8,128)(2,1)}, u32[]{:S(2)}, u32[]{:S(2)}) collective-permute-start(bf16[1024,1024]{1,0:T(8,128)(2,1)} %all-gather.4.cloned.1.call-done.refs_1_), channel_id=1, source_target_pairs={{0,1},{1,0},{2,3},{3,2},{4,5},{5,4},{6,7},{7,6},{8,9},{9,8},{10,11... | collective-permute-start | bytes 6291464 | tf_op jit(solution)/shard_map/ppermute | solution.py:56
  255.4 40.8 %copy-start.70 = (bf16[4,1024]{1,0:T(4,128)(2,1)S(1)}, bf16[4,1024]{1,0:T(4,128)(2,1)}, u32[]{:S(2)}) copy-start(bf16[4,1024]{1,0:T(4,128)(2,1)} %refs_7_.3) | copy-start | bytes 24580
  255.4 40.9 %copy-start.72 = (bf16[4,1024]{1,0:T(4,128)(2,1)S(1)}, bf16[4,1024]{1,0:T(4,128)(2,1)}, u32[]{:S(2)}) copy-start(bf16[4,1024]{1,0:T(4,128)(2,1)} %refs_8_.3) | copy-start | bytes 24580
  325.2 13.2 %collective-permute-start.6 = (f32[3,8,1024]{2,1,0:T(8,128)S(1)}, f32[3,8,1024]{2,1,0:T(8,128)S(1)}, u32[]{:S(2)}, u32[]{:S(2)}) collective-permute-start(f32[3,8,1024]{2,1,0:T(8,128)S(1)} %get-tuple-element.65.refs_20_), channel_id=1, source_target_pairs={{2,0},{4,2},{6,4},{3,1},{5,3},{7,5},{10,8},{12,10},{14,12},{11,9},... | collective-permute-start | bytes 294920 | tf_op jit(solution)/shard_map/ppermute | solution.py:21
  386.5 144.3 %reduce-scatter.12.cloned.1.call-start = ((), (), s32[]{:S(2)}) async-start(), calls=%async_computation.9 | async-start | bytes 3932160 | tf_op jit(solution)/shard_map/reduce_scatter | solution.py:867
  391.5 47.6 %collective-permute-start.7 = (bf16[1,256,2048]{2,1,0:T(8,128)(2,1)S(1)}, bf16[1,256,2048]{2,1,0:T(8,128)(2,1)}, u32[]{:S(2)}, u32[]{:S(2)}) collective-permute-start(bf16[1,256,2048]{2,1,0:T(8,128)(2,1)S(1)} %fusion.7), channel_id=1, source_target_pairs={{0,1},{1,0},{2,3},{3,2},{4,5},{5,4},{6,7},{7,6},{8,9},{9,8},{10,11... | collective-permute-start | bytes 3145736 | tf_op jit(solution)/shard_map/ppermute | solution.py:67
  442.5 5.0 collective-permute-start.8
  447.5 5.0 collective-permute-start.9
  452.5 12.3 %collective-permute-start.10 = (f32[30848]{0:T(1024)S(1)}, f32[30848]{0:T(1024)S(1)}, u32[]{:S(2)}, u32[]{:S(2)}) collective-permute-start(f32[30848]{0:T(1024)S(1)} %add.183), channel_id=1, source_target_pairs={{0,2},{2,0},{4,6},{6,4},{1,3},{3,1},{5,7},{7,5},{8,10},{10,8},{12,... | collective-permute-start | bytes 370184 | tf_op jit(solution)/shard_map/ppermute | solution.py:76
  464.8 14.5 %collective-permute-start.11 = (f32[30848]{0:T(1024)S(1)}, f32[30848]{0:T(1024)S(1)}, u32[]{:S(2)}, u32[]{:S(2)}) collective-permute-start(f32[30848]{0:T(1024)S(1)} %add.184), channel_id=1, source_target_pairs={{0,4},{2,6},{4,0},{6,2},{1,5},{3,7},{5,1},{7,3},{8,12},{10,14},{12... | collective-permute-start | bytes 370184 | tf_op jit(solution)/shard_map/ppermute | solution.py:76
  479.4 16.5 %collective-permute-start.16 = (f32[128]{0:T(128)S(1)}, f32[128]{0:T(128)S(1)}, u32[]{:S(2)}, u32[]{:S(2)}) collective-permute-start(f32[128]{0:T(128)S(1)} %slice.165), channel_id=1, source_target_pairs={{0,1},{1,0},{2,3},{3,2},{4,5},{5,4},{6,7},{7,6},{8,9},{9,8},{10,11... | collective-permute-start | bytes 1544 | tf_op jit(solution)/shard_map/ppermute | solution.py:76
  488.4 15.3 %collective-permute-start.20 = (bf16[2112,128]{1,0:T(8,128)(2,1)}, bf16[2112,128]{1,0:T(8,128)(2,1)S(1)}, u32[]{:S(2)}, u32[]{:S(2)}) collective-permute-start(bf16[2112,128]{1,0:T(8,128)(2,1)} %get-tuple-element.116), channel_id=1, source_target_pairs={{0,8},{8,0},{16,24},{24,16},{1,9},{9,1},{17,25},{25,17},{2,10},{10... | collective-permute-start | bytes 1622024 | tf_op jit(solution)/shard_map/ppermute | solution.py:35
  489.5 26.2 %collective-permute-start.21 = (bf16[2112,128]{1,0:T(8,128)(2,1)}, bf16[2112,128]{1,0:T(8,128)(2,1)S(1)}, u32[]{:S(2)}, u32[]{:S(2)}) collective-permute-start(bf16[2112,128]{1,0:T(8,128)(2,1)} %get-tuple-element.115), channel_id=1, source_target_pairs={{0,16},{8,24},{16,0},{24,8},{1,17},{9,25},{17,1},{25,9},{2,18},{10... | collective-permute-start | bytes 1622024 | tf_op jit(solution)/shard_map/ppermute | solution.py:35
  489.5 26.2 %collective-permute-start.22 = (bf16[2112,128]{1,0:T(8,128)(2,1)S(1)}, bf16[2112,128]{1,0:T(8,128)(2,1)S(1)}, u32[]{:S(2)}, u32[]{:S(2)}) collective-permute-start(bf16[2112,128]{1,0:T(8,128)(2,1)S(1)} %get-tuple-element.114), channel_id=1, source_target_pairs={{0,24},{8,16},{16,8},{24,0},{1,25},{9,17},{17,9},{25,1},{2,26},{10... | collective-permute-start | bytes 1622024 | tf_op jit(solution)/shard_map/ppermute | solution.py:35
  520.2 10.4 %collective-permute-start.17 = (bf16[256,128]{1,0:T(8,128)(2,1)S(1)}, bf16[256,128]{1,0:T(8,128)(2,1)S(1)}, u32[]{:S(2)}, u32[]{:S(2)}) collective-permute-start(bf16[256,128]{1,0:T(8,128)(2,1)S(1)} %bitcast.197), channel_id=1, source_target_pairs={{0,8},{8,0},{16,24},{24,16},{1,9},{9,1},{17,25},{25,17},{2,10},{10... | collective-permute-start | bytes 196616 | tf_op jit(solution)/shard_map/ppermute | solution.py:35
  521.1 9.4 %collective-permute-start.18 = (bf16[256,128]{1,0:T(8,128)(2,1)S(1)}, bf16[256,128]{1,0:T(8,128)(2,1)S(1)}, u32[]{:S(2)}, u32[]{:S(2)}) collective-permute-start(bf16[256,128]{1,0:T(8,128)(2,1)S(1)} %bitcast.198), channel_id=1, source_target_pairs={{0,16},{8,24},{16,0},{24,8},{1,17},{9,25},{17,1},{25,9},{2,18},{10... | collective-permute-start | bytes 196616 | tf_op jit(solution)/shard_map/ppermute | solution.py:35
  522.4 8.2 %collective-permute-start.19 = (bf16[256,128]{1,0:T(8,128)(2,1)S(1)}, bf16[256,128]{1,0:T(8,128)(2,1)S(1)}, u32[]{:S(2)}, u32[]{:S(2)}) collective-permute-start(bf16[256,128]{1,0:T(8,128)(2,1)S(1)} %bitcast.199), channel_id=1, source_target_pairs={{0,24},{8,16},{16,8},{24,0},{1,25},{9,17},{17,9},{25,1},{2,26},{10... | collective-permute-start | bytes 196616 | tf_op jit(solution)/shard_map/ppermute | solution.py:35
  534.4 7.6 %collective-permute-start.13 = (bf16[768,128]{1,0:T(8,128)(2,1)S(1)}, bf16[768,128]{1,0:T(8,128)(2,1)S(1)}, u32[]{:S(2)}, u32[]{:S(2)}) collective-permute-start(bf16[768,128]{1,0:T(8,128)(2,1)S(1)} %bitcast.188), channel_id=1, source_target_pairs={{0,8},{8,0},{16,24},{24,16},{1,9},{9,1},{17,25},{25,17},{2,10},{10... | collective-permute-start | bytes 589832 | tf_op jit(solution)/shard_map/ppermute | solution.py:35
  535.4 9.5 %collective-permute-start.14 = (bf16[768,128]{1,0:T(8,128)(2,1)S(1)}, bf16[768,128]{1,0:T(8,128)(2,1)S(1)}, u32[]{:S(2)}, u32[]{:S(2)}) collective-permute-start(bf16[768,128]{1,0:T(8,128)(2,1)S(1)} %bitcast.189), channel_id=1, source_target_pairs={{0,16},{8,24},{16,0},{24,8},{1,17},{9,25},{17,1},{25,9},{2,18},{10... | collective-permute-start | bytes 589832 | tf_op jit(solution)/shard_map/ppermute | solution.py:35
  536.6 8.3 %collective-permute-start.15 = (bf16[768,128]{1,0:T(8,128)(2,1)S(1)}, bf16[768,128]{1,0:T(8,128)(2,1)S(1)}, u32[]{:S(2)}, u32[]{:S(2)}) collective-permute-start(bf16[768,128]{1,0:T(8,128)(2,1)S(1)} %bitcast.190), channel_id=1, source_target_pairs={{0,24},{8,16},{16,8},{24,0},{1,25},{9,17},{17,9},{25,1},{2,26},{10... | collective-permute-start | bytes 589832 | tf_op jit(solution)/shard_map/ppermute | solution.py:35
  (111 other events, 524.3 us)
Sparse Core Ops, SparseCore 0:
  14.3 37.7 all-gather.5
  80.0 42.5 all-gather.3
  153.8 59.6 reduce-scatter.7
  229.1 64.4 reduce-scatter.9
  295.7 58.1 reduce-scatter.5
  386.6 23.5 reduce-scatter.13
  439.2 61.8 reduce-scatter.11

commit v3 on v2

v3 whole, which is shorter than its diff:
```python
import functools

import jax
import jax.numpy as jnp
from jax import lax
from jax.experimental import pallas as pl
from jax.experimental.pallas import tpu as pltpu
from jax.sharding import PartitionSpec as P

HEAD_DIM = 128


HIGH = lax.Precision.HIGHEST
EPSILON = 1e-05
UNIT_EPSILON = 1e-06
VMEM = 56 * 1024 * 1024
SHORT = pl.CostEstimate(flops=0, bytes_accessed=0, transcendentals=0)


def passed_along(value, axis, by):
    peers = lax.axis_size(axis)
    pairs = [(i, i + by) for i in range(peers) if 0 <= i + by < peers]
    return lax.ppermute(value, axis, pairs)


def swap_pairs(axis, by):
    peers = lax.axis_size(axis)
    return [(i, i ^ by) for i in range(peers)]


def exchanged(values, axis):
    peers = lax.axis_size(axis)
    own = lax.axis_index(axis)
    parts = [lax.dynamic_index_in_dim(values, own, 0, keepdims=False)]
    for by in range(1, peers):
        out = lax.dynamic_index_in_dim(values, own ^ by, 0, keepdims=False)
        parts.append(lax.ppermute(out, axis, swap_pairs(axis, by)))
    return parts


def spread(value, axis):
    peers = lax.axis_size(axis)
    return [value] + [
        lax.ppermute(value, axis, swap_pairs(axis, by)) for by in range(1, peers)
    ]


def in_order(parts, axis):
    stacked = jnp.stack(parts, 0)
    own = lax.axis_index(axis)
    return [
        lax.dynamic_index_in_dim(stacked, own ^ k, 0, keepdims=False) for k in range(len(parts))
    ]


def gather_head(value, axis):
    if lax.axis_size("head") == 2:
        other = lax.ppermute(value, "head", [(0, 1), (1, 0)])
        first = lax.axis_index("head") == 0
        return jnp.concatenate(
            [jnp.where(first, value, other), jnp.where(first, other, value)], axis
        )
    return lax.all_gather(value, "head", axis=axis, tiled=True)


def sum_head(value):
    low = value.astype(jnp.bfloat16)
    if lax.axis_size("head") == 2:
        other = lax.ppermute(low, "head", [(0, 1), (1, 0)])
        return low.astype(jnp.float32) + other.astype(jnp.float32)
    return lax.psum(low, "head").astype(jnp.float32)


def sum_doubling(value, axes):
    for axis in axes:
        by = 1
        while by < lax.axis_size(axis):
            value = value + lax.ppermute(value, axis, swap_pairs(axis, by))
            by *= 2
    return value


def own_half(value, width):
    return lax.dynamic_slice_in_dim(value, lax.axis_index("head") * width, width, value.ndim - 1)


def chain_state(maps, shifts, reverse):
    peers = lax.axis_size("seq")
    by = -1 if reverse else 1
    states = [passed_along(shifts.astype(jnp.bfloat16), "seq", by)]
    for step in range(peers - 2):
        out = (
            jnp.einsum("hij,hjk->hik", maps, states[-1].astype(jnp.float32), precision=HIGH)
            + shifts
        )
        states.append(passed_along(out.astype(jnp.bfloat16), "seq", by))
    return states[-1]


def inverse_rms(values):
    return lax.rsqrt(jnp.mean(values * values, axis=-1, keepdims=True) + EPSILON)


MESH = pl.DeviceIdType.MESH


def partner(own, by):
    other = own
    bit = 1
    while bit <= by:
        if by & bit:
            other = other + bit - 2 * bit * ((own // bit) % 2)
        bit *= 2
    return other


def place(name, index):
    return {name: index}


def meet(devices):
    barrier = pltpu.get_barrier_semaphore()
    for device in devices:
        pl.semaphore_signal(barrier, inc=1, device_id=device, device_id_type=MESH)
    pl.semaphore_wait(barrier, len(devices))


class Halves:
    def __init__(self, ways, source, out, sends, receives, hand_sends, hand_receives):
        own = lax.axis_index("dp")
        core = lax.axis_index("head")
        width = source.shape[1] // 2
        mine = pl.ds(pl.multiple_of(core * width, width), width)
        self.peers = [place("dp", partner(own, by)) for by in range(1, ways)]
        self.other = place("head", 1 - core)
        self.first = [
            pltpu.make_async_remote_copy(
                src_ref=source.at[:, mine],
                dst_ref=out.at[slot, :, mine],
                send_sem=sends.at[slot],
                recv_sem=receives.at[slot],
                device_id=peer,
                device_id_type=MESH,
            )
            for slot, peer in enumerate(self.peers)
        ]
        self.second = [
            pltpu.make_async_remote_copy(
                src_ref=out.at[slot, :, mine],
                dst_ref=out.at[slot, :, mine],
                send_sem=hand_sends.at[slot],
                recv_sem=hand_receives.at[slot],
                device_id=self.other,
                device_id_type=MESH,
            )
            for slot in range(ways - 1)
        ]

    def devices(self):
        return self.peers + [self.other]

    def start(self):
        for copy in self.first:
            copy.start()

    def hand_on(self):
        for copy, hand in zip(self.first, self.second):
            copy.wait_recv()
            hand.start()

    def finish(self):
        for copy, hand in zip(self.first, self.second):
            copy.wait_send()
            hand.wait()


def column_copies(ways, source, out, sends, receives):
    own = lax.axis_index("dp")
    width = source.shape[1] // ways
    copies = []
    for by in range(1, ways):
        peer = partner(own, by)
        copies.append(
            pltpu.make_async_remote_copy(
                src_ref=source.at[:, pl.ds(pl.multiple_of(peer * width, width), width)],
                dst_ref=out.at[by - 1],
                send_sem=sends.at[by - 1],
                recv_sem=receives.at[by - 1],
                device_id=place("dp", peer),
                device_id_type=MESH,
            )
        )
    return copies


def exchange_kernel(ways, kinds, *refs):
    count = len(kinds)
    sources, outs = refs[:count], refs[-6 - count : -6]
    sends, receives = refs[-6:-4]
    own = lax.axis_index("dp")
    shared = kinds[-1][0] == "halves"
    peers = [partner(own, by) for by in range(1, ways)]
    halves = Halves(ways, sources[-1], outs[-1], *refs[-4:]) if shared else None
    meet(halves.devices() if shared else [place("dp", peer) for peer in peers])
    if shared:
        halves.start()
    copies = []
    for index, (kind, source, out) in enumerate(zip(kinds, sources, outs)):
        if kind[0] == "halves":
            continue
        for by in range(1, ways):
            peer = peers[by - 1]
            if kind[0] == "rows":
                src = source.at[kind[1] : kind[2], peer]
            else:
                width = source.shape[1] // ways
                src = source.at[:, pl.ds(pl.multiple_of(peer * width, width), width)]
            copy = pltpu.make_async_remote_copy(
                src_ref=src,
                dst_ref=out.at[by - 1],
                send_sem=sends.at[index * (ways - 1) + by - 1],
                recv_sem=receives.at[index * (ways - 1) + by - 1],
                device_id=place("dp", peer),
                device_id_type=MESH,
            )
            copy.start()
            copies.append(copy)
    if shared:
        halves.hand_on()
    for copy in copies:
        copy.wait()
    if shared:
        halves.finish()


def plane_exchange(sources, kinds, tokens, number):
    ways = lax.axis_size("dp")
    shapes = []
    for source, kind in zip(sources, kinds):
        if kind[0] == "rows":
            shape = (ways - 1, kind[2] - kind[1]) + source.shape[2:]
        elif kind[0] == "columns":
            shape = (ways - 1, source.shape[0], source.shape[1] // ways)
        else:
            shape = (ways - 1,) + source.shape
        shapes.append(b16(*shape))
    anywhere = pl.BlockSpec(memory_space=pl.ANY)
    sems = pltpu.SemaphoreType.DMA((len(sources) * (ways - 1),))
    hand_sems = pltpu.SemaphoreType.DMA((ways - 1,))
    return pl.pallas_call(
        functools.partial(exchange_kernel, ways, kinds),
        out_shape=shapes,
        in_specs=[anywhere] * (len(sources) + len(tokens)),
        out_specs=[anywhere] * len(sources),
        scratch_shapes=[sems] * 2 + [hand_sems] * 4,
        compiler_params=pltpu.CompilerParams(
            collective_id=number, has_side_effects=True, vmem_limit_bytes=VMEM
        ),
        cost_estimate=SHORT,
    )(*sources, *tokens)


def halves(a):
    top = a.astype(jnp.bfloat16)
    return top, (a - top.astype(jnp.float32)).astype(jnp.bfloat16)


def dot_low(a, b, dims=(1, 0)):
    return lax.dot_general(
        a, b, (((dims[0],), (dims[1],)), ((), ())), preferred_element_type=jnp.float32
    )


def dot_left(a, b, dims=(1, 0)):
    top, rest = halves(a)
    return dot_low(top, b, dims) + dot_low(rest, b, dims)


def dot_right(a, b, dims=(1, 0)):
    top, rest = halves(b)
    return dot_low(a, top, dims) + dot_low(a, rest, dims)


def dot_both(a, b, dims=(1, 0)):
    a_top, a_rest = halves(a)
    b_top, b_rest = halves(b)
    return dot_low(a_top, b_top, dims) + (
        dot_low(a_top, b_rest, dims) + dot_low(a_rest, b_top, dims)
    )


def grid_marks(size):
    row = lax.broadcasted_iota(jnp.int32, (size, size), 0)
    col = lax.broadcasted_iota(jnp.int32, (size, size), 1)
    return row, col


def unit_lower_inverses(tiles):
    size = tiles[0].shape[0]
    row, col = grid_marks(size)
    unit = (row == col).astype(jnp.float32)
    base = 8
    near = (row // base == col // base) & (row > col)
    cores = [jnp.where(near, tile, 0.0) for tile in tiles]
    squares = [dot_both(core, core) for core in cores]
    fourths = [dot_both(square, square) for square in squares]
    found = [dot_both(unit - core, unit + square) for core, square in zip(cores, squares)]
    found = [dot_both(part, unit + fourth) for part, fourth in zip(found, fourths)]
    while base < size:
        wide = 2 * base
        near = (row // wide == col // wide) & (row // base > col // base)
        links = [jnp.where(near, tile, 0.0) for tile in tiles]
        steps = [dot_both(part, link) for part, link in zip(found, links)]
        found = [part - dot_both(step, part) for part, step in zip(found, steps)]
        base = wide
    return found


def lower_inverses(systems, tile):
    size = systems[0].shape[0]
    if size <= tile:
        return unit_lower_inverses(systems)
    half = size // 2
    diagonals = [s[:half, :half] for s in systems] + [s[half:, half:] for s in systems]
    found = lower_inverses(diagonals, tile)
    firsts, seconds = found[: len(systems)], found[len(systems) :]
    steps = [dot_both(second, s[half:, :half]) for second, s in zip(seconds, systems)]
    corners = [-dot_both(step, first) for step, first in zip(steps, firsts)]
    empty = jnp.zeros((half, half), jnp.float32)
    return [
        jnp.concatenate(
            [jnp.concatenate([first, empty], 1), jnp.concatenate([corner, second], 1)], 0
        )
        for first, corner, second in zip(firsts, corners, seconds)
    ]


RIM = 16


def conv_sum(ext, pre, rim, weights, taps, length):
    ext[:RIM, :] = rim.astype(jnp.float32)
    ext[RIM : RIM + length, :] = pre.astype(jnp.float32)
    first = RIM - taps + 1
    summed = weights[0:1, :] * ext[first : first + length, :]
    for tap in range(1, taps):
        summed = summed + weights[tap : tap + 1, :] * ext[first + tap : first + tap + length, :]
    return summed


def head_columns(refs, index):
    span = slice(index * HEAD_DIM, (index + 1) * HEAD_DIM)
    return [ref[:, span] for ref in refs]


def unit_scale(rows):
    return lax.rsqrt(jnp.sum(rows * rows, axis=-1, keepdims=True) + UNIT_EPSILON)


def column_of(values, index):
    lane = lax.broadcasted_iota(jnp.int32, values.shape, 1)
    return jnp.sum(jnp.where(lane == index, values, 0.0), axis=-1, keepdims=True)


def row_of(values, index):
    place = lax.broadcasted_iota(jnp.int32, values.shape, 0)
    return jnp.sum(jnp.where(place == index, values, 0.0), axis=0, keepdims=True)


def local_part(pres, rims, weights, logit, logit_t, live, live_t, ext, first, taps):
    length = live.shape[0]
    row, col = grid_marks(length)
    heads = range(pres[0].shape[1] // HEAD_DIM)
    queries, keys, values, systems, beta_rows = [], [], [], [], []
    for i in heads:
        span = slice(i * HEAD_DIM, (i + 1) * HEAD_DIM)
        active = []
        for pre, rim, weight in zip(pres, rims, weights):
            summed = conv_sum(
                ext, pre[:, span], rim[:, span], weight[:, span].astype(jnp.float32), taps, length
            )
            active.append(summed * jax.nn.sigmoid(summed))
        q, k, v = active
        q = (q * unit_scale(q)).astype(jnp.bfloat16)
        k = (k * unit_scale(k) * live).astype(jnp.bfloat16)
        v = v.astype(jnp.bfloat16)
        beta = jax.nn.sigmoid(column_of(logit, first + i)) * live
        beta_rows.append(jax.nn.sigmoid(row_of(logit_t, first + i)) * live_t)
        gram = dot_low(k, k, (1, 1))
        systems.append(jnp.where(row > col, beta * gram, 0.0))
        queries.append(q)
        keys.append(k)
        values.append(v)
    inverses = lower_inverses(systems, 128)
    wys = [
        dot_left(inverse * beta_row, jnp.concatenate([k, v], 1))
        for inverse, beta_row, k, v in zip(inverses, beta_rows, keys, values)
    ]
    wide = (HEAD_DIM, 2 * HEAD_DIM)
    place = lax.broadcasted_iota(jnp.int32, wide, 1)
    unit = (lax.broadcasted_iota(jnp.int32, wide, 0) == place).astype(jnp.float32)
    found = []
    for i in heads:
        ends = dot_right(keys[i], wys[i], (0, 0))
        ends = unit + jnp.where(place < HEAD_DIM, -ends, ends)
        scores = jnp.where(row >= col, dot_low(queries[i], keys[i], (1, 1)), 0.0)
        seen = dot_both(scores, wys[i])
        mix = jnp.concatenate(
            [queries[i].astype(jnp.float32) - seen[:, :HEAD_DIM], seen[:, HEAD_DIM:]], 1
        )
        found.append((queries[i], keys[i], values[i], wys[i], inverses[i], mix, ends))
    return found


def finish_part(mix, state, gain):
    mixed = mix[:, HEAD_DIM:] + dot_left(mix[:, :HEAD_DIM], state)
    scale = lax.rsqrt(jnp.mean(mixed * mixed, axis=-1, keepdims=True) + EPSILON)
    return mixed, (mixed * scale * gain).astype(jnp.bfloat16)


def back_local_part(d_out, mixed, gain, q, k, wy):
    row, col = grid_marks(q.shape[0])
    scale = lax.rsqrt(jnp.mean(mixed * mixed, axis=-1, keepdims=True) + EPSILON)
    weighted = gain * d_out
    inner = jnp.sum(weighted * mixed, axis=-1, keepdims=True)
    d_mixed = scale * weighted - mixed * (scale * scale * scale * inner / HEAD_DIM)
    gain_row = jnp.sum(d_out * mixed * scale, axis=0, keepdims=True)
    scores_t = jnp.where(col >= row, dot_low(k, q, (1, 1)), 0.0)
    d_fresh = dot_both(scores_t, d_mixed)
    d_end = dot_right(q, d_mixed, (0, 0)) - dot_both(wy[:, :HEAD_DIM], d_fresh, (0, 0))
    return d_mixed, d_fresh, d_end, gain_row


def back_part(q, k, v, wy, inverse, entering, leaving, d_mixed, d_fresh, logit, live):
    row, col = grid_marks(q.shape[0])
    d_fresh = d_fresh + dot_low(k, leaving)
    fresh = wy[:, HEAD_DIM:] - dot_left(wy[:, :HEAD_DIM], entering)
    d_scores = jnp.where(row >= col, dot_both(d_mixed, fresh, (1, 1)), 0.0)
    d_q = dot_left(d_mixed, entering, (1, 1)) + dot_left(d_scores, k)
    d_k = dot_left(d_scores, q, (0, 0)) + dot_left(fresh, leaving, (1, 1))
    d_wy = jnp.concatenate([-dot_left(d_fresh, entering, (1, 1)), d_fresh], 1)
    d_rhs = dot_both(inverse, d_wy, (0, 0))
    edges = jnp.where(row > col, -dot_both(d_rhs, wy, (1, 1)), 0.0)
    sig = jax.nn.sigmoid(logit)
    beta = sig * live
    both = jnp.concatenate([k, v], 1).astype(jnp.float32)
    gram = dot_low(k, k, (1, 1))
    d_beta = jnp.sum(d_rhs * both, axis=-1, keepdims=True) + jnp.sum(
        edges * gram, axis=-1, keepdims=True
    )
    scaled = beta * edges
    d_k = d_k + beta * d_rhs[:, :HEAD_DIM] + dot_left(scaled, k) + dot_left(scaled, k, (0, 0))
    d_v = beta * d_rhs[:, HEAD_DIM:]
    d_logit = d_beta * live * sig * (1.0 - sig)
    return d_q, d_k * live, d_v, d_logit


def back_conv_part(part, pre, rim, weight, grad, taps, ext, ext_back):
    length = pre.shape[0]
    weight = weight.astype(jnp.float32)
    summed = conv_sum(ext, pre, rim, weight, taps, length)
    gate = jax.nn.sigmoid(summed)
    if part < 2:
        active = summed * gate
        scale = unit_scale(active)
        inner = jnp.sum(active * grad, axis=-1, keepdims=True)
        grad = scale * grad - active * (scale * scale * scale * inner)
    d_conv = grad * gate * (1.0 + summed * (1.0 - gate))
    first = RIM - taps + 1
    rows = [
        jnp.sum(d_conv * ext[first + tap : first + tap + length, :], axis=0, keepdims=True)
        for tap in range(taps)
    ]
    ext_back[:8, :] = jnp.zeros((8, HEAD_DIM), jnp.float32)
    ext_back[8 : 8 + length, :] = d_conv
    ext_back[8 + length :, :] = jnp.zeros((8, HEAD_DIM), jnp.float32)
    own = jnp.zeros((length, HEAD_DIM), jnp.float32)
    before = jnp.zeros((8, HEAD_DIM), jnp.float32)
    for tap in range(taps):
        shift = taps - 1 - tap
        own = own + weight[tap : tap + 1, :] * ext_back[8 + shift : 8 + shift + length, :]
        before = before + weight[tap : tap + 1, :] * ext_back[shift : shift + 8, :]
    return own, before, jnp.concatenate(rows, 0)


def mixer_local_kernel(per_step, taps, *refs):
    pres, rims, weights = refs[:3], refs[3:6], refs[6:9]
    logit, logit_t, live, live_t = refs[9:13]
    q_out, k_out, v_out, wy_out, inv_out, mix_out, end_out, ext = refs[13:]
    found = local_part(
        pres, rims, weights, logit[...], logit_t[...], live[...], live_t[...], ext,
        pl.program_id(0) * per_step, taps,
    )
    for i, (q, k, v, wy, inverse, mix, ends) in enumerate(found):
        span = slice(i * HEAD_DIM, (i + 1) * HEAD_DIM)
        q_out[:, span] = q
        k_out[:, span] = k
        v_out[:, span] = v
        wy_out[i] = wy
        inv_out[i] = inverse
        mix_out[i] = mix
        end_out[i] = ends


def mixer_finish_kernel(per_step, mix, state, gain, mixed_out, head_out):
    for i in range(per_step):
        span = slice(i * HEAD_DIM, (i + 1) * HEAD_DIM)
        mixed_out[:, span], head_out[:, span] = finish_part(mix[i], state[i], gain[...])


def mixer_back_local_kernel(
    per_step, d_head, mixed_ref, gain_ref, q_ref, k_ref, wy,
    d_mixed_out, d_fresh_out, end_out, gain_out,
):
    gain_total = jnp.zeros((1, HEAD_DIM), jnp.float32)
    for i in range(per_step):
        d_out, mixed, q, k = head_columns((d_head, mixed_ref, q_ref, k_ref), i)
        d_mixed_out[i], d_fresh_out[i], end_out[i], gain_row = back_local_part(
            d_out, mixed, gain_ref[...], q, k, wy[i]
        )
        gain_total += gain_row

    @pl.when(pl.program_id(0) == 0)
    def _():
        gain_out[...] = jnp.zeros_like(gain_out)

    gain_out[...] += jnp.broadcast_to(gain_total, gain_out.shape)


def mixer_back_kernel(per_step, taps, *refs):
    pre_refs, rim_refs, weight_refs, (logit, live) = refs[:3], refs[3:6], refs[6:9], refs[9:11]
    (q_ref, k_ref, v_ref, wy, inv, state, d_mixed_ref, d_fresh_ref, d_state) = refs[11:20]
    d_q_out, d_k_out, d_v_out, tail_out, rim_out, conv_out, d_logit_out, ext, ext_back = refs[20:]
    length = live.shape[0]
    step = pl.program_id(0)

    @pl.when(step == 0)
    def _():
        d_logit_out[...] = jnp.zeros_like(d_logit_out)

    for i in range(per_step):
        q, k, v = head_columns((q_ref, k_ref, v_ref), i)
        *grads, d_logit = back_part(
            q, k, v, wy[i], inv[i], state[i], d_state[i], d_mixed_ref[i], d_fresh_ref[i],
            column_of(logit[...], step * per_step + i), live[...],
        )
        lane = lax.broadcasted_iota(jnp.int32, d_logit_out.shape, 1)
        d_logit_out[...] += jnp.where(lane == step * per_step + i, d_logit, 0.0)
        span = slice(i * HEAD_DIM, (i + 1) * HEAD_DIM)
        outs = (d_q_out, d_k_out, d_v_out)
        for part in range(3):
            own, before, rows = back_conv_part(
                part, pre_refs[part][:, span], rim_refs[part][:, span],
                weight_refs[part][:, span], grads[part], taps, ext, ext_back,
            )
            conv_out[part, :, span] = rows
            outs[part][:, span] = own.astype(jnp.bfloat16)
            tail_out[part, :, span] = own[length - 8 :, :]
            rim_out[part, :, span] = before


def mixer_specs(length, heads, per_step):
    width = per_step * HEAD_DIM

    def flat(rows):
        return pl.BlockSpec((rows, width), lambda h: (0, h))

    def whole(*shape):
        return pl.BlockSpec(shape, lambda h: (0,) * len(shape))

    def by_head(*shape):
        return pl.BlockSpec((per_step,) + shape, lambda h: (h,) + (0,) * len(shape))

    return flat, whole, by_head


def mixer_call(kernel, heads, per_step, ins, outs, scratch, flops, args):
    moved = sum(a.size * a.dtype.itemsize for a in args)
    return pl.pallas_call(
        kernel,
        grid=(heads // per_step,),
        in_specs=ins,
        out_specs=[spec for spec, _ in outs],
        out_shape=[shape for _, shape in outs],
        scratch_shapes=scratch,
        compiler_params=pltpu.CompilerParams(vmem_limit_bytes=VMEM),
        cost_estimate=SHORT,
    )(*args)


def f32(*shape):
    return jax.ShapeDtypeStruct(shape, jnp.float32)


def b16(*shape):
    return jax.ShapeDtypeStruct(shape, jnp.bfloat16)


def mixer_local(pres, rims, convs, logit, live, per_step):
    length, channels = pres[0].shape
    heads = channels // HEAD_DIM
    taps = convs[0].shape[0]
    flat, whole, by_head = mixer_specs(length, heads, per_step)
    args = (*pres, *rims, *convs, logit, logit.T, live, live.T)
    return mixer_call(
        functools.partial(mixer_local_kernel, per_step, taps),
        heads,
        per_step,
        [flat(length)] * 3
        + [flat(RIM)] * 3
        + [flat(taps)] * 3
        + [whole(length, heads), whole(heads, length), whole(length, 1), whole(1, length)],
        [(flat(length), b16(length, channels))] * 3
        + [
            (by_head(length, 2 * HEAD_DIM), f32(heads, length, 2 * HEAD_DIM)),
            (by_head(length, length), f32(heads, length, length)),
            (by_head(length, 2 * HEAD_DIM), f32(heads, length, 2 * HEAD_DIM)),
            (by_head(HEAD_DIM, 2 * HEAD_DIM), f32(heads, HEAD_DIM, 2 * HEAD_DIM)),
        ],
        [pltpu.VMEM((RIM + length, HEAD_DIM), jnp.float32)],
        heads * 2 * length**3 * 30,
        args,
    )


def mixer_finish(mix, state, gain, per_step):
    heads, length, _ = mix.shape
    flat, whole, by_head = mixer_specs(length, heads, per_step)
    return mixer_call(
        functools.partial(mixer_finish_kernel, per_step),
        heads,
        per_step,
        [by_head(length, 2 * HEAD_DIM), by_head(HEAD_DIM, HEAD_DIM), whole(1, HEAD_DIM)],
        [
            (flat(length), f32(length, heads * HEAD_DIM)),
            (flat(length), b16(length, heads * HEAD_DIM)),
        ],
        [],
        heads * 2 * length**3,
        (mix, state, gain),
    )


def mixer_back_local(d_head, mixed, gain, q, k, wy, per_step):
    heads, length, _ = wy.shape
    flat, whole, by_head = mixer_specs(length, heads, per_step)
    return mixer_call(
        functools.partial(mixer_back_local_kernel, per_step),
        heads,
        per_step,
        [flat(length)] * 2 + [whole(1, HEAD_DIM)] + [flat(length)] * 2 + [by_head(length, 2 * HEAD_DIM)],
        [
            (by_head(length, HEAD_DIM), f32(heads, length, HEAD_DIM)),
            (by_head(length, HEAD_DIM), f32(heads, length, HEAD_DIM)),
            (by_head(HEAD_DIM, HEAD_DIM), f32(heads, HEAD_DIM, HEAD_DIM)),
            (whole(8, HEAD_DIM), f32(8, HEAD_DIM)),
        ],
        [],
        heads * 2 * length**3 * 5,
        (d_head, mixed, gain, q, k, wy),
    )


def mixer_back(pres, rims, convs, logit, live, q, k, v, wy, inv, state, d_mixed, d_fresh, d_state, per_step):
    length, channels = pres[0].shape
    heads = channels // HEAD_DIM
    taps = convs[0].shape[0]
    flat, whole, by_head = mixer_specs(length, heads, per_step)
    three = pl.BlockSpec((3, 8, per_step * HEAD_DIM), lambda h: (0, 0, h))
    return mixer_call(
        functools.partial(mixer_back_kernel, per_step, taps),
        heads,
        per_step,
        [flat(length)] * 3
        + [flat(RIM)] * 3
        + [flat(taps)] * 3
        + [whole(length, heads), whole(length, 1)]
        + [flat(length)] * 3
        + [
            by_head(length, 2 * HEAD_DIM),
            by_head(length, length),
            by_head(HEAD_DIM, HEAD_DIM),
            by_head(length, HEAD_DIM),
            by_head(length, HEAD_DIM),
            by_head(HEAD_DIM, HEAD_DIM),
        ],
        [(flat(length), b16(length, channels))] * 3
        + [
            (three, f32(3, 8, channels)),
            (three, f32(3, 8, channels)),
            (
                pl.BlockSpec((3, taps, per_step * HEAD_DIM), lambda h: (0, 0, h)),
                f32(3, taps, channels),
            ),
            (whole(length, heads), f32(length, heads)),
        ],
        [
            pltpu.VMEM((RIM + length, HEAD_DIM), jnp.float32),
            pltpu.VMEM((16 + length, HEAD_DIM), jnp.float32),
        ],
        heads * 2 * length**3 * 20,
        (*pres, *rims, *convs, logit, live, q, k, v, wy, inv, state, d_mixed, d_fresh, d_state),
    )


def mixer_forward_kernel(per_step, taps, spans, *refs):
    pres, weights = refs[:3], refs[3:6]
    logit, logit_t, live, live_t, gain = refs[6:11]
    sources = refs[11:14]
    q_out, k_out, v_out, wy_out, inv_out, end_out, mixed_out, head_out, state_out, rim_out = refs[
        14:24
    ]
    ext, mix_all, rims, arriving, leaving, sends, receives, rim_sends, rim_receives = refs[24:]
    step = pl.program_id(0)
    position = lax.axis_index("seq")
    pairs = arriving.shape[0]
    length = live.shape[0]
    width = per_step * HEAD_DIM
    last = spans - 1
    after = place("seq", position + 1)

    def rim_copy(part):
        return pltpu.make_async_remote_copy(
            src_ref=sources[part].at[length - RIM :, :],
            dst_ref=rims.at[part],
            send_sem=rim_sends.at[part],
            recv_sem=rim_receives.at[part],
            device_id=after,
            device_id_type=MESH,
        )

    def state_copy(pair):
        return pltpu.make_async_remote_copy(
            src_ref=leaving.at[pair],
            dst_ref=arriving.at[pair],
            send_sem=sends.at[pair],
            recv_sem=receives.at[pair],
            device_id=after,
            device_id_type=MESH,
        )

    @pl.when(step == 0)
    def _():
        meet([place("seq", (position + last) % spans), place("seq", (position + 1) % spans)])

        @pl.when(position != last)
        def _():
            for part in range(3):
                rim_copy(part).start()

        @pl.when(position == 0)
        def _():
            rims[...] = jnp.zeros_like(rims)
            arriving[...] = jnp.zeros_like(arriving)

        @pl.when(position != 0)
        def _():
            for part in range(3):
                rim_copy(part).wait_recv()

        rim_out[...] = rims[...]

    @pl.when(step < pairs)
    def _():
        here = pl.ds(pl.multiple_of(step * width, width), width)
        found = local_part(
            pres, [rims[part, :, here] for part in range(3)], weights, logit[...], logit_t[...],
            live[...], live_t[...], ext, step * per_step, taps,
        )
        for i, (q, k, v, wy, inverse, mix, ends) in enumerate(found):
            span = slice(i * HEAD_DIM, (i + 1) * HEAD_DIM)
            q_out[:, span] = q
            k_out[:, span] = k
            v_out[:, span] = v
            wy_out[i] = wy
            inv_out[i] = inverse
            mix_all[step * per_step + i] = mix
            end_out[step * per_step + i] = ends

    pair = step - position

    @pl.when((pair >= 0) & (pair < pairs))
    def _():
        @pl.when(position != 0)
        def _():
            state_copy(pair).wait_recv()

        for i in range(per_step):
            ends = end_out[pair * per_step + i]
            moved = dot_left(ends[:, :HEAD_DIM], arriving[pair, i])
            leaving[pair, i] = (moved + ends[:, HEAD_DIM:]).astype(jnp.bfloat16)

        @pl.when(position != last)
        def _():
            state_copy(pair).start()

        for i in range(per_step):
            here = pl.ds(pl.multiple_of(pair * width + i * HEAD_DIM, HEAD_DIM), HEAD_DIM)
            state = arriving[pair, i]
            state_out[pair * per_step + i] = state
            mixed, head = finish_part(mix_all[pair * per_step + i], state, gain[...])
            mixed_out[:, here] = mixed
            head_out[:, here] = head

    @pl.when((step == pl.num_programs(0) - 1) & (position != last))
    def _():
        for part in range(3):
            rim_copy(part).wait_send()
        for index in range(pairs):
            state_copy(index).wait_send()


def mixer_forward(pres, convs, logit, live, gain, per_step, spans, number):
    length, channels = pres[0].shape
    heads = channels // HEAD_DIM
    pairs = heads // per_step
    taps = convs[0].shape[0]
    width = per_step * HEAD_DIM
    wide = (heads, length, 2 * HEAD_DIM)
    states = (heads, HEAD_DIM, HEAD_DIM)

    def at(step):
        return jnp.minimum(step, pairs - 1)

    def flat(rows):
        return pl.BlockSpec((rows, width), lambda s: (0, at(s)))

    def by_head(*shape):
        return pl.BlockSpec((per_step,) + shape, lambda s: (at(s),) + (0,) * len(shape))

    def whole(*shape):
        return pl.BlockSpec(shape, lambda s: (0,) * len(shape))

    anywhere = pl.BlockSpec(memory_space=pl.ANY)
    return pl.pallas_call(
        functools.partial(mixer_forward_kernel, per_step, taps, spans),
        grid=(pairs + spans - 1,),
        in_specs=[flat(length)] * 3
        + [flat(taps)] * 3
        + [whole(length, heads), whole(heads, length), whole(length, 1), whole(1, length)]
        + [whole(1, HEAD_DIM)]
        + [anywhere] * 3,
        out_specs=[flat(length)] * 3
        + [
            by_head(length, 2 * HEAD_DIM),
            by_head(length, length),
            whole(heads, HEAD_DIM, 2 * HEAD_DIM),
            whole(length, channels),
            whole(length, channels),
            whole(*states),
            whole(3, RIM, channels),
        ],
        out_shape=[b16(length, channels)] * 3
        + [
            f32(*wide),
            f32(heads, length, length),
            f32(heads, HEAD_DIM, 2 * HEAD_DIM),
            f32(length, channels),
            b16(length, channels),
            b16(*states),
            b16(3, RIM, channels),
        ],
        scratch_shapes=[
            pltpu.VMEM((RIM + length, HEAD_DIM), jnp.float32),
            pltpu.VMEM(wide, jnp.float32),
            pltpu.VMEM((3, RIM, channels), jnp.bfloat16),
            pltpu.VMEM((pairs, per_step, HEAD_DIM, HEAD_DIM), jnp.bfloat16),
            pltpu.VMEM((pairs, per_step, HEAD_DIM, HEAD_DIM), jnp.bfloat16),
            pltpu.SemaphoreType.DMA((pairs,)),
            pltpu.SemaphoreType.DMA((pairs,)),
            pltpu.SemaphoreType.DMA((3,)),
            pltpu.SemaphoreType.DMA((3,)),
        ],
        compiler_params=pltpu.CompilerParams(
            collective_id=number, has_side_effects=True, vmem_limit_bytes=VMEM
        ),
        cost_estimate=SHORT,
    )(*pres, *convs, logit, logit.T, live, live.T, gain, *pres)


def mixer_backward_kernel(per_step, taps, spans, ways, tokens, *refs):
    d_head, mixed_ref, q_one, k_one, wy_one, gain = refs[:6]
    pres, weights = refs[6:9], refs[9:12]
    q_ref, k_ref, v_ref, wy, inv = refs[12:17]
    logit, live, state, ends, rims = refs[17:22]
    head_source, residual, normed = refs[22 + tokens : 25 + tokens]
    d_q_out, d_k_out, d_v_out, conv_out, d_logit_out, gain_out = refs[25 + tokens : 31 + tokens]
    head_others, res_others, one_others = refs[31 + tokens : 34 + tokens]
    (
        d_mixed_all, d_fresh_all, d_end_all, arriving, sending, tails, rim_out, rim_in,
        ext, ext_back, sends, receives, rim_sends, rim_receives,
    ) = refs[34 + tokens : 48 + tokens]
    col_sends, col_receives, *half_sems = refs[48 + tokens :]
    halves = Halves(ways, residual, res_others, *half_sems[:4])
    later = Halves(ways, normed, one_others, *half_sems[4:])
    columns = column_copies(ways, head_source, head_others, col_sends, col_receives)
    step = pl.program_id(0)
    position = lax.axis_index("seq")
    pairs = arriving.shape[0]
    length = live.shape[0]
    last = spans - 1
    before_here = place("seq", position - 1)

    def state_copy(pair):
        return pltpu.make_async_remote_copy(
            src_ref=sending.at[pair],
            dst_ref=arriving.at[pair],
            send_sem=sends.at[pair],
            recv_sem=receives.at[pair],
            device_id=before_here,
            device_id_type=MESH,
        )

    def rim_copy():
        return pltpu.make_async_remote_copy(
            src_ref=rim_out,
            dst_ref=rim_in,
            send_sem=rim_sends.at[0],
            recv_sem=rim_receives.at[0],
            device_id=before_here,
            device_id_type=MESH,
        )

    @pl.when(step == 0)
    def _():
        meet(
            [place("seq", (position + last) % spans), place("seq", (position + 1) % spans)]
            + halves.devices()
        )
        halves.start()
        for copy in columns:
            copy.start()
        later.start()
        d_logit_out[...] = jnp.zeros_like(d_logit_out)
        gain_out[...] = jnp.zeros_like(gain_out)

        @pl.when(position == last)
        def _():
            arriving[...] = jnp.zeros_like(arriving)
            rim_in[...] = jnp.zeros_like(rim_in)

    @pl.when(step < pairs)
    def _():
        for i in range(per_step):
            d_out, mixed, q, k = head_columns((d_head, mixed_ref, q_one, k_one), i)
            d_mixed, d_fresh, d_end, gain_row = back_local_part(
                d_out, mixed, gain[...], q, k, wy_one[i]
            )
            d_mixed_all[step * per_step + i] = d_mixed
            d_fresh_all[step * per_step + i] = d_fresh
            d_end_all[step * per_step + i] = d_end
            gain_out[...] += jnp.broadcast_to(gain_row, gain_out.shape)

    pair = step - (last - position)

    @pl.when((pair >= 0) & (pair < pairs))
    def _():
        @pl.when(position != last)
        def _():
            state_copy(pair).wait_recv()

        for i in range(per_step):
            head = pair * per_step + i
            moved = dot_left(ends[head, :, :HEAD_DIM], arriving[pair, i], (0, 0))
            sending[pair, i] = (moved + d_end_all[head]).astype(jnp.bfloat16)

        @pl.when(position != 0)
        def _():
            state_copy(pair).start()

    ready = step - last

    @pl.when(ready >= 0)
    def _():
        outs = (d_q_out, d_k_out, d_v_out)
        for i in range(per_step):
            head = ready * per_step + i
            here = pl.ds(pl.multiple_of(head * HEAD_DIM, HEAD_DIM), HEAD_DIM)
            q, k, v = head_columns((q_ref, k_ref, v_ref), i)
            *grads, d_logit = back_part(
                q, k, v, wy[i], inv[i], state[head], arriving[ready, i],
                d_mixed_all[head], d_fresh_all[head], column_of(logit[...], head), live[...],
            )
            lane = lax.broadcasted_iota(jnp.int32, d_logit_out.shape, 1)
            d_logit_out[...] += jnp.where(lane == head, d_logit, 0.0)
            span = slice(i * HEAD_DIM, (i + 1) * HEAD_DIM)
            for part in range(3):
                own, before, rows = back_conv_part(
                    part, pres[part][:, span], rims[part, :, here],
                    weights[part][:, span], grads[part], taps, ext, ext_back,
                )
                conv_out[part, :, here] = rows
                outs[part][:, here] = own.astype(jnp.bfloat16)
                tails[part, :, here] = own[length - 16 :, :]
                rim_out[part, :, here] = before

    @pl.when(step == pl.num_programs(0) - 1)
    def _():
        @pl.when(position != 0)
        def _():
            rim_copy().start()

        halves.hand_on()
        later.hand_on()

        @pl.when(position != last)
        def _():
            rim_copy().wait_recv()

        for part, out in enumerate((d_q_out, d_k_out, d_v_out)):
            joined = tails[part] + jnp.concatenate(
                [jnp.zeros_like(rim_in[part]), rim_in[part]], 0
            )
            out[length - 16 :, :] = joined.astype(jnp.bfloat16)

        @pl.when(position != 0)
        def _():
            rim_copy().wait_send()
            for index in range(pairs):
                state_copy(index).wait_send()

        for copy in columns:
            copy.wait()
        halves.finish()
        later.finish()


def mixer_backward(
    d_head, mixed, gain, pres, rims, convs, logit, live, q, k, v, wy, inv, state, ends, tokens,
    head_out, residual, normed, per_step, spans, ways, number,
):
    length, channels = pres[0].shape
    heads = channels // HEAD_DIM
    pairs = heads // per_step
    taps = convs[0].shape[0]
    width = per_step * HEAD_DIM
    lag = spans - 1

    def early(step):
        return jnp.minimum(step, pairs - 1)

    def late(step):
        return jnp.maximum(step - lag, 0)

    def flat(rows, at):
        return pl.BlockSpec((rows, width), lambda s: (0, at(s)))

    def by_head(at, *shape):
        return pl.BlockSpec((per_step,) + shape, lambda s: (at(s),) + (0,) * len(shape))

    def whole(*shape):
        return pl.BlockSpec(shape, lambda s: (0,) * len(shape))

    wide = (length, 2 * HEAD_DIM)
    states = (pairs, per_step, HEAD_DIM, HEAD_DIM)
    return pl.pallas_call(
        functools.partial(mixer_backward_kernel, per_step, taps, spans, ways, len(tokens)),
        grid=(pairs + lag,),
        in_specs=[flat(length, early)] * 4
        + [by_head(early, *wide), whole(1, HEAD_DIM)]
        + [flat(length, late)] * 3
        + [flat(taps, late)] * 3
        + [flat(length, late)] * 3
        + [by_head(late, *wide), by_head(late, length, length)]
        + [whole(length, heads), whole(length, 1), whole(heads, HEAD_DIM, HEAD_DIM)]
        + [whole(heads, HEAD_DIM, 2 * HEAD_DIM), whole(3, RIM, channels)]
        + [pl.BlockSpec(memory_space=pl.ANY)] * (len(tokens) + 3),
        out_specs=[whole(length, channels)] * 3
        + [whole(3, taps, channels), whole(length, heads), whole(8, HEAD_DIM)]
        + [pl.BlockSpec(memory_space=pl.ANY)] * 3,
        out_shape=[b16(length, channels)] * 3
        + [f32(3, taps, channels), f32(length, heads), f32(8, HEAD_DIM)]
        + [b16(ways - 1, length, channels // ways)]
        + [b16(ways - 1, *residual.shape)] * 2,
        scratch_shapes=[
            pltpu.VMEM((heads, length, HEAD_DIM), jnp.float32),
            pltpu.VMEM((heads, length, HEAD_DIM), jnp.float32),
            pltpu.VMEM((heads, HEAD_DIM, HEAD_DIM), jnp.float32),
            pltpu.VMEM(states, jnp.bfloat16),
            pltpu.VMEM(states, jnp.bfloat16),
            pltpu.VMEM((3, 16, channels), jnp.float32),
            pltpu.VMEM((3, 8, channels), jnp.float32),
            pltpu.VMEM((3, 8, channels), jnp.float32),
            pltpu.VMEM((RIM + length, HEAD_DIM), jnp.float32),
            pltpu.VMEM((16 + length, HEAD_DIM), jnp.float32),
            pltpu.SemaphoreType.DMA((pairs,)),
            pltpu.SemaphoreType.DMA((pairs,)),
            pltpu.SemaphoreType.DMA((1,)),
            pltpu.SemaphoreType.DMA((1,)),
        ]
        + [pltpu.SemaphoreType.DMA((ways - 1,))] * 10,
        compiler_params=pltpu.CompilerParams(
            collective_id=number, has_side_effects=True, vmem_limit_bytes=VMEM
        ),
        cost_estimate=SHORT,
    )(
        d_head, mixed, q, k, wy, gain, *pres, *convs, q, k, v, wy, inv, logit, live, state, ends,
        rims, *tokens, head_out, residual, normed,
    )


def feed_kernel(
    x_ref, d_ref, gate_w, up_w, down_w, token, feed_out, d_x_out, turned_out, feed_sum, d_x_sum
):
    step = pl.program_id(0)
    x = x_ref[...]
    d_out = d_ref[...]
    gate = dot_low(x, gate_w[...])
    up = dot_low(x, up_w[...])
    d_hidden = dot_low(d_out, down_w[...], (1, 1))
    sig = jax.nn.sigmoid(gate)
    hidden = (gate * sig * up).astype(jnp.bfloat16)
    d_gate = (d_hidden * up * sig * (1.0 + gate * (1.0 - sig))).astype(jnp.bfloat16)
    d_up = (d_hidden * gate * sig).astype(jnp.bfloat16)
    for place, part in enumerate((hidden, d_gate, d_up)):
        turned_out[place] = part.T
    feed = dot_low(hidden, down_w[...])
    d_x = dot_low(d_gate, gate_w[...], (1, 1)) + dot_low(d_up, up_w[...], (1, 1))

    @pl.when(step == 0)
    def _():
        feed_sum[...] = feed
        d_x_sum[...] = d_x

    @pl.when(step > 0)
    def _():
        feed_sum[...] += feed
        d_x_sum[...] += d_x

    @pl.when(step == pl.num_programs(0) - 1)
    def _():
        feed_out[...] = feed_sum[...].astype(jnp.bfloat16)
        d_x_out[...] = d_x_sum[...].astype(jnp.bfloat16)


def feed_forward(x, d_out, gate_weight, up_weight, down_weight, token):
    length, width = x.shape
    units = gate_weight.shape[1]
    tile = 256 if units % 256 == 0 else units
    whole = pl.BlockSpec((length, width), lambda f: (0, 0))
    column = pl.BlockSpec((width, tile), lambda f: (0, f))
    return pl.pallas_call(
        feed_kernel,
        grid=(units // tile,),
        in_specs=[whole, whole, column, column]
        + [pl.BlockSpec((tile, width), lambda f: (f, 0)), pl.BlockSpec(memory_space=pl.ANY)],
        out_specs=[whole, whole, pl.BlockSpec((3, tile, length), lambda f: (0, f, 0))],
        out_shape=[b16(length, width), b16(length, width), b16(3, units, length)],
        scratch_shapes=[pltpu.VMEM((length, width), jnp.float32)] * 2,
        compiler_params=pltpu.CompilerParams(vmem_limit_bytes=VMEM),
        cost_estimate=SHORT,
    )(x, d_out, gate_weight, up_weight, down_weight, token)


def back_projection_kernel(ways, *refs):
    sources, d_logit, weights, beta_w = refs[:3], refs[3], refs[4:7], refs[7]
    shared, out, others = refs[8:11], refs[11], refs[12:15]
    sends, receives = refs[15:18], refs[18:21]
    step = pl.program_id(0)
    copies = [
        copy
        for part in range(3)
        for copy in column_copies(ways, shared[part], others[part], sends[part], receives[part])
    ]

    @pl.when(step == 0)
    def _():
        own = lax.axis_index("dp")
        meet([place("dp", partner(own, by)) for by in range(1, ways)])
        for copy in copies:
            copy.start()

    total = dot_low(d_logit[...], beta_w[...], (1, 1))
    for source, weight in zip(sources, weights):
        total = total + dot_low(source[...], weight[...], (1, 1))
    out[...] = total.astype(jnp.bfloat16)

    @pl.when(step == pl.num_programs(0) - 1)
    def _():
        for copy in copies:
            copy.wait()


def back_projection(sources, d_logit, weights, beta_weight, ways, number):
    length, channels = sources[0].shape
    width, heads = beta_weight.shape
    tile = width // 4
    anywhere = pl.BlockSpec(memory_space=pl.ANY)
    return pl.pallas_call(
        functools.partial(back_projection_kernel, ways),
        grid=(width // tile,),
        in_specs=[pl.BlockSpec((length, channels), lambda n: (0, 0))] * 3
        + [pl.BlockSpec((length, heads), lambda n: (0, 0))]
        + [pl.BlockSpec((tile, channels), lambda n: (n, 0))] * 3
        + [pl.BlockSpec((tile, heads), lambda n: (n, 0))]
        + [anywhere] * 3,
        out_specs=[pl.BlockSpec((length, tile), lambda n: (0, n))] + [anywhere] * 3,
        out_shape=[b16(length, width)] + [b16(ways - 1, length, channels // ways)] * 3,
        scratch_shapes=[pltpu.SemaphoreType.DMA((ways - 1,))] * 6,
        compiler_params=pltpu.CompilerParams(
            collective_id=number, has_side_effects=True, vmem_limit_bytes=VMEM
        ),
        cost_estimate=SHORT,
    )(*sources, d_logit, *weights, beta_weight, *sources)


def pieces_kernel(groups, slots, ways, turned, at, *refs):
    lefts = refs[: groups * slots]
    rights = refs[groups * slots : (groups + ways) * slots]
    out, left_all, right_all = refs[-3:]
    length = rights[0].shape[-2]
    rows = rights[0].shape[-1]
    count = left_all.shape[0] // groups

    @pl.when(pl.program_id(0) == 0)
    def _():
        for group in range(groups):
            for slot in range(slots):
                block = lefts[group * slots + slot][...]
                block = block.reshape(block.shape[-2:])
                left_all[
                    group * count : (group + 1) * count, slot * length : (slot + 1) * length
                ] = block if turned else block.T

    for slot in range(slots):
        for way in range(ways):
            right = rights[slot * ways + way][...]
            right_all[
                slot * length : (slot + 1) * length, way * rows : (way + 1) * rows
            ] = right.reshape(right.shape[-2:])
    out[0] = dot_low(left_all[...], right_all[...]).astype(jnp.bfloat16)


def span_pieces(lefts, count, rights, length, width, spans, turned, tokens=()):
    groups = len(lefts)
    lefts = [left for group in lefts for left in group]
    slots = len(rights)
    ways = lax.axis_size("dp")
    rows = width // (ways * spans)

    def left_block(block, at_place):
        return pl.BlockSpec(block, lambda s, at: at_place(at[0]))

    def right_block(block, at_place, way):
        return pl.BlockSpec(
            block + (rows,), lambda s, at: tuple(at_place(at[0])) + (way * spans + s,)
        )

    return pl.pallas_call(
        functools.partial(pieces_kernel, groups, slots, ways, turned),
        grid_spec=pltpu.PrefetchScalarGridSpec(
            num_scalar_prefetch=1,
            grid=(spans,),
            in_specs=[left_block(block, where) for _, block, where in lefts]
            + [right_block(block, where, way) for _, block, where in rights for way in range(ways)]
            + [pl.BlockSpec(memory_space=pl.ANY)] * len(tokens),
            out_specs=pl.BlockSpec((1, count, ways * rows), lambda s, at: (s, 0, 0)),
            scratch_shapes=[
                pltpu.VMEM((count, slots * length), jnp.bfloat16),
                pltpu.VMEM((slots * length, ways * rows), jnp.bfloat16),
            ],
        ),
        out_shape=b16(spans, count, ways * rows),
        compiler_params=pltpu.CompilerParams(vmem_limit_bytes=VMEM),
        cost_estimate=SHORT,
    )(
        lax.axis_index("dp")[None],
        *[array for array, _, _ in lefts],
        *[array for array, _, _ in rights for _ in range(ways)],
        *tokens,
    )


def widen_kernel(count, turned, *refs):
    for index in range(count):
        whole = refs[index][...].astype(jnp.float32)
        refs[count + index][...] = whole.T if turned[index] else whole


def widened(arrays, turned):
    inside = pl.BlockSpec(memory_space=pltpu.VMEM)
    shapes = [
        f32(*(array.shape[::-1] if turn else array.shape)) for array, turn in zip(arrays, turned)
    ]
    return pl.pallas_call(
        functools.partial(widen_kernel, len(arrays), turned),
        out_shape=shapes,
        in_specs=[inside] * len(arrays),
        out_specs=[inside] * len(arrays),
        compiler_params=pltpu.CompilerParams(vmem_limit_bytes=VMEM),
        cost_estimate=SHORT,
    )(*arrays)


def doublings(size):
    return [1 << bit for bit in range(size.bit_length() - 1)]


def finish_kernel(spans, ways, fed, *refs):
    out_raw, mix_raw, small = refs[:3]
    pieces, refs = refs[3 : 3 + fed], refs[3 + fed :]
    stages, small_out, refs = refs[: 4 + fed], refs[4 + fed], refs[5 + fed :]
    received, handed, totals, *refs = refs
    sends, receives, owner_sends, owner_receives, own_sems = refs[:5]
    small_in, small_sent, small_sends, small_receives = refs[5:]
    own = lax.axis_index("dp")
    position = lax.axis_index("seq")
    last = spans - 1
    rounds = spans - 1
    count = out_raw.shape[1]
    groups = 1 + mix_raw.shape[1] // count
    rows = stages[0].shape[1]
    peers = [partner(own, by) for by in range(1, ways)]

    def raw_at(group, shard):
        if group == 0:
            return out_raw.at[shard]
        return mix_raw.at[shard, (group - 1) * count : group * count, :]

    def line_copy(way, turn, group, src):
        step = 1 if way == 0 else -1
        slot = (way * rounds + turn) * groups + group
        return pltpu.make_async_remote_copy(
            src_ref=src,
            dst_ref=received.at[way, turn, group],
            send_sem=sends.at[slot],
            recv_sem=receives.at[slot],
            device_id=place("seq", position + step),
            device_id_type=MESH,
        )

    def owner_copies(index, source):
        high = source.shape[0]
        stage = stages[index]
        mine = stage.at[pl.ds(pl.multiple_of(own * high, high), high), :]
        copies = []
        for by, peer in enumerate(peers):
            copies.append(
                pltpu.make_async_remote_copy(
                    src_ref=source.at[:, pl.ds(pl.multiple_of(peer * rows, rows), rows)],
                    dst_ref=mine,
                    send_sem=owner_sends.at[index * (ways - 1) + by],
                    recv_sem=owner_receives.at[index * (ways - 1) + by],
                    device_id=place("dp", peer),
                    device_id_type=MESH,
                )
            )
        here = pltpu.make_async_copy(
            source.at[:, pl.ds(pl.multiple_of(own * rows, rows), rows)], mine, own_sems.at[index]
        )
        return copies + [here]

    partners = [place("dp", partner(own, by)) for by in doublings(ways)]
    partners += [place("seq", partner(position, by)) for by in doublings(spans)]
    partners += [place("head", 1 - lax.axis_index("head"))]

    def small_copy(turn):
        high = 8 if turn == len(partners) - 1 else small.shape[0]
        return pltpu.make_async_remote_copy(
            src_ref=small_sent.at[turn, :high, :],
            dst_ref=small_in.at[turn, :high, :],
            send_sem=small_sends.at[turn],
            recv_sem=small_receives.at[turn],
            device_id=partners[turn],
            device_id_type=MESH,
        )

    def small_turn(turn):
        if turn == 0:
            small_sent[0] = small[...]
        else:
            small_copy(turn - 1).wait_recv()
            if turn < len(partners):
                small_sent[turn] = small_sent[turn - 1] + small_in[turn - 1]
            else:
                small_out[...] = small_sent[turn - 1]
                small_out[:8, :] = small_sent[turn - 1, :8, :] + small_in[turn - 1, :8, :]
        if turn < len(partners):
            small_copy(turn).start()

    meet(
        [place("seq", (position + last) % spans), place("seq", (position + 1) % spans)]
        + [place("seq", partner(position, by)) for by in doublings(spans)[1:]]
        + [place("dp", peer) for peer in peers]
        + partners[-1:]
    )
    small_turn(0)
    along = (position, last - position)

    def source_send(way, index):
        turn, group = index // groups, index % groups
        shard = last - turn if way == 0 else turn
        if index >= 2:
            line_copy(way, (index - 2) // groups, (index - 2) % groups, totals.at[0]).wait_send()
        line_copy(way, turn, group, raw_at(group, shard)).start()

    for way in range(2):

        @pl.when(along[way] == 0)
        def _():
            for index in range(2):
                source_send(way, index)

    fed_copies = [owner_copies(index, piece) for index, piece in enumerate(pieces)]
    for copies in fed_copies:
        for copy in copies:
            copy.start()

    for way in range(2):

        @pl.when(along[way] == 0)
        def _():
            for index in range(2, groups + 2):
                source_send(way, index)

    for turn in range(1, rounds):
        for group in range(groups):
            for way in range(2):
                if turn * groups + group + 2 < rounds * groups:

                    @pl.when(along[way] == 0)
                    def _():
                        source_send(way, turn * groups + group + 2)

                shard = last - turn + position if way == 0 else turn - along[1]

                @pl.when((along[way] >= 1) & (along[way] <= turn))
                def _():
                    line_copy(way, turn - 1, group, handed.at[way, turn - 1, group]).wait_recv()
                    term = raw_at(group, shard)[...].astype(jnp.float32)
                    term = term + received[way, turn - 1, group].astype(jnp.float32)
                    handed[way, turn - 1, group] = term.astype(jnp.bfloat16)
                    line_copy(way, turn, group, handed.at[way, turn - 1, group]).start()

        small_turn(turn)

    for turn in range(rounds, len(partners) + 1):
        small_turn(turn)

    for group in range(groups):
        for way in range(2):

            @pl.when(along[way] >= 1)
            def _():
                line_copy(way, rounds - 1, group, totals.at[group]).wait_recv()

        total = raw_at(group, position)[...].astype(jnp.float32)
        for way in range(2):
            arrived = received[way, rounds - 1, group].astype(jnp.float32)
            total = total + jnp.where(along[way] >= 1, arrived, 0.0)
        totals[group] = total.astype(jnp.bfloat16)
        for copy in owner_copies(fed + group, totals.at[group]):
            copy.start()

    sources = list(pieces) + [totals.at[group] for group in range(groups)]
    for index, source in enumerate(sources):
        for copy in owner_copies(index, source):
            copy.wait()

    for turn in range(rounds):
        for way in range(2):

            @pl.when((along[way] >= 1) & (along[way] <= turn))
            def _():
                for group in range(groups):
                    line_copy(way, turn, group, totals.at[group]).wait_send()

    for way in range(2):

        @pl.when(along[way] == 0)
        def _():
            for group in range(groups - 2, groups):
                line_copy(way, rounds - 1, group, totals.at[group]).wait_send()

    for turn in range(len(partners)):
        small_copy(turn).wait_send()


def finished_gradients(out_raw, mix_raw, pieces, small, number):
    spans, ways = lax.axis_size("seq"), lax.axis_size("dp")
    _, count, wide = out_raw.shape
    groups = 1 + mix_raw.shape[1] // count
    rows = wide // ways
    fed = len(pieces)
    highs = [ways * piece.shape[0] for piece in pieces] + [ways * count] * groups
    inside = pl.BlockSpec(memory_space=pltpu.VMEM)
    shapes = [b16(high, rows) for high in highs]
    lines = (2, spans - 1, groups, count, wide)
    turns = len(doublings(ways)) + len(doublings(spans)) + 1
    return pl.pallas_call(
        functools.partial(finish_kernel, spans, ways, fed),
        out_shape=shapes + [f32(*small.shape)],
        in_specs=[inside] * 3 + [pl.BlockSpec(memory_space=pl.ANY)] * fed,
        out_specs=[inside] * (len(shapes) + 1),
        scratch_shapes=[
            pltpu.VMEM(lines, jnp.bfloat16),
            pltpu.VMEM((2, spans - 2, groups, count, wide), jnp.bfloat16),
            pltpu.VMEM((groups, count, wide), jnp.bfloat16),
        ]
        + [pltpu.SemaphoreType.DMA((2 * (spans - 1) * groups,))] * 2
        + [pltpu.SemaphoreType.DMA((len(highs) * (ways - 1),))] * 2
        + [pltpu.SemaphoreType.DMA((len(highs),))]
        + [pltpu.VMEM((turns,) + small.shape, jnp.float32)] * 2
        + [pltpu.SemaphoreType.DMA((turns,))] * 2,
        compiler_params=pltpu.CompilerParams(
            collective_id=number, has_side_effects=True, vmem_limit_bytes=VMEM
        ),
        cost_estimate=SHORT,
    )(out_raw, mix_raw, small, *pieces)


def shards(
    tokens_in,
    lengths,
    first_gain,
    query_weight,
    key_weight,
    value_weight,
    beta_weight,
    query_conv,
    key_conv,
    value_conv,
    mixer_gain,
    output_weight,
    second_gain,
    gate_weight,
    up_weight,
    down_weight,
    upstream,
):
    num_rows, local_len, local_width = tokens_in.shape
    full_width = query_weight.shape[0]
    channels = query_weight.shape[1]
    local_heads = beta_weight.shape[1]
    groups = lax.axis_size("head")
    ways = lax.axis_size("dp")
    spans = lax.axis_size("seq")
    positions = lax.axis_index("seq") * local_len + jnp.arange(local_len, dtype=jnp.int32)
    live_mask = (positions[None, :] < lengths[:, None]).astype(jnp.float32)
    masked_up = upstream * live_mask[..., None].astype(jnp.bfloat16)
    gains = jnp.stack([first_gain, second_gain] + [first_gain] * 14)
    everything = gather_head(jnp.concatenate([tokens_in[0], masked_up[0], gains], 0), 1)
    gathered = everything[None, :local_len]
    upstream_full = everything[None, local_len : 2 * local_len]
    gain_one = everything[2 * local_len].astype(jnp.float32)
    gain_two = everything[2 * local_len + 1].astype(jnp.float32)
    stream_full = gathered.astype(jnp.float32)
    scale_one = inverse_rms(stream_full)
    normed_one = (stream_full * scale_one * gain_one).astype(jnp.bfloat16)

    def scattered(pieces):
        return lax.psum_scatter(pieces, "seq", scatter_dimension=0, tiled=False)

    def to_owner(piece):
        c = piece.shape[0]
        blocks = piece.reshape(c, ways, -1).transpose(1, 0, 2)
        return jnp.stack(in_order(exchanged(blocks, "dp"), "dp"), 0)

    fused = groups == 2
    if fused:
        half_up = lax.all_gather(masked_up[0], "dp", axis=0, tiled=True)
        tokens_up = gather_head(half_up, 1)
    else:
        tokens_up = jnp.stack(spread(upstream_full[0], "dp")[1:])
    per_step = 2 if local_heads % 2 == 0 else 1
    pres = [
        jnp.dot(normed_one[0], weight, preferred_element_type=jnp.float32).astype(jnp.bfloat16)
        for weight in (query_weight, key_weight, value_weight)
    ]
    beta_logit = jnp.dot(normed_one[0], beta_weight, preferred_element_type=jnp.float32)
    convs = [query_conv, key_conv, value_conv]
    live_col = live_mask[0][:, None]
    head_gain = mixer_gain.astype(jnp.float32)[None, :]
    if fused:
        (
            query, key, value, wy, inverse, ends, mixed, head_out, entering, rims,
        ) = mixer_forward(pres, convs, beta_logit, live_col, head_gain, per_step, spans, 1)
    else:
        rims = passed_along(jnp.stack([pre[local_len - RIM :, :] for pre in pres]), "seq", 1)
        rims = [rims[0], rims[1], rims[2]]
        query, key, value, wy, inverse, mix, ends = mixer_local(
            pres, rims, convs, beta_logit, live_col, per_step
        )
        entering = chain_state(ends[:, :, :HEAD_DIM], ends[:, :, HEAD_DIM:], False)
        mixed, head_out = mixer_finish(mix, entering, head_gain, per_step)
    head_out = head_out[None]
    mixer_part = jnp.dot(head_out, output_weight, preferred_element_type=jnp.float32)
    stream_mid = stream_full + sum_head(mixer_part)
    scale_two = inverse_rms(stream_mid)
    normed_two = (stream_mid * scale_two * gain_two).astype(jnp.bfloat16)
    if fused:
        half_two = lax.all_gather(
            own_half(normed_two[0], local_width), "dp", axis=0, tiled=True
        )
    feed_part, d_two_part, turned = feed_forward(
        normed_two[0], upstream_full[0], gate_weight, up_weight, down_weight,
        half_up if fused else normed_two,
    )
    layer_out = own_half(stream_mid + sum_head(feed_part[None]), local_width).astype(jnp.bfloat16)
    units = turned.shape[1] // ways
    turned = turned.reshape(3, ways, units, local_len)

    def raw_piece(lefts, count, rights, is_turned, tokens=()):
        return span_pieces(
            lefts, count, rights, local_len, full_width, spans, is_turned, tokens
        )

    def slots_of(own, others):
        return [(own, (local_len,), lambda at: (0,))] + [
            (others, (1, local_len), lambda at, by=by: (by, 0)) for by in range(ways - 1)
        ]

    def by_position(array):
        return [(array, (local_len,), lambda at, by=by: (at ^ by,)) for by in range(ways)]

    def feed_slots(which, others, index):
        own = [(turned, (1, 1, units, local_len), lambda at: (which, at, 0, 0))]
        return own + [
            (others, (1, 1, units, local_len), lambda at, by=by: (by, index, 0, 0))
            for by in range(ways - 1)
        ]

    normed_full = normed_two[0]
    if fused:
        (hidden_others,) = plane_exchange([turned], [("rows", 0, 1)], [], 2)
        down_raw = raw_piece(
            [feed_slots(0, hidden_others, 0)], units, by_position(tokens_up), True
        )
        (d_others,) = plane_exchange([turned], [("rows", 1, 3)], [down_raw], 3)
        two_slots = by_position(gather_head(half_two, 1))
    else:
        hidden_others = jnp.stack(exchanged(turned[:1].transpose(1, 0, 2, 3), "dp")[1:])
        down_raw = raw_piece(
            [feed_slots(0, hidden_others, 0)], units, slots_of(upstream_full[0], tokens_up), True
        )
        d_others = jnp.stack(exchanged(turned[1:].transpose(1, 0, 2, 3), "dp")[1:])
        two_slots = slots_of(normed_full, jnp.stack(spread(normed_full, "dp")[1:]))
    down_piece = scattered(down_raw)
    gate_raw = raw_piece([feed_slots(1, d_others, 0)], units, two_slots, True)
    gate_piece = scattered(gate_raw)
    up_raw = raw_piece([feed_slots(2, d_others, 1)], units, two_slots, True, [gate_raw])
    up_piece = scattered(up_raw)
    d_two = sum_head(d_two_part[None])
    d_stream = (
        upstream_full.astype(jnp.float32)
        + scale_two * gain_two * d_two
        - stream_mid
        * scale_two
        * scale_two
        * scale_two
        * (jnp.sum(d_two * gain_two * stream_mid, axis=-1, keepdims=True) / full_width)
    )
    grad_second = own_half(jnp.sum(d_two * stream_mid * scale_two, axis=(0, 1)), local_width)
    residual_full = d_stream.astype(jnp.bfloat16)
    d_head_out = jnp.einsum(
        "rsd,cd->rsc", residual_full, output_weight, preferred_element_type=jnp.float32
    )
    if fused:
        (
            *mix_sources, grad_kernels, d_beta_logit, grad_gain_part, out_others, res_others,
            one_others,
        ) = mixer_backward(
            d_head_out[0], mixed, head_gain, pres, rims, convs, beta_logit, live_col,
            query, key, value, wy, inverse, entering, ends, [up_raw, down_piece],
            head_out[0], residual_full[0], normed_one[0], per_step, spans, ways, 4,
        )
    else:
        d_mixed, d_fresh, d_ends, grad_gain_part = mixer_back_local(
            d_head_out[0], mixed, head_gain, query, key, wy, per_step
        )
        leaving = chain_state(jnp.swapaxes(ends[:, :, :HEAD_DIM], 1, 2), d_ends, True)
        *d_pres, tails, d_rims, grad_kernels, d_beta_logit = mixer_back(
            pres, rims, convs, beta_logit, live_col, query, key, value, wy, inverse,
            entering, d_mixed, d_fresh, leaving, per_step,
        )
        tails = (tails + passed_along(d_rims, "seq", -1)).astype(jnp.bfloat16)
        mix_sources = [
            jnp.concatenate([part[: local_len - 8], tail], 0) for part, tail in zip(d_pres, tails)
        ]
    grad_gain_part = grad_gain_part[0]
    share_width = channels // ways
    residual = residual_full[0]
    if fused:
        d_one_part, *mix_others = back_projection(
            mix_sources, d_beta_logit.astype(jnp.bfloat16),
            [query_weight, key_weight, value_weight], beta_weight, ways, 5,
        )
    else:
        *mix_others, out_others = [
            jnp.stack(exchanged(part.reshape(local_len, ways, -1).transpose(1, 0, 2), "dp")[1:])
            for part in mix_sources + [head_out[0]]
        ]
        res_others = jnp.stack(spread(residual, "dp")[1:])

    def column_slots(own, others):
        if fused:
            first = [(own, (local_len, share_width), lambda at: (0, at))]
        else:
            mine = lax.dynamic_slice_in_dim(
                own, lax.axis_index("dp") * share_width, share_width, 1
            )
            first = [(mine, (local_len, share_width), lambda at: (0, 0))]
        return first + [
            (others, (1, local_len, share_width), lambda at, by=by: (by, 0, 0))
            for by in range(ways - 1)
        ]

    if fused:
        one_slots = slots_of(normed_one[0], one_others)
    else:
        one_slots = slots_of(normed_one[0], jnp.stack(spread(normed_one[0], "dp")[1:]))
    out_raw = raw_piece(
        [column_slots(head_out[0], out_others)], share_width, slots_of(residual, res_others), False,
        [gate_piece],
    )
    mix_raw = raw_piece(
        [column_slots(own, others) for own, others in zip(mix_sources, mix_others)],
        3 * share_width, one_slots, False, [out_raw],
    )
    d_logit_low = d_beta_logit.astype(jnp.bfloat16)
    if not fused:
        d_one_part = jnp.dot(d_logit_low, beta_weight.T, preferred_element_type=jnp.float32)
        for part, weight in zip(mix_sources, (query_weight, key_weight, value_weight)):
            d_one_part = d_one_part + jnp.dot(
                part, weight.T, preferred_element_type=jnp.float32
            )
    grad_beta_part = lax.dot_general(
        d_logit_low, normed_one[0], (((0,), (0,)), ((), ())), preferred_element_type=jnp.float32
    )
    d_one = sum_head(d_one_part[None])
    grad_tokens = own_half(
        d_stream
        + scale_one * gain_one * d_one
        - stream_full
        * scale_one
        * scale_one
        * scale_one
        * (jnp.sum(d_one * gain_one * stream_full, axis=-1, keepdims=True) / full_width),
        local_width,
    )
    grad_first = own_half(jnp.sum(d_one * stream_full * scale_one, axis=(0, 1)), local_width)
    lane = 128
    sizes = [HEAD_DIM, local_width, local_width, grad_kernels.size, grad_beta_part.size]
    parts = [grad_gain_part, grad_first, grad_second, grad_kernels, grad_beta_part]
    shares = [
        jnp.pad(part.reshape(-1, lane), ((0, -(size // lane) % 8), (0, 0)))
        for part, size in zip(parts, sizes)
    ]
    small = jnp.concatenate(shares, 0)
    if fused:
        *finished, small = finished_gradients(
            out_raw, mix_raw, [down_piece, gate_piece, up_piece], small, 6
        )
        down, gate, up, out, *mix = widened(
            finished, [False, True, True, False, True, True, True]
        )
        gain_total = small[0]
    else:
        small = sum_doubling(small, ("dp", "seq"))
        gain_total = sum_doubling(small[0], ("head",))
    starts = [0]
    for part in shares:
        starts.append(starts[-1] + part.shape[0])
    totals = [
        small[start : start + size // lane].reshape(part.shape)
        for start, size, part in zip(starts, sizes, parts)
    ]
    grad_first, grad_second, kernel_sum, beta_sum = totals[1:]
    share = lax.axis_index("dp") * spans + lax.axis_index("seq")
    rows = full_width // (ways * spans)
    grad_beta = lax.dynamic_slice_in_dim(beta_sum, share * rows, rows, 1).T
    if not fused:
        feed = to_owner(jnp.concatenate([down_piece, gate_piece, up_piece], 0))
        down, gate, up = [
            feed[:, place * units : (place + 1) * units].reshape(-1, rows).astype(jnp.float32)
            for place in range(3)
        ]
        gate, up = gate.T, up.T
        out = to_owner(scattered(out_raw)).reshape(-1, rows).astype(jnp.float32)
        mix = to_owner(scattered(mix_raw)).astype(jnp.float32)
        third = mix.shape[1] // 3
        mix = [mix[:, i * third : (i + 1) * third].reshape(-1, rows).T for i in range(3)]
    return (
        layer_out,
        grad_tokens,
        grad_first,
        mix[0],
        mix[1],
        mix[2],
        grad_beta,
        kernel_sum[0],
        kernel_sum[1],
        kernel_sum[2],
        gain_total,
        out,
        grad_second,
        gate,
        up,
        down,
    )


def solution(mesh):
    placed = (
        P("dp", "seq", "head"),
        P("dp"),
        P("head"),
        P(None, "head"),
        P(None, "head"),
        P(None, "head"),
        P(None, "head"),
        P(None, "head"),
        P(None, "head"),
        P(None, "head"),
        P(),
        P("head", None),
        P("head"),
        P(None, "head"),
        P(None, "head"),
        P("head", None),
        P("dp", "seq", "head"),
    )
    return jax.shard_map(
        shards,
        mesh=mesh,
        in_specs=placed,
        out_specs=(
            P("dp", "seq", "head"),
            P("dp", "seq", "head"),
            P("head"),
            P(("dp", "seq"), "head"),
            P(("dp", "seq"), "head"),
            P(("dp", "seq"), "head"),
            P(("dp", "seq"), "head"),
            P(None, "head"),
            P(None, "head"),
            P(None, "head"),
            P(),
            P("head", ("dp", "seq")),
            P("head"),
            P(("dp", "seq"), "head"),
            P(("dp", "seq"), "head"),
            P("head", ("dp", "seq")),
        ),
        check_vma=False,
    )
```

time: 565 us -> 440 us (0.78); the launches traced: 555 us -> 439 us
  local copies, waits for them, and re-layouts: 105 us -> 20.2 us
  waiting for transfers between devices: 75.5 us -> 5.89 us
  Pallas kernels: 283 us -> 351 us
  starting transfers between devices: 21.7 us -> 2.05 us
    pallas_call x13 -> x10, Pallas kernels: 121 us -> 258 us  [the longest x1 99.1 us: finished_gradients(): pl.pallas_call(functools.partial(finish_kernel, spans, ways, fed), out_sh...]
    pallas_call x4 -> x2, Pallas kernels: 134 us -> 63 us  [plane_exchange(): pl.pallas_call(functools.partial(exchange_kernel, ways, kinds), out_shape...]
    ppermute x16 -> x0, waiting for transfers between devices: 67.4 us -> none  [the longest x5 31.7 us: sum_doubling(): value = value + lax.ppermute(value, axis, swap_pairs(axis, by))]
    unnamed x244 -> x62, local copies, waits for them, and re-layouts: 75.2 us -> 8.39 us
    ppermute x16 -> x0, starting transfers between devices: 18.9 us -> none  [the longest x9 10.9 us: exchanged(): parts.append(lax.ppermute(out, axis, swap_pairs(axis, by)))]
    dot_general x5 -> x1, matrix products: 11.7 us -> 0.29 us  [shards(): lax.dot_general(d_logit_low, normed_one[0], (((0,), (0,)), ((), ())), pre...]
    slice x12 -> x1, local copies, waits for them, and re-layouts: 9.71 us -> 0.84 us  [shards(): small[start:start + size // lane].reshape(part.shape)]
  transfers between devices with their start and end apart: 30 -> 12, of which waited for: 14 -> 4; matrix products, arithmetic and copies ran while one was open for 13% -> 11% of each run, Pallas kernels for 48% -> 56%
where the time goes in v3:
time: 440 us; the launch traced here: 439 us
  Pallas kernels  351 us (80%)
  other arithmetic  30.9 us (7%)
  local copies, waits for them, and re-layouts  20.2 us (5%)
  between operations  15 us (3%)
  matrix products  13.8 us (3%)
  waiting for transfers between devices  5.89 us (1%)
    pallas_call x1, Pallas kernels, finished_gradients(): pl.pallas_call(functools.partial(finish_kernel, spans, ways, fed), out_sh...  99.1 us
    pallas_call x1, Pallas kernels, mixer_backward(): pl.pallas_call(functools.partial(mixer_backward_kernel, per_step, taps, s...  64.5 us
    pallas_call x2, Pallas kernels, plane_exchange(): pl.pallas_call(functools.partial(exchange_kernel, ways, kinds), out_shape...  63 us
    pallas_call x5, Pallas kernels, span_pieces(): pl.pallas_call(functools.partial(pieces_kernel, groups, slots, ways, turn...  37.4 us
    pallas_call x1, Pallas kernels, feed_forward(): pl.pallas_call(feed_kernel, grid=(units // tile,), in_specs=[whole, whole...  30.1 us
    pallas_call x1, Pallas kernels, mixer_forward(): pl.pallas_call(functools.partial(mixer_forward_kernel, per_step, taps, sp...  27.2 us
    pallas_call x1, Pallas kernels, back_projection(): pl.pallas_call(functools.partial(back_projection_kernel, ways), grid=(wid...  24.8 us
  transfers between devices with their start and end apart: 12, of which 4 were waited for; matrix products, arithmetic and copies ran while one was open for 11% of the time, Pallas kernels for 56%

profile of v3, /device:TPU:0, one launch (start us, length us, event | category | flops | bytes accessed | tf_op | source)
XLA Modules:
  0.0 438.7 jit_solution(563532861074723344)
XLA Ops:
  10.5 2.2 concatenate.15
  19.5 2.1 convolution_convert_fusion.1.refs_2_.refs_13_.refs_8_
  22.2 2.1 convolution_convert_fusion.2.refs_1_.refs_12_.refs_7_
  25.5 4.4 convolution_convert_fusion.3.refs_0_.refs_11_.refs_6_
  29.8 27.2 %shard_map.288 = (bf16[256,1024]{1,0:T(8,128)(2,1)}, bf16[256,1024]{1,0:T(8,128)(2,1)}, bf16[256,1024]{1,0:T(8,128)(2,1)}, f32[8,256,256]{2,1,0:T(8,128)}, f32[8...) custom-call(bf16[256,1024]{1,0:T(8,128)(2,1)} %convolution_convert_f, ...), custom_call_target="tpu_custom_call" | custom-call | tf_op jit(solution)/shard_map/pallas_call | solution.py:835
  57.0 2.4 fusion.5
  60.4 1.9 collective-permute-done.1
  62.3 2.1 multiply_reduce_fusion.2
  66.0 2.1 pad_maximum_fusion.2.d_ref
  69.3 30.1 %shard_map.289 = (bf16[256,2048]{1,0:T(8,128)(2,1)}, bf16[256,2048]{1,0:T(8,128)(2,1)}, bf16[3,2816,256]{2,1,0:T(8,128)(2,1)}) custom-call(bf16[256,2048]{1,0:T(8,128)(2,1)} %fusion.44.x_ref, bf16[256,2048]{1,0:T(8,128)(2,1)} %pad_maximum_fusion.2.d_ref, bf16[2048,2816]{1,0:T(8,128)(2,1)} %gate_w.1, bf16[2048,2816]{1,0:T(8,128)(2,1)} %up_w.1, ...), custom_call_target="tpu_custom_call" | custom-call | tf_op jit(solution)/shard_map/pallas_call | solution.py:1142
  99.4 27.6 %shard_map.290.refs_1_.refs_2_.refs_3_ = bf16[3,1,704,256]{3,2,1,0:T(8,128)(2,1)} custom-call(bf16[3,4,704,256]{3,2,1,0:T(8,128)(2,1)} %bitcast.89), custom_call_target="tpu_custom_call" | custom-call | tf_op jit(solution)/shard_map/pallas_call | solution.py:250
  127.1 1.9 broadcast_select_fusion.3
  128.9 2.5 pad_maximum_fusion.refs_4_.refs_5_.refs_6_.refs_7_.refs_8_.refs_9_.refs_10_.refs_11_.refs_12_.refs_13_.refs_14_.refs_15_.refs_16_.refs_17_.refs_18_.refs_19_
  131.4 7.9 %shard_map.291.refs_1_ = bf16[4,704,512]{2,1,0:T(8,128)(2,1)} custom-call(s32[1]{0:T(128)} %bitcast.16.at, bf16[3,4,704,256]{3,2,1,0:T(8,128)(2,1)} %bitcast.90, bf16[3,1,704,256]{3,2,1,0:T(8,128)(2,1)} %shard_map.290.refs_1_.refs_2_.refs_3_, bf16[3,1,704,256]{3,2,1,0:T(8,128)(2,1)} %shard_map.290.refs_1_.refs_2_.refs_3_, ...), custom_call_target="tpu_custom_call" | custom-call | tf_op jit(solution)/shard_map/pallas_call | solution.py:1249
  139.5 35.4 %shard_map.292.refs_1_.refs_2_.refs_3_ = bf16[3,2,704,256]{3,2,1,0:T(8,128)(2,1)} custom-call(bf16[3,4,704,256]{3,2,1,0:T(8,128)(2,1)} %bitcast.91, bf16[4,704,512]{2,1,0:T(8,128)(2,1)} %shard_map.291.refs_1_), custom_call_target="tpu_custom_call" | custom-call | tf_op jit(solution)/shard_map/pallas_call | solution.py:250
  175.2 2.5 pad_maximum_fusion.1.refs_4_.refs_5_.refs_6_.refs_7_.refs_8_.refs_9_.refs_10_.refs_11_.refs_12_.refs_13_.refs_14_.refs_15_.refs_16_.refs_17_.refs_18_.refs_19_
  177.6 7.9 %shard_map.293.refs_20_ = bf16[4,704,512]{2,1,0:T(8,128)(2,1)} custom-call(s32[1]{0:T(128)} %bitcast.16.at, bf16[3,4,704,256]{3,2,1,0:T(8,128)(2,1)} %bitcast.92, bf16[3,2,704,256]{3,2,1,0:T(8,128)(2,1)} %shard_map.292.refs_1_.refs_2_.refs_3_, bf16[3,2,704,256]{3,2,1,0:T(8,128)(2,1)} %shard_map.292.refs_1_.refs_2_.refs_3_, ...), custom_call_target="tpu_custom_call" | custom-call | tf_op jit(solution)/shard_map/pallas_call | solution.py:1249
  185.8 7.9 %shard_map.294.refs_22_ = bf16[4,704,512]{2,1,0:T(8,128)(2,1)} custom-call(s32[1]{0:T(128)} %bitcast.16.at, bf16[3,4,704,256]{3,2,1,0:T(8,128)(2,1)} %bitcast.93, bf16[3,2,704,256]{3,2,1,0:T(8,128)(2,1)} %shard_map.292.refs_1_.refs_2_.refs_3_, bf16[3,2,704,256]{3,2,1,0:T(8,128)(2,1)} %shard_map.292.refs_1_.refs_2_.refs_3_, ...), custom_call_target="tpu_custom_call" | custom-call | tf_op jit(solution)/shard_map/pallas_call | solution.py:1249
  197.7 2.0 multiply_reduce_fusion
  199.7 3.7 convert_bitcast_fusion.1
  203.4 2.3 fusion.28.refs_0_
  205.7 64.5 %shard_map.295 = (bf16[256,1024]{1,0:T(8,128)(2,1)}, bf16[256,1024]{1,0:T(8,128)(2,1)}, bf16[256,1024]{1,0:T(8,128)(2,1)}, f32[3,4,1024]{2,1,0:T(4,128)}, f32[25...) custom-call(f32[256,1024]{1,0:T(8,128)} %fusion.28.refs_0_, ...), custom_call_target="tpu_custom_call" | custom-call | tf_op jit(solution)/shard_map/pallas_call | solution.py:1056
  270.1 1.5 convert_element_type.145.refs_3_
  271.7 24.8 %shard_map.296 = (bf16[256,2048]{1,0:T(8,128)(2,1)}, bf16[3,256,256]{2,1,0:T(8,128)(2,1)}, bf16[3,256,256]{2,1,0:T(8,128)(2,1)}, bf16[3,256,256]{2,1,0:T(8,128)(2,1)}) custom-call(bf16[256,1024]{1,0:T(8,128)(2,1)} %get-tuple-element.70.refs_0_.refs_8_, bf16[256,1024]{1,0:T(8,128)(2,1)} %get-tuple-element.71.refs_1_.refs_9_.refs_4_, ...), custom_call_target="tpu_custom_call" | custom-call | tf_op jit(solution)/shard_map/pallas_call | solution.py:1189
  296.6 2.3 fusion.16
  300.2 2.4 fusion.12
  305.5 5.5 %shard_map.297.refs_28_.refs_0_ = bf16[4,256,512]{2,1,0:T(8,128)(2,1)} custom-call(s32[1]{0:T(128)} %bitcast.16.at, bf16[256,1024]{1,0:T(8,128)(2,1)} %get-tuple-element.57.refs_24_.refs_0_, bf16[3,256,256]{2,1,0:T(8,128)(2,1)} %get-tuple-element.75.refs_1_.refs_2_.refs_3_, bf16[3,256,256]{2,1,0:T(8,128)(2,1)} %get-tuple-element.75.refs_1_.refs_2_.refs_3_, ...), custom_call_target="tpu_custom_call" | custom-call | tf_op jit(solution)/shard_map/pallas_call | solution.py:1249
  311.0 8.2 %shard_map.298.refs_1_ = bf16[4,768,512]{2,1,0:T(8,128)(2,1)} custom-call(s32[1]{0:T(128)} %bitcast.16.at, bf16[256,1024]{1,0:T(8,128)(2,1)} %get-tuple-element.70.refs_0_.refs_8_, bf16[3,256,256]{2,1,0:T(8,128)(2,1)} %get-tuple-element.77.refs_1_.refs_2_.refs_3_, bf16[3,256,256]{2,1,0:T(8,128)(2,1)} %get-tuple-element.77.refs_1_.refs_2_.refs_3_, ...), custom_call_target="tpu_custom_call" | custom-call | tf_op jit(solution)/shard_map/pallas_call | solution.py:1249
  319.2 2.4 reduce-scatter.8.cloned.1.call-done
  321.6 99.1 %shard_map.299 = (bf16[2816,128]{1,0:T(8,128)(2,1)}, bf16[2816,128]{1,0:T(8,128)(2,1)}, bf16[2816,128]{1,0:T(8,128)(2,1)}, bf16[1024,128]{1,0:T(8,128)(2,1)}, bf...) custom-call(bf16[4,256,512]{2,1,0:T(8,128)(2,1)} %shard_map.297.refs_28_.re, ...), custom_call_target="tpu_custom_call" | custom-call | tf_op jit(solution)/shard_map/pallas_call | solution.py:1490
  422.0 1.3 slice_bitcast_fusion
  427.3 4.8 %shard_map.300 = (f32[2816,128]{1,0:T(8,128)}, f32[128,2816]{1,0:T(8,128)}, f32[128,2816]{1,0:T(8,128)}, f32[1024,128]{1,0:T(8,128)}, f32[128,1024]{1,0:T(8,128)...) custom-call(bf16[2816,128]{1,0:T(8,128)(2,1)} %get-tuple-element.84.refs_0_, bf16[2816,128]{1,0:T(8,128)(2,1)} %get-tuple-element.85.refs_1_, ...), custom_call_target="tpu_custom_call" | custom-call | tf_op jit(solution)/shard_map/pallas_call | solution.py:1285
  (127 shorter events, 29.0 us)
Async XLA Ops:
  7.2 6.0 %copy-start.16 = (bf16[1,256,1024]{2,1,0:T(8,128)(2,1)S(1)}, bf16[1,256,1024]{2,1,0:T(8,128)(2,1)}, u32[]{:S(2)}) copy-start(bf16[1,256,1024]{2,1,0:T(8,128)(2,1)} %param.33) | copy-start | bytes 1572868
  7.2 58.6 %all-gather.5.cloned.1.call-start = ((), (), s32[]{:S(2)}) async-start(), calls=%async_computation.6 | async-start | bytes 2621440 | tf_op jit(solution)/shard_map/all_gather | solution.py:1561
  10.5 5.0 %copy-start.28 = (bf16[128]{0:T(256)(128)(2,1)S(1)}, bf16[128]{0:T(256)(128)(2,1)}, u32[]{:S(2)}) copy-start(bf16[128]{0:T(256)(128)(2,1)} %param.27) | copy-start | bytes 772
  12.7 3.2 collective-permute-start
  14.1 125.3 %all-gather.7.cloned.1.call-start = ((), (), s32[]{:S(2)}) async-start(), calls=%async_computation.7 | async-start | bytes 2621440 | tf_op jit(solution)/shard_map/all_gather | solution.py:1592
  16.1 3.3 copy-start.13
  19.5 6.0 %copy-start = (bf16[256,2048]{1,0:T(8,128)(2,1)}, bf16[256,2048]{1,0:T(8,128)(2,1)S(1)}, u32[]{:S(2)}) copy-start(bf16[256,2048]{1,0:T(8,128)(2,1)S(1)} %fusion.6.refs_26_.refs_12_.refs_13_.refs_14_.refs_15_) | copy-start | bytes 3145732
  19.5 2.8 copy-start.12
  24.7 5.2 %copy-start.22 = (f32[256,8]{0,1:T(8,128)}, f32[256,8]{0,1:T(8,128)S(1)}, u32[]{:S(2)}) copy-start(f32[256,8]{0,1:T(8,128)S(1)} %fusion.27) | copy-start | bytes 24580
  25.5 31.6 %copy-start.26 = (bf16[1024,2048]{1,0:T(8,128)(2,1)S(1)}, bf16[1024,2048]{1,0:T(8,128)(2,1)}, u32[]{:S(2)}) copy-start(bf16[1024,2048]{1,0:T(8,128)(2,1)} %param.28) | copy-start | bytes 12582916
  57.0 5.3 %copy-start.4 = (bf16[256,2048]{1,0:T(8,128)(2,1)S(1)}, bf16[256,2048]{1,0:T(8,128)(2,1)}, u32[]{:S(2)}) copy-start(bf16[256,2048]{1,0:T(8,128)(2,1)} %copy-done.3) | copy-start | bytes 3145732
  59.4 2.9 collective-permute-start.1
  65.5 140.1 %reduce-scatter.4.cloned.1.call-start = ((), (), s32[]{:S(2)}) async-start(), calls=%async_computation.3 | async-start | bytes 3604480 | tf_op jit(solution)/shard_map/reduce_scatter | solution.py:1552
  65.8 61.3 %collective-permute-start.4 = (bf16[1024,1024]{1,0:T(8,128)(2,1)}, bf16[1024,1024]{1,0:T(8,128)(2,1)}, u32[]{:S(2)}, u32[]{:S(2)}) collective-permute-start(bf16[1024,1024]{1,0:T(8,128)(2,1)} %bitcast.94), channel_id=1, source_target_pairs={{0,1},{1,0},{2,3},{3,2},{4,5},{5,4},{6,7},{7,6},{8,9},{9,8},{10,11... | collective-permute-start | bytes 6291464 | tf_op jit(solution)/shard_map/ppermute | solution.py:58
  99.4 27.6 %copy-start.10 = (bf16[1,1024,1024]{2,1,0:T(8,128)(2,1)S(1)}, bf16[1,1024,1024]{2,1,0:T(8,128)(2,1)}, u32[]{:S(2)}) copy-start(bf16[1,1024,1024]{2,1,0:T(8,128)(2,1)} %all-gather.5.cloned.1.call-done) | copy-start | bytes 6291460
  139.3 166.2 %reduce-scatter.6.cloned.1.call-start = ((), (), s32[]{:S(2)}) async-start(), calls=%async_computation.4 | async-start | bytes 3604480 | tf_op jit(solution)/shard_map/reduce_scatter | solution.py:1552
  139.4 35.5 %copy-start.17 = (bf16[1,1024,1024]{2,1,0:T(8,128)(2,1)S(1)}, bf16[1,1024,1024]{2,1,0:T(8,128)(2,1)}, u32[]{:S(2)}) copy-start(bf16[1,1024,1024]{2,1,0:T(8,128)(2,1)} %all-gather.7.cloned.1.call-done) | copy-start | bytes 6291460
  139.4 35.5 %collective-permute-start.5 = (bf16[1024,1024]{1,0:T(8,128)(2,1)}, bf16[1024,1024]{1,0:T(8,128)(2,1)S(1)}, u32[]{:S(2)}, u32[]{:S(2)}) collective-permute-start(bf16[1024,1024]{1,0:T(8,128)(2,1)} %bitcast.101), channel_id=1, source_target_pairs={{0,1},{1,0},{2,3},{3,2},{4,5},{5,4},{6,7},{7,6},{8,9},{9,8},{10,11... | collective-permute-start | bytes 6291464 | tf_op jit(solution)/shard_map/ppermute | solution.py:58
  185.6 136.1 %reduce-scatter.8.cloned.1.call-start = ((), (), s32[]{:S(2)}) async-start(), calls=%async_computation.5 | async-start | bytes 3604480 | tf_op jit(solution)/shard_map/reduce_scatter | solution.py:1552
  195.0 2.8 collective-permute-start.3
  196.0 3.8 copy-start.9
  196.0 3.8 copy-start.15
  196.0 100.6 %collective-permute-start.2 = (bf16[1,256,2048]{2,1,0:T(8,128)(2,1)}, bf16[1,256,2048]{2,1,0:T(8,128)(2,1)}, u32[]{:S(2)}, u32[]{:S(2)}) collective-permute-start(bf16[1,256,2048]{2,1,0:T(8,128)(2,1)} %bitcast.105), channel_id=1, source_target_pairs={{0,1},{1,0},{2,3},{3,2},{4,5},{5,4},{6,7},{7,6},{8,9},{9,8},{10,11... | collective-permute-start | bytes 3145736 | tf_op jit(solution)/shard_map/ppermute | solution.py:69
  199.7 3.7 copy-start.27
  203.4 2.3 copy-start.2
  296.4 2.5 copy-start.23
  296.5 2.5 copy-start.1
  296.5 2.5 copy-start.19
  296.5 2.8 copy-start.24
  296.5 2.8 copy-start.25
  296.5 3.1 collective-permute-start.6
  302.7 2.8 copy-start.20
  (9 other events, 12.1 us)
Sparse Core Ops, SparseCore 0:
  14.3 37.7 all-gather.4
  65.6 51.9 all-gather.6
  139.4 58.1 reduce-scatter.3
  199.8 63.5 reduce-scatter.5
  265.6 56.0 reduce-scatter.7

commit v4 on v3

--- a/solution.py
+++ b/solution.py
@@ -61,6 +61,10 @@
             [jnp.where(first, value, other), jnp.where(first, other, value)], axis
         )
     return lax.all_gather(value, "head", axis=axis, tiled=True)
+
+
+def swapped(value):
+    return lax.ppermute(value, "head", [(0, 1), (1, 0)])
 
 
 def sum_head(value):
@@ -191,73 +195,6 @@
             )
         )
     return copies
-
-
-def exchange_kernel(ways, kinds, *refs):
-    count = len(kinds)
-    sources, outs = refs[:count], refs[-6 - count : -6]
-    sends, receives = refs[-6:-4]
-    own = lax.axis_index("dp")
-    shared = kinds[-1][0] == "halves"
-    peers = [partner(own, by) for by in range(1, ways)]
-    halves = Halves(ways, sources[-1], outs[-1], *refs[-4:]) if shared else None
-    meet(halves.devices() if shared else [place("dp", peer) for peer in peers])
-    if shared:
-        halves.start()
-    copies = []
-    for index, (kind, source, out) in enumerate(zip(kinds, sources, outs)):
-        if kind[0] == "halves":
-            continue
-        for by in range(1, ways):
-            peer = peers[by - 1]
-            if kind[0] == "rows":
-                src = source.at[kind[1] : kind[2], peer]
-            else:
-                width = source.shape[1] // ways
-                src = source.at[:, pl.ds(pl.multiple_of(peer * width, width), width)]
-            copy = pltpu.make_async_remote_copy(
-                src_ref=src,
-                dst_ref=out.at[by - 1],
-                send_sem=sends.at[index * (ways - 1) + by - 1],
-                recv_sem=receives.at[index * (ways - 1) + by - 1],
-                device_id=place("dp", peer),
-                device_id_type=MESH,
-            )
-            copy.start()
-            copies.append(copy)
-    if shared:
-        halves.hand_on()
-    for copy in copies:
-        copy.wait()
-    if shared:
-        halves.finish()
-
-
-def plane_exchange(sources, kinds, tokens, number):
-    ways = lax.axis_size("dp")
-    shapes = []
-    for source, kind in zip(sources, kinds):
-        if kind[0] == "rows":
-            shape = (ways - 1, kind[2] - kind[1]) + source.shape[2:]
-        elif kind[0] == "columns":
-            shape = (ways - 1, source.shape[0], source.shape[1] // ways)
-        else:
-            shape = (ways - 1,) + source.shape
-        shapes.append(b16(*shape))
-    anywhere = pl.BlockSpec(memory_space=pl.ANY)
-    sems = pltpu.SemaphoreType.DMA((len(sources) * (ways - 1),))
-    hand_sems = pltpu.SemaphoreType.DMA((ways - 1,))
-    return pl.pallas_call(
-        functools.partial(exchange_kernel, ways, kinds),
-        out_shape=shapes,
-        in_specs=[anywhere] * (len(sources) + len(tokens)),
-        out_specs=[anywhere] * len(sources),
-        scratch_shapes=[sems] * 2 + [hand_sems] * 4,
-        compiler_params=pltpu.CompilerParams(
-            collective_id=number, has_side_effects=True, vmem_limit_bytes=VMEM
-        ),
-        cost_estimate=SHORT,
-    )(*sources, *tokens)
 
 
 def halves(a):
@@ -810,7 +747,7 @@
             state_copy(index).wait_send()
 
 
-def mixer_forward(pres, convs, logit, live, gain, per_step, spans, number):
+def mixer_forward(pres, convs, logit, logit_t, live, gain, per_step, spans, number):
     length, channels = pres[0].shape
     heads = channels // HEAD_DIM
     pairs = heads // per_step
@@ -875,7 +812,7 @@
             collective_id=number, has_side_effects=True, vmem_limit_bytes=VMEM
         ),
         cost_estimate=SHORT,
-    )(*pres, *convs, logit, logit.T, live, live.T, gain, *pres)
+    )(*pres, *convs, logit, logit_t, live, live.T, gain, *pres)
 
 
 def mixer_backward_kernel(per_step, taps, spans, ways, tokens, *refs):
@@ -883,17 +820,17 @@
     pres, weights = refs[6:9], refs[9:12]
     q_ref, k_ref, v_ref, wy, inv = refs[12:17]
     logit, live, state, ends, rims = refs[17:22]
-    head_source, residual, normed = refs[22 + tokens : 25 + tokens]
+    head_source, residual, up_source = refs[22 + tokens : 25 + tokens]
     d_q_out, d_k_out, d_v_out, conv_out, d_logit_out, gain_out = refs[25 + tokens : 31 + tokens]
-    head_others, res_others, one_others = refs[31 + tokens : 34 + tokens]
+    head_others, res_others, up_others = refs[31 + tokens : 34 + tokens]
     (
         d_mixed_all, d_fresh_all, d_end_all, arriving, sending, tails, rim_out, rim_in,
         ext, ext_back, sends, receives, rim_sends, rim_receives,
     ) = refs[34 + tokens : 48 + tokens]
-    col_sends, col_receives, *half_sems = refs[48 + tokens :]
-    halves = Halves(ways, residual, res_others, *half_sems[:4])
-    later = Halves(ways, normed, one_others, *half_sems[4:])
-    columns = column_copies(ways, head_source, head_others, col_sends, col_receives)
+    col_sends, col_receives, up_sends, up_receives, *half_sems = refs[48 + tokens :]
+    halves = Halves(ways, residual, res_others, *half_sems)
+    columns = row_copies(ways, (2, 3), up_source, up_others, up_sends, up_receives)
+    columns += column_copies(ways, head_source, head_others, col_sends, col_receives)
     step = pl.program_id(0)
     position = lax.axis_index("seq")
     pairs = arriving.shape[0]
@@ -927,10 +864,9 @@
             [place("seq", (position + last) % spans), place("seq", (position + 1) % spans)]
             + halves.devices()
         )
-        halves.start()
         for copy in columns:
             copy.start()
-        later.start()
+        halves.start()
         d_logit_out[...] = jnp.zeros_like(d_logit_out)
         gain_out[...] = jnp.zeros_like(gain_out)
 
@@ -1001,7 +937,6 @@
             rim_copy().start()
 
         halves.hand_on()
-        later.hand_on()
 
         @pl.when(position != last)
         def _():
@@ -1022,12 +957,11 @@
         for copy in columns:
             copy.wait()
         halves.finish()
-        later.finish()
 
 
 def mixer_backward(
     d_head, mixed, gain, pres, rims, convs, logit, live, q, k, v, wy, inv, state, ends, tokens,
-    head_out, residual, normed, per_step, spans, ways, number,
+    head_out, residual, turned, per_step, spans, ways, number,
 ):
     length, channels = pres[0].shape
     heads = channels // HEAD_DIM
@@ -1071,7 +1005,7 @@
         out_shape=[b16(length, channels)] * 3
         + [f32(3, taps, channels), f32(length, heads), f32(8, HEAD_DIM)]
         + [b16(ways - 1, length, channels // ways)]
-        + [b16(ways - 1, *residual.shape)] * 2,
+        + [b16(ways - 1, *residual.shape), b16(ways - 1, 1, *turned.shape[2:])],
         scratch_shapes=[
             pltpu.VMEM((heads, length, HEAD_DIM), jnp.float32),
             pltpu.VMEM((heads, length, HEAD_DIM), jnp.float32),
@@ -1088,14 +1022,14 @@
             pltpu.SemaphoreType.DMA((1,)),
             pltpu.SemaphoreType.DMA((1,)),
         ]
-        + [pltpu.SemaphoreType.DMA((ways - 1,))] * 10,
+        + [pltpu.SemaphoreType.DMA((ways - 1,))] * 8,
         compiler_params=pltpu.CompilerParams(
             collective_id=number, has_side_effects=True, vmem_limit_bytes=VMEM
         ),
         cost_estimate=SHORT,
     )(
         d_head, mixed, q, k, wy, gain, *pres, *convs, q, k, v, wy, inv, logit, live, state, ends,
-        rims, *tokens, head_out, residual, normed,
+        rims, *tokens, head_out, residual, turned,
     )
 
 
@@ -1154,8 +1088,8 @@
 
 def back_projection_kernel(ways, *refs):
     sources, d_logit, weights, beta_w = refs[:3], refs[3], refs[4:7], refs[7]
-    shared, out, others = refs[8:11], refs[11], refs[12:15]
-    sends, receives = refs[15:18], refs[18:21]
+    shared, out, others = refs[8:11], refs[-10], refs[-9:-6]
+    sends, receives = refs[-6:-3], refs[-3:]
     step = pl.program_id(0)
     copies = [
         copy
@@ -1181,7 +1115,7 @@
             copy.wait()
 
 
-def back_projection(sources, d_logit, weights, beta_weight, ways, number):
+def back_projection(sources, d_logit, weights, beta_weight, ways, tokens, number):
     length, channels = sources[0].shape
     width, heads = beta_weight.shape
     tile = width // 4
@@ -1193,7 +1127,7 @@
         + [pl.BlockSpec((length, heads), lambda n: (0, 0))]
         + [pl.BlockSpec((tile, channels), lambda n: (n, 0))] * 3
         + [pl.BlockSpec((tile, heads), lambda n: (n, 0))]
-        + [anywhere] * 3,
+        + [anywhere] * (3 + len(tokens)),
         out_specs=[pl.BlockSpec((length, tile), lambda n: (0, n))] + [anywhere] * 3,
         out_shape=[b16(length, width)] + [b16(ways - 1, length, channels // ways)] * 3,
         scratch_shapes=[pltpu.SemaphoreType.DMA((ways - 1,))] * 6,
@@ -1201,7 +1135,284 @@
             collective_id=number, has_side_effects=True, vmem_limit_bytes=VMEM
         ),
         cost_estimate=SHORT,
-    )(*sources, d_logit, *weights, beta_weight, *sources)
+    )(*sources, d_logit, *weights, beta_weight, *sources, *tokens)
+
+
+def project_kernel(tokens, both_gains, q_w, k_w, v_w, beta_w, *refs):
+    q_out, k_out, v_out, logit_out, logit_t_out, stream_out, normed_out, half_out, gains_out = refs[
+        :9
+    ]
+    arriving, gains, gains_in, sends, receives = refs[9:]
+    step = pl.program_id(0)
+    half = tokens.shape[1]
+
+    @pl.when(step == 0)
+    def _():
+        core = lax.axis_index("head")
+        other = place("head", 1 - core)
+        mine = pl.ds(pl.multiple_of(core * half, half), half)
+        theirs = pl.ds(pl.multiple_of((1 - core) * half, half), half)
+        row = lax.broadcasted_iota(jnp.int32, gains.shape, 0)
+        both = both_gains[...].astype(jnp.float32)
+        gains[...] = jnp.where(row == 0, both[0:1], both[1:2]).astype(jnp.bfloat16)
+        meet([other])
+        copies = [
+            pltpu.make_async_remote_copy(
+                src_ref=source, dst_ref=target, send_sem=sends.at[index],
+                recv_sem=receives.at[index], device_id=other, device_id_type=MESH,
+            )
+            for index, (source, target) in enumerate(((tokens, arriving), (gains, gains_in)))
+        ]
+        for copy in copies:
+            copy.start()
+        stream_out[:, mine] = tokens[...]
+        gains_out[:, mine] = gains[...]
+        for copy in copies:
+            copy.wait()
+        stream_out[:, theirs] = arriving[...]
+        gains_out[:, theirs] = gains_in[...]
+        stream = stream_out[...].astype(jnp.float32)
+        scale = lax.rsqrt(jnp.mean(stream * stream, axis=-1, keepdims=True) + EPSILON)
+        gain = gains_out[...].astype(jnp.float32)[0:1]
+        normed_out[...] = (stream * scale * gain).astype(jnp.bfloat16)
+        half_out[...] = normed_out[:, mine]
+        logit_out[...] = dot_low(normed_out[...], beta_w[...], (1, 1))
+        logit_t_out[...] = dot_low(beta_w[...], normed_out[...], (1, 1))
+
+    for part, (weight, out) in enumerate(((q_w, q_out), (k_w, k_out), (v_w, v_out))):
+
+        @pl.when(step // 2 == part)
+        def _():
+            out[...] = dot_low(normed_out[...], weight[...]).astype(jnp.bfloat16)
+
+
+def projected(tokens, first_gain, second_gain, weights, beta_weight, number):
+    length, half = tokens.shape
+    width, channels = weights[0].shape
+    heads = beta_weight.shape[1]
+    tile = channels // 2
+
+    def whole(*shape):
+        return pl.BlockSpec(shape, lambda s: (0,) * len(shape))
+
+    def tiles(rows, part):
+        return pl.BlockSpec((rows, tile), lambda s: (0, jnp.clip(s - 2 * part, 0, 1)))
+
+    return pl.pallas_call(
+        project_kernel,
+        grid=(6,),
+        in_specs=[whole(length, half), whole(2, half)]
+        + [tiles(width, part) for part in range(3)]
+        + [whole(heads, width)],
+        out_specs=[tiles(length, part) for part in range(3)]
+        + [whole(length, heads), whole(heads, length), whole(length, width)]
+        + [whole(length, width), whole(length, half), whole(16, width)],
+        out_shape=[b16(length, channels)] * 3
+        + [f32(length, heads), f32(heads, length), b16(length, width)]
+        + [b16(length, width), b16(length, half), b16(16, width)],
+        scratch_shapes=[
+            pltpu.VMEM((length, half), jnp.bfloat16),
+            pltpu.VMEM((16, half), jnp.bfloat16),
+            pltpu.VMEM((16, half), jnp.bfloat16),
+            pltpu.SemaphoreType.DMA((2,)),
+            pltpu.SemaphoreType.DMA((2,)),
+        ],
+        compiler_params=pltpu.CompilerParams(
+            collective_id=number, has_side_effects=True, vmem_limit_bytes=VMEM
+        ),
+        cost_estimate=SHORT,
+    )(tokens, jnp.stack([first_gain, second_gain]), *weights, beta_weight.T)
+
+
+def units_kernel(
+    head_ref, out_w, stream_ref, gains, d_ref, live, gate_w, up_w, down_w, token,
+    turned_out, d_gate_out, d_up_out, hidden_out, stream_out, normed_out,
+    part_low, arriving, sends, receives,
+):
+    @pl.when(pl.program_id(0) == 0)
+    def _():
+        other = place("head", 1 - lax.axis_index("head"))
+        meet([other])
+        pieces = part_low.shape[0]
+        width = part_low.shape[2]
+        copies = []
+        for piece in range(pieces):
+            span = slice(piece * width, (piece + 1) * width)
+            part_low[piece] = dot_low(head_ref[...], out_w[:, span]).astype(jnp.bfloat16)
+            copy = pltpu.make_async_remote_copy(
+                src_ref=part_low.at[piece], dst_ref=arriving.at[piece],
+                send_sem=sends.at[piece], recv_sem=receives.at[piece],
+                device_id=other, device_id_type=MESH,
+            )
+            copy.start()
+            copies.append(copy)
+        squares = 0.0
+        for piece, copy in enumerate(copies):
+            span = slice(piece * width, (piece + 1) * width)
+            copy.wait()
+            both = part_low[piece].astype(jnp.float32) + arriving[piece].astype(jnp.float32)
+            stream = stream_ref[:, span].astype(jnp.float32) + both
+            stream_out[:, span] = stream
+            squares = squares + jnp.sum(stream * stream, axis=-1, keepdims=True)
+        scale = lax.rsqrt(squares / (pieces * width) + EPSILON)
+        gain = gains[...].astype(jnp.float32)[1:2]
+        normed_out[...] = (stream_out[...] * scale * gain).astype(jnp.bfloat16)
+
+    x = normed_out[...]
+    gate = dot_low(x, gate_w[...])
+    up = dot_low(x, up_w[...])
+    d_hidden = dot_low(d_ref[...], down_w[...], (1, 1))
+    sig = jax.nn.sigmoid(gate)
+    hidden = (gate * sig * up).astype(jnp.bfloat16)
+    d_gate = (d_hidden * up * sig * (1.0 + gate * (1.0 - sig))).astype(jnp.bfloat16)
+    d_up = (d_hidden * gate * sig).astype(jnp.bfloat16)
+    for index, (part, out) in enumerate(
+        ((hidden, hidden_out), (d_gate, d_gate_out), (d_up, d_up_out))
+    ):
+        out[...] = part
+        if index == 0:
+            part = (part.astype(jnp.float32) * live[...]).astype(jnp.bfloat16)
+        turned_out[index] = part.T
+
+
+def hidden_units(
+    head_out, out_weight, stream, gains, d_out, live, gate_weight, up_weight, down_weight, token,
+    number,
+):
+    length, width = stream.shape
+    channels = head_out.shape[1]
+    units = gate_weight.shape[1]
+    tile = 256
+    whole = pl.BlockSpec((length, width), lambda f: (0, 0))
+    column = pl.BlockSpec((width, tile), lambda f: (0, f))
+    flat = pl.BlockSpec((length, tile), lambda f: (0, f))
+    return pl.pallas_call(
+        units_kernel,
+        grid=(units // tile,),
+        in_specs=[
+            pl.BlockSpec((length, channels), lambda f: (0, 0)),
+            pl.BlockSpec((channels, width), lambda f: (0, 0)),
+            whole,
+            pl.BlockSpec((16, width), lambda f: (0, 0)),
+            whole,
+            pl.BlockSpec((length, 1), lambda f: (0, 0)),
+            column,
+            column,
+        ]
+        + [pl.BlockSpec((tile, width), lambda f: (f, 0)), pl.BlockSpec(memory_space=pl.ANY)],
+        out_specs=[pl.BlockSpec((3, tile, length), lambda f: (0, f, 0))] + [flat] * 3 + [whole] * 2,
+        out_shape=[b16(3, units, length)]
+        + [b16(length, units)] * 3
+        + [f32(length, width), b16(length, width)],
+        scratch_shapes=[pltpu.VMEM((4, length, width // 4), jnp.bfloat16)] * 2
+        + [pltpu.SemaphoreType.DMA((4,))] * 2,
+        compiler_params=pltpu.CompilerParams(
+            collective_id=number, has_side_effects=True, vmem_limit_bytes=VMEM
+        ),
+        cost_estimate=SHORT,
+    )(
+        head_out, out_weight, stream, gains, d_out, live, gate_weight, up_weight, down_weight,
+        token,
+    )
+
+
+def row_copies(ways, entries, source, out, sends, receives):
+    own = lax.axis_index("dp")
+    copies = []
+    for by in range(1, ways):
+        peer = partner(own, by)
+        copies.append(
+            pltpu.make_async_remote_copy(
+                src_ref=source.at[entries[0] : entries[1], peer],
+                dst_ref=out.at[by - 1],
+                send_sem=sends.at[by - 1],
+                recv_sem=receives.at[by - 1],
+                device_id=place("dp", peer),
+                device_id_type=MESH,
+            )
+        )
+    return copies
+
+
+def rows_kernel(ways, entries, source, *refs):
+    out, sends, receives = refs[-3:]
+    own = lax.axis_index("dp")
+    meet([place("dp", partner(own, by)) for by in range(1, ways)])
+    copies = row_copies(ways, entries, source, out, sends, receives)
+    for copy in copies:
+        copy.start()
+    for copy in copies:
+        copy.wait()
+
+
+def exchanged_rows(source, entries, tokens, number):
+    ways = lax.axis_size("dp")
+    anywhere = pl.BlockSpec(memory_space=pl.ANY)
+    return pl.pallas_call(
+        functools.partial(rows_kernel, ways, entries),
+        out_shape=b16(ways - 1, entries[1] - entries[0], *source.shape[2:]),
+        in_specs=[anywhere] * (1 + len(tokens)),
+        out_specs=anywhere,
+        scratch_shapes=[pltpu.SemaphoreType.DMA((ways - 1,))] * 2,
+        compiler_params=pltpu.CompilerParams(
+            collective_id=number, has_side_effects=True, vmem_limit_bytes=VMEM
+        ),
+        cost_estimate=SHORT,
+    )(source, *tokens)
+
+
+def feed_back_kernel(ways, entries, *refs):
+    d_gate, d_up, hidden, gate_w, up_w, down_w, source, normed = refs[:8]
+    d_x_out, feed_out, others, normed_others, sends, receives, *half_sems = refs[-10:]
+    halves = Halves(ways, normed, normed_others, *half_sems)
+    copies = row_copies(ways, entries, source, others, sends, receives)
+
+    @pl.when(pl.program_id(0) == 0)
+    def _():
+        meet(halves.devices())
+        halves.start()
+        for copy in copies:
+            copy.start()
+
+    d_x = dot_low(d_gate[...], gate_w[...], (1, 1)) + dot_low(d_up[...], up_w[...], (1, 1))
+    d_x_out[...] = d_x.astype(jnp.bfloat16)
+    feed_out[...] = dot_low(hidden[...], down_w[...]).astype(jnp.bfloat16)
+
+    @pl.when(pl.program_id(0) == pl.num_programs(0) - 1)
+    def _():
+        halves.hand_on()
+        for copy in copies:
+            copy.wait()
+        halves.finish()
+
+
+def feed_back(d_gate, d_up, hidden, weights, source, entries, normed, tokens, number):
+    ways = lax.axis_size("dp")
+    length, units = hidden.shape
+    width = normed.shape[1]
+    tile = width // 8
+    anywhere = pl.BlockSpec(memory_space=pl.ANY)
+    whole = pl.BlockSpec((length, units), lambda n: (0, 0))
+    row = pl.BlockSpec((tile, units), lambda n: (n, 0))
+    out = pl.BlockSpec((length, tile), lambda n: (0, n))
+    return pl.pallas_call(
+        functools.partial(feed_back_kernel, ways, entries),
+        grid=(8,),
+        in_specs=[whole] * 3
+        + [row, row, pl.BlockSpec((units, tile), lambda n: (0, n))]
+        + [anywhere] * (2 + len(tokens)),
+        out_specs=[out, out, anywhere, anywhere],
+        out_shape=[b16(length, width)] * 2
+        + [
+            b16(ways - 1, entries[1] - entries[0], *source.shape[2:]),
+            b16(ways - 1, length, width),
+        ],
+        scratch_shapes=[pltpu.SemaphoreType.DMA((ways - 1,))] * 6,
+        compiler_params=pltpu.CompilerParams(
+            collective_id=number, has_side_effects=True, vmem_limit_bytes=VMEM
+        ),
+        cost_estimate=SHORT,
+    )(d_gate, d_up, hidden, *weights, source, normed, *tokens)
 
 
 def pieces_kernel(groups, slots, ways, turned, at, *refs):
@@ -1241,10 +1452,12 @@
     def left_block(block, at_place):
         return pl.BlockSpec(block, lambda s, at: at_place(at[0]))
 
-    def right_block(block, at_place, way):
+    def right_block(block, at_place, column):
         return pl.BlockSpec(
-            block + (rows,), lambda s, at: tuple(at_place(at[0])) + (way * spans + s,)
-        )
+            block + (rows,), lambda s, at: tuple(at_place(at[0])) + (column(s),)
+        )
+
+    rights = [right for slot in rights for right in slot]
 
     return pl.pallas_call(
         functools.partial(pieces_kernel, groups, slots, ways, turned),
@@ -1252,7 +1465,7 @@
             num_scalar_prefetch=1,
             grid=(spans,),
             in_specs=[left_block(block, where) for _, block, where in lefts]
-            + [right_block(block, where, way) for _, block, where in rights for way in range(ways)]
+            + [right_block(block, where, column) for _, block, where, column in rights]
             + [pl.BlockSpec(memory_space=pl.ANY)] * len(tokens),
             out_specs=pl.BlockSpec((1, count, ways * rows), lambda s, at: (s, 0, 0)),
             scratch_shapes=[
@@ -1266,30 +1479,52 @@
     )(
         lax.axis_index("dp")[None],
         *[array for array, _, _ in lefts],
-        *[array for array, _, _ in rights for _ in range(ways)],
+        *[array for array, _, _, _ in rights],
         *tokens,
     )
 
 
-def widen_kernel(count, turned, *refs):
+def widen_kernel(count, turned, starts, share_of, *refs):
+    small = refs[count]
+    outs = refs[count + 1 :]
     for index in range(count):
         whole = refs[index][...].astype(jnp.float32)
-        refs[count + index][...] = whole.T if turned[index] else whole
-
-
-def widened(arrays, turned):
+        outs[index][...] = whole.T if turned[index] else whole
+    gain, first, second, taps, beta = outs[count], *outs[count + 1 : count + 3], outs[count + 3 : -1], outs[-1]
+    gain[...] = small[starts[0] : starts[0] + 1, :]
+    first[...] = small[starts[1] : starts[1] + first.shape[0], :]
+    second[...] = small[starts[2] : starts[2] + second.shape[0], :]
+    row = starts[3]
+    for out in taps:
+        high, wide = out.shape
+        for tap in range(high):
+            for lane in range(wide // 128):
+                out[tap : tap + 1, lane * 128 : (lane + 1) * 128] = small[row : row + 1, :]
+                row += 1
+    heads = beta.shape[1]
+    width = share_of[1] // 128
+    share = lax.axis_index("dp") * share_of[0] + lax.axis_index("seq")
+    rows = [small[pl.ds(starts[4] + head * width + share, 1), :] for head in range(heads)]
+    beta[...] = jnp.concatenate(rows, 0).T
+
+
+def widened(arrays, turned, small, starts, channels, taps, heads, width):
     inside = pl.BlockSpec(memory_space=pltpu.VMEM)
     shapes = [
         f32(*(array.shape[::-1] if turn else array.shape)) for array, turn in zip(arrays, turned)
     ]
+    shapes += [f32(1, 128), f32(width // 256, 128), f32(width // 256, 128)]
+    shapes += [f32(taps, channels)] * 3 + [f32(128, heads)]
     return pl.pallas_call(
-        functools.partial(widen_kernel, len(arrays), turned),
+        functools.partial(
+            widen_kernel, len(arrays), turned, starts, (lax.axis_size("seq"), width)
+        ),
         out_shape=shapes,
-        in_specs=[inside] * len(arrays),
-        out_specs=[inside] * len(arrays),
+        in_specs=[inside] * (len(arrays) + 1),
+        out_specs=[inside] * len(shapes),
         compiler_params=pltpu.CompilerParams(vmem_limit_bytes=VMEM),
         cost_estimate=SHORT,
-    )(*arrays)
+    )(*arrays, small)
 
 
 def doublings(size):
@@ -1304,6 +1539,7 @@
     sends, receives, owner_sends, owner_receives, own_sems = refs[:5]
     small_in, small_sent, small_sends, small_receives = refs[5:]
     own = lax.axis_index("dp")
+    core = lax.axis_index("head")
     position = lax.axis_index("seq")
     last = spans - 1
     rounds = spans - 1
@@ -1331,13 +1567,19 @@
 
     def owner_copies(index, source):
         high = source.shape[0]
+        turn = core * (ways // 2) if index == 0 or index > fed else 0
+
+        def block_of(peer):
+            start = ((peer + turn) % ways) * rows
+            return source.at[:, pl.ds(pl.multiple_of(start, rows), rows)]
+
         stage = stages[index]
         mine = stage.at[pl.ds(pl.multiple_of(own * high, high), high), :]
         copies = []
         for by, peer in enumerate(peers):
             copies.append(
                 pltpu.make_async_remote_copy(
-                    src_ref=source.at[:, pl.ds(pl.multiple_of(peer * rows, rows), rows)],
+                    src_ref=block_of(peer),
                     dst_ref=mine,
                     send_sem=owner_sends.at[index * (ways - 1) + by],
                     recv_sem=owner_receives.at[index * (ways - 1) + by],
@@ -1345,9 +1587,7 @@
                     device_id_type=MESH,
                 )
             )
-        here = pltpu.make_async_copy(
-            source.at[:, pl.ds(pl.multiple_of(own * rows, rows), rows)], mine, own_sems.at[index]
-        )
+        here = pltpu.make_async_copy(block_of(own), mine, own_sems.at[index])
         return copies + [here]
 
     partners = [place("dp", partner(own, by)) for by in doublings(ways)]
@@ -1413,6 +1653,23 @@
             for index in range(2, groups + 2):
                 source_send(way, index)
 
+    at_end = (position == 0) | (position == last)
+
+    def finish(group):
+        for way in range(2):
+
+            @pl.when(along[way] >= 1)
+            def _():
+                line_copy(way, rounds - 1, group, totals.at[group]).wait_recv()
+
+        total = raw_at(group, position)[...].astype(jnp.float32)
+        for way in range(2):
+            arrived = received[way, rounds - 1, group].astype(jnp.float32)
+            total = total + jnp.where(along[way] >= 1, arrived, 0.0)
+        totals[group] = total.astype(jnp.bfloat16)
+        for copy in owner_copies(fed + group, totals.at[group]):
+            copy.start()
+
     for turn in range(1, rounds):
         for group in range(groups):
             for way in range(2):
@@ -1432,25 +1689,21 @@
                     handed[way, turn - 1, group] = term.astype(jnp.bfloat16)
                     line_copy(way, turn, group, handed.at[way, turn - 1, group]).start()
 
+            if turn == rounds - 1:
+
+                @pl.when(at_end)
+                def _():
+                    finish(group)
+
         small_turn(turn)
 
     for turn in range(rounds, len(partners) + 1):
         small_turn(turn)
 
-    for group in range(groups):
-        for way in range(2):
-
-            @pl.when(along[way] >= 1)
-            def _():
-                line_copy(way, rounds - 1, group, totals.at[group]).wait_recv()
-
-        total = raw_at(group, position)[...].astype(jnp.float32)
-        for way in range(2):
-            arrived = received[way, rounds - 1, group].astype(jnp.float32)
-            total = total + jnp.where(along[way] >= 1, arrived, 0.0)
-        totals[group] = total.astype(jnp.bfloat16)
-        for copy in owner_copies(fed + group, totals.at[group]):
-            copy.start()
+    @pl.when(jnp.logical_not(at_end))
+    def _():
+        for group in range(groups):
+            finish(group)
 
     sources = list(pieces) + [totals.at[group] for group in range(groups)]
     for index, source in enumerate(sources):
@@ -1537,16 +1790,33 @@
     spans = lax.axis_size("seq")
     positions = lax.axis_index("seq") * local_len + jnp.arange(local_len, dtype=jnp.int32)
     live_mask = (positions[None, :] < lengths[:, None]).astype(jnp.float32)
-    masked_up = upstream * live_mask[..., None].astype(jnp.bfloat16)
-    gains = jnp.stack([first_gain, second_gain] + [first_gain] * 14)
-    everything = gather_head(jnp.concatenate([tokens_in[0], masked_up[0], gains], 0), 1)
-    gathered = everything[None, :local_len]
-    upstream_full = everything[None, local_len : 2 * local_len]
-    gain_one = everything[2 * local_len].astype(jnp.float32)
-    gain_two = everything[2 * local_len + 1].astype(jnp.float32)
-    stream_full = gathered.astype(jnp.float32)
-    scale_one = inverse_rms(stream_full)
-    normed_one = (stream_full * scale_one * gain_one).astype(jnp.bfloat16)
+    live_low = live_mask[..., None].astype(jnp.bfloat16)
+    fused = groups == 2
+    weights = [query_weight, key_weight, value_weight]
+    if fused:
+        *pres, beta_logit, logit_turned, gathered, normed_one, normed_half, gains = projected(
+            tokens_in[0], first_gain, second_gain, weights, beta_weight, 7
+        )
+        upstream_full = gather_head(upstream, 2) * live_low
+        half_up = lax.all_gather(upstream[0], "dp", axis=0, tiled=True)
+        half_one = lax.all_gather(normed_half, "dp", axis=0, tiled=True)
+    else:
+        gains = jnp.stack([first_gain, second_gain] + [first_gain] * 14)
+        masked_up = upstream[0] * live_low[0]
+        everything = gather_head(jnp.concatenate([tokens_in[0], masked_up, gains], 0), 1)
+        gathered = everything[:local_len]
+        upstream_full = everything[None, local_len : 2 * local_len]
+        gains = everything[2 * local_len :]
+        scale_one = inverse_rms(gathered.astype(jnp.float32))
+        normed_one = (
+            gathered.astype(jnp.float32) * scale_one * gains[0].astype(jnp.float32)
+        ).astype(jnp.bfloat16)
+        pres = [
+            jnp.dot(normed_one, weight, preferred_element_type=jnp.float32).astype(jnp.bfloat16)
+            for weight in weights
+        ]
+        beta_logit = jnp.dot(normed_one, beta_weight, preferred_element_type=jnp.float32)
+        tokens_up = jnp.stack(spread(upstream_full[0], "dp")[1:])
 
     def scattered(pieces):
         return lax.psum_scatter(pieces, "seq", scatter_dimension=0, tiled=False)
@@ -1556,25 +1826,20 @@
         blocks = piece.reshape(c, ways, -1).transpose(1, 0, 2)
         return jnp.stack(in_order(exchanged(blocks, "dp"), "dp"), 0)
 
-    fused = groups == 2
-    if fused:
-        half_up = lax.all_gather(masked_up[0], "dp", axis=0, tiled=True)
-        tokens_up = gather_head(half_up, 1)
-    else:
-        tokens_up = jnp.stack(spread(upstream_full[0], "dp")[1:])
     per_step = 2 if local_heads % 2 == 0 else 1
-    pres = [
-        jnp.dot(normed_one[0], weight, preferred_element_type=jnp.float32).astype(jnp.bfloat16)
-        for weight in (query_weight, key_weight, value_weight)
-    ]
-    beta_logit = jnp.dot(normed_one[0], beta_weight, preferred_element_type=jnp.float32)
+    gain_one, gain_two = gains[0].astype(jnp.float32), gains[1].astype(jnp.float32)
+    stream_full = gathered[None].astype(jnp.float32)
+    scale_one = inverse_rms(stream_full)
+    normed_one = normed_one[None]
     convs = [query_conv, key_conv, value_conv]
     live_col = live_mask[0][:, None]
     head_gain = mixer_gain.astype(jnp.float32)[None, :]
     if fused:
         (
             query, key, value, wy, inverse, ends, mixed, head_out, entering, rims,
-        ) = mixer_forward(pres, convs, beta_logit, live_col, head_gain, per_step, spans, 1)
+        ) = mixer_forward(
+            pres, convs, beta_logit, logit_turned, live_col, head_gain, per_step, spans, 1
+        )
     else:
         rims = passed_along(jnp.stack([pre[local_len - RIM :, :] for pre in pres]), "seq", 1)
         rims = [rims[0], rims[1], rims[2]]
@@ -1584,19 +1849,21 @@
         entering = chain_state(ends[:, :, :HEAD_DIM], ends[:, :, HEAD_DIM:], False)
         mixed, head_out = mixer_finish(mix, entering, head_gain, per_step)
     head_out = head_out[None]
-    mixer_part = jnp.dot(head_out, output_weight, preferred_element_type=jnp.float32)
-    stream_mid = stream_full + sum_head(mixer_part)
+    if fused:
+        turned, d_gate, d_up, hidden, stream_mid, normed_two = hidden_units(
+            head_out[0], output_weight, gathered, gains, upstream_full[0], live_col,
+            gate_weight, up_weight, down_weight, half_up, 8,
+        )
+        half_up, hidden = lax.optimization_barrier((half_up, hidden))
+        stream_mid, normed_two = stream_mid[None], normed_two[None]
+    else:
+        mixer_part = jnp.dot(head_out, output_weight, preferred_element_type=jnp.float32)
+        stream_mid = stream_full + sum_head(mixer_part)
+        normed_two = (stream_mid * inverse_rms(stream_mid) * gain_two).astype(jnp.bfloat16)
+        feed_part, d_two_part, turned = feed_forward(
+            normed_two[0], upstream_full[0], gate_weight, up_weight, down_weight, normed_two
+        )
     scale_two = inverse_rms(stream_mid)
-    normed_two = (stream_mid * scale_two * gain_two).astype(jnp.bfloat16)
-    if fused:
-        half_two = lax.all_gather(
-            own_half(normed_two[0], local_width), "dp", axis=0, tiled=True
-        )
-    feed_part, d_two_part, turned = feed_forward(
-        normed_two[0], upstream_full[0], gate_weight, up_weight, down_weight,
-        half_up if fused else normed_two,
-    )
-    layer_out = own_half(stream_mid + sum_head(feed_part[None]), local_width).astype(jnp.bfloat16)
     units = turned.shape[1] // ways
     turned = turned.reshape(3, ways, units, local_len)
 
@@ -1606,12 +1873,28 @@
         )
 
     def slots_of(own, others):
-        return [(own, (local_len,), lambda at: (0,))] + [
+        slots = [(own, (local_len,), lambda at: (0,))] + [
             (others, (1, local_len), lambda at, by=by: (by, 0)) for by in range(ways - 1)
         ]
-
-    def by_position(array):
-        return [(array, (local_len,), lambda at, by=by: (at ^ by,)) for by in range(ways)]
+        return [
+            [slot + ((lambda s, way=way: way * spans + s),) for way in range(ways)]
+            for slot in slots
+        ]
+
+    def halves_of(same, other):
+        half = ways // 2
+        return [
+            [
+                (
+                    same if way < half else other,
+                    (local_len,),
+                    lambda at, by=by: (at ^ by,),
+                    lambda s, way=way: (way % half) * spans + s,
+                )
+                for way in range(ways)
+            ]
+            for by in range(ways)
+        ]
 
     def feed_slots(which, others, index):
         own = [(turned, (1, 1, units, local_len), lambda at: (which, at, 0, 0))]
@@ -1622,12 +1905,15 @@
 
     normed_full = normed_two[0]
     if fused:
-        (hidden_others,) = plane_exchange([turned], [("rows", 0, 1)], [], 2)
+        hidden_others = exchanged_rows(turned, (0, 1), [half_one], 2)
         down_raw = raw_piece(
-            [feed_slots(0, hidden_others, 0)], units, by_position(tokens_up), True
-        )
-        (d_others,) = plane_exchange([turned], [("rows", 1, 3)], [down_raw], 3)
-        two_slots = by_position(gather_head(half_two, 1))
+            [feed_slots(0, hidden_others, 0)], units, halves_of(half_up, swapped(half_up)), True
+        )
+        d_two_part, feed_part, d_others, two_others = feed_back(
+            d_gate, d_up, hidden, [gate_weight, up_weight, down_weight], turned, (1, 2),
+            normed_full, [down_raw], 3,
+        )
+        two_slots = slots_of(normed_full, two_others)
     else:
         hidden_others = jnp.stack(exchanged(turned[:1].transpose(1, 0, 2, 3), "dp")[1:])
         down_raw = raw_piece(
@@ -1638,8 +1924,7 @@
     down_piece = scattered(down_raw)
     gate_raw = raw_piece([feed_slots(1, d_others, 0)], units, two_slots, True)
     gate_piece = scattered(gate_raw)
-    up_raw = raw_piece([feed_slots(2, d_others, 1)], units, two_slots, True, [gate_raw])
-    up_piece = scattered(up_raw)
+    layer_out = own_half(stream_mid + sum_head(feed_part[None]), local_width).astype(jnp.bfloat16)
     d_two = sum_head(d_two_part[None])
     d_stream = (
         upstream_full.astype(jnp.float32)
@@ -1658,11 +1943,11 @@
     if fused:
         (
             *mix_sources, grad_kernels, d_beta_logit, grad_gain_part, out_others, res_others,
-            one_others,
+            up_others,
         ) = mixer_backward(
             d_head_out[0], mixed, head_gain, pres, rims, convs, beta_logit, live_col,
-            query, key, value, wy, inverse, entering, ends, [up_raw, down_piece],
-            head_out[0], residual_full[0], normed_one[0], per_step, spans, ways, 4,
+            query, key, value, wy, inverse, entering, ends, [gate_raw, down_piece],
+            head_out[0], residual_full[0], turned, per_step, spans, ways, 4,
         )
     else:
         d_mixed, d_fresh, d_ends, grad_gain_part = mixer_back_local(
@@ -1678,12 +1963,17 @@
             jnp.concatenate([part[: local_len - 8], tail], 0) for part, tail in zip(d_pres, tails)
         ]
     grad_gain_part = grad_gain_part[0]
+    if fused:
+        up_raw = raw_piece([feed_slots(2, up_others, 0)], units, two_slots, True)
+    else:
+        up_raw = raw_piece([feed_slots(2, d_others, 1)], units, two_slots, True)
+    up_piece = scattered(up_raw)
     share_width = channels // ways
     residual = residual_full[0]
     if fused:
         d_one_part, *mix_others = back_projection(
             mix_sources, d_beta_logit.astype(jnp.bfloat16),
-            [query_weight, key_weight, value_weight], beta_weight, ways, 5,
+            weights, beta_weight, ways, [up_raw], 5,
         )
     else:
         *mix_others, out_others = [
@@ -1706,7 +1996,7 @@
         ]
 
     if fused:
-        one_slots = slots_of(normed_one[0], one_others)
+        one_slots = halves_of(half_one, swapped(half_one))
     else:
         one_slots = slots_of(normed_one[0], jnp.stack(spread(normed_one[0], "dp")[1:]))
     out_raw = raw_piece(
@@ -1747,29 +2037,31 @@
         for part, size in zip(parts, sizes)
     ]
     small = jnp.concatenate(shares, 0)
+    starts = [0]
+    for part in shares:
+        starts.append(starts[-1] + part.shape[0])
+    share = lax.axis_index("dp") * spans + lax.axis_index("seq")
+    rows = full_width // (ways * spans)
     if fused:
         *finished, small = finished_gradients(
             out_raw, mix_raw, [down_piece, gate_piece, up_piece], small, 6
         )
-        down, gate, up, out, *mix = widened(
-            finished, [False, True, True, False, True, True, True]
-        )
-        gain_total = small[0]
+        results = widened(
+            finished, [False, True, True, False, True, True, True],
+            small, starts, channels, query_conv.shape[0], local_heads, full_width,
+        )
+        down, gate, up, out, *mix = results[:7]
+        gain_total, grad_first, grad_second = [part.reshape(-1) for part in results[7:10]]
+        kernel_sum, grad_beta = results[10:13], results[13]
     else:
         small = sum_doubling(small, ("dp", "seq"))
         gain_total = sum_doubling(small[0], ("head",))
-    starts = [0]
-    for part in shares:
-        starts.append(starts[-1] + part.shape[0])
-    totals = [
-        small[start : start + size // lane].reshape(part.shape)
-        for start, size, part in zip(starts, sizes, parts)
-    ]
-    grad_first, grad_second, kernel_sum, beta_sum = totals[1:]
-    share = lax.axis_index("dp") * spans + lax.axis_index("seq")
-    rows = full_width // (ways * spans)
-    grad_beta = lax.dynamic_slice_in_dim(beta_sum, share * rows, rows, 1).T
-    if not fused:
+        totals = [
+            small[start : start + size // lane].reshape(part.shape)
+            for start, size, part in zip(starts, sizes, parts)
+        ]
+        grad_first, grad_second, kernel_sum, beta_sum = totals[1:]
+        grad_beta = lax.dynamic_slice_in_dim(beta_sum, share * rows, rows, 1).T
         feed = to_owner(jnp.concatenate([down_piece, gate_piece, up_piece], 0))
         down, gate, up = [
             feed[:, place * units : (place + 1) * units].reshape(-1, rows).astype(jnp.float32)

time: 440 us -> 413 us (0.939)
  the two profiles are of different devices: /device:TPU:0 before, /device:TPU:9 now
where the time goes in v4:
time: 413 us; the launch traced here: 412 us
  Pallas kernels  359 us (87%)
  other arithmetic  15.2 us (4%)
  between operations  14.9 us (4%)
  local copies, waits for them, and re-layouts  9.04 us (2%)
  waiting for transfers between devices  6 us (1%)
  starting transfers between devices  4.19 us (1%)
    pallas_call x1, Pallas kernels, finished_gradients(): pl.pallas_call(functools.partial(finish_kernel, spans, ways, fed), out_sh...  96.9 us
    pallas_call x1, Pallas kernels, mixer_backward(): pl.pallas_call(functools.partial(mixer_backward_kernel, per_step, taps, s...  56.8 us
    pallas_call x1, Pallas kernels, feed_back(): pl.pallas_call(functools.partial(feed_back_kernel, ways, entries), grid=(...  46.7 us
    pallas_call x5, Pallas kernels, span_pieces(): pl.pallas_call(functools.partial(pieces_kernel, groups, slots, ways, turn...  37.5 us
    pallas_call x1, Pallas kernels, hidden_units(): pl.pallas_call(units_kernel, grid=(units // tile,), in_specs=[pl.BlockSpe...  29.8 us
    pallas_call x1, Pallas kernels, mixer_forward(): pl.pallas_call(functools.partial(mixer_forward_kernel, per_step, taps, sp...  28.7 us
    pallas_call x1, Pallas kernels, back_projection(): pl.pallas_call(functools.partial(back_projection_kernel, ways), grid=(wid...  24.1 us
    pallas_call x1, Pallas kernels, exchanged_rows(): pl.pallas_call(functools.partial(rows_kernel, ways, entries), out_shape=b...  19.1 us
  transfers between devices with their start and end apart: 11, of which 2 were waited for; matrix products, arithmetic and copies ran while one was open for 5% of the time, Pallas kernels for 60%

profile of v4, /device:TPU:9, one launch (start us, length us, event | category | flops | bytes accessed | tf_op | source)
XLA Modules:
  0.0 412.1 jit_solution(5575745955403031737)
XLA Ops:
  10.7 14.6 %shard_map.288 = (bf16[256,1024]{1,0:T(8,128)(2,1)}, bf16[256,1024]{1,0:T(8,128)(2,1)}, bf16[256,1024]{1,0:T(8,128)(2,1)}, f32[256,8]{1,0:T(8,128)}, f32[8,256]{...) custom-call(bf16[256,1024]{1,0:T(8,128)(2,1)} %bitcast.90, ...), custom_call_target="tpu_custom_call" | custom-call | tf_op jit(solution)/shard_map/pallas_call | solution.py:1201
  27.8 28.7 %shard_map.289 = (bf16[256,1024]{1,0:T(8,128)(2,1)}, bf16[256,1024]{1,0:T(8,128)(2,1)}, bf16[256,1024]{1,0:T(8,128)(2,1)}, f32[8,256,256]{2,1,0:T(8,128)}, f32[8...) custom-call(bf16[256,1024]{1,0:T(8,128)(2,1)} %get-tuple-element.82., ...), custom_call_target="tpu_custom_call" | custom-call | tf_op jit(solution)/shard_map/pallas_call | solution.py:772
  56.6 0.8 copy-done.5
  57.6 1.2 maximum_multiply_fusion.d_ref
  58.8 29.8 %shard_map.290 = (bf16[3,2816,256]{2,1,0:T(8,128)(2,1)}, bf16[256,2816]{1,0:T(8,128)(2,1)}, bf16[256,2816]{1,0:T(8,128)(2,1)}, bf16[256,2816]{1,0:T(8,128)(2,1)}...) custom-call(bf16[256,1024]{1,0:T(8,128)(2,1)} %get-tuple-element.87.head_ref.refs_24_.refs_0_, bf16[1024,2048]{1,0:T(8,128)(2,1)} %out_w.1, ...), custom_call_target="tpu_custom_call" | custom-call | tf_op jit(solution)/shard_map/pallas_call | solution.py:1289
  89.0 19.1 %shard_map.291.refs_1_.refs_2_.refs_3_ = bf16[3,1,704,256]{3,2,1,0:T(8,128)(2,1)} custom-call(bf16[3,4,704,256]{3,2,1,0:T(8,128)(2,1)} %bitcast.74, bf16[1024,1024]{1,0:T(8,128)(2,1)} %all-gather.4.cloned.1.call-done.refs_0_.refs_12_.refs_13_.refs_16_.refs_17_.refs_20_.refs_21_.refs_24_.refs_25_), custom_call_target="tpu_custom_call" | custom-call | tf_op jit(solution)/shard_map/pallas_call | solution.py:1351
  108.1 7.9 %shard_map.292.refs_8_ = bf16[4,704,512]{2,1,0:T(8,128)(2,1)} custom-call(s32[1]{0:T(128)} %bitcast.9.at, bf16[3,4,704,256]{3,2,1,0:T(8,128)(2,1)} %bitcast.75, bf16[3,1,704,256]{3,2,1,0:T(8,128)(2,1)} %shard_map.291.refs_1_.refs_2_.refs_3_, bf16[3,1,704,256]{3,2,1,0:T(8,128)(2,1)} %shard_map.291.refs_1_.refs_2_.refs_3_, ...), custom_call_target="tpu_custom_call" | custom-call | tf_op jit(solution)/shard_map/pallas_call | solution.py:1462
  116.2 46.7 %shard_map.293 = (bf16[256,2048]{1,0:T(8,128)(2,1)}, bf16[256,2048]{1,0:T(8,128)(2,1)}, bf16[3,1,704,256]{3,2,1,0:T(8,128)(2,1)}, bf16[3,256,2048]{2,1,0:T(8,128)(2,1)}) custom-call(bf16[256,2816]{1,0:T(8,128)(2,1)} %get-tuple-element.91.refs_0_, bf16[256,2816]{1,0:T(8,128)(2,1)} %get-tuple-element.92.refs_1_, bf16[256,2816]{1,0:T(8,128)(2,1)} %get-tuple-element.94.refs_2_, ...), custom_call_target="tpu_custom_call" | custom-call | tf_op jit(solution)/shard_map/pallas_call | solution.py:1398
  162.9 7.7 %shard_map.294.refs_22_ = bf16[4,704,512]{2,1,0:T(8,128)(2,1)} custom-call(s32[1]{0:T(128)} %bitcast.9.at, bf16[3,4,704,256]{3,2,1,0:T(8,128)(2,1)} %bitcast.77, bf16[3,1,704,256]{3,2,1,0:T(8,128)(2,1)} %get-tuple-element.110.refs_1_.refs_2_.refs_3_, bf16[3,1,704,256]{3,2,1,0:T(8,128)(2,1)} %get-tuple-element.110.refs_1_.refs_2_.refs_3_, ...), custom_call_target="tpu_custom_call" | custom-call | tf_op jit(solution)/shard_map/pallas_call | solution.py:1462
  170.7 1.2 collective-permute-start.3
  171.9 0.8 slice_convert_fusion
  173.0 1.2 collective-permute-done.3
  174.2 0.8 multiply_reduce_fusion
  175.7 2.3 convert_bitcast_fusion.1
  178.7 2.3 fusion.13.refs_0_
  181.0 56.8 %shard_map.295 = (bf16[256,1024]{1,0:T(8,128)(2,1)}, bf16[256,1024]{1,0:T(8,128)(2,1)}, bf16[256,1024]{1,0:T(8,128)(2,1)}, f32[3,4,1024]{2,1,0:T(4,128)}, f32[25...) custom-call(f32[256,1024]{1,0:T(8,128)} %fusion.13.refs_0_, ...), custom_call_target="tpu_custom_call" | custom-call | tf_op jit(solution)/shard_map/pallas_call | solution.py:990
  237.8 7.7 %shard_map.296.refs_11_ = bf16[4,704,512]{2,1,0:T(8,128)(2,1)} custom-call(s32[1]{0:T(128)} %bitcast.9.at, bf16[3,4,704,256]{3,2,1,0:T(8,128)(2,1)} %bitcast.79, bf16[3,1,704,256]{3,2,1,0:T(8,128)(2,1)} %get-tuple-element.116.refs_1_.refs_2_.refs_3_, bf16[3,1,704,256]{3,2,1,0:T(8,128)(2,1)} %get-tuple-element.116.refs_1_.refs_2_.refs_3_, ...), custom_call_target="tpu_custom_call" | custom-call | tf_op jit(solution)/shard_map/pallas_call | solution.py:1462
  245.6 1.5 copy-done
  247.6 1.0 copy.33.refs_7_
  249.3 24.1 %shard_map.297 = (bf16[256,2048]{1,0:T(8,128)(2,1)}, bf16[3,256,256]{2,1,0:T(8,128)(2,1)}, bf16[3,256,256]{2,1,0:T(8,128)(2,1)}, bf16[3,256,256]{2,1,0:T(8,128)(2,1)}) custom-call(bf16[256,1024]{1,0:T(8,128)(2,1)} %get-tuple-element.112.refs_0_.refs_8_, bf16[256,1024]{1,0:T(8,128)(2,1)} %get-tuple-element.113.refs_1_.refs_9_.refs_4_, ...), custom_call_target="tpu_custom_call" | custom-call | tf_op jit(solution)/shard_map/pallas_call | solution.py:1123
  273.4 0.9 collective-permute-start.4
  274.6 2.6 fusion.10
  277.2 1.5 fusion.14
  278.8 5.6 %shard_map.298.refs_28_.refs_0_ = bf16[4,256,512]{2,1,0:T(8,128)(2,1)} custom-call(s32[1]{0:T(128)} %bitcast.9.at, bf16[256,1024]{1,0:T(8,128)(2,1)} %get-tuple-element.87.head_ref.refs_24_.refs_0_, bf16[3,256,256]{2,1,0:T(8,128)(2,1)} %get-tuple-element.118.refs_1_.refs_2_.refs_3_, bf16[3,256,256]{2,1,0:T(8,128)(2,1)} %get-tuple-element.118.refs_1_.refs_2_.refs_3_, ...), custom_call_target="tpu_custom_call" | custom-call | tf_op jit(solution)/shard_map/pallas_call | solution.py:1462
  284.4 8.7 %shard_map.299.refs_1_ = bf16[4,768,512]{2,1,0:T(8,128)(2,1)} custom-call(s32[1]{0:T(128)} %bitcast.9.at, bf16[256,1024]{1,0:T(8,128)(2,1)} %get-tuple-element.112.refs_0_.refs_8_, bf16[3,256,256]{2,1,0:T(8,128)(2,1)} %get-tuple-element.120.refs_1_.refs_2_.refs_3_, bf16[3,256,256]{2,1,0:T(8,128)(2,1)} %get-tuple-element.120.refs_1_.refs_2_.refs_3_, ...), custom_call_target="tpu_custom_call" | custom-call | tf_op jit(solution)/shard_map/pallas_call | solution.py:1462
  293.2 2.1 fusion.4
  295.8 1.1 copy-done.9
  296.9 1.2 dynamic-slice_subtract_fusion
  298.1 4.0 reduce-scatter.8.cloned.1.call-done
  302.1 96.9 %shard_map.300 = (bf16[2816,128]{1,0:T(8,128)(2,1)}, bf16[2816,128]{1,0:T(8,128)(2,1)}, bf16[2816,128]{1,0:T(8,128)(2,1)}, bf16[1024,128]{1,0:T(8,128)(2,1)}, bf...) custom-call(bf16[4,256,512]{2,1,0:T(8,128)(2,1)} %shard_map.298.refs_28_.re, ...), custom_call_target="tpu_custom_call" | custom-call | tf_op jit(solution)/shard_map/pallas_call | solution.py:1743
  399.1 4.9 %shard_map.301 = (f32[2816,128]{1,0:T(8,128)}, f32[128,2816]{1,0:T(8,128)}, f32[128,2816]{1,0:T(8,128)}, f32[1024,128]{1,0:T(8,128)}, f32[128,1024]{1,0:T(8,128)...) custom-call(bf16[2816,128]{1,0:T(8,128)(2,1)} %get-tuple-element.126, ...), custom_call_target="tpu_custom_call" | custom-call | tf_op jit(solution)/shard_map/pallas_call | solution.py:1518
  404.0 1.5 copy.34
  (90 shorter events, 10.1 us)
Async XLA Ops:
  7.2 51.6 %all-gather.6.cloned.1.call-start = ((), (), s32[]{:S(2)}) async-start(), calls=%async_computation.7 | async-start | bytes 2621440 | tf_op jit(solution)/shard_map/all_gather | solution.py:1801
  7.9 81.1 %all-gather.4.cloned.1.call-start = ((), (), s32[]{:S(2)}) async-start(), calls=%async_computation.3 | async-start | bytes 2621440 | tf_op jit(solution)/shard_map/all_gather | solution.py:1802
  8.0 48.5 %collective-permute-start = (bf16[1,256,1024]{2,1,0:T(8,128)(2,1)}, bf16[1,256,1024]{2,1,0:T(8,128)(2,1)S(1)}, u32[]{:S(2)}, u32[]{:S(2)}) collective-permute-start(bf16[1,256,1024]{2,1,0:T(8,128)(2,1)} %param.33), channel_id=1, source_target_pairs={{0,1},{1,0},{2,3},{3,2},{4,5},{5,4},{6,7},{7,6},{8,9},{9,8},{10,11... | collective-permute-start | bytes 1572872 | tf_op jit(solution)/shard_map/ppermute | solution.py:58
  10.7 16.6 %copy-start.22 = (bf16[128]{0:T(256)(128)(2,1)S(1)}, bf16[128]{0:T(256)(128)(2,1)}, u32[]{:S(2)}) copy-start(bf16[128]{0:T(256)(128)(2,1)} %param.27) | copy-start | bytes 772
  25.3 31.2 %copy-start.13 = (bf16[1,256,1024]{2,1,0:T(8,128)(2,1)S(1)}, bf16[1,256,1024]{2,1,0:T(8,128)(2,1)}, u32[]{:S(2)}) copy-start(bf16[1,256,1024]{2,1,0:T(8,128)(2,1)} %param.33) | copy-start | bytes 1572868
  25.3 155.7 %reduce-scatter.4.cloned.1.call-start = ((), (), s32[]{:S(2)}) async-start(), calls=%async_computation.4 | async-start | bytes 3604480 | tf_op jit(solution)/shard_map/reduce_scatter | solution.py:1822
  58.8 29.8 %copy-start.1 = (bf16[1,1024,1024]{2,1,0:T(8,128)(2,1)S(1)}, bf16[1,1024,1024]{2,1,0:T(8,128)(2,1)}, u32[]{:S(2)}) copy-start(bf16[1,1024,1024]{2,1,0:T(8,128)(2,1)} %all-gather.6.cloned.1.call-done) | copy-start | bytes 6291460
  88.5 19.5 %collective-permute-start.1 = (bf16[1024,1024]{1,0:T(8,128)(2,1)S(1)}, bf16[1024,1024]{1,0:T(8,128)(2,1)}, u32[]{:S(2)}, u32[]{:S(2)}) collective-permute-start(bf16[1024,1024]{1,0:T(8,128)(2,1)S(1)} %bitcast.73), channel_id=1, source_target_pairs={{0,1},{1,0},{2,3},{3,2},{4,5},{5,4},{6,7},{7,6},{8,9},{9,8},{10,11... | collective-permute-start | bytes 6291464 | tf_op jit(solution)/shard_map/ppermute | solution.py:67
  116.0 162.8 %reduce-scatter.6.cloned.1.call-start = ((), (), s32[]{:S(2)}) async-start(), calls=%async_computation.5 | async-start | bytes 3604480 | tf_op jit(solution)/shard_map/reduce_scatter | solution.py:1822
  162.9 7.8 %copy-start.10 = (bf16[256,2048]{1,0:T(8,128)(2,1)S(1)}, bf16[256,2048]{1,0:T(8,128)(2,1)}, u32[]{:S(2)}) copy-start(bf16[256,2048]{1,0:T(8,128)(2,1)} %get-tuple-element.100) | copy-start | bytes 3145732
  170.6 2.1 copy-start.3
  170.6 131.5 %reduce-scatter.8.cloned.1.call-start = ((), (), s32[]{:S(2)}) async-start(), calls=%async_computation.6 | async-start | bytes 3604480 | tf_op jit(solution)/shard_map/reduce_scatter | solution.py:1822
  170.7 3.5 collective-permute-start.3
  174.2 1.0 copy-start.6
  174.2 1.2 copy-start.8
  174.2 1.5 copy-start.11
  175.7 3.0 copy-start.12
  178.0 2.9 copy-start.2
  245.5 1.6 copy-start
  245.5 2.1 copy-start.17
  245.5 3.1 copy-start.18
  247.1 37.2 %collective-permute-start.5 = (bf16[1024,1024]{1,0:T(8,128)(2,1)S(1)}, bf16[1024,1024]{1,0:T(8,128)(2,1)}, u32[]{:S(2)}, u32[]{:S(2)}) collective-permute-start(bf16[1024,1024]{1,0:T(8,128)(2,1)S(1)} %copy-done), channel_id=1, source_target_pairs={{0,1},{1,0},{2,3},{3,2},{4,5},{5,4},{6,7},{7,6},{8,9},{9,8},{10,11... | collective-permute-start | bytes 6291464 | tf_op jit(solution)/shard_map/ppermute | solution.py:67
  247.2 27.4 %collective-permute-start.2 = (bf16[1,256,2048]{2,1,0:T(8,128)(2,1)}, bf16[1,256,2048]{2,1,0:T(8,128)(2,1)}, u32[]{:S(2)}, u32[]{:S(2)}) collective-permute-start(bf16[1,256,2048]{2,1,0:T(8,128)(2,1)} %bitcast.10), channel_id=1, source_target_pairs={{0,1},{1,0},{2,3},{3,2},{4,5},{5,4},{6,7},{7,6},{8,9},{9,8},{10,11... | collective-permute-start | bytes 3145736 | tf_op jit(solution)/shard_map/ppermute | solution.py:73
  249.3 25.0 %copy-start.4 = (bf16[256,2048]{1,0:T(8,128)(2,1)S(1)}, bf16[256,2048]{1,0:T(8,128)(2,1)}, u32[]{:S(2)}) copy-start(bf16[256,2048]{1,0:T(8,128)(2,1)} %get-tuple-element.88.stream_ref) | copy-start | bytes 3145732
  273.3 3.8 copy-start.19
  273.3 3.9 copy-start.15
  273.4 19.8 %collective-permute-start.4 = (bf16[1,256,2048]{2,1,0:T(8,128)(2,1)}, bf16[1,256,2048]{2,1,0:T(8,128)(2,1)}, u32[]{:S(2)}, u32[]{:S(2)}) collective-permute-start(bf16[1,256,2048]{2,1,0:T(8,128)(2,1)} %bitcast.88), channel_id=1, source_target_pairs={{0,1},{1,0},{2,3},{3,2},{4,5},{5,4},{6,7},{7,6},{8,9},{9,8},{10,11... | collective-permute-start | bytes 3145736 | tf_op jit(solution)/shard_map/ppermute | solution.py:73
  284.3 8.7 %copy-start.20 = (f32[8,128]{1,0:T(8,128)S(1)}, f32[8,128]{1,0:T(8,128)}, u32[]{:S(2)}) copy-start(f32[8,128]{1,0:T(8,128)} %get-tuple-element.123) | copy-start | bytes 12292
  284.4 8.7 %copy-start.21 = (pred[8]{0:T(512)(128)(4,1)S(1)}, pred[8]{0:T(512)(128)(4,1)}, u32[]{:S(2)}) copy-start(pred[8]{0:T(512)(128)(4,1)} %constant.31.clone.1) | copy-start | bytes 28
  284.4 8.8 %copy-start.14 = (bf16[256,2048]{1,0:T(8,128)(2,1)S(1)}, bf16[256,2048]{1,0:T(8,128)(2,1)}, u32[]{:S(2)}) copy-start(bf16[256,2048]{1,0:T(8,128)(2,1)} %get-tuple-element.117) | copy-start | bytes 3145732
  295.3 1.6 copy-start.9
  295.3 2.8 copy-start.16
  (2 other events, 1.8 us)
Sparse Core Ops, SparseCore 0:
  9.9 36.4 all-gather.5
  48.2 35.3 all-gather.3
  116.1 60.7 reduce-scatter.3
  179.0 63.7 reduce-scatter.5
  245.7 56.3 reduce-scatter.7

commit v5 on v4

--- a/solution.py
+++ b/solution.py
@@ -130,12 +130,15 @@
 
 
 class Halves:
-    def __init__(self, ways, source, out, sends, receives, hand_sends, hand_receives):
+    def __init__(
+        self, ways, source, out, sends, receives, hand_sends, hand_receives, distances=None
+    ):
         own = lax.axis_index("dp")
         core = lax.axis_index("head")
         width = source.shape[1] // 2
         mine = pl.ds(pl.multiple_of(core * width, width), width)
-        self.peers = [place("dp", partner(own, by)) for by in range(1, ways)]
+        distances = distances or list(range(1, ways))
+        self.peers = [place("dp", partner(own, by)) for by in distances]
         self.other = place("head", 1 - core)
         self.first = [
             pltpu.make_async_remote_copy(
@@ -157,7 +160,7 @@
                 device_id=self.other,
                 device_id_type=MESH,
             )
-            for slot in range(ways - 1)
+            for slot in range(len(distances))
         ]
 
     def devices(self):
@@ -640,14 +643,16 @@
     )
 
 
-def mixer_forward_kernel(per_step, taps, spans, *refs):
+def mixer_forward_kernel(per_step, taps, spans, ways, *refs):
     pres, weights = refs[:3], refs[3:6]
     logit, logit_t, live, live_t, gain = refs[6:11]
-    sources = refs[11:14]
+    sources, normed = refs[11:14], refs[14]
     q_out, k_out, v_out, wy_out, inv_out, end_out, mixed_out, head_out, state_out, rim_out = refs[
-        14:24
+        15:25
     ]
-    ext, mix_all, rims, arriving, leaving, sends, receives, rim_sends, rim_receives = refs[24:]
+    normed_others = refs[25]
+    ext, mix_all, rims, arriving, leaving, sends, receives, rim_sends, rim_receives = refs[26:35]
+    halves = Halves(ways, normed, normed_others, *refs[35:], distances=list(range(1, ways - 1)))
     step = pl.program_id(0)
     position = lax.axis_index("seq")
     pairs = arriving.shape[0]
@@ -666,24 +671,29 @@
             device_id_type=MESH,
         )
 
-    def state_copy(pair):
+    def state_copy(pair, i):
         return pltpu.make_async_remote_copy(
-            src_ref=leaving.at[pair],
-            dst_ref=arriving.at[pair],
-            send_sem=sends.at[pair],
-            recv_sem=receives.at[pair],
+            src_ref=leaving.at[pair, i],
+            dst_ref=arriving.at[pair, i],
+            send_sem=sends.at[pair * per_step + i],
+            recv_sem=receives.at[pair * per_step + i],
             device_id=after,
             device_id_type=MESH,
         )
 
     @pl.when(step == 0)
     def _():
-        meet([place("seq", (position + last) % spans), place("seq", (position + 1) % spans)])
+        meet(
+            [place("seq", (position + last) % spans), place("seq", (position + 1) % spans)]
+            + halves.devices()
+        )
 
         @pl.when(position != last)
         def _():
             for part in range(3):
                 rim_copy(part).start()
+
+        halves.start()
 
         @pl.when(position == 0)
         def _():
@@ -718,18 +728,19 @@
 
     @pl.when((pair >= 0) & (pair < pairs))
     def _():
-        @pl.when(position != 0)
-        def _():
-            state_copy(pair).wait_recv()
-
         for i in range(per_step):
+
+            @pl.when(position != 0)
+            def _():
+                state_copy(pair, i).wait_recv()
+
             ends = end_out[pair * per_step + i]
             moved = dot_left(ends[:, :HEAD_DIM], arriving[pair, i])
             leaving[pair, i] = (moved + ends[:, HEAD_DIM:]).astype(jnp.bfloat16)
 
-        @pl.when(position != last)
-        def _():
-            state_copy(pair).start()
+            @pl.when(position != last)
+            def _():
+                state_copy(pair, i).start()
 
         for i in range(per_step):
             here = pl.ds(pl.multiple_of(pair * width + i * HEAD_DIM, HEAD_DIM), HEAD_DIM)
@@ -739,15 +750,24 @@
             mixed_out[:, here] = mixed
             head_out[:, here] = head
 
-    @pl.when((step == pl.num_programs(0) - 1) & (position != last))
-    def _():
-        for part in range(3):
-            rim_copy(part).wait_send()
-        for index in range(pairs):
-            state_copy(index).wait_send()
-
-
-def mixer_forward(pres, convs, logit, logit_t, live, gain, per_step, spans, number):
+    @pl.when(step == pairs)
+    def _():
+        halves.hand_on()
+
+    @pl.when(step == pl.num_programs(0) - 1)
+    def _():
+        @pl.when(position != last)
+        def _():
+            for part in range(3):
+                rim_copy(part).wait_send()
+            for index in range(pairs):
+                for i in range(per_step):
+                    state_copy(index, i).wait_send()
+
+        halves.finish()
+
+
+def mixer_forward(pres, convs, logit, logit_t, live, gain, normed, per_step, spans, ways, number):
     length, channels = pres[0].shape
     heads = channels // HEAD_DIM
     pairs = heads // per_step
@@ -770,13 +790,13 @@
 
     anywhere = pl.BlockSpec(memory_space=pl.ANY)
     return pl.pallas_call(
-        functools.partial(mixer_forward_kernel, per_step, taps, spans),
+        functools.partial(mixer_forward_kernel, per_step, taps, spans, ways),
         grid=(pairs + spans - 1,),
         in_specs=[flat(length)] * 3
         + [flat(taps)] * 3
         + [whole(length, heads), whole(heads, length), whole(length, 1), whole(1, length)]
         + [whole(1, HEAD_DIM)]
-        + [anywhere] * 3,
+        + [anywhere] * 4,
         out_specs=[flat(length)] * 3
         + [
             by_head(length, 2 * HEAD_DIM),
@@ -786,6 +806,7 @@
             whole(length, channels),
             whole(*states),
             whole(3, RIM, channels),
+            anywhere,
         ],
         out_shape=[b16(length, channels)] * 3
         + [
@@ -796,6 +817,7 @@
             b16(length, channels),
             b16(*states),
             b16(3, RIM, channels),
+            b16(ways - 2, *normed.shape),
         ],
         scratch_shapes=[
             pltpu.VMEM((RIM + length, HEAD_DIM), jnp.float32),
@@ -803,16 +825,17 @@
             pltpu.VMEM((3, RIM, channels), jnp.bfloat16),
             pltpu.VMEM((pairs, per_step, HEAD_DIM, HEAD_DIM), jnp.bfloat16),
             pltpu.VMEM((pairs, per_step, HEAD_DIM, HEAD_DIM), jnp.bfloat16),
-            pltpu.SemaphoreType.DMA((pairs,)),
-            pltpu.SemaphoreType.DMA((pairs,)),
+            pltpu.SemaphoreType.DMA((heads,)),
+            pltpu.SemaphoreType.DMA((heads,)),
             pltpu.SemaphoreType.DMA((3,)),
             pltpu.SemaphoreType.DMA((3,)),
-        ],
+        ]
+        + [pltpu.SemaphoreType.DMA((ways - 2,))] * 4,
         compiler_params=pltpu.CompilerParams(
             collective_id=number, has_side_effects=True, vmem_limit_bytes=VMEM
         ),
         cost_estimate=SHORT,
-    )(*pres, *convs, logit, logit_t, live, live.T, gain, *pres)
+    )(*pres, *convs, logit, logit_t, live, live.T, gain, *pres, normed)
 
 
 def mixer_backward_kernel(per_step, taps, spans, ways, tokens, *refs):
@@ -829,7 +852,7 @@
     ) = refs[34 + tokens : 48 + tokens]
     col_sends, col_receives, up_sends, up_receives, *half_sems = refs[48 + tokens :]
     halves = Halves(ways, residual, res_others, *half_sems)
-    columns = row_copies(ways, (2, 3), up_source, up_others, up_sends, up_receives)
+    columns = row_copies(ways, (1, 2), up_source, up_others, up_sends, up_receives)
     columns += column_copies(ways, head_source, head_others, col_sends, col_receives)
     step = pl.program_id(0)
     position = lax.axis_index("seq")
@@ -1088,8 +1111,10 @@
 
 def back_projection_kernel(ways, *refs):
     sources, d_logit, weights, beta_w = refs[:3], refs[3], refs[4:7], refs[7]
-    shared, out, others = refs[8:11], refs[-10], refs[-9:-6]
-    sends, receives = refs[-6:-3], refs[-3:]
+    shared, normed = refs[8:11], refs[11]
+    out, others, normed_far = refs[-15], refs[-14:-11], refs[-11]
+    sends, receives = refs[-10:-7], refs[-7:-4]
+    far = Halves(ways, normed, normed_far, *refs[-4:], distances=[ways - 1])
     step = pl.program_id(0)
     copies = [
         copy
@@ -1100,22 +1125,25 @@
     @pl.when(step == 0)
     def _():
         own = lax.axis_index("dp")
-        meet([place("dp", partner(own, by)) for by in range(1, ways)])
+        meet([place("dp", partner(own, by)) for by in range(1, ways)] + [far.other])
         for copy in copies:
             copy.start()
-
-    total = dot_low(d_logit[...], beta_w[...], (1, 1))
+        far.start()
+
+    total = dot_low(d_logit[...].astype(jnp.bfloat16), beta_w[...])
     for source, weight in zip(sources, weights):
         total = total + dot_low(source[...], weight[...], (1, 1))
     out[...] = total.astype(jnp.bfloat16)
 
     @pl.when(step == pl.num_programs(0) - 1)
     def _():
+        far.hand_on()
         for copy in copies:
             copy.wait()
-
-
-def back_projection(sources, d_logit, weights, beta_weight, ways, tokens, number):
+        far.finish()
+
+
+def back_projection(sources, d_logit, weights, beta_weight, normed, ways, tokens, number):
     length, channels = sources[0].shape
     width, heads = beta_weight.shape
     tile = width // 4
@@ -1126,23 +1154,24 @@
         in_specs=[pl.BlockSpec((length, channels), lambda n: (0, 0))] * 3
         + [pl.BlockSpec((length, heads), lambda n: (0, 0))]
         + [pl.BlockSpec((tile, channels), lambda n: (n, 0))] * 3
-        + [pl.BlockSpec((tile, heads), lambda n: (n, 0))]
-        + [anywhere] * (3 + len(tokens)),
-        out_specs=[pl.BlockSpec((length, tile), lambda n: (0, n))] + [anywhere] * 3,
-        out_shape=[b16(length, width)] + [b16(ways - 1, length, channels // ways)] * 3,
-        scratch_shapes=[pltpu.SemaphoreType.DMA((ways - 1,))] * 6,
+        + [pl.BlockSpec((heads, tile), lambda n: (0, n))]
+        + [anywhere] * (4 + len(tokens)),
+        out_specs=[pl.BlockSpec((length, tile), lambda n: (0, n))] + [anywhere] * 4,
+        out_shape=[b16(length, width)]
+        + [b16(ways - 1, length, channels // ways)] * 3
+        + [b16(1, *normed.shape)],
+        scratch_shapes=[pltpu.SemaphoreType.DMA((ways - 1,))] * 6
+        + [pltpu.SemaphoreType.DMA((1,))] * 4,
         compiler_params=pltpu.CompilerParams(
             collective_id=number, has_side_effects=True, vmem_limit_bytes=VMEM
         ),
         cost_estimate=SHORT,
-    )(*sources, d_logit, *weights, beta_weight, *sources, *tokens)
-
-
-def project_kernel(tokens, both_gains, q_w, k_w, v_w, beta_w, *refs):
-    q_out, k_out, v_out, logit_out, logit_t_out, stream_out, normed_out, half_out, gains_out = refs[
-        :9
-    ]
-    arriving, gains, gains_in, sends, receives = refs[9:]
+    )(*sources, d_logit, *weights, beta_weight.T, *sources, normed, *tokens)
+
+
+def project_kernel(tokens, first_gain, second_gain, q_w, k_w, v_w, beta_w, *refs):
+    q_out, k_out, v_out, logit_out, logit_t_out, stream_out, normed_out, gains_out = refs[:8]
+    arriving, gains, gains_in, sends, receives = refs[8:]
     step = pl.program_id(0)
     half = tokens.shape[1]
 
@@ -1153,8 +1182,13 @@
         mine = pl.ds(pl.multiple_of(core * half, half), half)
         theirs = pl.ds(pl.multiple_of((1 - core) * half, half), half)
         row = lax.broadcasted_iota(jnp.int32, gains.shape, 0)
-        both = both_gains[...].astype(jnp.float32)
-        gains[...] = jnp.where(row == 0, both[0:1], both[1:2]).astype(jnp.bfloat16)
+        first, second = [
+            jnp.concatenate(
+                [part[...].astype(jnp.float32)[i : i + 1] for i in range(part.shape[0])], 1
+            )
+            for part in (first_gain, second_gain)
+        ]
+        gains[...] = jnp.where(row == 0, first, second).astype(jnp.bfloat16)
         meet([other])
         copies = [
             pltpu.make_async_remote_copy(
@@ -1175,7 +1209,6 @@
         scale = lax.rsqrt(jnp.mean(stream * stream, axis=-1, keepdims=True) + EPSILON)
         gain = gains_out[...].astype(jnp.float32)[0:1]
         normed_out[...] = (stream * scale * gain).astype(jnp.bfloat16)
-        half_out[...] = normed_out[:, mine]
         logit_out[...] = dot_low(normed_out[...], beta_w[...], (1, 1))
         logit_t_out[...] = dot_low(beta_w[...], normed_out[...], (1, 1))
 
@@ -1201,15 +1234,15 @@
     return pl.pallas_call(
         project_kernel,
         grid=(6,),
-        in_specs=[whole(length, half), whole(2, half)]
+        in_specs=[whole(length, half)] + [whole(half // 128, 128)] * 2
         + [tiles(width, part) for part in range(3)]
         + [whole(heads, width)],
         out_specs=[tiles(length, part) for part in range(3)]
         + [whole(length, heads), whole(heads, length), whole(length, width)]
-        + [whole(length, width), whole(length, half), whole(16, width)],
+        + [whole(length, width), whole(16, width)],
         out_shape=[b16(length, channels)] * 3
         + [f32(length, heads), f32(heads, length), b16(length, width)]
-        + [b16(length, width), b16(length, half), b16(16, width)],
+        + [b16(length, width), b16(16, width)],
         scratch_shapes=[
             pltpu.VMEM((length, half), jnp.bfloat16),
             pltpu.VMEM((16, half), jnp.bfloat16),
@@ -1221,18 +1254,39 @@
             collective_id=number, has_side_effects=True, vmem_limit_bytes=VMEM
         ),
         cost_estimate=SHORT,
-    )(tokens, jnp.stack([first_gain, second_gain]), *weights, beta_weight.T)
+    )(
+        tokens, first_gain.reshape(-1, 128), second_gain.reshape(-1, 128), *weights, beta_weight.T
+    )
 
 
 def units_kernel(
-    head_ref, out_w, stream_ref, gains, d_ref, live, gate_w, up_w, down_w, token,
-    turned_out, d_gate_out, d_up_out, hidden_out, stream_out, normed_out,
-    part_low, arriving, sends, receives,
+    ways, steps, head_ref, out_w, stream_ref, gains, d_own, d_other, live, gate_w, up_w, down_w,
+    token,
+    turned_out, d_gate_out, d_up_out, hidden_out, stream_out, normed_out, own_out, others,
+    part_low, arriving, turned_hidden, d_ref, sends, receives, hidden_sends, hidden_receives,
 ):
+    own = lax.axis_index("dp")
+    tile = hidden_out.shape[1]
+    part_rows = tile // ways
+
+    def hidden_copy(step, by):
+        peer = partner(own, by)
+        start = pl.multiple_of(step * tile + peer * part_rows, part_rows)
+        return pltpu.make_async_remote_copy(
+            src_ref=turned_hidden.at[pl.ds(start, part_rows), :],
+            dst_ref=others.at[
+                by - 1, pl.ds(pl.multiple_of(step * part_rows, part_rows), part_rows), :
+            ],
+            send_sem=hidden_sends.at[(by - 1) * steps + step],
+            recv_sem=hidden_receives.at[(by - 1) * steps + step],
+            device_id=place("dp", peer),
+            device_id_type=MESH,
+        )
+
     @pl.when(pl.program_id(0) == 0)
     def _():
         other = place("head", 1 - lax.axis_index("head"))
-        meet([other])
+        meet([other] + [place("dp", partner(own, by)) for by in range(1, ways)])
         pieces = part_low.shape[0]
         width = part_low.shape[2]
         copies = []
@@ -1246,6 +1300,12 @@
             )
             copy.start()
             copies.append(copy)
+        core = lax.axis_index("head")
+        half = d_own.shape[1]
+        for place_of, part in ((core, d_own), (1 - core, d_other)):
+            masked = part[...].astype(jnp.float32) * live[...]
+            here = pl.ds(pl.multiple_of(place_of * half, half), half)
+            d_ref[:, here] = masked.astype(jnp.bfloat16)
         squares = 0.0
         for piece, copy in enumerate(copies):
             span = slice(piece * width, (piece + 1) * width)
@@ -1270,15 +1330,29 @@
         ((hidden, hidden_out), (d_gate, d_gate_out), (d_up, d_up_out))
     ):
         out[...] = part
-        if index == 0:
-            part = (part.astype(jnp.float32) * live[...]).astype(jnp.bfloat16)
-        turned_out[index] = part.T
+        if index > 0:
+            turned_out[index - 1] = part.T
+    step = pl.program_id(0)
+    live_hidden = (hidden.astype(jnp.float32) * live[...]).astype(jnp.bfloat16)
+    turned_hidden[pl.ds(pl.multiple_of(step * tile, tile), tile), :] = live_hidden.T
+    for by in range(1, ways):
+        hidden_copy(step, by).start()
+    own_out[pl.ds(pl.multiple_of(step * part_rows, part_rows), part_rows), :] = turned_hidden[
+        pl.ds(pl.multiple_of(step * tile + own * part_rows, part_rows), part_rows), :
+    ]
+
+    @pl.when(step == steps - 1)
+    def _():
+        for index in range(steps):
+            for by in range(1, ways):
+                hidden_copy(index, by).wait()
 
 
 def hidden_units(
-    head_out, out_weight, stream, gains, d_out, live, gate_weight, up_weight, down_weight, token,
-    number,
+    head_out, out_weight, stream, gains, d_own, d_other, live, gate_weight, up_weight,
+    down_weight, token, number,
 ):
+    ways = lax.axis_size("dp")
     length, width = stream.shape
     channels = head_out.shape[1]
     units = gate_weight.shape[1]
@@ -1286,33 +1360,41 @@
     whole = pl.BlockSpec((length, width), lambda f: (0, 0))
     column = pl.BlockSpec((width, tile), lambda f: (0, f))
     flat = pl.BlockSpec((length, tile), lambda f: (0, f))
+    chunk = units // ways
     return pl.pallas_call(
-        units_kernel,
+        functools.partial(units_kernel, ways, units // tile),
         grid=(units // tile,),
         in_specs=[
             pl.BlockSpec((length, channels), lambda f: (0, 0)),
             pl.BlockSpec((channels, width), lambda f: (0, 0)),
             whole,
             pl.BlockSpec((16, width), lambda f: (0, 0)),
-            whole,
+            pl.BlockSpec((length, width // 2), lambda f: (0, 0)),
+            pl.BlockSpec((length, width // 2), lambda f: (0, 0)),
             pl.BlockSpec((length, 1), lambda f: (0, 0)),
             column,
             column,
         ]
         + [pl.BlockSpec((tile, width), lambda f: (f, 0)), pl.BlockSpec(memory_space=pl.ANY)],
-        out_specs=[pl.BlockSpec((3, tile, length), lambda f: (0, f, 0))] + [flat] * 3 + [whole] * 2,
-        out_shape=[b16(3, units, length)]
+        out_specs=[pl.BlockSpec((2, tile, length), lambda f: (0, f, 0))]
+        + [flat] * 3
+        + [whole] * 2
+        + [pl.BlockSpec((chunk, length), lambda f: (0, 0)), pl.BlockSpec(memory_space=pl.ANY)],
+        out_shape=[b16(2, units, length)]
         + [b16(length, units)] * 3
-        + [f32(length, width), b16(length, width)],
+        + [f32(length, width), b16(length, width)]
+        + [b16(chunk, length), b16(ways - 1, chunk, length)],
         scratch_shapes=[pltpu.VMEM((4, length, width // 4), jnp.bfloat16)] * 2
-        + [pltpu.SemaphoreType.DMA((4,))] * 2,
+        + [pltpu.VMEM((units, length), jnp.bfloat16), pltpu.VMEM((length, width), jnp.bfloat16)]
+        + [pltpu.SemaphoreType.DMA((4,))] * 2
+        + [pltpu.SemaphoreType.DMA(((ways - 1) * (units // tile),))] * 2,
         compiler_params=pltpu.CompilerParams(
             collective_id=number, has_side_effects=True, vmem_limit_bytes=VMEM
         ),
         cost_estimate=SHORT,
     )(
-        head_out, out_weight, stream, gains, d_out, live, gate_weight, up_weight, down_weight,
-        token,
+        head_out, out_weight, stream, gains, d_own, d_other, live, gate_weight, up_weight,
+        down_weight, token,
     )
 
 
@@ -1334,85 +1416,113 @@
     return copies
 
 
-def rows_kernel(ways, entries, source, *refs):
-    out, sends, receives = refs[-3:]
-    own = lax.axis_index("dp")
-    meet([place("dp", partner(own, by)) for by in range(1, ways)])
-    copies = row_copies(ways, entries, source, out, sends, receives)
-    for copy in copies:
-        copy.start()
-    for copy in copies:
-        copy.wait()
-
-
-def exchanged_rows(source, entries, tokens, number):
+def feed_back_kernel(ways, entries, *refs):
+    d_gate, d_up, hidden, gate_w, up_w, down_w = refs[:6]
+    up_own, up_other, live, gains, source, normed, stream_in, out_w_in = refs[6:14]
+    feed_out, d_stream_out, low_out, d_head_out, second_out, others, normed_others = refs[-20:-13]
+    d_x, arriving, masked, stream_ref, out_w = refs[-13:-8]
+    swap_sems, load_sems = refs[-8:-6]
+    sends, receives = refs[-6:-4]
+    halves = Halves(ways, normed, normed_others, *refs[-4:])
+    copies = row_copies(ways, entries, source, others, sends, receives)
+    step = pl.program_id(0)
+    tile = feed_out.shape[1]
+    width = d_x.shape[1]
+    loads = [
+        pltpu.make_async_copy(stream_in, stream_ref, load_sems.at[0]),
+        pltpu.make_async_copy(out_w_in, out_w, load_sems.at[1]),
+    ]
+
+    @pl.when(step == 0)
+    def _():
+        meet(halves.devices())
+        halves.start()
+        for copy in copies + loads:
+            copy.start()
+
+    d_tile = dot_low(d_gate[...], gate_w[...], (1, 1)) + dot_low(d_up[...], up_w[...], (1, 1))
+    d_x[:, pl.ds(pl.multiple_of(step * tile, tile), tile)] = d_tile.astype(jnp.bfloat16)
+    feed_out[...] = dot_low(hidden[...], down_w[...]).astype(jnp.bfloat16)
+
+    @pl.when(step == pl.num_programs(0) - 1)
+    def _():
+        swap = pltpu.make_async_remote_copy(
+            src_ref=d_x, dst_ref=arriving, send_sem=swap_sems.at[0], recv_sem=swap_sems.at[1],
+            device_id=halves.other, device_id_type=MESH,
+        )
+        swap.start()
+        core = lax.axis_index("head")
+        half = up_own.shape[1]
+        for place_of, part in ((core, up_own), (1 - core, up_other)):
+            here = pl.ds(pl.multiple_of(place_of * half, half), half)
+            masked[:, here] = (part[...].astype(jnp.float32) * live[...]).astype(jnp.bfloat16)
+        for copy in loads:
+            copy.wait()
+        swap.wait()
+        d_two = d_x[...].astype(jnp.float32) + arriving[...].astype(jnp.float32)
+        stream = stream_ref[...]
+        scale = lax.rsqrt(jnp.mean(stream * stream, axis=-1, keepdims=True) + EPSILON)
+        weighted = gains[...].astype(jnp.float32)[1:2] * d_two
+        inner = jnp.sum(weighted * stream, axis=-1, keepdims=True)
+        d_stream = (
+            masked[...].astype(jnp.float32)
+            + scale * weighted
+            - stream * (scale * scale * scale * inner / width)
+        )
+        second_out[...] = jnp.sum(d_two * stream * scale, axis=0, keepdims=True)
+        d_stream_out[...] = d_stream
+        low_out[...] = d_stream.astype(jnp.bfloat16)
+        d_head_out[...] = dot_low(low_out[...], out_w[...], (1, 1))
+        halves.hand_on()
+        for copy in copies:
+            copy.wait()
+        halves.finish()
+
+
+def feed_back(
+    d_gate, d_up, hidden, weights, up_own, up_other, live, gains, source, entries, normed, stream,
+    out_weight, tokens, number,
+):
     ways = lax.axis_size("dp")
+    length, units = hidden.shape
+    width = normed.shape[1]
+    channels = out_weight.shape[0]
+    tile = width // 8
     anywhere = pl.BlockSpec(memory_space=pl.ANY)
+    row = pl.BlockSpec((tile, units), lambda n: (n, 0))
+    out = pl.BlockSpec((length, tile), lambda n: (0, n))
+
+    def whole(*shape):
+        return pl.BlockSpec(shape, lambda n: (0,) * len(shape))
+
     return pl.pallas_call(
-        functools.partial(rows_kernel, ways, entries),
-        out_shape=b16(ways - 1, entries[1] - entries[0], *source.shape[2:]),
-        in_specs=[anywhere] * (1 + len(tokens)),
-        out_specs=anywhere,
-        scratch_shapes=[pltpu.SemaphoreType.DMA((ways - 1,))] * 2,
+        functools.partial(feed_back_kernel, ways, entries),
+        grid=(8,),
+        in_specs=[whole(length, units)] * 3
+        + [row, row, pl.BlockSpec((units, tile), lambda n: (0, n))]
+        + [whole(length, width // 2)] * 2
+        + [whole(length, 1), whole(16, width)]
+        + [anywhere] * (4 + len(tokens)),
+        out_specs=[out, whole(length, width), whole(length, width), whole(length, channels)]
+        + [whole(1, width), anywhere, anywhere],
+        out_shape=[
+            b16(length, width), f32(length, width), b16(length, width), f32(length, channels),
+            f32(1, width),
+            b16(ways - 1, entries[1] - entries[0], *source.shape[2:]),
+            b16(ways - 1, length, width),
+        ],
+        scratch_shapes=[pltpu.VMEM((length, width), jnp.bfloat16)] * 3
+        + [pltpu.VMEM((length, width), jnp.float32), pltpu.VMEM(out_weight.shape, jnp.bfloat16)]
+        + [pltpu.SemaphoreType.DMA((2,))] * 2
+        + [pltpu.SemaphoreType.DMA((ways - 1,))] * 6,
         compiler_params=pltpu.CompilerParams(
             collective_id=number, has_side_effects=True, vmem_limit_bytes=VMEM
         ),
         cost_estimate=SHORT,
-    )(source, *tokens)
-
-
-def feed_back_kernel(ways, entries, *refs):
-    d_gate, d_up, hidden, gate_w, up_w, down_w, source, normed = refs[:8]
-    d_x_out, feed_out, others, normed_others, sends, receives, *half_sems = refs[-10:]
-    halves = Halves(ways, normed, normed_others, *half_sems)
-    copies = row_copies(ways, entries, source, others, sends, receives)
-
-    @pl.when(pl.program_id(0) == 0)
-    def _():
-        meet(halves.devices())
-        halves.start()
-        for copy in copies:
-            copy.start()
-
-    d_x = dot_low(d_gate[...], gate_w[...], (1, 1)) + dot_low(d_up[...], up_w[...], (1, 1))
-    d_x_out[...] = d_x.astype(jnp.bfloat16)
-    feed_out[...] = dot_low(hidden[...], down_w[...]).astype(jnp.bfloat16)
-
-    @pl.when(pl.program_id(0) == pl.num_programs(0) - 1)
-    def _():
-        halves.hand_on()
-        for copy in copies:
-            copy.wait()
-        halves.finish()
-
-
-def feed_back(d_gate, d_up, hidden, weights, source, entries, normed, tokens, number):
-    ways = lax.axis_size("dp")
-    length, units = hidden.shape
-    width = normed.shape[1]
-    tile = width // 8
-    anywhere = pl.BlockSpec(memory_space=pl.ANY)
-    whole = pl.BlockSpec((length, units), lambda n: (0, 0))
-    row = pl.BlockSpec((tile, units), lambda n: (n, 0))
-    out = pl.BlockSpec((length, tile), lambda n: (0, n))
-    return pl.pallas_call(
-        functools.partial(feed_back_kernel, ways, entries),
-        grid=(8,),
-        in_specs=[whole] * 3
-        + [row, row, pl.BlockSpec((units, tile), lambda n: (0, n))]
-        + [anywhere] * (2 + len(tokens)),
-        out_specs=[out, out, anywhere, anywhere],
-        out_shape=[b16(length, width)] * 2
-        + [
-            b16(ways - 1, entries[1] - entries[0], *source.shape[2:]),
-            b16(ways - 1, length, width),
-        ],
-        scratch_shapes=[pltpu.SemaphoreType.DMA((ways - 1,))] * 6,
-        compiler_params=pltpu.CompilerParams(
-            collective_id=number, has_side_effects=True, vmem_limit_bytes=VMEM
-        ),
-        cost_estimate=SHORT,
-    )(d_gate, d_up, hidden, *weights, source, normed, *tokens)
+    )(
+        d_gate, d_up, hidden, *weights, up_own, up_other, live, gains, source, normed, stream,
+        out_weight, *tokens,
+    )
 
 
 def pieces_kernel(groups, slots, ways, turned, at, *refs):
@@ -1484,10 +1594,17 @@
     )
 
 
-def widen_kernel(count, turned, starts, share_of, *refs):
+def widen_kernel(count, turned, starts, share_of, ways, *refs):
     small = refs[count]
     outs = refs[count + 1 :]
-    for index in range(count):
+    chunk = refs[0].shape[0] // ways
+    part = 256 // ways
+    for way in range(ways):
+        for tile in range(chunk // part):
+            start = way * chunk + tile * part
+            to = tile * 256 + way * part
+            outs[0][to : to + part, :] = refs[0][start : start + part, :].astype(jnp.float32)
+    for index in range(1, count):
         whole = refs[index][...].astype(jnp.float32)
         outs[index][...] = whole.T if turned[index] else whole
     gain, first, second, taps, beta = outs[count], *outs[count + 1 : count + 3], outs[count + 3 : -1], outs[-1]
@@ -1501,11 +1618,11 @@
             for lane in range(wide // 128):
                 out[tap : tap + 1, lane * 128 : (lane + 1) * 128] = small[row : row + 1, :]
                 row += 1
-    heads = beta.shape[1]
+    heads = beta.shape[0]
     width = share_of[1] // 128
     share = lax.axis_index("dp") * share_of[0] + lax.axis_index("seq")
     rows = [small[pl.ds(starts[4] + head * width + share, 1), :] for head in range(heads)]
-    beta[...] = jnp.concatenate(rows, 0).T
+    beta[...] = jnp.concatenate(rows, 0)
 
 
 def widened(arrays, turned, small, starts, channels, taps, heads, width):
@@ -1514,10 +1631,11 @@
         f32(*(array.shape[::-1] if turn else array.shape)) for array, turn in zip(arrays, turned)
     ]
     shapes += [f32(1, 128), f32(width // 256, 128), f32(width // 256, 128)]
-    shapes += [f32(taps, channels)] * 3 + [f32(128, heads)]
+    shapes += [f32(taps, channels)] * 3 + [f32(heads, 128)]
     return pl.pallas_call(
         functools.partial(
-            widen_kernel, len(arrays), turned, starts, (lax.axis_size("seq"), width)
+            widen_kernel, len(arrays), turned, starts, (lax.axis_size("seq"), width),
+            lax.axis_size("dp"),
         ),
         out_shape=shapes,
         in_specs=[inside] * (len(arrays) + 1),
@@ -1531,7 +1649,7 @@
     return [1 << bit for bit in range(size.bit_length() - 1)]
 
 
-def finish_kernel(spans, ways, fed, *refs):
+def finish_kernel(spans, ways, fed, split, *refs):
     out_raw, mix_raw, small = refs[:3]
     pieces, refs = refs[3 : 3 + fed], refs[3 + fed :]
     stages, small_out, refs = refs[: 4 + fed], refs[4 + fed], refs[5 + fed :]
@@ -1543,15 +1661,16 @@
     position = lax.axis_index("seq")
     last = spans - 1
     rounds = spans - 1
-    count = out_raw.shape[1]
-    groups = 1 + mix_raw.shape[1] // count
+    whole = out_raw.shape[1]
+    count = whole // split
+    groups = split + mix_raw.shape[1] // count
     rows = stages[0].shape[1]
     peers = [partner(own, by) for by in range(1, ways)]
 
     def raw_at(group, shard):
-        if group == 0:
-            return out_raw.at[shard]
-        return mix_raw.at[shard, (group - 1) * count : group * count, :]
+        if group < split:
+            return out_raw.at[shard, group * count : (group + 1) * count, :]
+        return mix_raw.at[shard, (group - split) * count : (group - split + 1) * count, :]
 
     def line_copy(way, turn, group, src):
         step = 1 if way == 0 else -1
@@ -1567,14 +1686,18 @@
 
     def owner_copies(index, source):
         high = source.shape[0]
-        turn = core * (ways // 2) if index == 0 or index > fed else 0
+        turn = core * (ways // 2) if index == 0 else 0
 
         def block_of(peer):
             start = ((peer + turn) % ways) * rows
             return source.at[:, pl.ds(pl.multiple_of(start, rows), rows)]
 
-        stage = stages[index]
-        mine = stage.at[pl.ds(pl.multiple_of(own * high, high), high), :]
+        if index < fed:
+            stage, start = stages[index], own * high
+        else:
+            stage = stages[fed + (index - fed) // split]
+            start = own * whole + (index - fed) % split * high
+        mine = stage.at[pl.ds(pl.multiple_of(start, high), high), :]
         copies = []
         for by, peer in enumerate(peers):
             copies.append(
@@ -1627,18 +1750,21 @@
     small_turn(0)
     along = (position, last - position)
 
+    ahead = 6
+
     def source_send(way, index):
         turn, group = index // groups, index % groups
         shard = last - turn if way == 0 else turn
-        if index >= 2:
-            line_copy(way, (index - 2) // groups, (index - 2) % groups, totals.at[0]).wait_send()
+        if index >= ahead:
+            before = index - ahead
+            line_copy(way, before // groups, before % groups, totals.at[0]).wait_send()
         line_copy(way, turn, group, raw_at(group, shard)).start()
 
     for way in range(2):
 
         @pl.when(along[way] == 0)
         def _():
-            for index in range(2):
+            for index in range(ahead):
                 source_send(way, index)
 
     fed_copies = [owner_copies(index, piece) for index, piece in enumerate(pieces)]
@@ -1650,7 +1776,7 @@
 
         @pl.when(along[way] == 0)
         def _():
-            for index in range(2, groups + 2):
+            for index in range(ahead, groups + ahead):
                 source_send(way, index)
 
     at_end = (position == 0) | (position == last)
@@ -1673,11 +1799,11 @@
     for turn in range(1, rounds):
         for group in range(groups):
             for way in range(2):
-                if turn * groups + group + 2 < rounds * groups:
+                if turn * groups + group + ahead < rounds * groups:
 
                     @pl.when(along[way] == 0)
                     def _():
-                        source_send(way, turn * groups + group + 2)
+                        source_send(way, turn * groups + group + ahead)
 
                 shard = last - turn + position if way == 0 else turn - along[1]
 
@@ -1697,13 +1823,21 @@
 
         small_turn(turn)
 
-    for turn in range(rounds, len(partners) + 1):
-        small_turn(turn)
+    later = list(range(rounds, len(partners) + 1))
+
+    @pl.when(at_end)
+    def _():
+        for turn in later:
+            small_turn(turn)
 
     @pl.when(jnp.logical_not(at_end))
     def _():
+        done = 0
         for group in range(groups):
             finish(group)
+            while done < len(later) and (group + 1) * len(later) >= (done + 1) * groups:
+                small_turn(later[done])
+                done += 1
 
     sources = list(pieces) + [totals.at[group] for group in range(groups)]
     for index, source in enumerate(sources):
@@ -1722,7 +1856,7 @@
 
         @pl.when(along[way] == 0)
         def _():
-            for group in range(groups - 2, groups):
+            for group in range(groups - ahead, groups):
                 line_copy(way, rounds - 1, group, totals.at[group]).wait_send()
 
     for turn in range(len(partners)):
@@ -1731,17 +1865,20 @@
 
 def finished_gradients(out_raw, mix_raw, pieces, small, number):
     spans, ways = lax.axis_size("seq"), lax.axis_size("dp")
-    _, count, wide = out_raw.shape
-    groups = 1 + mix_raw.shape[1] // count
+    split = 2
+    _, whole, wide = out_raw.shape
+    count = whole // split
+    grads = 1 + mix_raw.shape[1] // whole
+    groups = grads * split
     rows = wide // ways
     fed = len(pieces)
-    highs = [ways * piece.shape[0] for piece in pieces] + [ways * count] * groups
+    highs = [ways * piece.shape[0] for piece in pieces] + [ways * whole] * grads
     inside = pl.BlockSpec(memory_space=pltpu.VMEM)
     shapes = [b16(high, rows) for high in highs]
     lines = (2, spans - 1, groups, count, wide)
     turns = len(doublings(ways)) + len(doublings(spans)) + 1
     return pl.pallas_call(
-        functools.partial(finish_kernel, spans, ways, fed),
+        functools.partial(finish_kernel, spans, ways, fed, split),
         out_shape=shapes + [f32(*small.shape)],
         in_specs=[inside] * 3 + [pl.BlockSpec(memory_space=pl.ANY)] * fed,
         out_specs=[inside] * (len(shapes) + 1),
@@ -1751,8 +1888,8 @@
             pltpu.VMEM((groups, count, wide), jnp.bfloat16),
         ]
         + [pltpu.SemaphoreType.DMA((2 * (spans - 1) * groups,))] * 2
-        + [pltpu.SemaphoreType.DMA((len(highs) * (ways - 1),))] * 2
-        + [pltpu.SemaphoreType.DMA((len(highs),))]
+        + [pltpu.SemaphoreType.DMA(((fed + groups) * (ways - 1),))] * 2
+        + [pltpu.SemaphoreType.DMA((fed + groups,))]
         + [pltpu.VMEM((turns,) + small.shape, jnp.float32)] * 2
         + [pltpu.SemaphoreType.DMA((turns,))] * 2,
         compiler_params=pltpu.CompilerParams(
@@ -1794,12 +1931,20 @@
     fused = groups == 2
     weights = [query_weight, key_weight, value_weight]
     if fused:
-        *pres, beta_logit, logit_turned, gathered, normed_one, normed_half, gains = projected(
+        *pres, beta_logit, logit_turned, gathered, normed_one, gains = projected(
             tokens_in[0], first_gain, second_gain, weights, beta_weight, 7
         )
-        upstream_full = gather_head(upstream, 2) * live_low
+        upstream_other = swapped(upstream[0])
+        upstream_other, beta_logit = lax.optimization_barrier((upstream_other, beta_logit))
+        first = lax.axis_index("head") == 0
+        upstream_full = live_low * jnp.concatenate(
+            [
+                jnp.where(first, upstream, upstream_other[None]),
+                jnp.where(first, upstream_other[None], upstream),
+            ],
+            2,
+        )
         half_up = lax.all_gather(upstream[0], "dp", axis=0, tiled=True)
-        half_one = lax.all_gather(normed_half, "dp", axis=0, tiled=True)
     else:
         gains = jnp.stack([first_gain, second_gain] + [first_gain] * 14)
         masked_up = upstream[0] * live_low[0]
@@ -1836,10 +1981,12 @@
     head_gain = mixer_gain.astype(jnp.float32)[None, :]
     if fused:
         (
-            query, key, value, wy, inverse, ends, mixed, head_out, entering, rims,
+            query, key, value, wy, inverse, ends, mixed, head_out, entering, rims, one_near,
         ) = mixer_forward(
-            pres, convs, beta_logit, logit_turned, live_col, head_gain, per_step, spans, 1
-        )
+            pres, convs, beta_logit, logit_turned, live_col, head_gain, normed_one[0],
+            per_step, spans, ways, 1,
+        )
+        half_up, mixed = lax.optimization_barrier((half_up, mixed))
     else:
         rims = passed_along(jnp.stack([pre[local_len - RIM :, :] for pre in pres]), "seq", 1)
         rims = [rims[0], rims[1], rims[2]]
@@ -1850,11 +1997,12 @@
         mixed, head_out = mixer_finish(mix, entering, head_gain, per_step)
     head_out = head_out[None]
     if fused:
-        turned, d_gate, d_up, hidden, stream_mid, normed_two = hidden_units(
-            head_out[0], output_weight, gathered, gains, upstream_full[0], live_col,
+        (
+            turned, d_gate, d_up, hidden, stream_mid, normed_two, own_hidden, hidden_others,
+        ) = hidden_units(
+            head_out[0], output_weight, gathered, gains, upstream[0], upstream_other, live_col,
             gate_weight, up_weight, down_weight, half_up, 8,
         )
-        half_up, hidden = lax.optimization_barrier((half_up, hidden))
         stream_mid, normed_two = stream_mid[None], normed_two[None]
     else:
         mixer_part = jnp.dot(head_out, output_weight, preferred_element_type=jnp.float32)
@@ -1865,7 +2013,7 @@
         )
     scale_two = inverse_rms(stream_mid)
     units = turned.shape[1] // ways
-    turned = turned.reshape(3, ways, units, local_len)
+    turned = turned.reshape(-1, ways, units, local_len)
 
     def raw_piece(lefts, count, rights, is_turned, tokens=()):
         return span_pieces(
@@ -1905,14 +2053,20 @@
 
     normed_full = normed_two[0]
     if fused:
-        hidden_others = exchanged_rows(turned, (0, 1), [half_one], 2)
+        hidden_slots = [(own_hidden, (units, local_len), lambda at: (0, 0))] + [
+            (hidden_others, (1, units, local_len), lambda at, by=by: (by, 0, 0))
+            for by in range(ways - 1)
+        ]
         down_raw = raw_piece(
-            [feed_slots(0, hidden_others, 0)], units, halves_of(half_up, swapped(half_up)), True
-        )
-        d_two_part, feed_part, d_others, two_others = feed_back(
-            d_gate, d_up, hidden, [gate_weight, up_weight, down_weight], turned, (1, 2),
-            normed_full, [down_raw], 3,
-        )
+            [hidden_slots], units, halves_of(half_up, swapped(half_up)), True
+        )
+        feed_part, d_stream, residual, d_head_out, second_row, d_others, two_others = feed_back(
+            d_gate, d_up, hidden, [gate_weight, up_weight, down_weight], upstream[0],
+            upstream_other, live_col, gains, turned, (0, 1), normed_full, stream_mid[0],
+            output_weight, [down_raw], 3,
+        )
+        d_stream, residual_full, d_head_out = d_stream[None], residual[None], d_head_out[None]
+        grad_second = own_half(second_row[0], local_width)
         two_slots = slots_of(normed_full, two_others)
     else:
         hidden_others = jnp.stack(exchanged(turned[:1].transpose(1, 0, 2, 3), "dp")[1:])
@@ -1922,24 +2076,26 @@
         d_others = jnp.stack(exchanged(turned[1:].transpose(1, 0, 2, 3), "dp")[1:])
         two_slots = slots_of(normed_full, jnp.stack(spread(normed_full, "dp")[1:]))
     down_piece = scattered(down_raw)
-    gate_raw = raw_piece([feed_slots(1, d_others, 0)], units, two_slots, True)
+    first = turned.shape[0] - 2
+    gate_raw = raw_piece([feed_slots(first, d_others, 0)], units, two_slots, True)
     gate_piece = scattered(gate_raw)
     layer_out = own_half(stream_mid + sum_head(feed_part[None]), local_width).astype(jnp.bfloat16)
-    d_two = sum_head(d_two_part[None])
-    d_stream = (
-        upstream_full.astype(jnp.float32)
-        + scale_two * gain_two * d_two
-        - stream_mid
-        * scale_two
-        * scale_two
-        * scale_two
-        * (jnp.sum(d_two * gain_two * stream_mid, axis=-1, keepdims=True) / full_width)
-    )
-    grad_second = own_half(jnp.sum(d_two * stream_mid * scale_two, axis=(0, 1)), local_width)
-    residual_full = d_stream.astype(jnp.bfloat16)
-    d_head_out = jnp.einsum(
-        "rsd,cd->rsc", residual_full, output_weight, preferred_element_type=jnp.float32
-    )
+    if not fused:
+        d_two = sum_head(d_two_part[None])
+        d_stream = (
+            upstream_full.astype(jnp.float32)
+            + scale_two * gain_two * d_two
+            - stream_mid
+            * scale_two
+            * scale_two
+            * scale_two
+            * (jnp.sum(d_two * gain_two * stream_mid, axis=-1, keepdims=True) / full_width)
+        )
+        grad_second = own_half(jnp.sum(d_two * stream_mid * scale_two, axis=(0, 1)), local_width)
+        residual_full = d_stream.astype(jnp.bfloat16)
+        d_head_out = jnp.einsum(
+            "rsd,cd->rsc", residual_full, output_weight, preferred_element_type=jnp.float32
+        )
     if fused:
         (
             *mix_sources, grad_kernels, d_beta_logit, grad_gain_part, out_others, res_others,
@@ -1964,16 +2120,15 @@
         ]
     grad_gain_part = grad_gain_part[0]
     if fused:
-        up_raw = raw_piece([feed_slots(2, up_others, 0)], units, two_slots, True)
+        up_raw = raw_piece([feed_slots(1, up_others, 0)], units, two_slots, True)
     else:
         up_raw = raw_piece([feed_slots(2, d_others, 1)], units, two_slots, True)
     up_piece = scattered(up_raw)
     share_width = channels // ways
     residual = residual_full[0]
     if fused:
-        d_one_part, *mix_others = back_projection(
-            mix_sources, d_beta_logit.astype(jnp.bfloat16),
-            weights, beta_weight, ways, [up_raw], 5,
+        d_one_part, *mix_others, one_far = back_projection(
+            mix_sources, d_beta_logit, weights, beta_weight, normed_one[0], ways, [up_raw], 5,
         )
     else:
         *mix_others, out_others = [
@@ -1996,7 +2151,8 @@
         ]
 
     if fused:
-        one_slots = halves_of(half_one, swapped(half_one))
+        one_slots = slots_of(normed_one[0], one_near)[: ways - 1]
+        one_slots += slots_of(normed_one[0], one_far)[1:2]
     else:
         one_slots = slots_of(normed_one[0], jnp.stack(spread(normed_one[0], "dp")[1:]))
     out_raw = raw_piece(
@@ -2052,7 +2208,7 @@
         )
         down, gate, up, out, *mix = results[:7]
         gain_total, grad_first, grad_second = [part.reshape(-1) for part in results[7:10]]
-        kernel_sum, grad_beta = results[10:13], results[13]
+        kernel_sum, grad_beta = results[10:13], results[13].T
     else:
         small = sum_doubling(small, ("dp", "seq"))
         gain_total = sum_doubling(small[0], ("head",))

time: 413 us -> 385 us (0.932)
  the two profiles are of different devices: /device:TPU:9 before, /device:TPU:0 now
where the time goes in v5:
time: 385 us; the launch traced here: 383 us
  Pallas kernels  352 us (91%)
  between operations  14.8 us (4%)
  other arithmetic  7.6 us (2%)
    pallas_call x1, Pallas kernels, finished_gradients(): pl.pallas_call(functools.partial(finish_kernel, spans, ways, fed, split),...  86.3 us
    pallas_call x1, Pallas kernels, mixer_backward(): pl.pallas_call(functools.partial(mixer_backward_kernel, per_step, taps, s...  54.8 us
    pallas_call x1, Pallas kernels, feed_back(): pl.pallas_call(functools.partial(feed_back_kernel, ways, entries), grid=(...  48.3 us
    pallas_call x1, Pallas kernels, back_projection(): pl.pallas_call(functools.partial(back_projection_kernel, ways), grid=(wid...  38 us
    pallas_call x5, Pallas kernels, span_pieces(): pl.pallas_call(functools.partial(pieces_kernel, groups, slots, ways, turn...  37 us
    pallas_call x1, Pallas kernels, mixer_forward(): pl.pallas_call(functools.partial(mixer_forward_kernel, per_step, taps, sp...  34.6 us
    pallas_call x1, Pallas kernels, hidden_units(): pl.pallas_call(functools.partial(units_kernel, ways, units // tile), grid...  34.4 us
    pallas_call x1, Pallas kernels, projected(): pl.pallas_call(project_kernel, grid=(6,), in_specs=[whole(length, half)]...  14.1 us
  transfers between devices with their start and end apart: 8, of which 1 were waited for; matrix products, arithmetic and copies ran while one was open for 2% of the time, Pallas kernels for 66%

profile of v5, /device:TPU:0, one launch (start us, length us, event | category | flops | bytes accessed | tf_op | source)
XLA Modules:
  0.0 383.2 jit_solution(9413176805173368701)
XLA Ops:
  7.2 0.7 all-gather.3.cloned.1.call-update
  8.0 0.5 collective-permute-start
  9.1 14.1 %shard_map.288 = (bf16[256,1024]{1,0:T(8,128)(2,1)}, bf16[256,1024]{1,0:T(8,128)(2,1)}, bf16[256,1024]{1,0:T(8,128)(2,1)}, f32[256,8]{1,0:T(8,128)}, f32[8,256]{...) custom-call(bf16[256,1024]{1,0:T(8,128)(2,1)} %bitcast.73, ...), custom_call_target="tpu_custom_call" | custom-call | tf_op jit(solution)/shard_map/pallas_call | solution.py:1234
  23.3 0.6 compare_convert_fusion.refs_9_
  23.8 0.7 fusion.11.refs_8_.live.refs_18_
  24.5 0.5 bitcast_convert_fusion.refs_10_.refs_5_
  25.0 34.6 %shard_map.289 = (bf16[256,1024]{1,0:T(8,128)(2,1)}, bf16[256,1024]{1,0:T(8,128)(2,1)}, bf16[256,1024]{1,0:T(8,128)(2,1)}, f32[8,256,256]{2,1,0:T(8,128)}, f32[8...) custom-call(bf16[256,1024]{1,0:T(8,128)(2,1)} %get-tuple-element.90., ...), custom_call_target="tpu_custom_call" | custom-call | tf_op jit(solution)/shard_map/pallas_call | solution.py:792
  59.6 0.4 collective-permute-start.1
  60.1 34.4 %shard_map.290 = (bf16[2,2816,256]{2,1,0:T(8,128)(2,1)}, bf16[256,2816]{1,0:T(8,128)(2,1)}, bf16[256,2816]{1,0:T(8,128)(2,1)}, bf16[256,2816]{1,0:T(8,128)(2,1)}...) custom-call(bf16[256,1024]{1,0:T(8,128)(2,1)} %get-tuple-element.97., ...), custom_call_target="tpu_custom_call" | custom-call | tf_op jit(solution)/shard_map/pallas_call | solution.py:1364
  94.5 1.3 copy-done
  95.8 7.9 %shard_map.291.refs_14_ = bf16[4,704,512]{2,1,0:T(8,128)(2,1)} custom-call(s32[1]{0:T(128)} %bitcast.10.at, bf16[704,256]{1,0:T(8,128)(2,1)} %get-tuple-element.109.refs_0_, bf16[3,704,256]{2,1,0:T(8,128)(2,1)} %get-tuple-element.110.refs_1_.refs_2_.refs_3_, bf16[3,704,256]{2,1,0:T(8,128)(2,1)} %get-tuple-element.110.refs_1_.refs_2_.refs_3_, ...), custom_call_target="tpu_custom_call" | custom-call | tf_op jit(solution)/shard_map/pallas_call | solution.py:1572
  103.7 0.2 reduce-scatter.6.cloned.1.call-start
  103.9 48.3 %shard_map.292 = (bf16[256,2048]{1,0:T(8,128)(2,1)}, f32[256,2048]{1,0:T(8,128)}, bf16[256,2048]{1,0:T(8,128)(2,1)}, f32[256,1024]{1,0:T(8,128)}, f32[1,2048]{1,...) custom-call(bf16[256,2816]{1,0:T(8,128)(2,1)} %get-tuple-element.104.refs_0_, ...), custom_call_target="tpu_custom_call" | custom-call | tf_op jit(solution)/shard_map/pallas_call | solution.py:1498
  152.2 7.6 %shard_map.293.refs_22_ = bf16[4,704,512]{2,1,0:T(8,128)(2,1)} custom-call(s32[1]{0:T(128)} %bitcast.10.at, bf16[2,4,704,256]{3,2,1,0:T(8,128)(2,1)} %bitcast.60, bf16[3,1,704,256]{3,2,1,0:T(8,128)(2,1)} %get-tuple-element.123.refs_1_.refs_2_.refs_3_, bf16[3,1,704,256]{3,2,1,0:T(8,128)(2,1)} %get-tuple-element.123.refs_1_.refs_2_.refs_3_, ...), custom_call_target="tpu_custom_call" | custom-call | tf_op jit(solution)/shard_map/pallas_call | solution.py:1572
  159.9 2.9 reduce-scatter.4.cloned.1.call-done
  162.7 54.8 %shard_map.294 = (bf16[256,1024]{1,0:T(8,128)(2,1)}, bf16[256,1024]{1,0:T(8,128)(2,1)}, bf16[256,1024]{1,0:T(8,128)(2,1)}, f32[3,4,1024]{2,1,0:T(4,128)}, f32[25...) custom-call(f32[256,1024]{1,0:T(8,128)} %get-tuple-element.113.refs_, ...), custom_call_target="tpu_custom_call" | custom-call | tf_op jit(solution)/shard_map/pallas_call | solution.py:1013
  217.6 7.7 %shard_map.295.refs_12_ = bf16[4,704,512]{2,1,0:T(8,128)(2,1)} custom-call(s32[1]{0:T(128)} %bitcast.10.at, bf16[2,4,704,256]{3,2,1,0:T(8,128)(2,1)} %bitcast.62, bf16[3,1,704,256]{3,2,1,0:T(8,128)(2,1)} %get-tuple-element.130.refs_1_.refs_2_.refs_3_, bf16[3,1,704,256]{3,2,1,0:T(8,128)(2,1)} %get-tuple-element.130.refs_1_.refs_2_.refs_3_, ...), custom_call_target="tpu_custom_call" | custom-call | tf_op jit(solution)/shard_map/pallas_call | solution.py:1572
  225.3 0.3 collective-permute-start.2
  225.7 0.8 slice_convert_fusion
  226.5 38.0 %shard_map.296 = (bf16[256,2048]{1,0:T(8,128)(2,1)}, bf16[3,256,256]{2,1,0:T(8,128)(2,1)}, bf16[3,256,256]{2,1,0:T(8,128)(2,1)}, bf16[3,256,256]{2,1,0:T(8,128)(2,1)}, bf16[1,256,2048]{2,1,0:T(8,128)(2,1)}) custom-call(bf16[256,1024]{1,0:T(8,128)(2,1)} %get-tuple-element.126.refs_0_.refs_8_, bf16[256,1024]{1,0:T(8,128)(2,1)} %get-tuple-element.127.refs_1_.refs_9_.refs_4_, ...), custom_call_target="tpu_custom_call" | custom-call | tf_op jit(solution)/shard_map/pallas_call | solution.py:1151
  264.4 0.4 collective-permute-start.3
  264.9 0.3 fusion.5
  265.2 2.2 fusion.10
  267.5 0.3 fusion.12
  267.8 5.5 %shard_map.297.refs_28_.refs_0_ = bf16[4,256,512]{2,1,0:T(8,128)(2,1)} custom-call(s32[1]{0:T(128)} %bitcast.10.at, bf16[256,1024]{1,0:T(8,128)(2,1)} %get-tuple-element.97.head_ref.refs_24_.refs_0_, bf16[3,256,256]{2,1,0:T(8,128)(2,1)} %get-tuple-element.132.refs_1_.refs_2_.refs_3_, bf16[3,256,256]{2,1,0:T(8,128)(2,1)} %get-tuple-element.132.refs_1_.refs_2_.refs_3_, ...), custom_call_target="tpu_custom_call" | custom-call | tf_op jit(solution)/shard_map/pallas_call | solution.py:1572
  273.4 8.3 %shard_map.298.refs_1_ = bf16[4,768,512]{2,1,0:T(8,128)(2,1)} custom-call(s32[1]{0:T(128)} %bitcast.10.at, bf16[256,1024]{1,0:T(8,128)(2,1)} %get-tuple-element.126.refs_0_.refs_8_, bf16[3,256,256]{2,1,0:T(8,128)(2,1)} %get-tuple-element.134.refs_1_.refs_2_.refs_3_, bf16[3,256,256]{2,1,0:T(8,128)(2,1)} %get-tuple-element.134.refs_1_.refs_2_.refs_3_, ...), custom_call_target="tpu_custom_call" | custom-call | tf_op jit(solution)/shard_map/pallas_call | solution.py:1572
  281.8 0.9 fusion.4
  282.8 0.4 fusion.9
  283.2 1.1 copy-done.7
  284.3 1.2 dynamic-slice_subtract_fusion
  285.5 86.3 %shard_map.299 = (bf16[2816,128]{1,0:T(8,128)(2,1)}, bf16[2816,128]{1,0:T(8,128)(2,1)}, bf16[2816,128]{1,0:T(8,128)(2,1)}, bf16[1024,128]{1,0:T(8,128)(2,1)}, bf...) custom-call(bf16[4,256,512]{2,1,0:T(8,128)(2,1)} %shard_map.297.refs_28_.re, ...), custom_call_target="tpu_custom_call" | custom-call | tf_op jit(solution)/shard_map/pallas_call | solution.py:1880
  371.8 4.9 %shard_map.300 = (f32[2816,128]{1,0:T(8,128)}, f32[128,2816]{1,0:T(8,128)}, f32[128,2816]{1,0:T(8,128)}, f32[1024,128]{1,0:T(8,128)}, f32[128,1024]{1,0:T(8,128)...) custom-call(bf16[2816,128]{1,0:T(8,128)(2,1)} %get-tuple-element.142, ...), custom_call_target="tpu_custom_call" | custom-call | tf_op jit(solution)/shard_map/pallas_call | solution.py:1635
  (50 shorter events, 0.4 us)
Async XLA Ops:
  7.2 52.5 %all-gather.3.cloned.1.call-start = ((), (), s32[]{:S(2)}) async-start(), calls=%async_computation.6 | async-start | bytes 2621440 | tf_op jit(solution)/shard_map/all_gather | solution.py:1947
  7.9 154.8 %reduce-scatter.4.cloned.1.call-start = ((), (), s32[]{:S(2)}) async-start(), calls=%async_computation.3 | async-start | bytes 3604480 | tf_op jit(solution)/shard_map/reduce_scatter | solution.py:1967
  8.0 17.1 %collective-permute-start = (bf16[256,1024]{1,0:T(8,128)(2,1)}, bf16[256,1024]{1,0:T(8,128)(2,1)S(1)}, u32[]{:S(2)}, u32[]{:S(2)}) collective-permute-start(bf16[256,1024]{1,0:T(8,128)(2,1)} %bitcast.63), channel_id=1, source_target_pairs={{0,1},{1,0},{2,3},{3,2},{4,5},{5,4},{6,7},{7,6},{8,9},{9,8},{10,11... | collective-permute-start | bytes 1572872 | tf_op jit(solution)/shard_map/ppermute | solution.py:67
  9.1 15.4 %copy-start.13 = (bf16[128]{0:T(256)(128)(2,1)S(1)}, bf16[128]{0:T(256)(128)(2,1)}, u32[]{:S(2)}) copy-start(bf16[128]{0:T(256)(128)(2,1)} %param.27) | copy-start | bytes 772
  25.0 34.6 %copy-start.4 = (bf16[256,1024]{1,0:T(8,128)(2,1)}, bf16[256,1024]{1,0:T(8,128)(2,1)S(1)}, u32[]{:S(2)}) copy-start(bf16[256,1024]{1,0:T(8,128)(2,1)S(1)} %collective-permute-done.d_other.refs_7_) | copy-start | bytes 1572868
  59.6 34.8 %collective-permute-start.1 = (bf16[1024,1024]{1,0:T(8,128)(2,1)}, bf16[1024,1024]{1,0:T(8,128)(2,1)S(1)}, u32[]{:S(2)}, u32[]{:S(2)}) collective-permute-start(bf16[1024,1024]{1,0:T(8,128)(2,1)} %bitcast.49), channel_id=1, source_target_pairs={{0,1},{1,0},{2,3},{3,2},{4,5},{5,4},{6,7},{7,6},{8,9},{9,8},{10,11... | collective-permute-start | bytes 6291464 | tf_op jit(solution)/shard_map/ppermute | solution.py:67
  94.5 1.3 copy-start
  103.7 164.1 %reduce-scatter.6.cloned.1.call-start = ((), (), s32[]{:S(2)}) async-start(), calls=%async_computation.4 | async-start | bytes 3604480 | tf_op jit(solution)/shard_map/reduce_scatter | solution.py:1967
  159.8 125.7 %reduce-scatter.8.cloned.1.call-start = ((), (), s32[]{:S(2)}) async-start(), calls=%async_computation.5 | async-start | bytes 3604480 | tf_op jit(solution)/shard_map/reduce_scatter | solution.py:1967
  225.3 39.9 %collective-permute-start.2 = (bf16[1,256,2048]{2,1,0:T(8,128)(2,1)}, bf16[1,256,2048]{2,1,0:T(8,128)(2,1)}, u32[]{:S(2)}, u32[]{:S(2)}) collective-permute-start(bf16[1,256,2048]{2,1,0:T(8,128)(2,1)} %bitcast.11), channel_id=1, source_target_pairs={{0,1},{1,0},{2,3},{3,2},{4,5},{5,4},{6,7},{7,6},{8,9},{9,8},{10,11... | collective-permute-start | bytes 3145736 | tf_op jit(solution)/shard_map/ppermute | solution.py:73
  226.4 38.5 %copy-start.2 = (bf16[256,2048]{1,0:T(8,128)(2,1)S(1)}, bf16[256,2048]{1,0:T(8,128)(2,1)}, u32[]{:S(2)}) copy-start(bf16[256,2048]{1,0:T(8,128)(2,1)} %get-tuple-element.98.stream_ref) | copy-start | bytes 3145732
  226.4 38.7 %copy-start.11 = (f32[1,2048]{1,0:T(1,128)S(1)}, f32[1,2048]{1,0:T(1,128)}, u32[]{:S(2)}) copy-start(f32[1,2048]{1,0:T(1,128)} %get-tuple-element.140) | copy-start | bytes 24580
  226.4 38.8 %copy-start.3 = (f32[256,2048]{1,0:T(8,128)S(1)}, f32[256,2048]{1,0:T(8,128)}, u32[]{:S(2)}) copy-start(f32[256,2048]{1,0:T(8,128)} %get-tuple-element.103.refs_12_) | copy-start | bytes 6291460
  264.4 3.1 copy-start.9
  264.4 3.1 copy-start.1
  264.4 3.1 copy-start.6
  264.4 17.3 %collective-permute-start.3 = (bf16[1,256,2048]{2,1,0:T(8,128)(2,1)}, bf16[1,256,2048]{2,1,0:T(8,128)(2,1)S(1)}, u32[]{:S(2)}, u32[]{:S(2)}) collective-permute-start(bf16[1,256,2048]{2,1,0:T(8,128)(2,1)} %bitcast.71), channel_id=1, source_target_pairs={{0,1},{1,0},{2,3},{3,2},{4,5},{5,4},{6,7},{7,6},{8,9},{9,8},{10,11... | collective-permute-start | bytes 3145736 | tf_op jit(solution)/shard_map/ppermute | solution.py:73
  273.4 8.3 %copy-start.10 = (f32[8,128]{1,0:T(8,128)S(1)}, f32[8,128]{1,0:T(8,128)}, u32[]{:S(2)}) copy-start(f32[8,128]{1,0:T(8,128)} %get-tuple-element.139) | copy-start | bytes 12292
  273.4 8.3 %copy-start.12 = (pred[8]{0:T(512)(128)(4,1)S(1)}, pred[8]{0:T(512)(128)(4,1)}, u32[]{:S(2)}) copy-start(pred[8]{0:T(512)(128)(4,1)} %constant.30.clone.1) | copy-start | bytes 28
  273.4 8.4 %copy-start.5 = (bf16[256,2048]{1,0:T(8,128)(2,1)S(1)}, bf16[256,2048]{1,0:T(8,128)(2,1)}, u32[]{:S(2)}) copy-start(bf16[256,2048]{1,0:T(8,128)(2,1)} %get-tuple-element.131) | copy-start | bytes 3145732
  282.7 1.6 copy-start.7
  282.7 2.8 copy-start.8
Sparse Core Ops, SparseCore 0:
  9.9 46.9 all-gather.2
  103.8 58.8 reduce-scatter.3
  165.0 63.0 reduce-scatter.5
  230.3 54.7 reduce-scatter.7

commit v6 on v5

--- a/solution.py
+++ b/solution.py
@@ -746,7 +746,9 @@
             here = pl.ds(pl.multiple_of(pair * width + i * HEAD_DIM, HEAD_DIM), HEAD_DIM)
             state = arriving[pair, i]
             state_out[pair * per_step + i] = state
-            mixed, head = finish_part(mix_all[pair * per_step + i], state, gain[...])
+            mixed, head = finish_part(
+                mix_all[pair * per_step + i], state, gain[...].astype(jnp.float32)
+            )
             mixed_out[:, here] = mixed
             head_out[:, here] = head
 
@@ -767,7 +769,9 @@
         halves.finish()
 
 
-def mixer_forward(pres, convs, logit, logit_t, live, gain, normed, per_step, spans, ways, number):
+def mixer_forward(
+    pres, convs, logit, logit_t, live, live_t, gain, normed, per_step, spans, ways, number
+):
     length, channels = pres[0].shape
     heads = channels // HEAD_DIM
     pairs = heads // per_step
@@ -835,7 +839,7 @@
             collective_id=number, has_side_effects=True, vmem_limit_bytes=VMEM
         ),
         cost_estimate=SHORT,
-    )(*pres, *convs, logit, logit_t, live, live.T, gain, *pres, normed)
+    )(*pres, *convs, logit, logit_t, live, live_t, gain, *pres, normed)
 
 
 def mixer_backward_kernel(per_step, taps, spans, ways, tokens, *refs):
@@ -903,7 +907,7 @@
         for i in range(per_step):
             d_out, mixed, q, k = head_columns((d_head, mixed_ref, q_one, k_one), i)
             d_mixed, d_fresh, d_end, gain_row = back_local_part(
-                d_out, mixed, gain[...], q, k, wy_one[i]
+                d_out, mixed, gain[...].astype(jnp.float32), q, k, wy_one[i]
             )
             d_mixed_all[step * per_step + i] = d_mixed
             d_fresh_all[step * per_step + i] = d_fresh
@@ -1169,9 +1173,9 @@
     )(*sources, d_logit, *weights, beta_weight.T, *sources, normed, *tokens)
 
 
-def project_kernel(tokens, first_gain, second_gain, q_w, k_w, v_w, beta_w, *refs):
+def project_kernel(lengths, tokens, first_gain, second_gain, q_w, k_w, v_w, beta_w, *refs):
     q_out, k_out, v_out, logit_out, logit_t_out, stream_out, normed_out, gains_out = refs[:8]
-    arriving, gains, gains_in, sends, receives = refs[8:]
+    live_out, live_t_out, arriving, gains, gains_in, sends, receives = refs[8:]
     step = pl.program_id(0)
     half = tokens.shape[1]
 
@@ -1199,6 +1203,10 @@
         ]
         for copy in copies:
             copy.start()
+        left = lengths[0] - lax.axis_index("seq") * tokens.shape[0]
+        for axis, out in ((0, live_out), (1, live_t_out)):
+            index = lax.broadcasted_iota(jnp.int32, out.shape, axis)
+            out[...] = jnp.where(index < left, 1.0, 0.0)
         stream_out[:, mine] = tokens[...]
         gains_out[:, mine] = gains[...]
         for copy in copies:
@@ -1219,7 +1227,7 @@
             out[...] = dot_low(normed_out[...], weight[...]).astype(jnp.bfloat16)
 
 
-def projected(tokens, first_gain, second_gain, weights, beta_weight, number):
+def projected(lengths, tokens, first_gain, second_gain, weights, beta_weight, number):
     length, half = tokens.shape
     width, channels = weights[0].shape
     heads = beta_weight.shape[1]
@@ -1234,15 +1242,16 @@
     return pl.pallas_call(
         project_kernel,
         grid=(6,),
-        in_specs=[whole(length, half)] + [whole(half // 128, 128)] * 2
+        in_specs=[pl.BlockSpec(memory_space=pltpu.SMEM), whole(length, half)]
+        + [whole(half // 128, 128)] * 2
         + [tiles(width, part) for part in range(3)]
         + [whole(heads, width)],
         out_specs=[tiles(length, part) for part in range(3)]
         + [whole(length, heads), whole(heads, length), whole(length, width)]
-        + [whole(length, width), whole(16, width)],
+        + [whole(length, width), whole(16, width), whole(length, 1), whole(1, length)],
         out_shape=[b16(length, channels)] * 3
         + [f32(length, heads), f32(heads, length), b16(length, width)]
-        + [b16(length, width), b16(16, width)],
+        + [b16(length, width), b16(16, width), f32(length, 1), f32(1, length)],
         scratch_shapes=[
             pltpu.VMEM((length, half), jnp.bfloat16),
             pltpu.VMEM((16, half), jnp.bfloat16),
@@ -1255,16 +1264,21 @@
         ),
         cost_estimate=SHORT,
     )(
-        tokens, first_gain.reshape(-1, 128), second_gain.reshape(-1, 128), *weights, beta_weight.T
+        lengths, tokens, first_gain.reshape(-1, 128), second_gain.reshape(-1, 128), *weights,
+        beta_weight.T,
     )
 
 
 def units_kernel(
     ways, steps, head_ref, out_w, stream_ref, gains, d_own, d_other, live, gate_w, up_w, down_w,
-    token,
-    turned_out, d_gate_out, d_up_out, hidden_out, stream_out, normed_out, own_out, others,
-    part_low, arriving, turned_hidden, d_ref, sends, receives, hidden_sends, hidden_receives,
+    plane, turned_out, d_gate_out, d_up_out, hidden_out, stream_out, normed_out, own_out, others,
+    plane_out, part_low, arriving, turned_hidden, d_ref, sends, receives, hidden_sends,
+    hidden_receives, plane_sems,
 ):
+    plane_copy = pltpu.make_async_remote_copy(
+        src_ref=plane, dst_ref=plane_out, send_sem=plane_sems.at[0], recv_sem=plane_sems.at[1],
+        device_id=place("head", 1 - lax.axis_index("head")), device_id_type=MESH,
+    )
     own = lax.axis_index("dp")
     tile = hidden_out.shape[1]
     part_rows = tile // ways
@@ -1302,6 +1316,7 @@
             copies.append(copy)
         core = lax.axis_index("head")
         half = d_own.shape[1]
+        plane_copy.start()
         for place_of, part in ((core, d_own), (1 - core, d_other)):
             masked = part[...].astype(jnp.float32) * live[...]
             here = pl.ds(pl.multiple_of(place_of * half, half), half)
@@ -1346,11 +1361,12 @@
         for index in range(steps):
             for by in range(1, ways):
                 hidden_copy(index, by).wait()
+        plane_copy.wait()
 
 
 def hidden_units(
     head_out, out_weight, stream, gains, d_own, d_other, live, gate_weight, up_weight,
-    down_weight, token, number,
+    down_weight, plane, number,
 ):
     ways = lax.axis_size("dp")
     length, width = stream.shape
@@ -1379,22 +1395,24 @@
         out_specs=[pl.BlockSpec((2, tile, length), lambda f: (0, f, 0))]
         + [flat] * 3
         + [whole] * 2
-        + [pl.BlockSpec((chunk, length), lambda f: (0, 0)), pl.BlockSpec(memory_space=pl.ANY)],
+        + [pl.BlockSpec((chunk, length), lambda f: (0, 0))]
+        + [pl.BlockSpec(memory_space=pl.ANY)] * 2,
         out_shape=[b16(2, units, length)]
         + [b16(length, units)] * 3
         + [f32(length, width), b16(length, width)]
-        + [b16(chunk, length), b16(ways - 1, chunk, length)],
+        + [b16(chunk, length), b16(ways - 1, chunk, length), b16(*plane.shape)],
         scratch_shapes=[pltpu.VMEM((4, length, width // 4), jnp.bfloat16)] * 2
         + [pltpu.VMEM((units, length), jnp.bfloat16), pltpu.VMEM((length, width), jnp.bfloat16)]
         + [pltpu.SemaphoreType.DMA((4,))] * 2
-        + [pltpu.SemaphoreType.DMA(((ways - 1) * (units // tile),))] * 2,
+        + [pltpu.SemaphoreType.DMA(((ways - 1) * (units // tile),))] * 2
+        + [pltpu.SemaphoreType.DMA((2,))],
         compiler_params=pltpu.CompilerParams(
             collective_id=number, has_side_effects=True, vmem_limit_bytes=VMEM
         ),
         cost_estimate=SHORT,
     )(
         head_out, out_weight, stream, gains, d_own, d_other, live, gate_weight, up_weight,
-        down_weight, token,
+        down_weight, plane,
     )
 
 
@@ -1931,8 +1949,10 @@
     fused = groups == 2
     weights = [query_weight, key_weight, value_weight]
     if fused:
-        *pres, beta_logit, logit_turned, gathered, normed_one, gains = projected(
-            tokens_in[0], first_gain, second_gain, weights, beta_weight, 7
+        (
+            *pres, beta_logit, logit_turned, gathered, normed_one, gains, live_col, live_row,
+        ) = projected(
+            lengths, tokens_in[0], first_gain, second_gain, weights, beta_weight, 7
         )
         upstream_other = swapped(upstream[0])
         upstream_other, beta_logit = lax.optimization_barrier((upstream_other, beta_logit))
@@ -1977,16 +1997,16 @@
     scale_one = inverse_rms(stream_full)
     normed_one = normed_one[None]
     convs = [query_conv, key_conv, value_conv]
-    live_col = live_mask[0][:, None]
-    head_gain = mixer_gain.astype(jnp.float32)[None, :]
+    if not fused:
+        live_col = live_mask[0][:, None]
+    head_gain = mixer_gain[None, :] if fused else mixer_gain.astype(jnp.float32)[None, :]
     if fused:
         (
             query, key, value, wy, inverse, ends, mixed, head_out, entering, rims, one_near,
         ) = mixer_forward(
-            pres, convs, beta_logit, logit_turned, live_col, head_gain, normed_one[0],
+            pres, convs, beta_logit, logit_turned, live_col, live_row, head_gain, normed_one[0],
             per_step, spans, ways, 1,
         )
-        half_up, mixed = lax.optimization_barrier((half_up, mixed))
     else:
         rims = passed_along(jnp.stack([pre[local_len - RIM :, :] for pre in pres]), "seq", 1)
         rims = [rims[0], rims[1], rims[2]]
@@ -1999,6 +2019,7 @@
     if fused:
         (
             turned, d_gate, d_up, hidden, stream_mid, normed_two, own_hidden, hidden_others,
+            other_up,
         ) = hidden_units(
             head_out[0], output_weight, gathered, gains, upstream[0], upstream_other, live_col,
             gate_weight, up_weight, down_weight, half_up, 8,
@@ -2058,7 +2079,7 @@
             for by in range(ways - 1)
         ]
         down_raw = raw_piece(
-            [hidden_slots], units, halves_of(half_up, swapped(half_up)), True
+            [hidden_slots], units, halves_of(half_up, other_up), True
         )
         feed_part, d_stream, residual, d_head_out, second_row, d_others, two_others = feed_back(
             d_gate, d_up, hidden, [gate_weight, up_weight, down_weight], upstream[0],

time: 385 us -> 383 us (level)
  transfers between devices with their start and end apart: 8 -> 7, of which waited for: 1 -> 1; matrix products, arithmetic and copies ran while one was open for 2% -> 2% of each run, Pallas kernels for 66% -> 57%
where the time goes in v6:
time: 383 us; the launch traced here: 381 us
  Pallas kernels  351 us (92%)
  between operations  14.8 us (4%)
  other arithmetic  5.84 us (2%)
  waiting for transfers between devices  5.77 us (2%)
    pallas_call x1, Pallas kernels, finished_gradients(): pl.pallas_call(functools.partial(finish_kernel, spans, ways, fed, split),...  86.3 us
    pallas_call x1, Pallas kernels, mixer_backward(): pl.pallas_call(functools.partial(mixer_backward_kernel, per_step, taps, s...  55 us
    pallas_call x1, Pallas kernels, feed_back(): pl.pallas_call(functools.partial(feed_back_kernel, ways, entries), grid=(...  48.1 us
    pallas_call x1, Pallas kernels, back_projection(): pl.pallas_call(functools.partial(back_projection_kernel, ways), grid=(wid...  37.9 us
    pallas_call x5, Pallas kernels, span_pieces(): pl.pallas_call(functools.partial(pieces_kernel, groups, slots, ways, turn...  37.1 us
    pallas_call x1, Pallas kernels, hidden_units(): pl.pallas_call(functools.partial(units_kernel, ways, units // tile), grid...  34.6 us
    pallas_call x1, Pallas kernels, mixer_forward(): pl.pallas_call(functools.partial(mixer_forward_kernel, per_step, taps, sp...  32.9 us
    pallas_call x1, Pallas kernels, projected(): pl.pallas_call(project_kernel, grid=(6,), in_specs=[pl.BlockSpec(memory_s...  14.3 us
  transfers between devices with their start and end apart: 7, of which 1 were waited for; matrix products, arithmetic and copies ran while one was open for 2% of the time, Pallas kernels for 57%

profile of v6, /device:TPU:0, one launch (start us, length us, event | category | flops | bytes accessed | tf_op | source)
XLA Modules:
  0.0 380.8 jit_solution(5528598188515964209)
XLA Ops:
  7.2 0.0 all-gather.3.cloned.1.call-start
  7.2 0.7 all-gather.3.cloned.1.call-update
  7.9 0.0 reduce-scatter.4.cloned.1.call-start
  8.0 0.5 collective-permute-start
  9.1 14.3 %shard_map.288 = (bf16[256,1024]{1,0:T(8,128)(2,1)}, bf16[256,1024]{1,0:T(8,128)(2,1)}, bf16[256,1024]{1,0:T(8,128)(2,1)}, f32[256,8]{1,0:T(8,128)}, f32[8,256]{...) custom-call(s32[1]{0:T(128)S(6)} %copy.37.lengths, ...), custom_call_target="tpu_custom_call" | custom-call | tf_op jit(solution)/shard_map/pallas_call | solution.py:1242
  23.4 32.9 %shard_map.289 = (bf16[256,1024]{1,0:T(8,128)(2,1)}, bf16[256,1024]{1,0:T(8,128)(2,1)}, bf16[256,1024]{1,0:T(8,128)(2,1)}, f32[8,256,256]{2,1,0:T(8,128)}, f32[8...) custom-call(bf16[256,1024]{1,0:T(8,128)(2,1)} %get-tuple-element.91., ...), custom_call_target="tpu_custom_call" | custom-call | tf_op jit(solution)/shard_map/pallas_call | solution.py:796
  56.4 0.0 all-gather.3.cloned.1.call-done
  56.4 34.6 %shard_map.290 = (bf16[2,2816,256]{2,1,0:T(8,128)(2,1)}, bf16[256,2816]{1,0:T(8,128)(2,1)}, bf16[256,2816]{1,0:T(8,128)(2,1)}, bf16[256,2816]{1,0:T(8,128)(2,1)}...) custom-call(bf16[256,1024]{1,0:T(8,128)(2,1)} %get-tuple-element.100, ...), custom_call_target="tpu_custom_call" | custom-call | tf_op jit(solution)/shard_map/pallas_call | solution.py:1380
  91.0 7.9 %shard_map.291.refs_14_ = bf16[4,704,512]{2,1,0:T(8,128)(2,1)} custom-call(s32[1]{0:T(128)} %bitcast.9.at, bf16[704,256]{1,0:T(8,128)(2,1)} %get-tuple-element.110.refs_0_, bf16[3,704,256]{2,1,0:T(8,128)(2,1)} %get-tuple-element.111.refs_1_.refs_2_.refs_3_, bf16[3,704,256]{2,1,0:T(8,128)(2,1)} %get-tuple-element.111.refs_1_.refs_2_.refs_3_, ...), custom_call_target="tpu_custom_call" | custom-call | tf_op jit(solution)/shard_map/pallas_call | solution.py:1590
  99.0 0.2 reduce-scatter.6.cloned.1.call-start
  99.2 48.1 %shard_map.292 = (bf16[256,2048]{1,0:T(8,128)(2,1)}, f32[256,2048]{1,0:T(8,128)}, bf16[256,2048]{1,0:T(8,128)(2,1)}, f32[256,1024]{1,0:T(8,128)}, f32[1,2048]{1,...) custom-call(bf16[256,2816]{1,0:T(8,128)(2,1)} %get-tuple-element.105.refs_0_, ...), custom_call_target="tpu_custom_call" | custom-call | tf_op jit(solution)/shard_map/pallas_call | solution.py:1516
  147.3 7.7 %shard_map.293.refs_22_ = bf16[4,704,512]{2,1,0:T(8,128)(2,1)} custom-call(s32[1]{0:T(128)} %bitcast.9.at, bf16[2,4,704,256]{3,2,1,0:T(8,128)(2,1)} %bitcast.54, bf16[3,1,704,256]{3,2,1,0:T(8,128)(2,1)} %get-tuple-element.125.refs_1_.refs_2_.refs_3_, bf16[3,1,704,256]{3,2,1,0:T(8,128)(2,1)} %get-tuple-element.125.refs_1_.refs_2_.refs_3_, ...), custom_call_target="tpu_custom_call" | custom-call | tf_op jit(solution)/shard_map/pallas_call | solution.py:1590
  155.0 0.0 reduce-scatter.8.cloned.1.call-start
  155.1 5.0 %reduce-scatter.4.cloned.1.call-done = bf16[1,704,512]{2,1,0:T(8,128)(2,1)} async-done(((bf16[4,704,512]{2,1,0:T(8,128)(2,1)}), bf16[1,704,512]{2,1,0:T(8,128)(2,1)}) %reduce-scatter.4.cloned.1.call-update) | async-done | bytes 720912 | tf_op jit(solution)/shard_map/reduce_scatter | solution.py:1987
  160.0 55.0 %shard_map.294 = (bf16[256,1024]{1,0:T(8,128)(2,1)}, bf16[256,1024]{1,0:T(8,128)(2,1)}, bf16[256,1024]{1,0:T(8,128)(2,1)}, f32[3,4,1024]{2,1,0:T(4,128)}, f32[25...) custom-call(f32[256,1024]{1,0:T(8,128)} %get-tuple-element.115.refs_, ...), custom_call_target="tpu_custom_call" | custom-call | tf_op jit(solution)/shard_map/pallas_call | solution.py:1017
  215.1 7.7 %shard_map.295.refs_12_ = bf16[4,704,512]{2,1,0:T(8,128)(2,1)} custom-call(s32[1]{0:T(128)} %bitcast.9.at, bf16[2,4,704,256]{3,2,1,0:T(8,128)(2,1)} %bitcast.56, bf16[3,1,704,256]{3,2,1,0:T(8,128)(2,1)} %get-tuple-element.132.refs_1_.refs_2_.refs_3_, bf16[3,1,704,256]{3,2,1,0:T(8,128)(2,1)} %get-tuple-element.132.refs_1_.refs_2_.refs_3_, ...), custom_call_target="tpu_custom_call" | custom-call | tf_op jit(solution)/shard_map/pallas_call | solution.py:1590
  222.9 0.4 collective-permute-start.1
  223.2 0.8 slice_convert_fusion
  224.0 37.9 %shard_map.296 = (bf16[256,2048]{1,0:T(8,128)(2,1)}, bf16[3,256,256]{2,1,0:T(8,128)(2,1)}, bf16[3,256,256]{2,1,0:T(8,128)(2,1)}, bf16[3,256,256]{2,1,0:T(8,128)(2,1)}, bf16[1,256,2048]{2,1,0:T(8,128)(2,1)}) custom-call(bf16[256,1024]{1,0:T(8,128)(2,1)} %get-tuple-element.128.refs_0_.refs_8_, bf16[256,1024]{1,0:T(8,128)(2,1)} %get-tuple-element.129.refs_1_.refs_9_.refs_4_, ...), custom_call_target="tpu_custom_call" | custom-call | tf_op jit(solution)/shard_map/pallas_call | solution.py:1155
  262.0 0.4 collective-permute-start.2
  262.4 0.3 fusion.5
  262.8 2.2 fusion.10
  265.0 0.3 fusion.11
  265.4 5.5 %shard_map.297.refs_28_.refs_0_ = bf16[4,256,512]{2,1,0:T(8,128)(2,1)} custom-call(s32[1]{0:T(128)} %bitcast.9.at, bf16[256,1024]{1,0:T(8,128)(2,1)} %get-tuple-element.100.head_ref.refs_24_.refs_0_, bf16[3,256,256]{2,1,0:T(8,128)(2,1)} %get-tuple-element.134.refs_1_.refs_2_.refs_3_, bf16[3,256,256]{2,1,0:T(8,128)(2,1)} %get-tuple-element.134.refs_1_.refs_2_.refs_3_, ...), custom_call_target="tpu_custom_call" | custom-call | tf_op jit(solution)/shard_map/pallas_call | solution.py:1590
  270.9 8.3 %shard_map.298.refs_1_ = bf16[4,768,512]{2,1,0:T(8,128)(2,1)} custom-call(s32[1]{0:T(128)} %bitcast.9.at, bf16[256,1024]{1,0:T(8,128)(2,1)} %get-tuple-element.128.refs_0_.refs_8_, bf16[3,256,256]{2,1,0:T(8,128)(2,1)} %get-tuple-element.136.refs_1_.refs_2_.refs_3_, bf16[3,256,256]{2,1,0:T(8,128)(2,1)} %get-tuple-element.136.refs_1_.refs_2_.refs_3_, ...), custom_call_target="tpu_custom_call" | custom-call | tf_op jit(solution)/shard_map/pallas_call | solution.py:1590
  279.2 0.1 constant_dynamic-update-slice_fusion.4
  279.3 0.9 fusion.4
  280.3 0.4 fusion.9
  280.7 1.1 copy-done.6
  281.8 1.2 dynamic-slice_subtract_fusion
  283.0 86.3 %shard_map.299 = (bf16[2816,128]{1,0:T(8,128)(2,1)}, bf16[2816,128]{1,0:T(8,128)(2,1)}, bf16[2816,128]{1,0:T(8,128)(2,1)}, bf16[1024,128]{1,0:T(8,128)(2,1)}, bf...) custom-call(bf16[4,256,512]{2,1,0:T(8,128)(2,1)} %shard_map.297.refs_28_.re, ...), custom_call_target="tpu_custom_call" | custom-call | tf_op jit(solution)/shard_map/pallas_call | solution.py:1898
  369.3 4.9 %shard_map.300 = (f32[2816,128]{1,0:T(8,128)}, f32[128,2816]{1,0:T(8,128)}, f32[128,2816]{1,0:T(8,128)}, f32[1024,128]{1,0:T(8,128)}, f32[128,1024]{1,0:T(8,128)...) custom-call(bf16[2816,128]{1,0:T(8,128)(2,1)} %get-tuple-element.144, ...), custom_call_target="tpu_custom_call" | custom-call | tf_op jit(solution)/shard_map/pallas_call | solution.py:1653
  (41 shorter events, 0.2 us)
Async XLA Ops:
  7.2 49.2 %all-gather.3.cloned.1.call-start = ((), (), s32[]{:S(2)}) async-start(), calls=%async_computation.6 | async-start | bytes 2621440 | tf_op jit(solution)/shard_map/all_gather | solution.py:1967
  7.9 152.1 %reduce-scatter.4.cloned.1.call-start = ((), (), s32[]{:S(2)}) async-start(), calls=%async_computation.3 | async-start | bytes 3604480 | tf_op jit(solution)/shard_map/reduce_scatter | solution.py:1987
  8.0 15.4 %collective-permute-start = (bf16[256,1024]{1,0:T(8,128)(2,1)}, bf16[256,1024]{1,0:T(8,128)(2,1)S(1)}, u32[]{:S(2)}, u32[]{:S(2)}) collective-permute-start(bf16[256,1024]{1,0:T(8,128)(2,1)} %bitcast.57), channel_id=1, source_target_pairs={{0,1},{1,0},{2,3},{3,2},{4,5},{5,4},{6,7},{7,6},{8,9},{9,8},{10,11... | collective-permute-start | bytes 1572872 | tf_op jit(solution)/shard_map/ppermute | solution.py:67
  23.4 33.0 %copy-start.3 = (bf16[256,1024]{1,0:T(8,128)(2,1)}, bf16[256,1024]{1,0:T(8,128)(2,1)S(1)}, u32[]{:S(2)}) copy-start(bf16[256,1024]{1,0:T(8,128)(2,1)S(1)} %collective-permute-done.d_other.refs_7_) | copy-start | bytes 1572868
  99.0 166.4 %reduce-scatter.6.cloned.1.call-start = ((), (), s32[]{:S(2)}) async-start(), calls=%async_computation.4 | async-start | bytes 3604480 | tf_op jit(solution)/shard_map/reduce_scatter | solution.py:1987
  155.0 128.0 %reduce-scatter.8.cloned.1.call-start = ((), (), s32[]{:S(2)}) async-start(), calls=%async_computation.5 | async-start | bytes 3604480 | tf_op jit(solution)/shard_map/reduce_scatter | solution.py:1987
  222.9 39.9 %collective-permute-start.1 = (bf16[1,256,2048]{2,1,0:T(8,128)(2,1)}, bf16[1,256,2048]{2,1,0:T(8,128)(2,1)}, u32[]{:S(2)}, u32[]{:S(2)}) collective-permute-start(bf16[1,256,2048]{2,1,0:T(8,128)(2,1)} %bitcast.10), channel_id=1, source_target_pairs={{0,1},{1,0},{2,3},{3,2},{4,5},{5,4},{6,7},{7,6},{8,9},{9,8},{10,11... | collective-permute-start | bytes 3145736 | tf_op jit(solution)/shard_map/ppermute | solution.py:73
  224.0 38.4 %copy-start.1 = (bf16[256,2048]{1,0:T(8,128)(2,1)S(1)}, bf16[256,2048]{1,0:T(8,128)(2,1)}, u32[]{:S(2)}) copy-start(bf16[256,2048]{1,0:T(8,128)(2,1)} %get-tuple-element.101.stream_ref) | copy-start | bytes 3145732
  224.0 38.7 %copy-start.10 = (f32[1,2048]{1,0:T(1,128)S(1)}, f32[1,2048]{1,0:T(1,128)}, u32[]{:S(2)}) copy-start(f32[1,2048]{1,0:T(1,128)} %get-tuple-element.142) | copy-start | bytes 24580
  224.0 38.8 %copy-start.2 = (f32[256,2048]{1,0:T(8,128)S(1)}, f32[256,2048]{1,0:T(8,128)}, u32[]{:S(2)}) copy-start(f32[256,2048]{1,0:T(8,128)} %get-tuple-element.104.refs_12_) | copy-start | bytes 6291460
  261.9 3.1 copy-start.8
  262.0 3.1 copy-start
  262.0 3.1 copy-start.5
  262.0 17.3 %collective-permute-start.2 = (bf16[1,256,2048]{2,1,0:T(8,128)(2,1)}, bf16[1,256,2048]{2,1,0:T(8,128)(2,1)S(1)}, u32[]{:S(2)}, u32[]{:S(2)}) collective-permute-start(bf16[1,256,2048]{2,1,0:T(8,128)(2,1)} %bitcast.65), channel_id=1, source_target_pairs={{0,1},{1,0},{2,3},{3,2},{4,5},{5,4},{6,7},{7,6},{8,9},{9,8},{10,11... | collective-permute-start | bytes 3145736 | tf_op jit(solution)/shard_map/ppermute | solution.py:73
  270.9 8.3 %copy-start.9 = (f32[8,128]{1,0:T(8,128)S(1)}, f32[8,128]{1,0:T(8,128)}, u32[]{:S(2)}) copy-start(f32[8,128]{1,0:T(8,128)} %get-tuple-element.141) | copy-start | bytes 12292
  270.9 8.3 %copy-start.11 = (pred[8]{0:T(512)(128)(4,1)S(1)}, pred[8]{0:T(512)(128)(4,1)}, u32[]{:S(2)}) copy-start(pred[8]{0:T(512)(128)(4,1)} %constant.26.clone.1) | copy-start | bytes 28
  270.9 8.4 %copy-start.4 = (bf16[256,2048]{1,0:T(8,128)(2,1)S(1)}, bf16[256,2048]{1,0:T(8,128)(2,1)}, u32[]{:S(2)}) copy-start(bf16[256,2048]{1,0:T(8,128)(2,1)} %get-tuple-element.133) | copy-start | bytes 3145732
  280.2 1.6 copy-start.6
  280.2 2.8 copy-start.7
Sparse Core Ops, SparseCore 0:
  9.9 45.2 all-gather.2
  99.1 60.9 reduce-scatter.3
  162.4 63.0 reduce-scatter.5
  227.6 54.9 reduce-scatter.7

commit v7 on v6

--- a/solution.py
+++ b/solution.py
@@ -1273,7 +1273,7 @@
     ways, steps, head_ref, out_w, stream_ref, gains, d_own, d_other, live, gate_w, up_w, down_w,
     plane, turned_out, d_gate_out, d_up_out, hidden_out, stream_out, normed_out, own_out, others,
     plane_out, part_low, arriving, turned_hidden, d_ref, sends, receives, hidden_sends,
-    hidden_receives, plane_sems,
+    hidden_receives, plane_sems, out_tiles, load_sems,
 ):
     plane_copy = pltpu.make_async_remote_copy(
         src_ref=plane, dst_ref=plane_out, send_sem=plane_sems.at[0], recv_sem=plane_sems.at[1],
@@ -1300,13 +1300,24 @@
     @pl.when(pl.program_id(0) == 0)
     def _():
         other = place("head", 1 - lax.axis_index("head"))
+        block = out_tiles.shape[2]
+        loads = [
+            pltpu.make_async_copy(
+                out_w.at[:, index * block : (index + 1) * block],
+                out_tiles.at[index],
+                load_sems.at[index],
+            )
+            for index in range(out_tiles.shape[0])
+        ]
+        for load in loads:
+            load.start()
         meet([other] + [place("dp", partner(own, by)) for by in range(1, ways)])
         pieces = part_low.shape[0]
         width = part_low.shape[2]
         copies = []
         for piece in range(pieces):
-            span = slice(piece * width, (piece + 1) * width)
-            part_low[piece] = dot_low(head_ref[...], out_w[:, span]).astype(jnp.bfloat16)
+            loads[piece].wait()
+            part_low[piece] = dot_low(head_ref[...], out_tiles[piece]).astype(jnp.bfloat16)
             copy = pltpu.make_async_remote_copy(
                 src_ref=part_low.at[piece], dst_ref=arriving.at[piece],
                 send_sem=sends.at[piece], recv_sem=receives.at[piece],
@@ -1382,7 +1393,7 @@
         grid=(units // tile,),
         in_specs=[
             pl.BlockSpec((length, channels), lambda f: (0, 0)),
-            pl.BlockSpec((channels, width), lambda f: (0, 0)),
+            pl.BlockSpec(memory_space=pl.ANY),
             whole,
             pl.BlockSpec((16, width), lambda f: (0, 0)),
             pl.BlockSpec((length, width // 2), lambda f: (0, 0)),
@@ -1405,7 +1416,8 @@
         + [pltpu.VMEM((units, length), jnp.bfloat16), pltpu.VMEM((length, width), jnp.bfloat16)]
         + [pltpu.SemaphoreType.DMA((4,))] * 2
         + [pltpu.SemaphoreType.DMA(((ways - 1) * (units // tile),))] * 2
-        + [pltpu.SemaphoreType.DMA((2,))],
+        + [pltpu.SemaphoreType.DMA((2,))]
+        + [pltpu.VMEM((4, channels, width // 4), jnp.bfloat16), pltpu.SemaphoreType.DMA((4,))],
         compiler_params=pltpu.CompilerParams(
             collective_id=number, has_side_effects=True, vmem_limit_bytes=VMEM
         ),

time: 383 us -> 382 us (level)
  no operation moved by 1% of the time
where the time goes in v7:
time: 382 us; the launch traced here: 380 us
  Pallas kernels  350 us (92%)
  between operations  14.8 us (4%)
  other arithmetic  5.84 us (2%)
  waiting for transfers between devices  5.77 us (2%)
    pallas_call x1, Pallas kernels, finished_gradients(): pl.pallas_call(functools.partial(finish_kernel, spans, ways, fed, split),...  86.3 us
    pallas_call x1, Pallas kernels, mixer_backward(): pl.pallas_call(functools.partial(mixer_backward_kernel, per_step, taps, s...  55 us
    pallas_call x1, Pallas kernels, feed_back(): pl.pallas_call(functools.partial(feed_back_kernel, ways, entries), grid=(...  48.1 us
    pallas_call x1, Pallas kernels, back_projection(): pl.pallas_call(functools.partial(back_projection_kernel, ways), grid=(wid...  37.9 us
    pallas_call x5, Pallas kernels, span_pieces(): pl.pallas_call(functools.partial(pieces_kernel, groups, slots, ways, turn...  37.1 us
    pallas_call x1, Pallas kernels, hidden_units(): pl.pallas_call(functools.partial(units_kernel, ways, units // tile), grid...  33.5 us
    pallas_call x1, Pallas kernels, mixer_forward(): pl.pallas_call(functools.partial(mixer_forward_kernel, per_step, taps, sp...  32.9 us
    pallas_call x1, Pallas kernels, projected(): pl.pallas_call(project_kernel, grid=(6,), in_specs=[pl.BlockSpec(memory_s...  14.3 us
  transfers between devices with their start and end apart: 7, of which 1 were waited for; matrix products, arithmetic and copies ran while one was open for 2% of the time, Pallas kernels for 57%

profile of v7, /device:TPU:0, one launch (start us, length us, event | category | flops | bytes accessed | tf_op | source)
XLA Modules:
  0.0 379.7 jit_solution(2168098717100612334)
XLA Ops:
  7.2 0.0 all-gather.3.cloned.1.call-start
  7.2 0.7 all-gather.3.cloned.1.call-update
  7.9 0.0 reduce-scatter.4.cloned.1.call-start
  8.0 0.5 collective-permute-start
  9.1 14.3 %shard_map.288 = (bf16[256,1024]{1,0:T(8,128)(2,1)}, bf16[256,1024]{1,0:T(8,128)(2,1)}, bf16[256,1024]{1,0:T(8,128)(2,1)}, f32[256,8]{1,0:T(8,128)}, f32[8,256]{...) custom-call(s32[1]{0:T(128)S(6)} %copy.37.lengths, ...), custom_call_target="tpu_custom_call" | custom-call | tf_op jit(solution)/shard_map/pallas_call | solution.py:1242
  23.4 32.9 %shard_map.289 = (bf16[256,1024]{1,0:T(8,128)(2,1)}, bf16[256,1024]{1,0:T(8,128)(2,1)}, bf16[256,1024]{1,0:T(8,128)(2,1)}, f32[8,256,256]{2,1,0:T(8,128)}, f32[8...) custom-call(bf16[256,1024]{1,0:T(8,128)(2,1)} %get-tuple-element.91., ...), custom_call_target="tpu_custom_call" | custom-call | tf_op jit(solution)/shard_map/pallas_call | solution.py:796
  56.4 0.0 all-gather.3.cloned.1.call-done
  56.4 33.5 %shard_map.290 = (bf16[2,2816,256]{2,1,0:T(8,128)(2,1)}, bf16[256,2816]{1,0:T(8,128)(2,1)}, bf16[256,2816]{1,0:T(8,128)(2,1)}, bf16[256,2816]{1,0:T(8,128)(2,1)}...) custom-call(bf16[256,1024]{1,0:T(8,128)(2,1)} %get-tuple-element.100, ...), custom_call_target="tpu_custom_call" | custom-call | tf_op jit(solution)/shard_map/pallas_call | solution.py:1391
  89.9 7.9 %shard_map.291.refs_14_ = bf16[4,704,512]{2,1,0:T(8,128)(2,1)} custom-call(s32[1]{0:T(128)} %bitcast.9.at, bf16[704,256]{1,0:T(8,128)(2,1)} %get-tuple-element.110.refs_0_, bf16[3,704,256]{2,1,0:T(8,128)(2,1)} %get-tuple-element.111.refs_1_.refs_2_.refs_3_, bf16[3,704,256]{2,1,0:T(8,128)(2,1)} %get-tuple-element.111.refs_1_.refs_2_.refs_3_, ...), custom_call_target="tpu_custom_call" | custom-call | tf_op jit(solution)/shard_map/pallas_call | solution.py:1602
  97.9 0.2 reduce-scatter.6.cloned.1.call-start
  98.1 48.1 %shard_map.292 = (bf16[256,2048]{1,0:T(8,128)(2,1)}, f32[256,2048]{1,0:T(8,128)}, bf16[256,2048]{1,0:T(8,128)(2,1)}, f32[256,1024]{1,0:T(8,128)}, f32[1,2048]{1,...) custom-call(bf16[256,2816]{1,0:T(8,128)(2,1)} %get-tuple-element.105.refs_0_, ...), custom_call_target="tpu_custom_call" | custom-call | tf_op jit(solution)/shard_map/pallas_call | solution.py:1528
  146.2 7.6 %shard_map.293.refs_22_ = bf16[4,704,512]{2,1,0:T(8,128)(2,1)} custom-call(s32[1]{0:T(128)} %bitcast.9.at, bf16[2,4,704,256]{3,2,1,0:T(8,128)(2,1)} %bitcast.54, bf16[3,1,704,256]{3,2,1,0:T(8,128)(2,1)} %get-tuple-element.125.refs_1_.refs_2_.refs_3_, bf16[3,1,704,256]{3,2,1,0:T(8,128)(2,1)} %get-tuple-element.125.refs_1_.refs_2_.refs_3_, ...), custom_call_target="tpu_custom_call" | custom-call | tf_op jit(solution)/shard_map/pallas_call | solution.py:1602
  153.9 0.0 reduce-scatter.8.cloned.1.call-start
  153.9 5.0 %reduce-scatter.4.cloned.1.call-done = bf16[1,704,512]{2,1,0:T(8,128)(2,1)} async-done(((bf16[4,704,512]{2,1,0:T(8,128)(2,1)}), bf16[1,704,512]{2,1,0:T(8,128)(2,1)}) %reduce-scatter.4.cloned.1.call-update) | async-done | bytes 720912 | tf_op jit(solution)/shard_map/reduce_scatter | solution.py:1999
  158.9 55.0 %shard_map.294 = (bf16[256,1024]{1,0:T(8,128)(2,1)}, bf16[256,1024]{1,0:T(8,128)(2,1)}, bf16[256,1024]{1,0:T(8,128)(2,1)}, f32[3,4,1024]{2,1,0:T(4,128)}, f32[25...) custom-call(f32[256,1024]{1,0:T(8,128)} %get-tuple-element.115.refs_, ...), custom_call_target="tpu_custom_call" | custom-call | tf_op jit(solution)/shard_map/pallas_call | solution.py:1017
  213.9 7.7 %shard_map.295.refs_12_ = bf16[4,704,512]{2,1,0:T(8,128)(2,1)} custom-call(s32[1]{0:T(128)} %bitcast.9.at, bf16[2,4,704,256]{3,2,1,0:T(8,128)(2,1)} %bitcast.56, bf16[3,1,704,256]{3,2,1,0:T(8,128)(2,1)} %get-tuple-element.132.refs_1_.refs_2_.refs_3_, bf16[3,1,704,256]{3,2,1,0:T(8,128)(2,1)} %get-tuple-element.132.refs_1_.refs_2_.refs_3_, ...), custom_call_target="tpu_custom_call" | custom-call | tf_op jit(solution)/shard_map/pallas_call | solution.py:1602
  221.7 0.4 collective-permute-start.1
  222.1 0.8 slice_convert_fusion
  222.9 37.9 %shard_map.296 = (bf16[256,2048]{1,0:T(8,128)(2,1)}, bf16[3,256,256]{2,1,0:T(8,128)(2,1)}, bf16[3,256,256]{2,1,0:T(8,128)(2,1)}, bf16[3,256,256]{2,1,0:T(8,128)(2,1)}, bf16[1,256,2048]{2,1,0:T(8,128)(2,1)}) custom-call(bf16[256,1024]{1,0:T(8,128)(2,1)} %get-tuple-element.128.refs_0_.refs_8_, bf16[256,1024]{1,0:T(8,128)(2,1)} %get-tuple-element.129.refs_1_.refs_9_.refs_4_, ...), custom_call_target="tpu_custom_call" | custom-call | tf_op jit(solution)/shard_map/pallas_call | solution.py:1155
  260.8 0.4 collective-permute-start.2
  261.3 0.3 fusion.5
  261.6 2.2 fusion.10
  263.9 0.3 fusion.11
  264.2 5.5 %shard_map.297.refs_28_.refs_0_ = bf16[4,256,512]{2,1,0:T(8,128)(2,1)} custom-call(s32[1]{0:T(128)} %bitcast.9.at, bf16[256,1024]{1,0:T(8,128)(2,1)} %get-tuple-element.100.head_ref.refs_24_.refs_0_, bf16[3,256,256]{2,1,0:T(8,128)(2,1)} %get-tuple-element.134.refs_1_.refs_2_.refs_3_, bf16[3,256,256]{2,1,0:T(8,128)(2,1)} %get-tuple-element.134.refs_1_.refs_2_.refs_3_, ...), custom_call_target="tpu_custom_call" | custom-call | tf_op jit(solution)/shard_map/pallas_call | solution.py:1602
  269.8 8.3 %shard_map.298.refs_1_ = bf16[4,768,512]{2,1,0:T(8,128)(2,1)} custom-call(s32[1]{0:T(128)} %bitcast.9.at, bf16[256,1024]{1,0:T(8,128)(2,1)} %get-tuple-element.128.refs_0_.refs_8_, bf16[3,256,256]{2,1,0:T(8,128)(2,1)} %get-tuple-element.136.refs_1_.refs_2_.refs_3_, bf16[3,256,256]{2,1,0:T(8,128)(2,1)} %get-tuple-element.136.refs_1_.refs_2_.refs_3_, ...), custom_call_target="tpu_custom_call" | custom-call | tf_op jit(solution)/shard_map/pallas_call | solution.py:1602
  278.1 0.1 constant_dynamic-update-slice_fusion.4
  278.2 0.9 fusion.4
  279.1 0.4 fusion.9
  279.5 1.1 copy-done.6
  280.7 1.2 dynamic-slice_subtract_fusion
  281.9 86.3 %shard_map.299 = (bf16[2816,128]{1,0:T(8,128)(2,1)}, bf16[2816,128]{1,0:T(8,128)(2,1)}, bf16[2816,128]{1,0:T(8,128)(2,1)}, bf16[1024,128]{1,0:T(8,128)(2,1)}, bf...) custom-call(bf16[4,256,512]{2,1,0:T(8,128)(2,1)} %shard_map.297.refs_28_.re, ...), custom_call_target="tpu_custom_call" | custom-call | tf_op jit(solution)/shard_map/pallas_call | solution.py:1910
  368.2 4.9 %shard_map.300 = (f32[2816,128]{1,0:T(8,128)}, f32[128,2816]{1,0:T(8,128)}, f32[128,2816]{1,0:T(8,128)}, f32[1024,128]{1,0:T(8,128)}, f32[128,1024]{1,0:T(8,128)...) custom-call(bf16[2816,128]{1,0:T(8,128)(2,1)} %get-tuple-element.144, ...), custom_call_target="tpu_custom_call" | custom-call | tf_op jit(solution)/shard_map/pallas_call | solution.py:1665
  (41 shorter events, 0.2 us)
Async XLA Ops:
  7.2 49.2 %all-gather.3.cloned.1.call-start = ((), (), s32[]{:S(2)}) async-start(), calls=%async_computation.6 | async-start | bytes 2621440 | tf_op jit(solution)/shard_map/all_gather | solution.py:1979
  7.9 151.0 %reduce-scatter.4.cloned.1.call-start = ((), (), s32[]{:S(2)}) async-start(), calls=%async_computation.3 | async-start | bytes 3604480 | tf_op jit(solution)/shard_map/reduce_scatter | solution.py:1999
  8.0 15.4 %collective-permute-start = (bf16[256,1024]{1,0:T(8,128)(2,1)}, bf16[256,1024]{1,0:T(8,128)(2,1)S(1)}, u32[]{:S(2)}, u32[]{:S(2)}) collective-permute-start(bf16[256,1024]{1,0:T(8,128)(2,1)} %bitcast.57), channel_id=1, source_target_pairs={{0,1},{1,0},{2,3},{3,2},{4,5},{5,4},{6,7},{7,6},{8,9},{9,8},{10,11... | collective-permute-start | bytes 1572872 | tf_op jit(solution)/shard_map/ppermute | solution.py:67
  23.4 33.0 %copy-start.3 = (bf16[256,1024]{1,0:T(8,128)(2,1)}, bf16[256,1024]{1,0:T(8,128)(2,1)S(1)}, u32[]{:S(2)}) copy-start(bf16[256,1024]{1,0:T(8,128)(2,1)S(1)} %collective-permute-done.d_other.refs_7_) | copy-start | bytes 1572868
  97.9 166.4 %reduce-scatter.6.cloned.1.call-start = ((), (), s32[]{:S(2)}) async-start(), calls=%async_computation.4 | async-start | bytes 3604480 | tf_op jit(solution)/shard_map/reduce_scatter | solution.py:1999
  153.9 128.0 %reduce-scatter.8.cloned.1.call-start = ((), (), s32[]{:S(2)}) async-start(), calls=%async_computation.5 | async-start | bytes 3604480 | tf_op jit(solution)/shard_map/reduce_scatter | solution.py:1999
  221.7 39.9 %collective-permute-start.1 = (bf16[1,256,2048]{2,1,0:T(8,128)(2,1)}, bf16[1,256,2048]{2,1,0:T(8,128)(2,1)}, u32[]{:S(2)}, u32[]{:S(2)}) collective-permute-start(bf16[1,256,2048]{2,1,0:T(8,128)(2,1)} %bitcast.10), channel_id=1, source_target_pairs={{0,1},{1,0},{2,3},{3,2},{4,5},{5,4},{6,7},{7,6},{8,9},{9,8},{10,11... | collective-permute-start | bytes 3145736 | tf_op jit(solution)/shard_map/ppermute | solution.py:73
  222.8 38.4 %copy-start.1 = (bf16[256,2048]{1,0:T(8,128)(2,1)S(1)}, bf16[256,2048]{1,0:T(8,128)(2,1)}, u32[]{:S(2)}) copy-start(bf16[256,2048]{1,0:T(8,128)(2,1)} %get-tuple-element.101.stream_ref) | copy-start | bytes 3145732
  222.8 38.7 %copy-start.10 = (f32[1,2048]{1,0:T(1,128)S(1)}, f32[1,2048]{1,0:T(1,128)}, u32[]{:S(2)}) copy-start(f32[1,2048]{1,0:T(1,128)} %get-tuple-element.142) | copy-start | bytes 24580
  222.8 38.8 %copy-start.2 = (f32[256,2048]{1,0:T(8,128)S(1)}, f32[256,2048]{1,0:T(8,128)}, u32[]{:S(2)}) copy-start(f32[256,2048]{1,0:T(8,128)} %get-tuple-element.104.refs_12_) | copy-start | bytes 6291460
  260.8 3.1 copy-start.8
  260.8 3.1 copy-start
  260.8 3.1 copy-start.5
  260.8 17.3 %collective-permute-start.2 = (bf16[1,256,2048]{2,1,0:T(8,128)(2,1)}, bf16[1,256,2048]{2,1,0:T(8,128)(2,1)S(1)}, u32[]{:S(2)}, u32[]{:S(2)}) collective-permute-start(bf16[1,256,2048]{2,1,0:T(8,128)(2,1)} %bitcast.65), channel_id=1, source_target_pairs={{0,1},{1,0},{2,3},{3,2},{4,5},{5,4},{6,7},{7,6},{8,9},{9,8},{10,11... | collective-permute-start | bytes 3145736 | tf_op jit(solution)/shard_map/ppermute | solution.py:73
  269.8 8.3 %copy-start.9 = (f32[8,128]{1,0:T(8,128)S(1)}, f32[8,128]{1,0:T(8,128)}, u32[]{:S(2)}) copy-start(f32[8,128]{1,0:T(8,128)} %get-tuple-element.141) | copy-start | bytes 12292
  269.8 8.3 %copy-start.11 = (pred[8]{0:T(512)(128)(4,1)S(1)}, pred[8]{0:T(512)(128)(4,1)}, u32[]{:S(2)}) copy-start(pred[8]{0:T(512)(128)(4,1)} %constant.26.clone.1) | copy-start | bytes 28
  269.8 8.4 %copy-start.4 = (bf16[256,2048]{1,0:T(8,128)(2,1)S(1)}, bf16[256,2048]{1,0:T(8,128)(2,1)}, u32[]{:S(2)}) copy-start(bf16[256,2048]{1,0:T(8,128)(2,1)} %get-tuple-element.133) | copy-start | bytes 3145732
  279.0 1.6 copy-start.6
  279.1 2.8 copy-start.7
Sparse Core Ops, SparseCore 0:
  9.9 45.2 all-gather.2
  98.0 60.9 reduce-scatter.3
  161.2 63.1 reduce-scatter.5
  226.5 54.9 reduce-scatter.7
